TPU v7x, 32 devices: a whole 2x2x4 slice. The times are simulated.
32 devices in a mesh: groups: 2 (over x), node: 16 (over z, y, core).
Axes of the slice: x: 2, y: 2, z: 4, core: 2. Of those that a mesh axis runs over, the one named last changes fastest.
Arguments:
- grid_in: bfloat16 [16384, 1024], P(('groups', 'node')), parts along dimension 0, may hold values from -6 to 6
- mesh_in: bfloat16 [4096, 1024], P(('groups', 'node')), parts along dimension 0, may hold values from -6 to 6
- own_src: int32 [32768], P(('groups', 'node')), parts along dimension 0, may hold values from 0 to 511, as said below
- own_dst: int32 [32768], P(('groups', 'node')), parts along dimension 0, may hold values from 0 to 127
- side_src: int32 [131072], P(('groups', 'node')), parts along dimension 0, may hold values from 0 to 511, as said below
- side_dst: int32 [131072], P(('groups', 'node')), parts along dimension 0, may hold values from 0 to 127
- side_count: int32 [64], P(('groups', 'node')), parts along dimension 0, may hold values from 0 to 2048, as said below
- far_src: int32 [2048], P(('groups', 'node')), parts along dimension 0, may hold values from 0 to 511
- far_dst: int32 [2048], P(('groups', 'node')), parts along dimension 0, may hold values from 0 to 127
- far_count: int32 [512], P(('groups', 'node')), parts along dimension 0, may hold values from 0 to 4, as said below
- window: int32 [2, 4096], P(None, ('groups', 'node')), parts along dimension 1, may hold values from 1 to 128, as said below
- cotangent: bfloat16 [4096, 1024], P(('groups', 'node')), parts along dimension 0, may hold values from -6 to 6
- w_edge: bfloat16 [1024, 1024], replicated, may hold values from -0.09375 to 0.09375
- w_qkv: bfloat16 [1024, 3072], replicated, may hold values from -4 to 4
- w_out: bfloat16 [1024, 1024], replicated, may hold values from -0.1875 to 0.1875
Outputs:
- mesh_out: bfloat16 [4096, 1024], P(('groups', 'node')), parts along dimension 0
- mesh_grad: bfloat16 [4096, 1024], P(('groups', 'node')), parts along dimension 0
There are 2 independent parts, one for each index of `groups`. A program takes and returns all parts, laid end to end along the dimension named above; an argument that names none is the same for every part. Nothing has to cross between parts.
Inputs may be any that keep to these rules, and one draw needn't show every extreme that they name: `own_src`: each device's 1024 slots name every one of its 512 grid nodes exactly twice. `side_src`: slots toward the device before name grid nodes below 128; slots toward the device after name grid nodes from 384 on. `side_count`: the first device's count toward the device before it and the last device's count toward the device after it are 0, all others at least 512; one device sends 2048 live slots to both sides and receives 2048 from both. `far_count`: 0 where sender and receiver are the same or adjacent devices, at least 1 otherwise; one receiving device gets 4 live slots from every device not adjacent to it. `window`: both 1 and 128 occur in each row.
All inputs are finite; a program needn't handle non-finite values.
Results may differ from a plain program's by a relative error of at most 0.01.
Values may be sent and summed in bfloat16 or wider, within the bound.
No kernel may reach another device: no remote copies, remote signals or barrier semaphores. Data moves between devices by JAX's collectives and lax.ppermute only.
A program may use at most 128 MiB of HBM per device.

v0:
```python
import jax
import jax.numpy as jnp
from jax import lax
from jax.sharding import PartitionSpec as P

HEADS = 16
BAND = 128


def with_halo(cells, sides, width):
    for axis, dim in sides:
        count = lax.axis_size(axis)
        ends = count - 1
        head = lax.slice_in_dim(cells, 0, width, axis=dim)
        tail = lax.slice_in_dim(cells, cells.shape[dim] - width, cells.shape[dim], axis=dim)
        cells = jnp.concatenate(
            [
                lax.ppermute(tail, axis, [(i, (i + 1) % count) for i in range(ends)]),
                cells,
                lax.ppermute(head, axis, [((i + 1) % count, i) for i in range(ends)]),
            ],
            axis=dim,
        )
    return cells


def layer_stats(latent):
    values = latent.astype(jnp.float32)
    row_mean = jnp.mean(values, -1, keepdims=True)
    centred = values - row_mean
    variance = jnp.mean(centred * centred, -1, keepdims=True)
    inv_std = lax.rsqrt(variance + 1e-05)
    return (centred * inv_std, inv_std)


def window_mask(query_pos, key_pos, reach_back, reach_ahead, node_total):
    key_at = key_pos[None, :]
    query_at = query_pos[:, None]
    inside = (key_at >= 0) & (key_at < node_total)
    return (
        inside
        & (key_at >= query_at - reach_back[:, None])
        & (key_at <= query_at + reach_ahead[:, None])
    )


def attend_forward(query_rows, key_rows, value_rows, keep_mask, score_scale):
    scores = (
        jnp.einsum("qhe,khe->hqk", query_rows, key_rows, preferred_element_type=jnp.float32)
        * score_scale
    )
    scores = jnp.where(keep_mask[None], scores, -jnp.inf)
    row_max = jnp.max(scores, -1, keepdims=True)
    shifted = jnp.exp(scores - row_max)
    row_probs = shifted / jnp.sum(shifted, -1, keepdims=True)
    weights = row_probs.astype(jnp.bfloat16)
    output = jnp.einsum(
        "hqk,khe->qhe", weights, value_rows, preferred_element_type=jnp.float32
    ).astype(jnp.bfloat16)
    return (output, row_probs, weights)


def attend_backward(query_rows, key_rows, value_rows, row_probs, weights, grad_out, score_scale):
    grad_prob = jnp.einsum("qhe,khe->hqk", grad_out, value_rows, preferred_element_type=jnp.float32)
    grad_score = (
        row_probs * (grad_prob - jnp.sum(row_probs * grad_prob, -1, keepdims=True))
    ).astype(jnp.bfloat16)
    grad_query = (
        jnp.einsum("hqk,khe->qhe", grad_score, key_rows, preferred_element_type=jnp.float32)
        * score_scale
    )
    grad_key = (
        jnp.einsum("hqk,qhe->khe", grad_score, query_rows, preferred_element_type=jnp.float32)
        * score_scale
    )
    grad_value = jnp.einsum("hqk,qhe->khe", weights, grad_out, preferred_element_type=jnp.float32)
    return (grad_query, grad_key, grad_value)


def select_rows(indices, source_rows):
    onehot = (
        indices[:, None] == jnp.arange(source_rows.shape[0], dtype=jnp.int32)[None, :]
    ).astype(jnp.bfloat16)
    return jnp.dot(onehot, source_rows, preferred_element_type=jnp.float32).astype(jnp.bfloat16)


def land_rows(targets, messages, mesh_rows):
    landing = (jnp.arange(mesh_rows, dtype=jnp.int32)[:, None] == targets[None, :]).astype(
        jnp.bfloat16
    )
    return jnp.dot(landing, messages, preferred_element_type=jnp.float32)


def body(
    grid_in,
    mesh_in,
    own_src,
    own_dst,
    side_src,
    side_dst,
    side_count,
    far_src,
    far_dst,
    far_count,
    window,
    cotangent,
    w_edge,
    w_qkv,
    w_out,
):
    devices = lax.axis_size("node")
    own_index = lax.axis_index("node")
    grid_rows, channels = grid_in.shape
    mesh_rows = mesh_in.shape[0]
    head_count = HEADS
    head_dim = channels // head_count
    side_slots = side_src.shape[0] // 2
    band_width = BAND
    far_slots = far_src.shape[0]
    far_depth = far_slots // devices
    score_scale = head_dim ** (-0.5)
    node_total = devices * mesh_rows
    nothing = jnp.zeros((), jnp.bfloat16)
    projected = jnp.dot(grid_in, w_edge, preferred_element_type=jnp.float32).astype(jnp.bfloat16)
    active = jax.nn.gelu(projected.astype(jnp.float32), approximate=True).astype(jnp.bfloat16)
    aggregate = land_rows(own_dst, select_rows(own_src, active), mesh_rows)
    far_rank = jnp.arange(far_slots, dtype=jnp.int32) % far_depth
    far_live = far_rank < jnp.repeat(far_count, far_depth)
    far_payload = jnp.where(far_live[:, None], select_rows(far_src, active), nothing)
    far_targets = jnp.where(far_live, far_dst, mesh_rows)
    got_payload, got_targets = (
        lax.all_to_all(
            far_payload.reshape(devices, far_depth, channels),
            "node",
            split_axis=0,
            concat_axis=0,
            tiled=True,
        ),
        lax.all_to_all(
            far_targets.reshape(devices, far_depth), "node", split_axis=0, concat_axis=0, tiled=True
        ),
    )
    aggregate = aggregate + land_rows(
        got_targets.reshape(far_slots), got_payload.reshape(far_slots, channels), mesh_rows
    )
    side_rank = jnp.arange(2 * side_slots, dtype=jnp.int32) % side_slots
    side_live = side_rank < jnp.repeat(side_count, side_slots)
    low_band = active[:band_width]
    high_band = active[grid_rows - band_width :]
    band_local = jnp.concatenate(
        [side_src[:side_slots], side_src[side_slots:] - (grid_rows - band_width)], 0
    )
    low_payload = select_rows(band_local[:side_slots], low_band)
    high_payload = select_rows(band_local[side_slots:], high_band)
    side_payload = jnp.where(
        side_live[:, None], jnp.concatenate([low_payload, high_payload], 0), nothing
    )
    side_targets = jnp.where(side_live, side_dst, mesh_rows)
    near_payload = with_halo(side_payload, (("node", 0),), side_slots)
    near_targets = with_halo(side_targets, (("node", 0),), side_slots)
    incoming = jnp.concatenate([near_payload[:side_slots], near_payload[3 * side_slots :]], 0)
    incoming_targets = jnp.concatenate(
        [near_targets[:side_slots], near_targets[3 * side_slots :]], 0
    )
    aggregate = aggregate + land_rows(incoming_targets, incoming, mesh_rows)
    latent = (mesh_in.astype(jnp.float32) + aggregate).astype(jnp.bfloat16)
    normal, inv_std = layer_stats(latent)
    normed = normal.astype(jnp.bfloat16)
    qkv_rows = jnp.dot(normed, w_qkv, preferred_element_type=jnp.float32).astype(jnp.bfloat16)
    grad_att = lax.dot_general(
        cotangent, w_out, (((1,), (1,)), ((), ())), preferred_element_type=jnp.float32
    ).astype(jnp.bfloat16)
    query_rows = qkv_rows[:, :channels].reshape(mesh_rows, head_count, head_dim)
    widened = with_halo(qkv_rows[:, channels:], (("node", 0),), mesh_rows)
    key_rows = widened[:, :channels].reshape(3 * mesh_rows, head_count, head_dim)
    value_rows = widened[:, channels:].reshape(3 * mesh_rows, head_count, head_dim)
    query_pos = own_index * mesh_rows + jnp.arange(mesh_rows, dtype=jnp.int32)
    key_pos = own_index * mesh_rows - mesh_rows + jnp.arange(3 * mesh_rows, dtype=jnp.int32)
    keep_mask = window_mask(query_pos, key_pos, window[0], window[1], node_total)
    output, row_probs, weights = attend_forward(
        query_rows, key_rows, value_rows, keep_mask, score_scale
    )
    attention = output.reshape(mesh_rows, channels)
    grad_query, grad_key, grad_value = attend_backward(
        query_rows,
        key_rows,
        value_rows,
        row_probs,
        weights,
        grad_att.reshape(mesh_rows, head_count, head_dim),
        score_scale,
    )
    grad_kv = jnp.concatenate(
        [grad_key.reshape(3 * mesh_rows, channels), grad_value.reshape(3 * mesh_rows, channels)], 1
    )
    outer = jnp.concatenate([grad_kv[:mesh_rows], grad_kv[2 * mesh_rows :]], 0)
    returned = with_halo(outer, (("node", 0),), mesh_rows)
    own_kv = grad_kv[mesh_rows : 2 * mesh_rows] + returned[:mesh_rows] + returned[3 * mesh_rows :]
    grad_qkv = jnp.concatenate([grad_query.reshape(mesh_rows, channels), own_kv], 1).astype(
        jnp.bfloat16
    )
    mesh_out = (
        latent.astype(jnp.float32) + jnp.dot(attention, w_out, preferred_element_type=jnp.float32)
    ).astype(jnp.bfloat16)
    grad_normed = lax.dot_general(
        grad_qkv, w_qkv, (((1,), (1,)), ((), ())), preferred_element_type=jnp.float32
    )
    centred_grad = (
        grad_normed
        - jnp.mean(grad_normed, -1, keepdims=True)
        - normal * jnp.mean(grad_normed * normal, -1, keepdims=True)
    )
    mesh_grad = (cotangent.astype(jnp.float32) + inv_std * centred_grad).astype(jnp.bfloat16)
    return (mesh_out, mesh_grad)


def solution(mesh):
    placed = (
        P(("groups", "node"), None),
        P(("groups", "node"), None),
        P(("groups", "node")),
        P(("groups", "node")),
        P(("groups", "node")),
        P(("groups", "node")),
        P(("groups", "node")),
        P(("groups", "node")),
        P(("groups", "node")),
        P(("groups", "node")),
        P(None, ("groups", "node")),
        P(("groups", "node"), None),
        P(),
        P(),
        P(),
    )
    return jax.shard_map(
        body,
        mesh=mesh,
        in_specs=placed,
        out_specs=(P(("groups", "node"), None), P(("groups", "node"), None)),
        check_vma=False,
    )
```

profile of v0, /device:TPU:1, one launch (start us, length us, event | category | flops | bytes accessed | tf_op | source)
XLA Modules:
  0.0 190.5 jit_solution(16395404084957798534)
XLA Ops:
  0.6 0.9 fusion.76
  1.5 0.7 copy-done
  2.3 2.9 %fusion.11 = bf16[512,1024]{1,0:T(8,128)(2,1)S(1)} fusion(bf16[512,1024]{1,0:T(8,128)(2,1)} %param.15, bf16[1024,1024]{1,0:T(8,128)(2,1)S(1)} %copy-done), kind=kOutput, calls=%fused_computation.27 | convolution fusion | flops 1079508992 | bytes 4194304 | tf_op jit(solution)/shard_map/dot_general | solution.py:124
  5.1 1.5 convolution_convert_fusion
  6.7 1.5 convolution_convert_fusion.1
  8.3 0.1 broadcast_bitcast_fusion
  8.4 4.0 %maximum_select_fusion = bf16[4096,1024]{1,0:T(8,128)(2,1)S(1)} fusion(bf16[2048,1024]{1,0:T(8,128)(2,1)S(1)} %convolution_convert_fusion, bf16[2048,1024]{1,0:T(8,128)(2,1)S(1)} %convolution_convert_fusion.1, pred[4096]{0:T(1024)(128)(4,1)S(1)} %get-tuple-element.5), kind=kLoop, calls=%fused_computation.1 | loop fusion | flops 20971520 | bytes 16781312 | tf_op jit(solution)/shard_map/jit(_where)/select_n | solution.py:155
  12.5 3.7 %fusion.73 = (bf16[2048,1024]{1,0:T(8,128)(2,1)}, bf16[2048,1024]{1,0:T(8,128)(2,1)}) fusion(bf16[4096,1024]{1,0:T(8,128)(2,1)S(1)} %maximum_select_fusion), kind=kLoop, calls=%fused_computation.116 | loop fusion | bytes 16777216 | tf_op jit(solution)/shard_map/slice | solution.py:15
  16.2 2.0 %collective-permute-start.3 = (bf16[2048,1024]{1,0:T(8,128)(2,1)}, bf16[2048,1024]{1,0:T(8,128)(2,1)}, u32[]{:S(2)}, u32[]{:S(2)}) collective-permute-start(bf16[2048,1024]{1,0:T(8,128)(2,1)} %get-tuple-element.9), channel_id=1, source_target_pairs={{1,0},{2,1},{3,2},{4,3},{5,4},{6,5},{7,6},{8,7},{9,8},{10,9},{11,1... | collective-permute-start | bytes 12582920 | tf_op jit(solution)/shard_map/ppermute | solution.py:20
  18.2 4.5 %collective-permute-start.2 = (bf16[2048,1024]{1,0:T(8,128)(2,1)}, bf16[2048,1024]{1,0:T(8,128)(2,1)}, u32[]{:S(2)}, u32[]{:S(2)}) collective-permute-start(bf16[2048,1024]{1,0:T(8,128)(2,1)} %get-tuple-element.8), channel_id=1, source_target_pairs={{0,1},{1,2},{2,3},{3,4},{4,5},{5,6},{6,7},{7,8},{8,9},{9,10},{10,1... | collective-permute-start | bytes 12582920 | tf_op jit(solution)/shard_map/ppermute | solution.py:18
  22.7 0.1 broadcast_in_dim.44
  22.7 0.1 reshape.206
  22.8 0.5 broadcast_select_fusion.1
  23.4 0.7 all_to_all.9
  24.1 7.2 %all-to-all-start = ((s32[16,1,4]{2,1,0:T(1,128)}), s32[16,1,4]{2,1,0:T(1,128)S(1)}, u32[]{:S(2)}, u32[]{:S(2)}) async-start(s32[16,1,4]{2,1,0:T(1,128)} %bitcast), calls=%async_computation | async-start | bytes 16384 | tf_op jit(solution)/shard_map/all_to_all | solution.py:139
  31.2 0.6 fusion.75
  31.8 2.0 %collective-permute-start.1 = (s32[2048]{0:T(1024)}, s32[2048]{0:T(1024)}, u32[]{:S(2)}, u32[]{:S(2)}) collective-permute-start(s32[2048]{0:T(1024)} %get-tuple-element.15), channel_id=1, source_target_pairs={{1,0},{2,1},{3,2},{4,3},{5,4},{6,5},{7,6},{8,7},{9,8},{10,9},{11,1... | collective-permute-start | bytes 24584 | tf_op jit(solution)/shard_map/ppermute | solution.py:20
  33.9 3.7 %collective-permute-start = (s32[2048]{0:T(1024)S(1)}, s32[2048]{0:T(1024)}, u32[]{:S(2)}, u32[]{:S(2)}) collective-permute-start(s32[2048]{0:T(1024)S(1)} %get-tuple-element.14), channel_id=1, source_target_pairs={{0,1},{1,2},{2,3},{3,4},{4,5},{5,6},{6,7},{7,8},{8,9},{9,10},{10,1... | collective-permute-start | bytes 24584 | tf_op jit(solution)/shard_map/ppermute | solution.py:18
  37.6 2.4 %fusion.12 = f32[128,1024]{1,0:T(8,128)} fusion(bf16[512,1024]{1,0:T(8,128)(2,1)S(1)} %fusion.11, s32[1024]{0:T(1024)S(1)} %copy-done.15, s32[1024]{0:T(1024)S(1)} %copy-done.16), kind=kOutput, calls=%fused_computation.29 | convolution fusion | flops 1343881216 | bytes 1581056 | tf_op jit(solution)/shard_map/dot_general | solution.py:91
  39.9 1.0 fusion.32
  41.0 0.7 reshape.207
  41.7 70.8 %all-to-all-done = s32[16,1,4]{2,1,0:T(1,128)S(1)} async-done(((s32[16,1,4]{2,1,0:T(1,128)}), s32[16,1,4]{2,1,0:T(1,128)S(1)}, u32[]{:S(2)}, u32[]{:S(2)}) %all-to-all-start) | async-done | bytes 288 | tf_op jit(solution)/shard_map/all_to_all | solution.py:139
  112.5 6.2 %all-to-all-start.1 = ((bf16[16,4,1024]{2,1,0:T(4,128)(2,1)}), bf16[16,4,1024]{2,1,0:T(4,128)(2,1)S(1)}, u32[]{:S(2)}, u32[]{:S(2)}) async-start(bf16[16,4,1024]{2,1,0:T(4,128)(2,1)} %reshape.207), calls=%async_computation.1 | async-start | bytes 262144 | tf_op jit(solution)/shard_map/all_to_all | solution.py:132
  118.7 0.8 convolution_convert_fusion.4
  119.6 0.8 copy.33
  120.4 0.6 broadcast.177
  121.0 0.7 reduce.3
  121.7 0.1 eq.104
  121.8 0.7 pad_add_fusion
  122.5 3.0 %all-to-all-done.1 = bf16[16,4,1024]{2,1,0:T(4,128)(2,1)S(1)} async-done(((bf16[16,4,1024]{2,1,0:T(4,128)(2,1)}), bf16[16,4,1024]{2,1,0:T(4,128)(2,1)S(1)}, u32[]{:S(2)}, u32[]{:S(2)}) %all-to-all-start.1) | async-done | bytes 131104 | tf_op jit(solution)/shard_map/all_to_all | solution.py:132
  125.6 0.2 convolution_add_fusion
  125.9 5.0 %fusion.77 = (f32[128]{0:T(128)S(1)}, f32[128,1024]{1,0:T(8,128)S(1)}) fusion(f32[128,1024]{1,0:T(8,128)S(1)} %convolution_add_fusion, bf16[2048,1024]{1,0:T(8,128)(2,1)} %collective-permute-done.3, bf16[2048,1024]{1,0:T(8,128)(2,1)} %collective-permute-done.2, s32[4096]{0:T(1024)S(1)} %pad_add_fusion, bf16[128,1024]{1,0:T(8,128)(2,1)} %param.16), kind=kOutput, calls=%fused_computation.120 | convolution fusion | flops 1091829632 | bytes 9716224 | tf_op jit(solution)/shard_map/dot_general | solution.py:91
  130.9 0.2 multiply_reduce_fusion.2
  131.1 1.1 convolution_convert_fusion.2
  132.2 3.1 %collective-permute-start.5 = (bf16[128,2048]{1,0:T(8,128)(2,1)S(1)}, bf16[128,2048]{1,0:T(8,128)(2,1)}, u32[]{:S(2)}, u32[]{:S(2)}) collective-permute-start(bf16[128,2048]{1,0:T(8,128)(2,1)S(1)} %slice.74), channel_id=1, source_target_pairs={{1,0},{2,1},{3,2},{4,3},{5,4},{6,5},{7,6},{8,7},{9,8},{10,9},{11,1... | collective-permute-start | bytes 1572872 | tf_op jit(solution)/shard_map/ppermute | solution.py:20
  135.3 2.7 %collective-permute-start.4 = (bf16[128,2048]{1,0:T(8,128)(2,1)S(1)}, bf16[128,2048]{1,0:T(8,128)(2,1)}, u32[]{:S(2)}, u32[]{:S(2)}) collective-permute-start(bf16[128,2048]{1,0:T(8,128)(2,1)S(1)} %slice.74), channel_id=1, source_target_pairs={{0,1},{1,2},{2,3},{3,4},{4,5},{5,6},{6,7},{7,8},{8,9},{9,10},{10,1... | collective-permute-start | bytes 1572872 | tf_op jit(solution)/shard_map/ppermute | solution.py:18
  138.0 0.1 compare_and_fusion
  138.2 0.8 copy.31
  139.0 3.8 %collective-permute-done.5 = bf16[128,2048]{1,0:T(8,128)(2,1)} collective-permute-done((bf16[128,2048]{1,0:T(8,128)(2,1)S(1)}, bf16[128,2048]{1,0:T(8,128)(2,1)}, u32[]{:S(2)}, u32[]{:S(2)}) %collective-permute-start.5) | collective-permute-done | bytes 524320 | tf_op jit(solution)/shard_map/ppermute | solution.py:20
  142.8 4.9 %collective-permute-done.4 = bf16[128,2048]{1,0:T(8,128)(2,1)} collective-permute-done((bf16[128,2048]{1,0:T(8,128)(2,1)S(1)}, bf16[128,2048]{1,0:T(8,128)(2,1)}, u32[]{:S(2)}, u32[]{:S(2)}) %collective-permute-start.4) | collective-permute-done | bytes 524320 | tf_op jit(solution)/shard_map/ppermute | solution.py:18
  147.7 1.3 pad_maximum_fusion
  149.1 1.0 fusion.74
  150.1 1.2 copy.30
  151.2 1.5 copy.32
  152.7 3.7 %fusion.78 = (f32[16,128]{1,0:T(8,128)S(1)}, f32[16,128,384]{2,1,0:T(8,128)}) fusion(pred[128,384]{1,0:T(8,128)(4,1)S(1)} %compare_and_fusion, bf16[128,16,64]{0,2,1:T(8,128)(2,1)} %bitcast.58, bf16[384,16,64]{0,2,1:T(8,128)(2,1)S(1)} %bitcast.55), kind=kOutput, calls=%fused_computation.121 | convolution fusion | flops 103809408 | bytes 4251648 | tf_op jit(solution)/shard_map/sub | solution.py:54
  156.4 2.6 %fusion.45 = f32[16,64,384]{2,1,0:T(8,128)S(1)} fusion(bf16[128,16,64]{0,2,1:T(8,128)(2,1)} %bitcast.63, f32[16,128,384]{2,1,0:T(8,128)} %get-tuple-element.23, f32[16,128]{1,0:T(8,128)S(1)} %get-tuple-element.22), kind=kOutput, calls=%fused_computation.67 | convolution fusion | flops 102236160 | bytes 4988928 | tf_op jit(solution)/shard_map/hqk,qhe->khe/dot_general | solution.py:76
  159.0 0.3 copy-done.3
  159.3 0.2 copy-done.7
  159.5 0.1 copy-done.9
  159.6 1.0 multiply_reduce_fusion
  160.6 0.7 multiply_convert_fusion
  161.4 0.2 copy-done.6
  161.6 0.4 convolution_multiply_fusion
  162.0 0.1 fusion.33
  162.1 1.9 %collective-permute-start.7 = (f32[128,2048]{0,1:T(8,128)S(1)}, f32[128,2048]{0,1:T(8,128)S(1)}, u32[]{:S(2)}, u32[]{:S(2)}) collective-permute-start(f32[128,2048]{0,1:T(8,128)S(1)} %get-tuple-element.11), channel_id=1, source_target_pairs={{1,0},{2,1},{3,2},{4,3},{5,4},{6,5},{7,6},{8,7},{9,8},{10,9},{11,1... | collective-permute-start | bytes 3145736 | tf_op jit(solution)/shard_map/ppermute | solution.py:20
  164.1 4.5 %collective-permute-start.6 = (f32[128,2048]{0,1:T(8,128)S(1)}, f32[128,2048]{0,1:T(8,128)S(1)}, u32[]{:S(2)}, u32[]{:S(2)}) collective-permute-start(f32[128,2048]{0,1:T(8,128)S(1)} %get-tuple-element.10), channel_id=1, source_target_pairs={{0,1},{1,2},{2,3},{3,4},{4,5},{5,6},{6,7},{7,8},{8,9},{9,10},{10,1... | collective-permute-start | bytes 3145736 | tf_op jit(solution)/shard_map/ppermute | solution.py:18
  168.6 0.8 fusion.31
  169.4 0.9 convolution_convert_fusion.5
  170.3 1.2 fusion.30
  171.5 7.6 %collective-permute-done.7 = f32[128,2048]{0,1:T(8,128)S(1)} collective-permute-done((f32[128,2048]{0,1:T(8,128)S(1)}, f32[128,2048]{0,1:T(8,128)S(1)}, u32[]{:S(2)}, u32[]{:S(2)}) %collective-permute-start.7) | collective-permute-done | bytes 1048608 | tf_op jit(solution)/shard_map/ppermute | solution.py:20
  179.1 7.8 %collective-permute-done.6 = f32[128,2048]{0,1:T(8,128)S(1)} collective-permute-done((f32[128,2048]{0,1:T(8,128)S(1)}, f32[128,2048]{0,1:T(8,128)S(1)}, u32[]{:S(2)}, u32[]{:S(2)}) %collective-permute-start.6) | collective-permute-done | bytes 1048608 | tf_op jit(solution)/shard_map/ppermute | solution.py:18
  186.9 0.1 fusion.37
  187.1 2.4 %fusion.70 = (f32[128]{0:T(128)S(1)}, f32[128]{0:T(128)S(1)}, f32[128,1024]{1,0:T(8,128)S(1)}) fusion(f32[128]{0:T(128)S(1)} %add_rsqrt_fusion, f32[128,1024]{1,0:T(8,128)S(1)} %get-tuple-element.21, f32[128]{0:T(128)S(1)} %broadcast_multiply_fusion.2, bf16[1024,3072]{1,0:T(8,128)(2,1)S(1)} %bitcast.50, bf16[128,2048]{0,1:T(8,128)(2,1)S(1)} %fusion.37, ...), kind=kOutput, calls=%fused_computation.115 | convolution fusion | flops 807534336 | bytes 8128512 | tf_op jit(solution)/shard_map/dot_general | solution.py:205
  189.5 1.0 add_convert_fusion
  (54 shorter events, 0.3 us)
Async XLA Ops:
  0.6 1.6 copy-start
  6.7 1.6 copy-start.12
  6.7 1.7 copy-start.10
  12.4 10.3 %copy-start.13 = (s32[16]{0:T(128)S(1)}, s32[16]{0:T(128)}, u32[]{:S(2)}) copy-start(s32[16]{0:T(128)} %param.24) | copy-start | bytes 196
  12.4 10.4 %copy-start.14 = (s32[64]{0:T(128)S(1)}, s32[64]{0:T(128)}, u32[]{:S(2)}) copy-start(s32[64]{0:T(128)} %param.23) | copy-start | bytes 772
  12.4 25.1 %copy-start.15 = (s32[1024]{0:T(1024)S(1)}, s32[1024]{0:T(1024)}, u32[]{:S(2)}) copy-start(s32[1024]{0:T(1024)} %param.17) | copy-start | bytes 12292
  12.4 25.1 %copy-start.16 = (s32[1024]{0:T(1024)S(1)}, s32[1024]{0:T(1024)}, u32[]{:S(2)}) copy-start(s32[1024]{0:T(1024)} %param.18) | copy-start | bytes 12292
  16.2 109.6 %collective-permute-start.3 = (bf16[2048,1024]{1,0:T(8,128)(2,1)}, bf16[2048,1024]{1,0:T(8,128)(2,1)}, u32[]{:S(2)}, u32[]{:S(2)}) collective-permute-start(bf16[2048,1024]{1,0:T(8,128)(2,1)} %get-tuple-element.9), channel_id=1, source_target_pairs={{1,0},{2,1},{3,2},{4,3},{5,4},{6,5},{7,6},{8,7},{9,8},{10,9},{11,1... | collective-permute-start | bytes 12582920 | tf_op jit(solution)/shard_map/ppermute | solution.py:20
  18.2 107.7 %collective-permute-start.2 = (bf16[2048,1024]{1,0:T(8,128)(2,1)}, bf16[2048,1024]{1,0:T(8,128)(2,1)}, u32[]{:S(2)}, u32[]{:S(2)}) collective-permute-start(bf16[2048,1024]{1,0:T(8,128)(2,1)} %get-tuple-element.8), channel_id=1, source_target_pairs={{0,1},{1,2},{2,3},{3,4},{4,5},{5,6},{6,7},{7,8},{8,9},{9,10},{10,1... | collective-permute-start | bytes 12582920 | tf_op jit(solution)/shard_map/ppermute | solution.py:18
  24.1 88.4 %all-to-all-start = ((s32[16,1,4]{2,1,0:T(1,128)}), s32[16,1,4]{2,1,0:T(1,128)S(1)}, u32[]{:S(2)}, u32[]{:S(2)}) async-start(s32[16,1,4]{2,1,0:T(1,128)} %bitcast), calls=%async_computation | async-start | bytes 16384 | tf_op jit(solution)/shard_map/all_to_all | solution.py:139
  31.8 90.0 %collective-permute-start.1 = (s32[2048]{0:T(1024)}, s32[2048]{0:T(1024)}, u32[]{:S(2)}, u32[]{:S(2)}) collective-permute-start(s32[2048]{0:T(1024)} %get-tuple-element.15), channel_id=1, source_target_pairs={{1,0},{2,1},{3,2},{4,3},{5,4},{6,5},{7,6},{8,7},{9,8},{10,9},{11,1... | collective-permute-start | bytes 24584 | tf_op jit(solution)/shard_map/ppermute | solution.py:20
  33.8 84.8 %copy-start.2 = (bf16[1024,1024]{1,0:T(8,128)(2,1)S(1)}, bf16[1024,1024]{1,0:T(8,128)(2,1)}, u32[]{:S(2)}) copy-start(bf16[1024,1024]{1,0:T(8,128)(2,1)} %param.29) | copy-start | bytes 6291460
  33.9 84.8 %copy-start.4 = (bf16[128,1024]{1,0:T(8,128)(2,1)S(1)}, bf16[128,1024]{1,0:T(8,128)(2,1)}, u32[]{:S(2)}) copy-start(bf16[128,1024]{1,0:T(8,128)(2,1)} %param.26) | copy-start | bytes 786436
  33.9 87.9 %collective-permute-start = (s32[2048]{0:T(1024)S(1)}, s32[2048]{0:T(1024)}, u32[]{:S(2)}, u32[]{:S(2)}) collective-permute-start(s32[2048]{0:T(1024)S(1)} %get-tuple-element.14), channel_id=1, source_target_pairs={{0,1},{1,2},{2,3},{3,4},{4,5},{5,6},{6,7},{7,8},{8,9},{9,10},{10,1... | collective-permute-start | bytes 24584 | tf_op jit(solution)/shard_map/ppermute | solution.py:18
  41.0 84.6 %copy-start.8 = (f32[128,1024]{1,0:T(8,128)S(1)}, f32[128,1024]{1,0:T(8,128)}, u32[]{:S(2)}) copy-start(f32[128,1024]{1,0:T(8,128)} %fusion.12) | copy-start | bytes 1572868
  112.5 13.1 %all-to-all-start.1 = ((bf16[16,4,1024]{2,1,0:T(4,128)(2,1)}), bf16[16,4,1024]{2,1,0:T(4,128)(2,1)S(1)}, u32[]{:S(2)}, u32[]{:S(2)}) async-start(bf16[16,4,1024]{2,1,0:T(4,128)(2,1)} %reshape.207), calls=%async_computation.1 | async-start | bytes 262144 | tf_op jit(solution)/shard_map/all_to_all | solution.py:132
  125.6 5.5 %slice-start = ((s8[6291456]{0:T(1024)(128)(4,1)}), s8[4194304]{0:T(1024)(128)(4,1)S(1)}, s32[]{:S(2)}) async-start(s8[6291456]{0:T(1024)(128)(4,1)} %bitcast.47), calls=%async_computation.2 | async-start | bytes 8388608
  125.8 5.3 %slice-start.1 = ((s8[6291456]{0:T(1024)(128)(4,1)}), s8[2097152]{0:T(1024)(128)(4,1)S(1)}, s32[]{:S(2)}) async-start(s8[6291456]{0:T(1024)(128)(4,1)} %bitcast.47), calls=%async_computation.3 | async-start | bytes 4194304
  131.1 6.9 %copy-start.11 = (s32[2,128]{1,0:T(2,128)S(1)}, s32[2,128]{1,0:T(2,128)}, u32[]{:S(2)}) copy-start(s32[2,128]{1,0:T(2,128)} %param.25) | copy-start | bytes 3076
  132.2 10.6 %collective-permute-start.5 = (bf16[128,2048]{1,0:T(8,128)(2,1)S(1)}, bf16[128,2048]{1,0:T(8,128)(2,1)}, u32[]{:S(2)}, u32[]{:S(2)}) collective-permute-start(bf16[128,2048]{1,0:T(8,128)(2,1)S(1)} %slice.74), channel_id=1, source_target_pairs={{1,0},{2,1},{3,2},{4,3},{5,4},{6,5},{7,6},{8,7},{9,8},{10,9},{11,1... | collective-permute-start | bytes 1572872 | tf_op jit(solution)/shard_map/ppermute | solution.py:20
  135.3 12.4 %collective-permute-start.4 = (bf16[128,2048]{1,0:T(8,128)(2,1)S(1)}, bf16[128,2048]{1,0:T(8,128)(2,1)}, u32[]{:S(2)}, u32[]{:S(2)}) collective-permute-start(bf16[128,2048]{1,0:T(8,128)(2,1)S(1)} %slice.74), channel_id=1, source_target_pairs={{0,1},{1,2},{2,3},{3,4},{4,5},{5,6},{6,7},{7,8},{8,9},{9,10},{10,1... | collective-permute-start | bytes 1572872 | tf_op jit(solution)/shard_map/ppermute | solution.py:18
  156.4 2.9 %copy-start.3 = (f32[16,128,384]{2,1,0:T(8,128)S(1)}, f32[16,128,384]{2,1,0:T(8,128)}, u32[]{:S(2)}) copy-start(f32[16,128,384]{2,1,0:T(8,128)} %get-tuple-element.23) | copy-start | bytes 9437188
  156.4 3.1 %copy-start.7 = (bf16[384,1024]{0,1:T(8,128)(2,1)S(1)}, bf16[384,1024]{0,1:T(8,128)(2,1)}, u32[]{:S(2)}) copy-start(bf16[384,1024]{0,1:T(8,128)(2,1)} %copy.30) | copy-start | bytes 2359300
  156.4 3.2 %copy-start.9 = (bf16[128,1024]{0,1:T(8,128)(2,1)S(1)}, bf16[128,1024]{0,1:T(8,128)(2,1)}, u32[]{:S(2)}) copy-start(bf16[128,1024]{0,1:T(8,128)(2,1)} %copy.33) | copy-start | bytes 786436
  160.6 1.0 copy-start.6
  162.1 17.0 %collective-permute-start.7 = (f32[128,2048]{0,1:T(8,128)S(1)}, f32[128,2048]{0,1:T(8,128)S(1)}, u32[]{:S(2)}, u32[]{:S(2)}) collective-permute-start(f32[128,2048]{0,1:T(8,128)S(1)} %get-tuple-element.11), channel_id=1, source_target_pairs={{1,0},{2,1},{3,2},{4,3},{5,4},{6,5},{7,6},{8,7},{9,8},{10,9},{11,1... | collective-permute-start | bytes 3145736 | tf_op jit(solution)/shard_map/ppermute | solution.py:20
  164.1 22.8 %collective-permute-start.6 = (f32[128,2048]{0,1:T(8,128)S(1)}, f32[128,2048]{0,1:T(8,128)S(1)}, u32[]{:S(2)}, u32[]{:S(2)}) collective-permute-start(f32[128,2048]{0,1:T(8,128)S(1)} %get-tuple-element.10), channel_id=1, source_target_pairs={{0,1},{1,2},{2,3},{3,4},{4,5},{5,6},{6,7},{7,8},{8,9},{9,10},{10,1... | collective-permute-start | bytes 3145736 | tf_op jit(solution)/shard_map/ppermute | solution.py:18
  168.6 18.5 %slice-start.2 = ((s8[6291456]{0:T(1024)(128)(4,1)}), s8[4194304]{0:T(1024)(128)(4,1)S(1)}, s32[]{:S(2)}) async-start(s8[6291456]{0:T(1024)(128)(4,1)} %bitcast.49), calls=%async_computation.4 | async-start | bytes 8388608
  169.4 17.7 %slice-start.3 = ((s8[6291456]{0:T(1024)(128)(4,1)}), s8[2097152]{0:T(1024)(128)(4,1)S(1)}, s32[]{:S(2)}) async-start(s8[6291456]{0:T(1024)(128)(4,1)} %bitcast.49), calls=%async_computation.5 | async-start | bytes 4194304
  187.0 3.4 %copy-start.1 = (bf16[1024,1024]{1,0:T(8,128)(2,1)S(1)}, bf16[1024,1024]{1,0:T(8,128)(2,1)}, u32[]{:S(2)}) copy-start(bf16[1024,1024]{1,0:T(8,128)(2,1)} %param.27) | copy-start | bytes 6291460
  187.1 2.4 %copy-start.5 = (bf16[128,1024]{1,0:T(8,128)(2,1)S(1)}, bf16[128,1024]{1,0:T(8,128)(2,1)}, u32[]{:S(2)}) copy-start(bf16[128,1024]{1,0:T(8,128)(2,1)} %param.26) | copy-start | bytes 786436
where the time goes:
time: 193 us; the launch traced here: 190 us
  waiting for transfers between devices  98 us (51%)
  starting transfers between devices  37.7 us (20%)
  matrix products  29.4 us (15%)
  local copies, waits for them, and re-layouts  13.7 us (7%)
  other arithmetic  10.5 us (5%)
    all_to_all x1, waiting for transfers between devices, body(): lax.all_to_all(far_targets.reshape(devices, far_depth), 'node', split_axi...  70.8 us
    ppermute x4, starting transfers between devices, with_halo(): lax.ppermute(tail, axis, [(i, (i + 1) % count) for i in range(ends)])  15.3 us
    ppermute x4, waiting for transfers between devices, with_halo(): lax.ppermute(tail, axis, [(i, (i + 1) % count) for i in range(ends)])  12.7 us
    ppermute x4, waiting for transfers between devices, with_halo(): lax.ppermute(head, axis, [((i + 1) % count, i) for i in range(ends)])  11.4 us
    ppermute x4, starting transfers between devices, with_halo(): lax.ppermute(head, axis, [((i + 1) % count, i) for i in range(ends)])  8.95 us
    dot_general x3, matrix products, land_rows(): return jnp.dot(landing, messages, preferred_element_type=jnp.float32)  7.56 us
    all_to_all x1, starting transfers between devices, body(): lax.all_to_all(far_targets.reshape(devices, far_depth), 'node', split_axi...  7.18 us
    all_to_all x1, starting transfers between devices, body(): lax.all_to_all(far_payload.reshape(devices, far_depth, channels), 'node',...  6.19 us
  transfers between devices with their start and end apart: 10, of which 6 were waited for; matrix products, arithmetic and copies ran while one was open for 7% of the time, Pallas kernels for 0%

commit v1 on v0

v1 whole, which is shorter than its diff:
```python
import jax
import jax.numpy as jnp
from jax import lax
from jax.sharding import PartitionSpec as P

HEADS = 16
BAND = 128
F32 = jnp.float32
BF16 = jnp.bfloat16


def exchange(toward_low, toward_high, axis):
    ends = lax.axis_size(axis) - 1
    from_high = lax.ppermute(toward_low, axis, [(i + 1, i) for i in range(ends)])
    from_low = lax.ppermute(toward_high, axis, [(i, i + 1) for i in range(ends)])
    return from_low, from_high


def onehot_cols(indices, rows):
    return (jnp.arange(rows, dtype=jnp.int32)[:, None] == indices[None, :].astype(jnp.int32)).astype(
        BF16
    )


def edge_counts(dst, src, dst_rows, src_rows):
    return lax.dot_general(
        onehot_cols(dst, dst_rows),
        onehot_cols(src, src_rows),
        (((1,), (1,)), ((), ())),
        preferred_element_type=F32,
    )


def exact_halves(counts):
    upper = counts.astype(BF16)
    lower = (counts - upper.astype(F32)).astype(BF16)
    return upper, lower


def activate(rows, w_edge):
    projected = jnp.dot(rows, w_edge, preferred_element_type=F32).astype(BF16)
    return jax.nn.gelu(projected.astype(F32), approximate=True).astype(BF16)


def layer_stats(latent):
    values = latent.astype(F32)
    row_mean = jnp.mean(values, -1, keepdims=True)
    centred = values - row_mean
    variance = jnp.mean(centred * centred, -1, keepdims=True)
    inv_std = lax.rsqrt(variance + 1e-05)
    return (centred * inv_std, inv_std)


def body(
    grid_in,
    mesh_in,
    own_src,
    own_dst,
    side_src,
    side_dst,
    side_count,
    far_src,
    far_dst,
    far_count,
    window,
    cotangent,
    w_edge,
    w_qkv,
    w_out,
):
    devices = lax.axis_size("node")
    own_index = lax.axis_index("node")
    grid_rows, channels = grid_in.shape
    mesh_rows = mesh_in.shape[0]
    heads = HEADS
    head_dim = channels // heads
    side_slots = side_src.shape[0] // 2
    far_slots = far_src.shape[0]
    far_depth = far_slots // devices
    scale = head_dim ** (-0.5)

    far_live = jnp.arange(far_slots, dtype=jnp.int32) % far_depth < jnp.repeat(far_count, far_depth)
    far_target = jnp.where(far_live, far_dst, mesh_rows).astype(BF16)
    far_rows = lax.dot_general(
        onehot_cols(far_src, grid_rows),
        grid_in,
        (((0,), (0,)), ((), ())),
        preferred_element_type=F32,
    ).astype(BF16)
    far_message = jnp.concatenate(
        [far_rows, jnp.broadcast_to(far_target[:, None], (far_slots, 128))], 1
    )

    def side_message(k, rows, src):
        live = jnp.arange(side_slots, dtype=jnp.int32) < side_count[k]
        dst = jnp.where(live, side_dst[k * side_slots : (k + 1) * side_slots], mesh_rows)
        meta = jnp.concatenate([src, dst, window.reshape(-1)]).astype(BF16)
        meta_rows = -(-meta.shape[0] // (16 * channels)) * 16
        meta = jnp.pad(meta, (0, meta_rows * channels - meta.shape[0])).reshape(meta_rows, channels)
        return jnp.concatenate([rows, cotangent, meta], 0)

    toward_low = side_message(0, grid_in[:BAND], side_src[:side_slots])
    toward_high = side_message(
        1, grid_in[grid_rows - BAND :], side_src[side_slots:] - (grid_rows - BAND)
    )
    from_low, from_high = exchange(toward_low, toward_high, "node")
    got_far = lax.all_to_all(
        far_message.reshape(devices, far_depth, channels + 128),
        "node",
        split_axis=0,
        concat_axis=0,
        tiled=True,
    ).reshape(far_slots, channels + 128)

    own_active = activate(grid_in, w_edge)
    own_counts = edge_counts(own_dst, own_src, mesh_rows, grid_rows).astype(BF16)
    aggregate = jnp.dot(own_counts, own_active, preferred_element_type=F32)

    def unpack(message):
        meta = message[BAND + mesh_rows :].reshape(-1)
        src = meta[:side_slots]
        dst = meta[side_slots : 2 * side_slots]
        reach = meta[2 * side_slots : 2 * side_slots + 2 * mesh_rows].astype(jnp.int32)
        return message[BAND : BAND + mesh_rows], src, dst, reach.reshape(2, mesh_rows)

    low_cot, low_src, low_dst, low_window = unpack(from_low)
    high_cot, high_src, high_dst, high_window = unpack(from_high)
    band_active = activate(jnp.concatenate([from_low[:BAND], from_high[:BAND]], 0), w_edge)
    low_upper, low_lower = exact_halves(edge_counts(low_dst, low_src, mesh_rows, BAND))
    high_upper, high_lower = exact_halves(edge_counts(high_dst, high_src, mesh_rows, BAND))
    side_counts = jnp.concatenate([low_upper, high_upper, low_lower, high_lower], 1)
    aggregate = aggregate + jnp.dot(
        side_counts, jnp.concatenate([band_active, band_active], 0), preferred_element_type=F32
    )

    far_active = activate(got_far[:, :channels], w_edge)
    far_landing = onehot_cols(got_far[:, channels], mesh_rows)
    aggregate = aggregate + jnp.dot(far_landing, far_active, preferred_element_type=F32)

    latent = (mesh_in.astype(F32) + aggregate).astype(BF16)
    normal, inv_std = layer_stats(latent)
    normed = normal.astype(BF16)
    low_normed, high_normed = exchange(normed, normed, "node")

    all_cot = jnp.concatenate([low_cot, cotangent, high_cot], 0)
    grad_att = lax.dot_general(
        all_cot, w_out, (((1,), (1,)), ((), ())), preferred_element_type=F32
    ).astype(BF16)
    grad_heads = grad_att.reshape(3 * mesh_rows, heads, head_dim)

    all_normed = jnp.concatenate([low_normed, normed, high_normed], 0)
    qkv_rows = jnp.dot(all_normed, w_qkv, preferred_element_type=F32).astype(BF16)
    qkv_heads = qkv_rows.reshape(3 * mesh_rows, 3, heads, head_dim)
    query_all, key_all, value_all = qkv_heads[:, 0], qkv_heads[:, 1], qkv_heads[:, 2]
    own = slice(mesh_rows, 2 * mesh_rows)

    place = jnp.arange(3 * mesh_rows, dtype=jnp.int32)
    first = (own_index - 1) * mesh_rows
    inside = (place + first >= 0) & (place + first < devices * mesh_rows)
    all_window = jnp.concatenate([low_window, window, high_window], 1)
    reach_from = place - all_window[0]
    reach_to = place + all_window[1]

    def keep(keys, queries):
        return (
            (place[keys][None, :] >= reach_from[queries][:, None])
            & (place[keys][None, :] <= reach_to[queries][:, None])
            & inside[keys][None, :]
        )

    every = slice(0, 3 * mesh_rows)
    own_query, own_grad = query_all[own], grad_heads[own]
    scores = jnp.einsum("qhe,khe->hqk", own_query, key_all, preferred_element_type=F32) * scale
    scores = jnp.where(keep(every, own)[None], scores, -jnp.inf)
    row_max = jnp.max(scores, -1, keepdims=True)
    shifted = jnp.exp(scores - row_max)
    inv_sum = 1.0 / jnp.sum(shifted, -1, keepdims=True)
    row_probs = shifted * inv_sum
    grad_prob = jnp.einsum("qhe,khe->hqk", own_grad, value_all, preferred_element_type=F32)
    delta = jnp.sum(row_probs * grad_prob, -1, keepdims=True)
    stats = jnp.concatenate([row_max, inv_sum, delta], -1)
    low_stats, high_stats = exchange(stats, stats, "node")

    weights = row_probs.astype(BF16)
    attention = jnp.einsum("hqk,khe->qhe", weights, value_all, preferred_element_type=F32).astype(
        BF16
    )
    mesh_out = (
        latent.astype(F32)
        + jnp.dot(attention.reshape(mesh_rows, channels), w_out, preferred_element_type=F32)
    ).astype(BF16)
    grad_score = (row_probs * (grad_prob - delta)).astype(BF16)
    grad_query = (
        jnp.einsum("hqk,khe->qhe", grad_score, key_all, preferred_element_type=F32) * scale
    )
    grad_key = jnp.einsum(
        "hqk,qhe->khe", grad_score[:, :, own], own_query, preferred_element_type=F32
    )
    grad_value = jnp.einsum(
        "hqk,qhe->khe", weights[:, :, own], own_grad, preferred_element_type=F32
    )

    def near(whole):
        return jnp.concatenate([whole[:mesh_rows], whole[2 * mesh_rows :]], 0)

    near_query, near_grad = near(query_all), near(grad_heads)
    near_stats = jnp.concatenate([low_stats, high_stats], 1)
    near_keep = near(keep(own, every))
    near_scores = (
        jnp.einsum("qhe,khe->hqk", near_query, key_all[own], preferred_element_type=F32) * scale
    )
    near_scores = jnp.where(near_keep[None], near_scores, -jnp.inf)
    near_probs = jnp.exp(near_scores - near_stats[..., :1]) * near_stats[..., 1:2]
    near_grad_prob = jnp.einsum(
        "qhe,khe->hqk", near_grad, value_all[own], preferred_element_type=F32
    )
    near_grad_score = (near_probs * (near_grad_prob - near_stats[..., 2:])).astype(BF16)
    grad_key = grad_key + jnp.einsum(
        "hqk,qhe->khe", near_grad_score, near_query, preferred_element_type=F32
    )
    grad_value = grad_value + jnp.einsum(
        "hqk,qhe->khe", near_probs.astype(BF16), near_grad, preferred_element_type=F32
    )
    grad_qkv = jnp.concatenate(
        [
            grad_query.reshape(mesh_rows, channels),
            (grad_key * scale).reshape(mesh_rows, channels),
            grad_value.reshape(mesh_rows, channels),
        ],
        1,
    ).astype(BF16)
    grad_normed = lax.dot_general(
        grad_qkv, w_qkv, (((1,), (1,)), ((), ())), preferred_element_type=F32
    )
    centred_grad = (
        grad_normed
        - jnp.mean(grad_normed, -1, keepdims=True)
        - normal * jnp.mean(grad_normed * normal, -1, keepdims=True)
    )
    mesh_grad = (cotangent.astype(F32) + inv_std * centred_grad).astype(BF16)
    return (mesh_out, mesh_grad)


def solution(mesh):
    rows = P(("groups", "node"), None)
    flat = P(("groups", "node"))
    placed = (rows, rows) + (flat,) * 8 + (P(None, ("groups", "node")), rows, P(), P(), P())
    return jax.shard_map(
        body, mesh=mesh, in_specs=placed, out_specs=(rows, rows), check_vma=False
    )
```

time: 193 us -> 97.5 us (0.51)
  the two profiles are of different devices: /device:TPU:1 before, /device:TPU:26 now
where the time goes in v1:
time: 97.5 us; the launch traced here: 96.5 us
  matrix products  38.4 us (39%)
  starting transfers between devices  25.1 us (26%)
  local copies, waits for them, and re-layouts  17.4 us (18%)
  other arithmetic  11.1 us (11%)
  waiting for transfers between devices  3.23 us (3%)
  between operations  1.25 us (1%)
    ppermute x3, starting transfers between devices, exchange(): lax.ppermute(toward_low, axis, [(i + 1, i) for i in range(ends)])  13.9 us
    dot_general x1, matrix products, body(): jnp.dot(all_normed, w_qkv, preferred_element_type=F32).astype(BF16)  7.08 us
    ppermute x3, starting transfers between devices, exchange(): lax.ppermute(toward_high, axis, [(i, i + 1) for i in range(ends)])  5.96 us
    dot_general x1, matrix products, body(): lax.dot_general(grad_qkv, w_qkv, (((1,), (1,)), ((), ())), preferred_elem...  5.33 us
    all_to_all x1, starting transfers between devices, body(): lax.all_to_all(far_message.reshape(devices, far_depth, channels + 128), '...  5.17 us
    dot_general x1, matrix products, body(): jnp.einsum('hqk,qhe->khe', near_grad_score, near_query, preferred_element...  4.81 us
    convert_element_type x1, local copies, waits for them, and re-layouts, body(): jnp.dot(all_normed, w_qkv, preferred_element_type=F32).astype(BF16)  4.27 us
    slice x5, local copies, waits for them, and re-layouts, near(): return jnp.concatenate([whole[:mesh_rows], whole[2 * mesh_rows:]], 0)  3.57 us
  transfers between devices with their start and end apart: 7, of which 1 were waited for; matrix products, arithmetic and copies ran while one was open for 20% of the time, Pallas kernels for 0%

profile of v1, /device:TPU:26, one launch (start us, length us, event | category | flops | bytes accessed | tf_op | source)
XLA Modules:
  0.0 96.5 jit_solution(16685950816395392470)
XLA Ops:
  0.7 1.4 %fusion.142 = (s32[1]{0:T(128)}, s32[1]{0:T(128)}) fusion(s32[2]{0:T(128)} %param.21), kind=kLoop, calls=%fused_computation.235 | loop fusion | bytes 16 | tf_op jit(solution)/shard_map/slice | solution.py:95
  2.1 0.7 convert_bitcast_fusion.4
  2.8 2.0 %select_convert_fusion.1 = (bf16[2048]{0:T(1024)(128)(2,1)S(1)}, bf16[2048]{0:T(1024)(128)(2,1)S(1)}, bf16[2048]{0:T(1024)(128)(2,1)S(1)}, bf16[2048]{0:T(1024)(128)(2,1)S(1)}) fusion(s32[4096]{0:T(1024)} %param.20, s32[]{:T(128)} %bitcast, s32[]{:T(128)} %bitcast.2, s32[4096]{0:T(1024)} %param.19), kind=kLoop, calls=%fused_computation.183 | loop fusion | flops 18432 | bytes 49160 | tf_op jit(solution)/shard_map/convert.19
  4.9 1.1 %fusion.137 = (bf16[128,1024]{1,0:T(8,128)(2,1)S(1)}, bf16[128,1024]{1,0:T(8,128)(2,1)S(1)}) fusion(bf16[512,1024]{1,0:T(8,128)(2,1)} %param.15), kind=kLoop, calls=%fused_computation.230 | loop fusion | bytes 1048576 | tf_op jit(solution)/shard_map/slice | solution.py:104
  6.0 2.1 %fusion.68 = (bf16[272,1024]{1,0:T(8,128)(2,1)}, bf16[272,1024]{1,0:T(8,128)(2,1)}) fusion(bf16[128,1024]{1,0:T(8,128)(2,1)} %param.26, bf16[16,1024]{1,0:T(8,128)(2,1)S(1)} %reshape.226, bf16[128,1024]{1,0:T(8,128)(2,1)S(1)} %get-tuple-element.14, bf16[16,1024]{1,0:T(8,128)(2,1)S(1)} %reshape.227, bf16[128,1024]{1,0:T(8,128)(2,1)S(1)} %get-tuple-element.15), kind=kLoop, calls=%fused_computation.102 | loop fusion | flops 3063808 | bytes 1966080 | tf_op jit(solution)/shard_map/concatenate | solution.py:100
  8.1 1.9 %collective-permute-start = (bf16[272,1024]{1,0:T(8,128)(2,1)}, bf16[272,1024]{1,0:T(8,128)(2,1)}, u32[]{:S(2)}, u32[]{:S(2)}) collective-permute-start(bf16[272,1024]{1,0:T(8,128)(2,1)} %get-tuple-element.27), channel_id=1, source_target_pairs={{0,1},{1,2},{2,3},{3,4},{4,5},{5,6},{6,7},{7,8},{8,9},{9,10},{10,1... | collective-permute-start | bytes 1671176 | tf_op jit(solution)/shard_map/ppermute | solution.py:15
  10.0 4.5 %collective-permute-start.1 = (bf16[272,1024]{1,0:T(8,128)(2,1)}, bf16[272,1024]{1,0:T(8,128)(2,1)}, u32[]{:S(2)}, u32[]{:S(2)}) collective-permute-start(bf16[272,1024]{1,0:T(8,128)(2,1)} %get-tuple-element.28), channel_id=1, source_target_pairs={{1,0},{2,1},{3,2},{4,3},{5,4},{6,5},{7,6},{8,7},{9,8},{10,9},{11,1... | collective-permute-start | bytes 1671176 | tf_op jit(solution)/shard_map/ppermute | solution.py:14
  14.6 0.3 convolution_convert_fusion.5
  14.9 0.1 broadcast_in_dim.34
  15.0 0.1 reshape.228
  15.1 0.1 broadcast_in_dim.40
  15.2 0.7 reshape.229
  15.9 5.2 %all-to-all-start = ((bf16[16,4,1152]{2,1,0:T(4,128)(2,1)}), bf16[16,4,1152]{2,1,0:T(4,128)(2,1)S(1)}, u32[]{:S(2)}, u32[]{:S(2)}) async-start(bf16[16,4,1152]{2,1,0:T(4,128)(2,1)} %reshape.229), calls=%async_computation | async-start | bytes 294912 | tf_op jit(solution)/shard_map/all_to_all | solution.py:107
  21.1 0.6 fusion.19
  21.7 2.6 %fusion.18 = f32[128,1024]{1,0:T(8,128)} fusion(bf16[128,512]{1,0:T(8,128)(2,1)S(1)} %fusion.19, bf16[512,1024]{1,0:T(8,128)(2,1)S(1)} %copy-done.2, bf16[1024,1024]{1,0:T(8,128)(2,1)S(1)} %copy-done), kind=kOutput, calls=%fused_computation.44 | convolution fusion | flops 1213726720 | bytes 3801088 | tf_op jit(solution)/shard_map/dot_general | solution.py:117
  24.3 3.2 %all-to-all-done = bf16[16,4,1152]{2,1,0:T(4,128)(2,1)S(1)} async-done(((bf16[16,4,1152]{2,1,0:T(4,128)(2,1)}), bf16[16,4,1152]{2,1,0:T(4,128)(2,1)S(1)}, u32[]{:S(2)}, u32[]{:S(2)}) %all-to-all-start) | async-done | bytes 147488 | tf_op jit(solution)/shard_map/all_to_all | solution.py:107
  27.5 0.1 convert_reduce_fusion
  27.6 1.5 %fusion.91 = f32[128,1024]{1,0:T(8,128)} fusion(bf16[1024,1024]{1,0:T(8,128)(2,1)S(1)} %copy-done, bf16[64,1152]{1,0:T(8,128)(2,1)S(1)} %reshape.230, s32[64]{0:T(128)S(1)} %convert_reduce_fusion), kind=kOutput, calls=%fused_computation.133 | convolution fusion | flops 151724032 | bytes 2753024 | tf_op jit(solution)/shard_map/dot_general | solution.py:138
  29.1 0.8 convert_bitcast_fusion.3
  30.0 0.8 convert_bitcast_fusion.1
  30.8 0.4 subtract_convert_fusion.1
  31.2 0.4 subtract_convert_fusion
  31.6 1.1 %fusion.139 = (bf16[128,1024]{1,0:T(8,128)(2,1)S(1)}, bf16[128,1024]{1,0:T(8,128)(2,1)S(1)}) fusion(bf16[272,1024]{1,0:T(8,128)(2,1)} %collective-permute-done), kind=kLoop, calls=%fused_computation.232 | loop fusion | bytes 1048576 | tf_op jit(solution)/shard_map/slice | solution.py:124
  32.7 1.1 %fusion.140 = (bf16[128,1024]{1,0:T(8,128)(2,1)S(1)}, bf16[128,1024]{1,0:T(8,128)(2,1)S(1)}) fusion(bf16[272,1024]{1,0:T(8,128)(2,1)} %collective-permute-done.1), kind=kLoop, calls=%fused_computation.233 | loop fusion | bytes 1048576 | tf_op jit(solution)/shard_map/slice | solution.py:124
  33.8 0.9 fusion.26
  34.7 0.1 copy-done.8
  34.8 0.1 copy-done.14
  34.9 0.2 copy-done.18
  35.1 0.4 fusion.143
  35.5 0.2 multiply_reduce_fusion.2
  35.7 0.8 fusion.81
  36.6 2.0 %collective-permute-start.2 = (bf16[128,1024]{1,0:T(8,128)(2,1)}, bf16[128,1024]{1,0:T(8,128)(2,1)}, u32[]{:S(2)}, u32[]{:S(2)}) collective-permute-start(bf16[128,1024]{1,0:T(8,128)(2,1)} %fusion.81), channel_id=1, source_target_pairs={{0,1},{1,2},{2,3},{3,4},{4,5},{5,6},{6,7},{7,8},{8,9},{9,10},{10,1... | collective-permute-start | bytes 786440 | tf_op jit(solution)/shard_map/ppermute | solution.py:15
  38.6 4.6 %collective-permute-start.3 = (bf16[128,1024]{1,0:T(8,128)(2,1)}, bf16[128,1024]{1,0:T(8,128)(2,1)}, u32[]{:S(2)}, u32[]{:S(2)}) collective-permute-start(bf16[128,1024]{1,0:T(8,128)(2,1)} %fusion.81), channel_id=1, source_target_pairs={{1,0},{2,1},{3,2},{4,3},{5,4},{6,5},{7,6},{8,7},{9,8},{10,9},{11,1... | collective-permute-start | bytes 786440 | tf_op jit(solution)/shard_map/ppermute | solution.py:14
  43.2 0.8 slice.250
  44.0 0.8 slice.248
  44.9 2.6 %convolution_convert_fusion.2 = bf16[384,1024]{1,0:T(8,128)(2,1)S(1)} fusion(bf16[1024,1024]{1,0:T(8,128)(2,1)} %param.29, bf16[128,1024]{1,0:T(8,128)(2,1)S(1)} %get-tuple-element.21, bf16[128,1024]{1,0:T(8,128)(2,1)S(1)} %copy-done.5, bf16[128,1024]{1,0:T(8,128)(2,1)S(1)} %get-tuple-element.19), kind=kOutput, calls=%fused_computation.27 | convolution fusion | flops 808058880 | bytes 3670016 | tf_op jit(solution)/shard_map/dot_general | solution.py:146
  47.5 0.8 fusion.138
  48.3 0.2 and_and_fusion
  48.5 1.1 %copy.33 = bf16[128,1024]{0,1:T(8,128)(2,1)S(1)} copy(bf16[128,1024]{1,0:T(8,128)(2,1)} %get-tuple-element.18) | data formatting | bytes 524288 | tf_op jit(solution)/shard_map/slice | solution.py:172
  49.7 1.8 %copy.34 = bf16[128,1024]{0,1:T(8,128)(2,1)} copy(bf16[128,1024]{1,0:T(8,128)(2,1)} %get-tuple-element.16) | data formatting | bytes 524288 | tf_op jit(solution)/shard_map/slice | solution.py:204
  51.5 0.8 copy.35
  52.3 0.1 fusion.94
  52.5 7.1 %convolution_convert_fusion = bf16[384,3072]{1,0:T(8,128)(2,1)} fusion(bf16[1024,3072]{1,0:T(8,128)(2,1)} %param.28, bf16[128,1024]{1,0:T(8,128)(2,1)} %collective-permute-done.3, bf16[128,1024]{1,0:T(8,128)(2,1)} %fusion.81, bf16[128,1024]{1,0:T(8,128)(2,1)} %collective-permute-done.2), kind=kOutput, calls=%fused_computation | convolution fusion | flops 2419458048 | bytes 9437184 | tf_op jit(solution)/shard_map/dot_general | solution.py:152
  59.5 4.3 %copy.32 = bf16[384,3072]{0,1:T(8,128)(2,1)} copy(bf16[384,3072]{1,0:T(8,128)(2,1)} %convolution_convert_fusion) | data formatting | bytes 4718592 | tf_op jit(solution)/shard_map/convert_element_type | solution.py:152
  63.8 1.9 %fusion = (f32[16,128]{1,0:T(8,128)S(1)}, f32[16,128,384]{2,1,0:T(8,128)S(1)}) fusion(pred[128,384]{1,0:T(8,128)(4,1)S(1)} %fusion.94, bf16[384,3,16,64]{0,3,2,1:T(8,128)(2,1)} %bitcast.94), kind=kOutput, calls=%fused_computation.9 | convolution fusion | flops 103020544 | bytes 4251648 | tf_op jit(solution)/shard_map/qhe,khe->hqk/dot_general | solution.py:173
  65.8 1.1 %fusion.49 = f32[16,128]{1,0:T(8,128)S(1)} fusion(f32[16,128]{1,0:T(8,128)S(1)} %get-tuple-element.46, f32[16,128,384]{2,1,0:T(8,128)S(1)} %get-tuple-element.47, pred[128,384]{1,0:T(8,128)(4,1)S(1)} %fusion.94), kind=kLoop, calls=%fused_computation.79 | loop fusion | flops 3143680 | bytes 3211264 | tf_op jit(solution)/shard_map/reduce_sum | solution.py:177
  66.8 0.6 copy-done.1
  67.4 1.5 %multiply_reduce_fusion = (f32[16,128]{1,0:T(8,128)S(1)}, f32[16,128,384]{2,1,0:T(8,128)S(1)}) fusion(f32[16,128]{1,0:T(8,128)S(1)} %get-tuple-element.39, f32[16,128]{1,0:T(8,128)S(1)} %get-tuple-element.46, f32[16,128,384]{2,1,0:T(8,128)S(1)} %get-tuple-element.47, pred[128,384]{1,0:T(8,128)(4,1)S(1)} %fusion.94, bf16[128,16,64]{0,2,1:T(8,128)(2,1)S(1)} %bitcast.102, ...), kind=kOutput, calls=%fused_computation.6 | convolution fusion | flops 105379840 | bytes 7413760 | tf_op jit(solution)/shard_map/qhe,khe->hqk/dot_general | solution.py:179
  68.9 1.1 %multiply_convert_fusion = (bf16[16,128,384]{2,1,0:T(8,128)(2,1)S(1)}, bf16[16,128,384]{2,1,0:T(8,128)(2,1)S(1)}) fusion(f32[16,128,384]{2,1,0:T(8,128)S(1)} %get-tuple-element.49, f32[16,128]{1,0:T(8,128)S(1)} %get-tuple-element.48, f32[16,128]{1,0:T(8,128)S(1)} %get-tuple-element.39, f32[16,128]{1,0:T(8,128)S(1)} %get-tuple-element.46, ...), kind=kLoop, calls=%fused_computation.5 | loop fusion | flops 6291456 | bytes 9510912 | tf_op jit(solution)/shard_map/convert_element_type | solution.py:192
  70.1 1.5 %fusion.17 = bf16[16,64,128]{2,1,0:T(8,128)(2,1)} fusion(bf16[16,128,384]{2,1,0:T(8,128)(2,1)S(1)} %get-tuple-element.10, bf16[384,3,16,64]{0,3,2,1:T(8,128)(2,1)S(1)} %bitcast.97), kind=kOutput, calls=%fused_computation.43 | convolution fusion | flops 100925440 | bytes 2621440 | tf_op jit(solution)/shard_map/hqk,khe->qhe/dot_general | solution.py:194
  71.6 1.1 %fusion.72 = f32[16,64,128]{2,1,0:T(8,128)} fusion(bf16[16,128,384]{2,1,0:T(8,128)(2,1)S(1)} %get-tuple-element.10, bf16[384,3,16,64]{0,3,2,1:T(8,128)(2,1)S(1)} %bitcast.98), kind=kOutput, calls=%fused_computation.106 | convolution fusion | flops 33554432 | bytes 1310720 | tf_op jit(solution)/shard_map/hqk,qhe->khe/dot_general | solution.py:196
  72.7 2.0 %collective-permute-start.4 = (f32[16,128,3]{1,0,2:T(8,128)S(1)}, f32[16,128,3]{1,0,2:T(8,128)S(1)}, u32[]{:S(2)}, u32[]{:S(2)}) collective-permute-start(f32[16,128,3]{1,0,2:T(8,128)S(1)} %pad_maximum_fusion.10), channel_id=1, source_target_pairs={{0,1},{1,2},{2,3},{3,4},{4,5},{5,6},{6,7},{7,8},{8,9},{9,10},{10,1... | collective-permute-start | bytes 73736 | tf_op jit(solution)/shard_map/ppermute | solution.py:15
  74.7 4.8 %collective-permute-start.5 = (f32[16,128,3]{1,0,2:T(8,128)S(1)}, f32[16,128,3]{1,0,2:T(8,128)S(1)}, u32[]{:S(2)}, u32[]{:S(2)}) collective-permute-start(f32[16,128,3]{1,0,2:T(8,128)S(1)} %pad_maximum_fusion.10), channel_id=1, source_target_pairs={{1,0},{2,1},{3,2},{4,3},{5,4},{6,5},{7,6},{8,7},{9,8},{10,9},{11,1... | collective-permute-start | bytes 73736 | tf_op jit(solution)/shard_map/ppermute | solution.py:14
  79.5 0.1 slice_bitcast_fusion.12
  79.6 0.8 convolution_convert_fusion.4
  80.4 1.2 %fusion.16 = bf16[128,1024]{1,0:T(8,128)(2,1)} fusion(f32[128,1024]{1,0:T(8,128)S(1)} %get-tuple-element.45, bf16[128,1024]{0,1:T(8,128)(2,1)S(1)} %bitcast.104, bf16[1024,1024]{1,0:T(8,128)(2,1)S(1)} %copy-done.3), kind=kOutput, calls=%fused_computation.42 | convolution fusion | flops 268697600 | bytes 3145728 | tf_op jit(solution)/shard_map/dot_general | solution.py:190
  81.6 0.5 fusion.82
  82.1 0.3 fusion.70
  82.4 0.1 copy-done.9
  82.6 0.1 copy-done.10
  82.6 2.7 %fusion.12 = bf16[16,64,128]{2,1,0:T(8,128)(2,1)} fusion(f32[16,64,128]{2,1,0:T(8,128)S(1)} %fusion.70, f32[16,256,128]{2,1,0:T(8,128)S(1)} %fusion.82, f32[16,256]{1,0:T(8,128)S(1)} %get-tuple-element.30, f32[16,256]{1,0:T(8,128)S(1)} %get-tuple-element.31, pred[256,128]{1,0:T(8,128)(4,1)S(1)} %pad_add_fusion, bf16[128,16,64]{0,2,1:T(8,128)(2,1)S(1)} %bitcast.109, ...), kind=kOutput, calls=%fused_computation.37 | convolution fusion | flops 71041024 | bytes 3473408 | tf_op jit(solution)/shard_map/hqk,qhe->khe/dot_general | solution.py:221
  85.4 4.8 %fusion.15 = bf16[16,64,128]{2,1,0:T(8,128)(2,1)} fusion(f32[16,64,128]{2,1,0:T(8,128)} %fusion.72, f32[16,256,128]{2,1,0:T(8,128)} %copy-done.4, f32[16,256]{1,0:T(8,128)S(1)} %get-tuple-element.29, f32[16,256]{1,0:T(8,128)S(1)} %get-tuple-element.30, f32[16,256]{1,0:T(8,128)S(1)} %get-tuple-element.31, pred[256,128]{1,0:T(8,128)(4,1)S(1)} %pad_add_fusion, ...), kind=kOutput, calls=%fused_computation.40 | convolution fusion | flops 140378112 | bytes 4276224 | tf_op jit(solution)/shard_map/hqk,qhe->khe/dot_general | solution.py:218
  90.2 5.3 %fusion.136 = (f32[128]{0:T(128)S(1)}, f32[128]{0:T(128)S(1)}, f32[128,1024]{1,0:T(8,128)S(1)}) fusion(f32[128]{0:T(128)S(1)} %add_rsqrt_fusion, f32[128,1024]{1,0:T(8,128)S(1)} %get-tuple-element.45, f32[128]{0:T(128)S(1)} %broadcast_multiply_fusion.2, bf16[1024,3072]{1,0:T(8,128)(2,1)} %param.28, bf16[128,1024]{0,1:T(8,128)(2,1)} %bitcast.116, ...), kind=kOutput, calls=%fused_computation.229 | convolution fusion | flops 808320768 | bytes 8128512 | tf_op jit(solution)/shard_map/dot_general | solution.py:232
  95.5 1.0 add_convert_fusion
  (75 shorter events, 0.4 us)
Async XLA Ops:
  0.6 21.0 %copy-start = (bf16[1024,1024]{1,0:T(8,128)(2,1)S(1)}, bf16[1024,1024]{1,0:T(8,128)(2,1)}, u32[]{:S(2)}) copy-start(bf16[1024,1024]{1,0:T(8,128)(2,1)} %param.27) | copy-start | bytes 6291460
  0.6 13.9 %copy-start.2 = (bf16[512,1024]{1,0:T(8,128)(2,1)S(1)}, bf16[512,1024]{1,0:T(8,128)(2,1)}, u32[]{:S(2)}) copy-start(bf16[512,1024]{1,0:T(8,128)(2,1)} %param.15) | copy-start | bytes 3145732
  0.7 13.9 %copy-start.12 = (s32[64]{0:T(128)S(1)}, s32[64]{0:T(128)}, u32[]{:S(2)}) copy-start(s32[64]{0:T(128)} %param.22) | copy-start | bytes 772
  4.9 10.0 %copy-start.13 = (s32[16]{0:T(128)S(1)}, s32[16]{0:T(128)}, u32[]{:S(2)}) copy-start(s32[16]{0:T(128)} %param.24) | copy-start | bytes 196
  4.9 10.2 %copy-start.17 = (s32[64]{0:T(128)S(1)}, s32[64]{0:T(128)}, u32[]{:S(2)}) copy-start(s32[64]{0:T(128)} %param.23) | copy-start | bytes 772
  6.0 15.1 %copy-start.15 = (s32[1024]{0:T(1024)S(1)}, s32[1024]{0:T(1024)}, u32[]{:S(2)}) copy-start(s32[1024]{0:T(1024)} %param.17) | copy-start | bytes 12292
  6.0 15.1 %copy-start.16 = (s32[1024]{0:T(1024)S(1)}, s32[1024]{0:T(1024)}, u32[]{:S(2)}) copy-start(s32[1024]{0:T(1024)} %param.18) | copy-start | bytes 12292
  8.1 21.0 %collective-permute-start = (bf16[272,1024]{1,0:T(8,128)(2,1)}, bf16[272,1024]{1,0:T(8,128)(2,1)}, u32[]{:S(2)}, u32[]{:S(2)}) collective-permute-start(bf16[272,1024]{1,0:T(8,128)(2,1)} %get-tuple-element.27), channel_id=1, source_target_pairs={{0,1},{1,2},{2,3},{3,4},{4,5},{5,6},{6,7},{7,8},{8,9},{9,10},{10,1... | collective-permute-start | bytes 1671176 | tf_op jit(solution)/shard_map/ppermute | solution.py:15
  10.0 20.0 %collective-permute-start.1 = (bf16[272,1024]{1,0:T(8,128)(2,1)}, bf16[272,1024]{1,0:T(8,128)(2,1)}, u32[]{:S(2)}, u32[]{:S(2)}) collective-permute-start(bf16[272,1024]{1,0:T(8,128)(2,1)} %get-tuple-element.28), channel_id=1, source_target_pairs={{1,0},{2,1},{3,2},{4,3},{5,4},{6,5},{7,6},{8,7},{9,8},{10,9},{11,1... | collective-permute-start | bytes 1671176 | tf_op jit(solution)/shard_map/ppermute | solution.py:14
  15.9 11.6 %all-to-all-start = ((bf16[16,4,1152]{2,1,0:T(4,128)(2,1)}), bf16[16,4,1152]{2,1,0:T(4,128)(2,1)S(1)}, u32[]{:S(2)}, u32[]{:S(2)}) async-start(bf16[16,4,1152]{2,1,0:T(4,128)(2,1)} %reshape.229), calls=%async_computation | async-start | bytes 294912 | tf_op jit(solution)/shard_map/all_to_all | solution.py:107
  33.8 1.0 %copy-start.8 = (f32[128,1024]{1,0:T(8,128)S(1)}, f32[128,1024]{1,0:T(8,128)}, u32[]{:S(2)}) copy-start(f32[128,1024]{1,0:T(8,128)} %fusion.91) | copy-start | bytes 1572868
  33.8 1.1 %copy-start.14 = (bf16[128,1024]{1,0:T(8,128)(2,1)S(1)}, bf16[128,1024]{1,0:T(8,128)(2,1)}, u32[]{:S(2)}) copy-start(bf16[128,1024]{1,0:T(8,128)(2,1)} %param.16) | copy-start | bytes 786436
  33.8 1.3 %copy-start.18 = (f32[128,1024]{1,0:T(8,128)S(1)}, f32[128,1024]{1,0:T(8,128)}, u32[]{:S(2)}) copy-start(f32[128,1024]{1,0:T(8,128)} %fusion.18) | copy-start | bytes 1572868
  35.1 9.7 %copy-start.11 = (s32[2,128]{1,0:T(2,128)S(1)}, s32[2,128]{1,0:T(2,128)}, u32[]{:S(2)}) copy-start(s32[2,128]{1,0:T(2,128)} %param.25) | copy-start | bytes 3076
  35.1 9.8 %copy-start.5 = (bf16[128,1024]{1,0:T(8,128)(2,1)S(1)}, bf16[128,1024]{1,0:T(8,128)(2,1)}, u32[]{:S(2)}) copy-start(bf16[128,1024]{1,0:T(8,128)(2,1)} %param.26) | copy-start | bytes 786436
  36.6 15.9 %collective-permute-start.2 = (bf16[128,1024]{1,0:T(8,128)(2,1)}, bf16[128,1024]{1,0:T(8,128)(2,1)}, u32[]{:S(2)}, u32[]{:S(2)}) collective-permute-start(bf16[128,1024]{1,0:T(8,128)(2,1)} %fusion.81), channel_id=1, source_target_pairs={{0,1},{1,2},{2,3},{3,4},{4,5},{5,6},{6,7},{7,8},{8,9},{9,10},{10,1... | collective-permute-start | bytes 786440 | tf_op jit(solution)/shard_map/ppermute | solution.py:15
  38.6 13.9 %collective-permute-start.3 = (bf16[128,1024]{1,0:T(8,128)(2,1)}, bf16[128,1024]{1,0:T(8,128)(2,1)}, u32[]{:S(2)}, u32[]{:S(2)}) collective-permute-start(bf16[128,1024]{1,0:T(8,128)(2,1)} %fusion.81), channel_id=1, source_target_pairs={{1,0},{2,1},{3,2},{4,3},{5,4},{6,5},{7,6},{8,7},{9,8},{10,9},{11,1... | collective-permute-start | bytes 786440 | tf_op jit(solution)/shard_map/ppermute | solution.py:14
  65.8 1.7 %copy-start.1 = (bf16[384,3072]{0,1:T(8,128)(2,1)S(1)}, bf16[384,3072]{0,1:T(8,128)(2,1)}, u32[]{:S(2)}) copy-start(bf16[384,3072]{0,1:T(8,128)(2,1)} %copy.32) | copy-start | bytes 7077892
  72.7 7.7 %copy-start.3 = (bf16[1024,1024]{1,0:T(8,128)(2,1)S(1)}, bf16[1024,1024]{1,0:T(8,128)(2,1)}, u32[]{:S(2)}) copy-start(bf16[1024,1024]{1,0:T(8,128)(2,1)} %param.29) | copy-start | bytes 6291460
  72.7 9.7 %collective-permute-start.4 = (f32[16,128,3]{1,0,2:T(8,128)S(1)}, f32[16,128,3]{1,0,2:T(8,128)S(1)}, u32[]{:S(2)}, u32[]{:S(2)}) collective-permute-start(f32[16,128,3]{1,0,2:T(8,128)S(1)} %pad_maximum_fusion.10), channel_id=1, source_target_pairs={{0,1},{1,2},{2,3},{3,4},{4,5},{5,6},{6,7},{7,8},{8,9},{9,10},{10,1... | collective-permute-start | bytes 73736 | tf_op jit(solution)/shard_map/ppermute | solution.py:15
  74.7 7.7 %collective-permute-start.5 = (f32[16,128,3]{1,0,2:T(8,128)S(1)}, f32[16,128,3]{1,0,2:T(8,128)S(1)}, u32[]{:S(2)}, u32[]{:S(2)}) collective-permute-start(f32[16,128,3]{1,0,2:T(8,128)S(1)} %pad_maximum_fusion.10), channel_id=1, source_target_pairs={{1,0},{2,1},{3,2},{4,3},{5,4},{6,5},{7,6},{8,7},{9,8},{10,9},{11,1... | collective-permute-start | bytes 73736 | tf_op jit(solution)/shard_map/ppermute | solution.py:14
  79.6 2.0 %copy-start.6 = (bf16[128,16,64]{0,2,1:T(8,128)(2,1)}, bf16[128,16,64]{0,2,1:T(8,128)(2,1)S(1)}, u32[]{:S(2)}) copy-start(bf16[128,16,64]{0,2,1:T(8,128)(2,1)S(1)} %get-tuple-element.13) | copy-start | bytes 786436
  81.6 1.0 copy-start.9
  81.6 1.0 %copy-start.10 = (bf16[128,1024]{0,1:T(8,128)(2,1)S(1)}, bf16[128,1024]{0,1:T(8,128)(2,1)}, u32[]{:S(2)}) copy-start(bf16[128,1024]{0,1:T(8,128)(2,1)} %copy.35) | copy-start | bytes 786436
  82.1 3.3 %copy-start.4 = (f32[16,256,128]{2,1,0:T(8,128)}, f32[16,256,128]{2,1,0:T(8,128)S(1)}, u32[]{:S(2)}) copy-start(f32[16,256,128]{2,1,0:T(8,128)S(1)} %fusion.82) | copy-start | bytes 6291460
  82.6 2.7 %copy-start.7 = (bf16[128,16,64]{0,2,1:T(8,128)(2,1)S(1)}, bf16[128,16,64]{0,2,1:T(8,128)(2,1)}, u32[]{:S(2)}) copy-start(bf16[128,16,64]{0,2,1:T(8,128)(2,1)} %copy-done.6) | copy-start | bytes 786436

commit v2 on v1

v2 whole, which is shorter than its diff:
```python
import functools

import jax
import jax.numpy as jnp
from jax import lax
from jax.experimental import pallas as pl
from jax.experimental.pallas import tpu as pltpu
from jax.sharding import PartitionSpec as P

HEADS = 16
BAND = 128
LANES = 128
F32 = jnp.float32
BF16 = jnp.bfloat16
I32 = jnp.int32
VMEM_LIMIT = 44 * 2**20


def mm(a, b):
    return lax.dot_general(a, b, (((1,), (0,)), ((), ())), preferred_element_type=F32)


def mm_nt(a, b):
    return lax.dot_general(a, b, (((1,), (1,)), ((), ())), preferred_element_type=F32)


def mm_tn(a, b):
    return lax.dot_general(a, b, (((0,), (0,)), ((), ())), preferred_element_type=F32)


def iota(shape, dim):
    return lax.broadcasted_iota(I32, shape, dim)


def call(kernel, outs, args, smem=(), name=None):
    specs = [
        pl.BlockSpec(memory_space=pltpu.SMEM if i in smem else pltpu.VMEM)
        for i in range(len(args))
    ]
    return pl.pallas_call(
        kernel,
        out_shape=[jax.ShapeDtypeStruct(shape, dtype) for shape, dtype in outs],
        in_specs=specs,
        out_specs=[pl.BlockSpec(memory_space=pltpu.VMEM) for _ in outs],
        compiler_params=pltpu.CompilerParams(vmem_limit_bytes=VMEM_LIMIT),
        name=name,
    )(*args)


def exchange(toward_low, toward_high, axis):
    ends = lax.axis_size(axis) - 1
    from_high = lax.ppermute(toward_low, axis, [(i + 1, i) for i in range(ends)])
    from_low = lax.ppermute(toward_high, axis, [(i, i + 1) for i in range(ends)])
    return from_low, from_high


def gelu(projected):
    x = projected.astype(BF16).astype(F32)
    inner = (2.0 / jnp.pi) ** 0.5 * (x + 0.044715 * (x * x * x))
    return (0.5 * x * (1.0 + jnp.tanh(inner))).astype(BF16)


def onehot_rows(index_rows, count):
    parts = [
        jnp.where(iota((count, row.shape[1]), 0) == row, 1.0, 0.0).astype(BF16)
        for row in index_rows
    ]
    return parts[0] if len(parts) == 1 else jnp.concatenate(parts, 1)


def norm_stats(latent):
    values = latent.astype(F32)
    row_mean = jnp.mean(values, -1, keepdims=True)
    centred = values - row_mean
    variance = jnp.mean(centred * centred, -1, keepdims=True)
    inv_std = lax.rsqrt(variance + 1e-05)
    return centred * inv_std, inv_std


def pack_kernel(
    far_count, side_count, grid, cot, window, side_src, side_dst, far_src, far_dst, far_out, low_out, high_out
):
    grid_rows, channels = grid.shape
    mesh_rows = cot.shape[0]
    slots = far_src.shape[1]
    devices = far_count.shape[0]
    depth = slots // devices
    slot = iota((1, slots), 1)
    live = jnp.zeros((1, slots), I32)
    for r in range(devices):
        live = jnp.where(slot // depth == r, far_count[r], live)
    target = jnp.where(slot % depth < live, far_dst[...], mesh_rows).astype(F32)
    place = slot // depth * (2 * depth) + slot % depth
    select = onehot_rows([far_src[...]], grid_rows)
    spread = mm_nt(select, onehot_rows([place], 2 * slots)).astype(BF16)
    rows = mm_tn(spread, grid[...])
    column = jnp.sum(
        jnp.where(iota((2 * slots, slots), 0) == place + depth, target, 0.0), 1, keepdims=True
    )
    far_out[...] = (rows + column).astype(BF16)
    count = side_src.shape[0] // 2
    for k, out in ((0, low_out), (1, high_out)):
        start = 0 if k == 0 else grid_rows - BAND
        out[:BAND] = grid[start : start + BAND]
        out[BAND : BAND + mesh_rows] = cot[...]
        rank = iota((count, LANES), 0) * LANES + iota((count, LANES), 1)
        src = side_src[k * count : (k + 1) * count] - start
        dst = jnp.where(rank < side_count[k], side_dst[k * count : (k + 1) * count], mesh_rows)
        reach = jnp.concatenate([window[...], jnp.zeros((count - 2, mesh_rows), I32)], 0)
        blank = jnp.zeros((count, channels - 2 * LANES - mesh_rows), I32)
        meta = jnp.concatenate([src, dst, reach, blank], 1)
        out[BAND + mesh_rows :] = meta.astype(F32).astype(BF16)


def own_kernel(grid, w_edge, mesh_in, own_src, own_dst, cot, w_out, partial_out, grad_out):
    grid_rows = grid.shape[0]
    mesh_rows = mesh_in.shape[0]
    active = gelu(mm(grid[...], w_edge[...]))
    rows = own_src.shape[0]
    src = onehot_rows([own_src[r : r + 1] for r in range(rows)], grid_rows)
    dst = onehot_rows([own_dst[r : r + 1] for r in range(rows)], mesh_rows)
    counts = mm_nt(dst, src).astype(BF16)
    partial_out[...] = mesh_in[...].astype(F32) + mm(counts, active)
    grad_out[...] = mm_nt(cot[...], w_out[...]).astype(BF16)


def side_kernel(low, high, w_edge, w_out, partial, partial_out, grad_out, window_out):
    mesh_rows = partial.shape[0]
    active = gelu(mm(jnp.concatenate([low[:BAND], high[:BAND]], 0), w_edge[...]))
    uppers, lowers = [], []
    for side in (low, high):
        meta = side[BAND + mesh_rows :].astype(F32).astype(I32)
        count = meta.shape[0]
        src = onehot_rows([meta[r : r + 1, :LANES] for r in range(count)], BAND)
        dst = onehot_rows([meta[r : r + 1, LANES : 2 * LANES] for r in range(count)], mesh_rows)
        counts = mm_nt(dst, src)
        upper = counts.astype(BF16)
        uppers.append(upper)
        lowers.append((counts - upper.astype(F32)).astype(BF16))
        reach = meta[:8, 2 * LANES : 2 * LANES + mesh_rows]
        at = 0 if side is low else mesh_rows
        window_out[:, at : at + mesh_rows] = reach
    counts = jnp.concatenate(uppers + lowers, 1)
    partial_out[...] = partial[...] + mm(counts, jnp.concatenate([active, active], 0))
    both = jnp.concatenate([low[BAND : BAND + mesh_rows], high[BAND : BAND + mesh_rows]], 0)
    grad_out[...] = mm_nt(both, w_out[...]).astype(BF16)


def latent_kernel(depth, far, w_edge, partial, latent_out, normed_out):
    mesh_rows = partial.shape[0]
    slots = far.shape[0]
    rows = far[...]
    active = gelu(mm(rows, w_edge[...]))
    target = pltpu.roll(rows[:, :LANES].astype(F32), slots - depth, 0)
    target = target if mesh_rows == LANES else jnp.broadcast_to(target[:, :1], (slots, mesh_rows))
    is_row = iota((slots, mesh_rows), 0) % (2 * depth) < depth
    hit = (target == iota((slots, mesh_rows), 1).astype(F32)) & is_row
    landing = jnp.where(hit, 1.0, 0.0).astype(BF16)
    latent = (partial[...] + mm_tn(landing, active)).astype(BF16)
    latent_out[...] = latent
    normal, _ = norm_stats(latent)
    normed_out[...] = normal.astype(BF16)


def project_kernel(normed, w_qkv, qkv_out):
    qkv_out[...] = mm(normed[...], w_qkv[...]).astype(BF16)


def halves(rows, scale=None):
    first = iota(rows.shape, 1) < rows.shape[1] // 2
    if scale is not None:
        rows = rows * jnp.asarray(scale, rows.dtype)
    zero = jnp.zeros_like(rows)
    return jnp.concatenate([jnp.where(first, rows, zero), jnp.where(first, zero, rows)], 0)


def merge(stacked):
    m = stacked.shape[0] // 2
    first = iota((m, stacked.shape[1]), 1) < stacked.shape[1] // 2
    return jnp.where(first, stacked[:m], stacked[m:])


def attend_kernel(
    scale,
    pair,
    low_normed,
    high_normed,
    w_qkv,
    own_qkv,
    own_grad,
    window,
    stats_out,
    att_out,
    gq_out,
    gk_out,
    gv_out,
    near_q_out,
    kv,
):
    m, channels = low_normed.shape
    devices = lax.axis_size("node")
    me = lax.axis_index("node")
    near = mm(jnp.concatenate([low_normed[...], high_normed[...]], 0), w_qkv[...]).astype(BF16)
    near_q_out[...] = near[:, :channels] * jnp.asarray(scale, BF16)
    kv[:m] = near[:m, channels:]
    kv[m : 2 * m] = own_qkv[:, channels:]
    kv[2 * m :] = near[m:, channels:]
    key_at = iota((3 * m, m), 0)
    query_at = iota((3 * m, m), 1) + m
    inside = (key_at >= jnp.where(me == 0, m, 0)) & (
        key_at < jnp.where(me == devices - 1, 2 * m, 3 * m)
    )
    keep = (
        inside & (key_at >= query_at - window[0:1, :]) & (key_at <= query_at + window[1:2, :])
    )
    bias = jnp.where(keep, 0.0, -jnp.inf).astype(F32)
    bias = jnp.concatenate([bias, bias], 1)
    pairs = channels // pair
    for p in range(pairs):
        cols = slice(p * pair, (p + 1) * pair)
        key = kv[:, cols]
        value = kv[:, channels + p * pair : channels + (p + 1) * pair]
        q2 = halves(own_qkv[:, cols], scale)
        g2 = halves(own_grad[:, cols])
        scores = mm_nt(key, q2) + bias
        top = jnp.max(scores, 0, keepdims=True)
        shifted = jnp.exp(scores - top)
        inv_sum = 1.0 / jnp.sum(shifted, 0, keepdims=True)
        probs = shifted * inv_sum
        weights = probs.astype(BF16)
        grad_prob = mm_nt(value, g2)
        delta = jnp.sum(probs * grad_prob, 0, keepdims=True)
        grad_score = (probs * (grad_prob - delta)).astype(BF16)
        stats_out[p : p + 1] = top
        stats_out[pairs + p : pairs + p + 1] = inv_sum
        stats_out[2 * pairs + p : 2 * pairs + p + 1] = delta
        att_out[:, cols] = merge(mm_tn(weights, value)).astype(BF16)
        gq_out[:, cols] = (merge(mm_tn(grad_score, key)) * scale).astype(BF16)
        gk_out[:, cols] = mm(grad_score[m : 2 * m], q2)
        gv_out[:, cols] = mm(weights[m : 2 * m], g2)


def output_kernel(latent, attention, w_out, grad_query, w_qkv, mesh_out, grad_normed):
    channels = latent.shape[1]
    mesh_out[...] = (latent[...].astype(F32) + mm(attention[...], w_out[...])).astype(BF16)
    grad_normed[...] = mm_nt(grad_query[...], w_qkv[:, :channels])


def finish_kernel(
    pair,
    low_stats,
    high_stats,
    near_window,
    near_q,
    near_grad,
    own_qkv,
    grad_key,
    grad_value,
    grad_normed,
    w_qkv,
    latent,
    cot,
    grad_out,
    grad_kv,
):
    m, channels = latent.shape
    key_at = iota((m, 2 * m), 0) + m
    lane = iota((m, 2 * m), 1)
    query_at = jnp.where(lane < m, lane, lane + m)
    keep = (key_at >= query_at - near_window[0:1, :]) & (key_at <= query_at + near_window[1:2, :])
    bias = jnp.where(keep, 0.0, -jnp.inf).astype(F32)
    pairs = channels // pair

    def stat(row, second):
        lanes = slice(m, 2 * m) if second else slice(0, m)
        return jnp.concatenate([low_stats[row : row + 1, lanes], high_stats[row : row + 1, lanes]], 1)

    for p in range(pairs):
        cols = slice(p * pair, (p + 1) * pair)
        key2 = halves(own_qkv[:, channels + p * pair : channels + (p + 1) * pair])
        value2 = halves(own_qkv[:, 2 * channels + p * pair : 2 * channels + (p + 1) * pair])
        query = near_q[:, cols]
        grad = near_grad[:, cols]
        scores = mm_nt(key2, query)
        grad_prob = mm_nt(value2, grad)
        weights, grad_scores = [], []
        for h in range(2):
            half = slice(h * m, (h + 1) * m)
            probs = jnp.exp(scores[half] + bias - stat(p, h)) * stat(pairs + p, h)
            weights.append(probs.astype(BF16))
            grad_scores.append((probs * (grad_prob[half] - stat(2 * pairs + p, h))).astype(BF16))
        gk = grad_key[:, cols] + merge(mm(jnp.concatenate(grad_scores, 0), query))
        gv = grad_value[:, cols] + merge(mm(jnp.concatenate(weights, 0), grad))
        grad_kv[:, cols] = gk.astype(BF16)
        grad_kv[:, channels + p * pair : channels + (p + 1) * pair] = gv.astype(BF16)
    total = grad_normed[...] + mm_nt(grad_kv[...], w_qkv[:, channels:])
    normal, inv_std = norm_stats(latent[...])
    centred = (
        total
        - jnp.mean(total, -1, keepdims=True)
        - normal * jnp.mean(total * normal, -1, keepdims=True)
    )
    grad_out[...] = (cot[...].astype(F32) + inv_std * centred).astype(BF16)


def body(
    grid_in,
    mesh_in,
    own_src,
    own_dst,
    side_src,
    side_dst,
    side_count,
    far_src,
    far_dst,
    far_count,
    window,
    cotangent,
    w_edge,
    w_qkv,
    w_out,
):
    devices = lax.axis_size("node")
    grid_rows, channels = grid_in.shape
    m = mesh_in.shape[0]
    far_slots = far_src.shape[0]
    far_depth = far_slots // devices
    head_dim = channels // HEADS
    pair = 2 * head_dim
    pairs = channels // pair
    scale = head_dim ** (-0.5)
    meta_rows = side_src.shape[0] // (2 * LANES)

    far_message, toward_low, toward_high = call(
        pack_kernel,
        [
            ((2 * far_slots, channels), BF16),
            ((BAND + m + meta_rows, channels), BF16),
            ((BAND + m + meta_rows, channels), BF16),
        ],
        [
            far_count,
            side_count,
            grid_in,
            cotangent,
            window,
            side_src.reshape(-1, LANES),
            side_dst.reshape(-1, LANES),
            far_src.reshape(1, far_slots),
            far_dst.reshape(1, far_slots),
        ],
        smem=(0, 1),
        name="pack",
    )
    got_far = lax.all_to_all(
        far_message.reshape(devices, 2 * far_depth, channels),
        "node",
        split_axis=0,
        concat_axis=0,
        tiled=True,
    ).reshape(2 * far_slots, channels)
    from_low, from_high = exchange(toward_low, toward_high, "node")

    partial, own_grad = call(
        own_kernel,
        [((m, channels), F32), ((m, channels), BF16)],
        [
            grid_in,
            w_edge,
            mesh_in,
            own_src.reshape(-1, LANES),
            own_dst.reshape(-1, LANES),
            cotangent,
            w_out,
        ],
        name="own",
    )
    partial, near_grad, near_window = call(
        side_kernel,
        [((m, channels), F32), ((2 * m, channels), BF16), ((8, 2 * m), I32)],
        [from_low, from_high, w_edge, w_out, partial],
        name="side",
    )
    latent, normed = call(
        functools.partial(latent_kernel, far_depth),
        [((m, channels), BF16), ((m, channels), BF16)],
        [got_far, w_edge, partial],
        name="latent",
    )
    low_normed, high_normed = exchange(normed, normed, "node")
    (own_qkv,) = call(project_kernel, [((m, 3 * channels), BF16)], [normed, w_qkv], name="project")

    stats, attention, grad_query, grad_key, grad_value, near_q = pl.pallas_call(
        functools.partial(attend_kernel, scale, pair),
        out_shape=[
            jax.ShapeDtypeStruct((3 * pairs, 2 * m), F32),
            jax.ShapeDtypeStruct((m, channels), BF16),
            jax.ShapeDtypeStruct((m, channels), BF16),
            jax.ShapeDtypeStruct((m, channels), F32),
            jax.ShapeDtypeStruct((m, channels), F32),
            jax.ShapeDtypeStruct((2 * m, channels), BF16),
        ],
        in_specs=[pl.BlockSpec(memory_space=pltpu.VMEM)] * 6,
        out_specs=[pl.BlockSpec(memory_space=pltpu.VMEM)] * 6,
        scratch_shapes=[pltpu.VMEM((3 * m, 2 * channels), BF16)],
        compiler_params=pltpu.CompilerParams(vmem_limit_bytes=VMEM_LIMIT),
        name="attend",
    )(low_normed, high_normed, w_qkv, own_qkv, own_grad, window)
    low_stats, high_stats = exchange(stats, stats, "node")

    mesh_out, grad_normed = call(
        output_kernel,
        [((m, channels), BF16), ((m, channels), F32)],
        [latent, attention, w_out, grad_query, w_qkv],
        name="output",
    )
    mesh_grad = pl.pallas_call(
        functools.partial(finish_kernel, pair),
        out_shape=jax.ShapeDtypeStruct((m, channels), BF16),
        in_specs=[pl.BlockSpec(memory_space=pltpu.VMEM)] * 12,
        out_specs=pl.BlockSpec(memory_space=pltpu.VMEM),
        scratch_shapes=[pltpu.VMEM((m, 2 * channels), BF16)],
        compiler_params=pltpu.CompilerParams(vmem_limit_bytes=VMEM_LIMIT),
        name="finish",
    )(
        low_stats,
        high_stats,
        near_window,
        near_q,
        near_grad,
        own_qkv,
        grad_key,
        grad_value,
        grad_normed,
        w_qkv,
        latent,
        cotangent,
    )
    return (mesh_out, mesh_grad)


def solution(mesh):
    rows = P(("groups", "node"), None)
    flat = P(("groups", "node"))
    placed = (rows, rows) + (flat,) * 8 + (P(None, ("groups", "node")), rows, P(), P(), P())
    return jax.shard_map(
        body, mesh=mesh, in_specs=placed, out_specs=(rows, rows), check_vma=False
    )
```

time: 97.5 us -> 72.5 us (0.74)
  the two profiles are of different devices: /device:TPU:26 before, /device:TPU:1 now
where the time goes in v2:
time: 72.5 us; the launch traced here: 71.4 us
  starting transfers between devices  22.9 us (32%)
  local copies, waits for them, and re-layouts  22.2 us (31%)
  Pallas kernels  21.9 us (30%)
  waiting for transfers between devices  3.55 us (5%)
  between operations  0.85 us (1%)
    unnamed x60, local copies, waits for them, and re-layouts  22.2 us
    pallas_call x6, Pallas kernels, call(): pl.pallas_call(kernel, out_shape=[jax.ShapeDtypeStruct(shape, dtype) for...  11.6 us
    ppermute x3, starting transfers between devices, exchange(): lax.ppermute(toward_high, axis, [(i, i + 1) for i in range(ends)])  9.98 us
    all_to_all x1, starting transfers between devices, body(): lax.all_to_all(far_message.reshape(devices, 2 * far_depth, channels), 'no...  6.47 us
    ppermute x3, starting transfers between devices, exchange(): lax.ppermute(toward_low, axis, [(i + 1, i) for i in range(ends)])  6.43 us
    pallas_call x1, Pallas kernels, body(): pl.pallas_call(functools.partial(attend_kernel, scale, pair), out_shape=[...  6.04 us
    pallas_call x1, Pallas kernels, body(): pl.pallas_call(functools.partial(finish_kernel, pair), out_shape=jax.Shap...  4.24 us
    ppermute x3, waiting for transfers between devices, exchange(): lax.ppermute(toward_low, axis, [(i + 1, i) for i in range(ends)])  3.54 us
  transfers between devices with their start and end apart: 7, of which 2 were waited for; matrix products, arithmetic and copies ran while one was open for 0% of the time, Pallas kernels for 12%

profile of v2, /device:TPU:1, one launch (start us, length us, event | category | flops | bytes accessed | tf_op | source)
XLA Modules:
  0.0 71.4 jit_solution(16292355082667334731)
XLA Ops:
  0.6 0.0 copy-start.8
  0.6 1.2 %copy-done.8 = bf16[512,1024]{1,0:T(8,128)(2,1)S(1)} copy-done((bf16[512,1024]{1,0:T(8,128)(2,1)S(1)}, bf16[512,1024]{1,0:T(8,128)(2,1)}, u32[]{:S(2)}) %copy-start.8) | copy-done | bytes 1048600
  1.9 0.0 copy-start.10
  1.9 0.9 %copy-done.10 = bf16[128,1024]{1,0:T(8,128)(2,1)S(1)} copy-done((bf16[128,1024]{1,0:T(8,128)(2,1)S(1)}, bf16[128,1024]{1,0:T(8,128)(2,1)}, u32[]{:S(2)}) %copy-start.10) | copy-done | bytes 262168
  2.8 0.0 copy-start.20
  2.8 0.7 %copy-done.20 = s32[4096]{0:T(1024)S(1)} copy-done((s32[4096]{0:T(1024)S(1)}, s32[4096]{0:T(1024)}, u32[]{:S(2)}) %copy-start.20) | copy-done | bytes 16408
  3.5 0.0 copy-start.21
  3.5 0.7 %copy-done.21 = s32[4096]{0:T(1024)S(1)} copy-done((s32[4096]{0:T(1024)S(1)}, s32[4096]{0:T(1024)}, u32[]{:S(2)}) %copy-start.21) | copy-done | bytes 16408
  4.2 0.7 copy-done.22
  4.9 0.7 copy-done.26
  5.6 0.7 copy-done.27
  6.2 0.7 copy-done.28
  6.9 0.7 copy-done.29
  7.5 2.1 %pack.1 = (bf16[128,1024]{1,0:T(8,128)(2,1)}, bf16[272,1024]{1,0:T(8,128)(2,1)}, bf16[272,1024]{1,0:T(8,128)(2,1)}) custom-call(s32[16]{0:T(128)S(1)} %copy-done.26, s32[2]{0:T(128)S(1)} %copy-done.27, bf16[512,1024]{1,0:T(8,128)(2,1)S(1)} %copy-done.8, bf16[128,1024]{1,0:T(8,128)(2,1)S(1)} %copy-done.10, s32[2,128]{1,0:T(2,128)S(1)} %copy-done.22, ...), custom_call_target="tpu_custom_call" | custom-call | tf_op jit(solution)/shard_map/pack/pallas_call | solution.py:40
  9.7 4.5 %collective-permute-start = (bf16[272,1024]{1,0:T(8,128)(2,1)}, bf16[272,1024]{1,0:T(8,128)(2,1)}, u32[]{:S(2)}, u32[]{:S(2)}) collective-permute-start(bf16[272,1024]{1,0:T(8,128)(2,1)} %get-tuple-element.21), channel_id=1, source_target_pairs={{0,1},{1,2},{2,3},{3,4},{4,5},{5,6},{6,7},{7,8},{8,9},{9,10},{10,1... | collective-permute-start | bytes 1671176 | tf_op jit(solution)/shard_map/ppermute | solution.py:53
  14.2 1.9 %collective-permute-start.1 = (bf16[272,1024]{1,0:T(8,128)(2,1)}, bf16[272,1024]{1,0:T(8,128)(2,1)}, u32[]{:S(2)}, u32[]{:S(2)}) collective-permute-start(bf16[272,1024]{1,0:T(8,128)(2,1)} %get-tuple-element.22), channel_id=1, source_target_pairs={{1,0},{2,1},{3,2},{4,3},{5,4},{6,5},{7,6},{8,7},{9,8},{10,9},{11,1... | collective-permute-start | bytes 1671176 | tf_op jit(solution)/shard_map/ppermute | solution.py:52
  16.1 6.5 %all-to-all-start = ((bf16[16,8,1024]{2,1,0:T(8,128)(2,1)}), bf16[16,8,1024]{2,1,0:T(8,128)(2,1)S(1)}, u32[]{:S(2)}, u32[]{:S(2)}) async-start(bf16[16,8,1024]{2,1,0:T(8,128)(2,1)} %bitcast.4), calls=%async_computation | async-start | bytes 524288 | tf_op jit(solution)/shard_map/all_to_all | solution.py:355
  22.6 0.0 copy-done.9
  22.6 0.0 copy-start.3
  22.6 1.6 %copy-done.3 = bf16[1024,1024]{1,0:T(8,128)(2,1)S(1)} copy-done((bf16[1024,1024]{1,0:T(8,128)(2,1)S(1)}, bf16[1024,1024]{1,0:T(8,128)(2,1)}, u32[]{:S(2)}) %copy-start.3) | copy-done | bytes 2097176
  24.2 1.6 %copy-done.5 = bf16[1024,1024]{1,0:T(8,128)(2,1)S(1)} copy-done((bf16[1024,1024]{1,0:T(8,128)(2,1)S(1)}, bf16[1024,1024]{1,0:T(8,128)(2,1)}, u32[]{:S(2)}) %copy-start.5) | copy-done | bytes 2097176
  25.8 0.9 %copy-done.11 = bf16[128,1024]{1,0:T(8,128)(2,1)S(1)} copy-done((bf16[128,1024]{1,0:T(8,128)(2,1)S(1)}, bf16[128,1024]{1,0:T(8,128)(2,1)}, u32[]{:S(2)}) %copy-start.11) | copy-done | bytes 262168
  26.7 0.9 %copy-done.17 = bf16[128,1024]{1,0:T(8,128)(2,1)S(1)} copy-done((bf16[128,1024]{1,0:T(8,128)(2,1)S(1)}, bf16[128,1024]{1,0:T(8,128)(2,1)}, u32[]{:S(2)}) %copy-start.17) | copy-done | bytes 262168
  27.7 0.7 copy-done.24
  28.4 0.7 copy-done.25
  29.1 2.7 %own.1 = (f32[128,1024]{1,0:T(8,128)S(1)}, bf16[128,1024]{1,0:T(8,128)(2,1)S(1)}) custom-call(bf16[512,1024]{1,0:T(8,128)(2,1)S(1)} %copy-done.9, bf16[1024,1024]{1,0:T(8,128)(2,1)S(1)} %copy-done.3, bf16[128,1024]{1,0:T(8,128)(2,1)S(1)} %copy-done.17, s32[8,128]{1,0:T(8,128)S(1)} %bitcast.11, s32[8,128]{1,0:T(8,128)S(1)} %bitcast.12, ...), custom_call_target="tpu_custom_call" | custom-call | tf_op jit(solution)/shard_map/own/pallas_call | solution.py:40
  31.7 0.0 copy-start.18
  31.7 0.7 copy-done.18
  32.4 0.0 collective-permute-done.low
  32.4 0.0 collective-permute-done.1.high
  32.4 0.0 copy-done.4
  32.4 0.0 copy-done.6
  32.5 3.3 %side.1 = (f32[128,1024]{1,0:T(8,128)S(1)}, bf16[256,1024]{1,0:T(8,128)(2,1)S(1)}, s32[8,256]{1,0:T(8,128)S(1)}) custom-call(bf16[272,1024]{1,0:T(8,128)(2,1)} %collective-permute-done.low, bf16[272,1024]{1,0:T(8,128)(2,1)} %collective-permute-done.1.high, bf16[1024,1024]{1,0:T(8,128)(2,1)S(1)} %copy-done.4, bf16[1024,1024]{1,0:T(8,128)(2,1)S(1)} %copy-done.6, ...), custom_call_target="tpu_custom_call" | custom-call | tf_op jit(solution)/shard_map/side/pallas_call | solution.py:40
  35.8 0.0 copy-start.15
  35.8 0.8 %copy-done.15 = f32[128,1024]{1,0:T(8,128)} copy-done((f32[128,1024]{1,0:T(8,128)}, f32[128,1024]{1,0:T(8,128)S(1)}, u32[]{:S(2)}) %copy-start.15) | copy-done | bytes 524312
  36.5 0.0 all-to-all-done
  36.5 1.0 %copy-done.16 = f32[128,1024]{1,0:T(8,128)S(1)} copy-done((f32[128,1024]{1,0:T(8,128)S(1)}, f32[128,1024]{1,0:T(8,128)}, u32[]{:S(2)}) %copy-start.16) | copy-done | bytes 524312
  37.6 0.9 %latent.1 = (bf16[128,1024]{1,0:T(8,128)(2,1)S(1)}, bf16[128,1024]{1,0:T(8,128)(2,1)S(1)}) custom-call(bf16[128,1024]{1,0:T(8,128)(2,1)S(1)} %bitcast.8, bf16[1024,1024]{1,0:T(8,128)(2,1)S(1)} %copy-done.4, f32[128,1024]{1,0:T(8,128)S(1)} %copy-done.16), custom_call_target="tpu_custom_call" | custom-call | tf_op jit(solution)/shard_map/latent/pallas_call | solution.py:40
  38.5 0.0 copy-start.23
  38.5 3.5 %collective-permute-start.2 = (bf16[128,1024]{1,0:T(8,128)(2,1)S(1)}, bf16[128,1024]{1,0:T(8,128)(2,1)S(1)}, u32[]{:S(2)}, u32[]{:S(2)}) collective-permute-start(bf16[128,1024]{1,0:T(8,128)(2,1)S(1)} %get-tuple-element.26.normed), channel_id=1, source_target_pairs={{0,1},{1,2},{2,3},{3,4},{4,5},{5,6},{6,7},{7,8},{8,9},{9,10},{10,1... | collective-permute-start | bytes 786440 | tf_op jit(solution)/shard_map/ppermute | solution.py:53
  42.1 2.1 %collective-permute-start.3 = (bf16[128,1024]{1,0:T(8,128)(2,1)S(1)}, bf16[128,1024]{1,0:T(8,128)(2,1)S(1)}, u32[]{:S(2)}, u32[]{:S(2)}) collective-permute-start(bf16[128,1024]{1,0:T(8,128)(2,1)S(1)} %get-tuple-element.26.normed), channel_id=1, source_target_pairs={{1,0},{2,1},{3,2},{4,3},{5,4},{6,5},{7,6},{8,7},{9,8},{10,9},{11,1... | collective-permute-start | bytes 786440 | tf_op jit(solution)/shard_map/ppermute | solution.py:52
  44.2 0.0 copy-start
  44.2 2.8 %copy-done = bf16[1024,3072]{1,0:T(8,128)(2,1)S(1)} copy-done((bf16[1024,3072]{1,0:T(8,128)(2,1)S(1)}, bf16[1024,3072]{1,0:T(8,128)(2,1)}, u32[]{:S(2)}) %copy-start) | copy-done | bytes 6291480
  47.0 1.0 %project.1.own_qkv = bf16[128,3072]{1,0:T(8,128)(2,1)S(1)} custom-call(bf16[128,1024]{1,0:T(8,128)(2,1)S(1)} %get-tuple-element.26.normed, bf16[1024,3072]{1,0:T(8,128)(2,1)S(1)} %copy-done), custom_call_target="tpu_custom_call" | custom-call | tf_op jit(solution)/shard_map/project/pallas_call | solution.py:40
  48.0 0.0 collective-permute-done.2.low_normed
  48.0 1.8 %collective-permute-done.3.high_normed = bf16[128,1024]{1,0:T(8,128)(2,1)S(1)} collective-permute-done((bf16[128,1024]{1,0:T(8,128)(2,1)S(1)}, bf16[128,1024]{1,0:T(8,128)(2,1)S(1)}, u32[]{:S(2)}, u32[]{:S(2)}) %collective-permute-start.3) | collective-permute-done | bytes 262176 | tf_op jit(solution)/shard_map/ppermute | solution.py:52
  49.8 0.0 copy-done.23
  49.8 0.0 copy-done.19
  49.8 2.8 %copy-done.1 = bf16[1024,3072]{1,0:T(8,128)(2,1)S(1)} copy-done((bf16[1024,3072]{1,0:T(8,128)(2,1)S(1)}, bf16[1024,3072]{1,0:T(8,128)(2,1)}, u32[]{:S(2)}) %copy-start.1) | copy-done | bytes 6291480
  52.6 6.0 %attend.1 = (f32[24,256]{1,0:T(8,128)S(1)}, bf16[128,1024]{1,0:T(8,128)(2,1)S(1)}, bf16[128,1024]{1,0:T(8,128)(2,1)S(1)}, f32[128,1024]{1,0:T(8,128)S(1)}, f32[1...) custom-call(bf16[128,1024]{1,0:T(8,128)(2,1)S(1)} %collective-permute-done.2.low_normed, ...), custom_call_target="tpu_custom_call" | custom-call | tf_op jit(solution)/shard_map/attend/pallas_call | solution.py:393
  58.6 0.0 copy-start.13
  58.6 0.8 %copy-done.13 = bf16[256,1024]{1,0:T(8,128)(2,1)} copy-done((bf16[256,1024]{1,0:T(8,128)(2,1)}, bf16[256,1024]{1,0:T(8,128)(2,1)S(1)}, u32[]{:S(2)}) %copy-start.13) | copy-done | bytes 524312
  59.4 1.9 %collective-permute-start.4 = (f32[24,256]{1,0:T(8,128)S(1)}, f32[24,256]{1,0:T(8,128)S(1)}, u32[]{:S(2)}, u32[]{:S(2)}) collective-permute-start(f32[24,256]{1,0:T(8,128)S(1)} %get-tuple-element.31), channel_id=1, source_target_pairs={{0,1},{1,2},{2,3},{3,4},{4,5},{5,6},{6,7},{7,8},{8,9},{9,10},{10,1... | collective-permute-start | bytes 73736 | tf_op jit(solution)/shard_map/ppermute | solution.py:53
  61.3 2.4 %collective-permute-start.5 = (f32[24,256]{1,0:T(8,128)S(1)}, f32[24,256]{1,0:T(8,128)S(1)}, u32[]{:S(2)}, u32[]{:S(2)}) collective-permute-start(f32[24,256]{1,0:T(8,128)S(1)} %get-tuple-element.31), channel_id=1, source_target_pairs={{1,0},{2,1},{3,2},{4,3},{5,4},{6,5},{7,6},{8,7},{9,8},{10,9},{11,1... | collective-permute-start | bytes 73736 | tf_op jit(solution)/shard_map/ppermute | solution.py:52
  63.7 0.0 copy-done.7
  63.7 0.0 copy-done.2
  63.7 0.0 copy-start.12
  63.8 0.0 copy-start.14
  63.8 1.7 %output.1 = (bf16[128,1024]{1,0:T(8,128)(2,1)}, f32[128,1024]{1,0:T(8,128)S(1)}) custom-call(bf16[128,1024]{1,0:T(8,128)(2,1)S(1)} %get-tuple-element.25.latent, bf16[128,1024]{1,0:T(8,128)(2,1)S(1)} %get-tuple-element.28.attention, bf16[1024,1024]{1,0:T(8,128)(2,1)S(1)} %copy-done.7, bf16[128,1024]{1,0:T(8,128)(2,1)S(1)} %get-tuple-element.29.grad_query, ...), custom_call_target="tpu_custom_call" | custom-call | tf_op jit(solution)/shard_map/output/pallas_call | solution.py:40
  65.4 0.0 collective-permute-done.4.low_stats
  65.4 1.8 %collective-permute-done.5.high_stats = f32[24,256]{1,0:T(8,128)S(1)} collective-permute-done((f32[24,256]{1,0:T(8,128)S(1)}, f32[24,256]{1,0:T(8,128)S(1)}, u32[]{:S(2)}, u32[]{:S(2)}) %collective-permute-start.5) | collective-permute-done | bytes 24608 | tf_op jit(solution)/shard_map/ppermute | solution.py:52
  67.2 0.0 copy-done.12
  67.2 0.0 copy-done.14
  67.2 4.2 %finish.1 = bf16[128,1024]{1,0:T(8,128)(2,1)} custom-call(f32[24,256]{1,0:T(8,128)S(1)} %collective-permute-done.4.low_stats, f32[24,256]{1,0:T(8,128)S(1)} %collective-permute-done.5.high_stats, s32[8,256]{1,0:T(8,128)S(1)} %get-tuple-element.32.near_window, bf16[256,1024]{1,0:T(8,128)(2,1)S(1)} %copy-done.14, ...), custom_call_target="tpu_custom_call" | custom-call | tf_op jit(solution)/shard_map/finish/pallas_call | solution.py:417
  (18 shorter events, 0.0 us)
Async XLA Ops:
  0.6 1.2 %copy-start.8 = (bf16[512,1024]{1,0:T(8,128)(2,1)S(1)}, bf16[512,1024]{1,0:T(8,128)(2,1)}, u32[]{:S(2)}) copy-start(bf16[512,1024]{1,0:T(8,128)(2,1)} %grid.3) | copy-start | bytes 3145732
  1.9 0.9 %copy-start.10 = (bf16[128,1024]{1,0:T(8,128)(2,1)S(1)}, bf16[128,1024]{1,0:T(8,128)(2,1)}, u32[]{:S(2)}) copy-start(bf16[128,1024]{1,0:T(8,128)(2,1)} %cot.5) | copy-start | bytes 786436
  2.8 0.7 %copy-start.20 = (s32[4096]{0:T(1024)S(1)}, s32[4096]{0:T(1024)}, u32[]{:S(2)}) copy-start(s32[4096]{0:T(1024)} %param.19) | copy-start | bytes 49156
  3.5 0.7 %copy-start.21 = (s32[4096]{0:T(1024)S(1)}, s32[4096]{0:T(1024)}, u32[]{:S(2)}) copy-start(s32[4096]{0:T(1024)} %param.20) | copy-start | bytes 49156
  4.2 0.7 copy-start.22
  4.9 0.7 copy-start.26
  5.6 0.7 copy-start.27
  6.2 0.7 copy-start.28
  6.9 0.7 copy-start.29
  7.5 15.0 %copy-start.9 = (bf16[512,1024]{1,0:T(8,128)(2,1)S(1)}, bf16[512,1024]{1,0:T(8,128)(2,1)}, u32[]{:S(2)}) copy-start(bf16[512,1024]{1,0:T(8,128)(2,1)} %grid.3) | copy-start | bytes 3145732
  9.7 22.8 %collective-permute-start = (bf16[272,1024]{1,0:T(8,128)(2,1)}, bf16[272,1024]{1,0:T(8,128)(2,1)}, u32[]{:S(2)}, u32[]{:S(2)}) collective-permute-start(bf16[272,1024]{1,0:T(8,128)(2,1)} %get-tuple-element.21), channel_id=1, source_target_pairs={{0,1},{1,2},{2,3},{3,4},{4,5},{5,6},{6,7},{7,8},{8,9},{9,10},{10,1... | collective-permute-start | bytes 1671176 | tf_op jit(solution)/shard_map/ppermute | solution.py:53
  14.2 18.2 %collective-permute-start.1 = (bf16[272,1024]{1,0:T(8,128)(2,1)}, bf16[272,1024]{1,0:T(8,128)(2,1)}, u32[]{:S(2)}, u32[]{:S(2)}) collective-permute-start(bf16[272,1024]{1,0:T(8,128)(2,1)} %get-tuple-element.22), channel_id=1, source_target_pairs={{1,0},{2,1},{3,2},{4,3},{5,4},{6,5},{7,6},{8,7},{9,8},{10,9},{11,1... | collective-permute-start | bytes 1671176 | tf_op jit(solution)/shard_map/ppermute | solution.py:52
  16.1 20.4 %all-to-all-start = ((bf16[16,8,1024]{2,1,0:T(8,128)(2,1)}), bf16[16,8,1024]{2,1,0:T(8,128)(2,1)S(1)}, u32[]{:S(2)}, u32[]{:S(2)}) async-start(bf16[16,8,1024]{2,1,0:T(8,128)(2,1)} %bitcast.4), calls=%async_computation | async-start | bytes 524288 | tf_op jit(solution)/shard_map/all_to_all | solution.py:355
  22.6 1.6 %copy-start.3 = (bf16[1024,1024]{1,0:T(8,128)(2,1)S(1)}, bf16[1024,1024]{1,0:T(8,128)(2,1)}, u32[]{:S(2)}) copy-start(bf16[1024,1024]{1,0:T(8,128)(2,1)} %w_edge.5) | copy-start | bytes 6291460
  24.2 1.6 %copy-start.5 = (bf16[1024,1024]{1,0:T(8,128)(2,1)S(1)}, bf16[1024,1024]{1,0:T(8,128)(2,1)}, u32[]{:S(2)}) copy-start(bf16[1024,1024]{1,0:T(8,128)(2,1)} %w_out.5) | copy-start | bytes 6291460
  25.8 0.9 %copy-start.11 = (bf16[128,1024]{1,0:T(8,128)(2,1)S(1)}, bf16[128,1024]{1,0:T(8,128)(2,1)}, u32[]{:S(2)}) copy-start(bf16[128,1024]{1,0:T(8,128)(2,1)} %cot.5) | copy-start | bytes 786436
  26.7 0.9 %copy-start.17 = (bf16[128,1024]{1,0:T(8,128)(2,1)S(1)}, bf16[128,1024]{1,0:T(8,128)(2,1)}, u32[]{:S(2)}) copy-start(bf16[128,1024]{1,0:T(8,128)(2,1)} %mesh_in.1) | copy-start | bytes 786436
  27.7 0.7 copy-start.24
  28.4 0.7 copy-start.25
  29.1 3.4 %copy-start.4 = (bf16[1024,1024]{1,0:T(8,128)(2,1)S(1)}, bf16[1024,1024]{1,0:T(8,128)(2,1)}, u32[]{:S(2)}) copy-start(bf16[1024,1024]{1,0:T(8,128)(2,1)} %w_edge.5) | copy-start | bytes 6291460
  29.1 3.4 %copy-start.6 = (bf16[1024,1024]{1,0:T(8,128)(2,1)S(1)}, bf16[1024,1024]{1,0:T(8,128)(2,1)}, u32[]{:S(2)}) copy-start(bf16[1024,1024]{1,0:T(8,128)(2,1)} %w_out.5) | copy-start | bytes 6291460
  31.7 0.7 copy-start.18
  35.8 0.8 %copy-start.15 = (f32[128,1024]{1,0:T(8,128)}, f32[128,1024]{1,0:T(8,128)S(1)}, u32[]{:S(2)}) copy-start(f32[128,1024]{1,0:T(8,128)S(1)} %get-tuple-element.24.partial) | copy-start | bytes 1572868
  36.5 1.0 %copy-start.16 = (f32[128,1024]{1,0:T(8,128)S(1)}, f32[128,1024]{1,0:T(8,128)}, u32[]{:S(2)}) copy-start(f32[128,1024]{1,0:T(8,128)} %copy-done.15) | copy-start | bytes 1572868
  38.5 11.3 %copy-start.23 = (s32[2,128]{1,0:T(2,128)S(1)}, s32[2,128]{1,0:T(2,128)}, u32[]{:S(2)}) copy-start(s32[2,128]{1,0:T(2,128)} %window.3) | copy-start | bytes 3076
  38.5 9.5 %collective-permute-start.2 = (bf16[128,1024]{1,0:T(8,128)(2,1)S(1)}, bf16[128,1024]{1,0:T(8,128)(2,1)S(1)}, u32[]{:S(2)}, u32[]{:S(2)}) collective-permute-start(bf16[128,1024]{1,0:T(8,128)(2,1)S(1)} %get-tuple-element.26.normed), channel_id=1, source_target_pairs={{0,1},{1,2},{2,3},{3,4},{4,5},{5,6},{6,7},{7,8},{8,9},{9,10},{10,1... | collective-permute-start | bytes 786440 | tf_op jit(solution)/shard_map/ppermute | solution.py:53
  42.1 7.7 %collective-permute-start.3 = (bf16[128,1024]{1,0:T(8,128)(2,1)S(1)}, bf16[128,1024]{1,0:T(8,128)(2,1)S(1)}, u32[]{:S(2)}, u32[]{:S(2)}) collective-permute-start(bf16[128,1024]{1,0:T(8,128)(2,1)S(1)} %get-tuple-element.26.normed), channel_id=1, source_target_pairs={{1,0},{2,1},{3,2},{4,3},{5,4},{6,5},{7,6},{8,7},{9,8},{10,9},{11,1... | collective-permute-start | bytes 786440 | tf_op jit(solution)/shard_map/ppermute | solution.py:52
  44.2 2.8 %copy-start = (bf16[1024,3072]{1,0:T(8,128)(2,1)S(1)}, bf16[1024,3072]{1,0:T(8,128)(2,1)}, u32[]{:S(2)}) copy-start(bf16[1024,3072]{1,0:T(8,128)(2,1)} %w_qkv.7) | copy-start | bytes 18874372
  47.0 2.8 %copy-start.19 = (bf16[128,1024]{1,0:T(8,128)(2,1)S(1)}, bf16[128,1024]{1,0:T(8,128)(2,1)}, u32[]{:S(2)}) copy-start(bf16[128,1024]{1,0:T(8,128)(2,1)} %copy-done.18) | copy-start | bytes 786436
  47.0 16.7 %copy-start.7 = (bf16[1024,1024]{1,0:T(8,128)(2,1)S(1)}, bf16[1024,1024]{1,0:T(8,128)(2,1)}, u32[]{:S(2)}) copy-start(bf16[1024,1024]{1,0:T(8,128)(2,1)} %w_out.5) | copy-start | bytes 6291460
  49.8 2.8 %copy-start.1 = (bf16[1024,3072]{1,0:T(8,128)(2,1)S(1)}, bf16[1024,3072]{1,0:T(8,128)(2,1)}, u32[]{:S(2)}) copy-start(bf16[1024,3072]{1,0:T(8,128)(2,1)} %w_qkv.7) | copy-start | bytes 18874372
  52.6 11.2 %copy-start.2 = (bf16[1024,3072]{1,0:T(8,128)(2,1)S(1)}, bf16[1024,3072]{1,0:T(8,128)(2,1)}, u32[]{:S(2)}) copy-start(bf16[1024,3072]{1,0:T(8,128)(2,1)} %w_qkv.7) | copy-start | bytes 18874372
  58.6 0.8 %copy-start.13 = (bf16[256,1024]{1,0:T(8,128)(2,1)}, bf16[256,1024]{1,0:T(8,128)(2,1)S(1)}, u32[]{:S(2)}) copy-start(bf16[256,1024]{1,0:T(8,128)(2,1)S(1)} %get-tuple-element.33.near_q) | copy-start | bytes 1572868
  59.4 6.0 %collective-permute-start.4 = (f32[24,256]{1,0:T(8,128)S(1)}, f32[24,256]{1,0:T(8,128)S(1)}, u32[]{:S(2)}, u32[]{:S(2)}) collective-permute-start(f32[24,256]{1,0:T(8,128)S(1)} %get-tuple-element.31), channel_id=1, source_target_pairs={{0,1},{1,2},{2,3},{3,4},{4,5},{5,6},{6,7},{7,8},{8,9},{9,10},{10,1... | collective-permute-start | bytes 73736 | tf_op jit(solution)/shard_map/ppermute | solution.py:53
  61.3 5.9 %collective-permute-start.5 = (f32[24,256]{1,0:T(8,128)S(1)}, f32[24,256]{1,0:T(8,128)S(1)}, u32[]{:S(2)}, u32[]{:S(2)}) collective-permute-start(f32[24,256]{1,0:T(8,128)S(1)} %get-tuple-element.31), channel_id=1, source_target_pairs={{1,0},{2,1},{3,2},{4,3},{5,4},{6,5},{7,6},{8,7},{9,8},{10,9},{11,1... | collective-permute-start | bytes 73736 | tf_op jit(solution)/shard_map/ppermute | solution.py:52
  63.7 3.4 %copy-start.12 = (bf16[128,1024]{1,0:T(8,128)(2,1)S(1)}, bf16[128,1024]{1,0:T(8,128)(2,1)}, u32[]{:S(2)}) copy-start(bf16[128,1024]{1,0:T(8,128)(2,1)} %cot.5) | copy-start | bytes 786436
  63.8 3.4 %copy-start.14 = (bf16[256,1024]{1,0:T(8,128)(2,1)S(1)}, bf16[256,1024]{1,0:T(8,128)(2,1)}, u32[]{:S(2)}) copy-start(bf16[256,1024]{1,0:T(8,128)(2,1)} %copy-done.13) | copy-start | bytes 1572868

commit v3 on v2

--- a/solution.py
+++ b/solution.py
@@ -13,7 +13,7 @@
 F32 = jnp.float32
 BF16 = jnp.bfloat16
 I32 = jnp.int32
-VMEM_LIMIT = 44 * 2**20
+VMEM_LIMIT = 28 * 2**20
 
 
 def mm(a, b):
@@ -32,19 +32,31 @@
     return lax.broadcasted_iota(I32, shape, dim)
 
 
-def call(kernel, outs, args, smem=(), name=None):
+def call(kernel, outs, args, hbm=(), scratch=(), name=None):
+    args = [pltpu.with_memory_space_constraint(a, pltpu.HBM) if i in hbm else a for i, a in enumerate(args)]
     specs = [
-        pl.BlockSpec(memory_space=pltpu.SMEM if i in smem else pltpu.VMEM)
-        for i in range(len(args))
+        pl.BlockSpec(memory_space=pltpu.HBM if i in hbm else pltpu.VMEM) for i in range(len(args))
     ]
     return pl.pallas_call(
         kernel,
         out_shape=[jax.ShapeDtypeStruct(shape, dtype) for shape, dtype in outs],
         in_specs=specs,
         out_specs=[pl.BlockSpec(memory_space=pltpu.VMEM) for _ in outs],
+        scratch_shapes=list(scratch),
         compiler_params=pltpu.CompilerParams(vmem_limit_bytes=VMEM_LIMIT),
         name=name,
     )(*args)
+
+
+def start_all(pairs, sems):
+    copies = [pltpu.make_async_copy(src, dst, sems.at[i]) for i, (src, dst) in enumerate(pairs)]
+    for copy in copies:
+        copy.start()
+    return copies
+
+
+def like(*arrays):
+    return [pltpu.VMEM(a.shape, a.dtype) for a in arrays]
 
 
 def exchange(toward_low, toward_high, axis):
@@ -78,18 +90,57 @@
 
 
 def pack_kernel(
-    far_count, side_count, grid, cot, window, side_src, side_dst, far_src, far_dst, far_out, low_out, high_out
+    grid_hbm,
+    cot_hbm,
+    window_hbm,
+    side_src_hbm,
+    side_dst_hbm,
+    side_count_hbm,
+    far_src_hbm,
+    far_dst_hbm,
+    far_count_hbm,
+    far_out,
+    low_out,
+    high_out,
+    grid,
+    window,
+    side_src,
+    side_dst,
+    side_count,
+    far_src,
+    far_dst,
+    far_count,
+    sems,
 ):
     grid_rows, channels = grid.shape
-    mesh_rows = cot.shape[0]
+    mesh_rows = cot_hbm.shape[0]
     slots = far_src.shape[1]
-    devices = far_count.shape[0]
+    devices = far_count.shape[1]
     depth = slots // devices
+    first = grid_rows - BAND
+    copies = start_all(
+        [
+            (far_src_hbm, far_src),
+            (far_dst_hbm, far_dst),
+            (far_count_hbm, far_count),
+            (grid_hbm, grid),
+            (side_src_hbm, side_src),
+            (side_dst_hbm, side_dst),
+            (side_count_hbm, side_count),
+            (window_hbm, window),
+            (grid_hbm.at[pl.ds(0, BAND)], low_out.at[pl.ds(0, BAND)]),
+            (grid_hbm.at[pl.ds(first, BAND)], high_out.at[pl.ds(0, BAND)]),
+            (cot_hbm, low_out.at[pl.ds(BAND, mesh_rows)]),
+            (cot_hbm, high_out.at[pl.ds(BAND, mesh_rows)]),
+        ],
+        sems,
+    )
+    for copy in copies[:4]:
+        copy.wait()
     slot = iota((1, slots), 1)
-    live = jnp.zeros((1, slots), I32)
-    for r in range(devices):
-        live = jnp.where(slot // depth == r, far_count[r], live)
-    target = jnp.where(slot % depth < live, far_dst[...], mesh_rows).astype(F32)
+    receiver = jnp.where(iota((devices, slots), 0) == iota((devices, slots), 1) // depth, 1.0, 0.0)
+    live = mm(far_count[...].astype(F32).astype(BF16), receiver.astype(BF16))
+    target = jnp.where((slot % depth).astype(F32) < live, far_dst[...].astype(F32), 1.0 * mesh_rows)
     place = slot // depth * (2 * depth) + slot % depth
     select = onehot_rows([far_src[...]], grid_rows)
     spread = mm_nt(select, onehot_rows([place], 2 * slots)).astype(BF16)
@@ -98,30 +149,70 @@
         jnp.where(iota((2 * slots, slots), 0) == place + depth, target, 0.0), 1, keepdims=True
     )
     far_out[...] = (rows + column).astype(BF16)
+    for copy in copies[4:]:
+        copy.wait()
     count = side_src.shape[0] // 2
     for k, out in ((0, low_out), (1, high_out)):
-        start = 0 if k == 0 else grid_rows - BAND
-        out[:BAND] = grid[start : start + BAND]
-        out[BAND : BAND + mesh_rows] = cot[...]
         rank = iota((count, LANES), 0) * LANES + iota((count, LANES), 1)
-        src = side_src[k * count : (k + 1) * count] - start
-        dst = jnp.where(rank < side_count[k], side_dst[k * count : (k + 1) * count], mesh_rows)
+        src = side_src[k * count : (k + 1) * count] - k * first
+        live = rank < side_count[:, k : k + 1]
+        dst = jnp.where(live, side_dst[k * count : (k + 1) * count], mesh_rows)
         reach = jnp.concatenate([window[...], jnp.zeros((count - 2, mesh_rows), I32)], 0)
         blank = jnp.zeros((count, channels - 2 * LANES - mesh_rows), I32)
         meta = jnp.concatenate([src, dst, reach, blank], 1)
         out[BAND + mesh_rows :] = meta.astype(F32).astype(BF16)
 
 
-def own_kernel(grid, w_edge, mesh_in, own_src, own_dst, cot, w_out, partial_out, grad_out):
+def own_kernel(
+    grid_hbm,
+    mesh_in_hbm,
+    own_src_hbm,
+    own_dst_hbm,
+    cot_hbm,
+    w_edge_hbm,
+    w_out_hbm,
+    w_qkv_hbm,
+    partial_out,
+    grad_out,
+    w_edge,
+    w_out,
+    w_qkv,
+    grid,
+    mesh_in,
+    own_src,
+    own_dst,
+    cot,
+    sems,
+):
     grid_rows = grid.shape[0]
     mesh_rows = mesh_in.shape[0]
-    active = gelu(mm(grid[...], w_edge[...]))
+    copies = start_all(
+        [
+            (own_src_hbm, own_src),
+            (own_dst_hbm, own_dst),
+            (w_edge_hbm, w_edge),
+            (grid_hbm, grid),
+            (mesh_in_hbm, mesh_in),
+            (cot_hbm, cot),
+            (w_out_hbm, w_out),
+            (w_qkv_hbm, w_qkv),
+        ],
+        sems,
+    )
+    for copy in copies[:2]:
+        copy.wait()
     rows = own_src.shape[0]
     src = onehot_rows([own_src[r : r + 1] for r in range(rows)], grid_rows)
     dst = onehot_rows([own_dst[r : r + 1] for r in range(rows)], mesh_rows)
     counts = mm_nt(dst, src).astype(BF16)
+    for copy in copies[2:5]:
+        copy.wait()
+    active = gelu(mm(grid[...], w_edge[...]))
     partial_out[...] = mesh_in[...].astype(F32) + mm(counts, active)
+    for copy in copies[5:7]:
+        copy.wait()
     grad_out[...] = mm_nt(cot[...], w_out[...]).astype(BF16)
+    copies[7].wait()
 
 
 def side_kernel(low, high, w_edge, w_out, partial, partial_out, grad_out, window_out):
@@ -188,7 +279,7 @@
     w_qkv,
     own_qkv,
     own_grad,
-    window,
+    window_hbm,
     stats_out,
     att_out,
     gq_out,
@@ -196,7 +287,10 @@
     gv_out,
     near_q_out,
     kv,
+    window,
+    sems,
 ):
+    fetch = start_all([(window_hbm, window)], sems)
     m, channels = low_normed.shape
     devices = lax.axis_size("node")
     me = lax.axis_index("node")
@@ -205,6 +299,7 @@
     kv[:m] = near[:m, channels:]
     kv[m : 2 * m] = own_qkv[:, channels:]
     kv[2 * m :] = near[m:, channels:]
+    fetch[0].wait()
     key_at = iota((3 * m, m), 0)
     query_at = iota((3 * m, m), 1) + m
     inside = (key_at >= jnp.where(me == 0, m, 0)) & (
@@ -259,10 +354,13 @@
     grad_normed,
     w_qkv,
     latent,
-    cot,
+    cot_hbm,
     grad_out,
     grad_kv,
+    cot,
+    sems,
 ):
+    fetch = start_all([(cot_hbm, cot)], sems)
     m, channels = latent.shape
     key_at = iota((m, 2 * m), 0) + m
     lane = iota((m, 2 * m), 1)
@@ -300,6 +398,7 @@
         - jnp.mean(total, -1, keepdims=True)
         - normal * jnp.mean(total * normal, -1, keepdims=True)
     )
+    fetch[0].wait()
     grad_out[...] = (cot[...].astype(F32) + inv_std * centred).astype(BF16)
 
 
@@ -331,6 +430,10 @@
     scale = head_dim ** (-0.5)
     meta_rows = side_src.shape[0] // (2 * LANES)
 
+    side_src, side_dst = side_src.reshape(-1, LANES), side_dst.reshape(-1, LANES)
+    own_src, own_dst = own_src.reshape(-1, LANES), own_dst.reshape(-1, LANES)
+    far_src, far_dst = far_src.reshape(1, -1), far_dst.reshape(1, -1)
+    side_count, far_count = side_count.reshape(1, -1), far_count.reshape(1, -1)
     far_message, toward_low, toward_high = call(
         pack_kernel,
         [
@@ -339,17 +442,21 @@
             ((BAND + m + meta_rows, channels), BF16),
         ],
         [
-            far_count,
-            side_count,
             grid_in,
             cotangent,
             window,
-            side_src.reshape(-1, LANES),
-            side_dst.reshape(-1, LANES),
-            far_src.reshape(1, far_slots),
-            far_dst.reshape(1, far_slots),
-        ],
-        smem=(0, 1),
+            side_src,
+            side_dst,
+            side_count,
+            far_src,
+            far_dst,
+            far_count,
+        ],
+        hbm=range(9),
+        scratch=like(
+            grid_in, window, side_src, side_dst, side_count, far_src, far_dst, far_count
+        )
+        + [pltpu.SemaphoreType.DMA((12,))],
         name="pack",
     )
     got_far = lax.all_to_all(
@@ -361,18 +468,19 @@
     ).reshape(2 * far_slots, channels)
     from_low, from_high = exchange(toward_low, toward_high, "node")
 
-    partial, own_grad = call(
+    partial, own_grad, w_edge, w_out, w_qkv = call(
         own_kernel,
-        [((m, channels), F32), ((m, channels), BF16)],
-        [
-            grid_in,
-            w_edge,
-            mesh_in,
-            own_src.reshape(-1, LANES),
-            own_dst.reshape(-1, LANES),
-            cotangent,
-            w_out,
-        ],
+        [
+            ((m, channels), F32),
+            ((m, channels), BF16),
+            (w_edge.shape, BF16),
+            (w_out.shape, BF16),
+            (w_qkv.shape, BF16),
+        ],
+        [grid_in, mesh_in, own_src, own_dst, cotangent, w_edge, w_out, w_qkv],
+        hbm=range(8),
+        scratch=like(grid_in, mesh_in, own_src, own_dst, cotangent)
+        + [pltpu.SemaphoreType.DMA((8,))],
         name="own",
     )
     partial, near_grad, near_window = call(
@@ -390,22 +498,23 @@
     low_normed, high_normed = exchange(normed, normed, "node")
     (own_qkv,) = call(project_kernel, [((m, 3 * channels), BF16)], [normed, w_qkv], name="project")
 
-    stats, attention, grad_query, grad_key, grad_value, near_q = pl.pallas_call(
+    stats, attention, grad_query, grad_key, grad_value, near_q = call(
         functools.partial(attend_kernel, scale, pair),
-        out_shape=[
-            jax.ShapeDtypeStruct((3 * pairs, 2 * m), F32),
-            jax.ShapeDtypeStruct((m, channels), BF16),
-            jax.ShapeDtypeStruct((m, channels), BF16),
-            jax.ShapeDtypeStruct((m, channels), F32),
-            jax.ShapeDtypeStruct((m, channels), F32),
-            jax.ShapeDtypeStruct((2 * m, channels), BF16),
-        ],
-        in_specs=[pl.BlockSpec(memory_space=pltpu.VMEM)] * 6,
-        out_specs=[pl.BlockSpec(memory_space=pltpu.VMEM)] * 6,
-        scratch_shapes=[pltpu.VMEM((3 * m, 2 * channels), BF16)],
-        compiler_params=pltpu.CompilerParams(vmem_limit_bytes=VMEM_LIMIT),
+        [
+            ((3 * pairs, 2 * m), F32),
+            ((m, channels), BF16),
+            ((m, channels), BF16),
+            ((m, channels), F32),
+            ((m, channels), F32),
+            ((2 * m, channels), BF16),
+        ],
+        [low_normed, high_normed, w_qkv, own_qkv, own_grad, window],
+        hbm=(5,),
+        scratch=[pltpu.VMEM((3 * m, 2 * channels), BF16)]
+        + like(window)
+        + [pltpu.SemaphoreType.DMA((1,))],
         name="attend",
-    )(low_normed, high_normed, w_qkv, own_qkv, own_grad, window)
+    )
     low_stats, high_stats = exchange(stats, stats, "node")
 
     mesh_out, grad_normed = call(
@@ -414,27 +523,28 @@
         [latent, attention, w_out, grad_query, w_qkv],
         name="output",
     )
-    mesh_grad = pl.pallas_call(
+    (mesh_grad,) = call(
         functools.partial(finish_kernel, pair),
-        out_shape=jax.ShapeDtypeStruct((m, channels), BF16),
-        in_specs=[pl.BlockSpec(memory_space=pltpu.VMEM)] * 12,
-        out_specs=pl.BlockSpec(memory_space=pltpu.VMEM),
-        scratch_shapes=[pltpu.VMEM((m, 2 * channels), BF16)],
-        compiler_params=pltpu.CompilerParams(vmem_limit_bytes=VMEM_LIMIT),
+        [((m, channels), BF16)],
+        [
+            low_stats,
+            high_stats,
+            near_window,
+            near_q,
+            near_grad,
+            own_qkv,
+            grad_key,
+            grad_value,
+            grad_normed,
+            w_qkv,
+            latent,
+            cotangent,
+        ],
+        hbm=(11,),
+        scratch=[pltpu.VMEM((m, 2 * channels), BF16)]
+        + like(cotangent)
+        + [pltpu.SemaphoreType.DMA((1,))],
         name="finish",
-    )(
-        low_stats,
-        high_stats,
-        near_window,
-        near_q,
-        near_grad,
-        own_qkv,
-        grad_key,
-        grad_value,
-        grad_normed,
-        w_qkv,
-        latent,
-        cotangent,
     )
     return (mesh_out, mesh_grad)
 

time: 72.5 us -> 64.4 us (0.89)
  the two profiles are of different devices: /device:TPU:1 before, /device:TPU:8 now
where the time goes in v3:
time: 64.4 us; the launch traced here: 63.9 us
  Pallas kernels  25 us (39%)
  starting transfers between devices  22.6 us (35%)
  local copies, waits for them, and re-layouts  10.2 us (16%)
  waiting for transfers between devices  5.15 us (8%)
  between operations  0.95 us (1%)
    pallas_call x8, Pallas kernels, call(): pl.pallas_call(kernel, out_shape=[jax.ShapeDtypeStruct(shape, dtype) for...  25 us
    ppermute x3, starting transfers between devices, exchange(): lax.ppermute(toward_low, axis, [(i + 1, i) for i in range(ends)])  11.3 us
    unnamed x22, local copies, waits for them, and re-layouts  10.2 us
    ppermute x3, starting transfers between devices, exchange(): lax.ppermute(toward_high, axis, [(i, i + 1) for i in range(ends)])  5.94 us
    all_to_all x1, starting transfers between devices, body(): lax.all_to_all(far_message.reshape(devices, 2 * far_depth, channels), 'no...  5.41 us
    ppermute x3, waiting for transfers between devices, exchange(): lax.ppermute(toward_high, axis, [(i, i + 1) for i in range(ends)])  5.14 us
  transfers between devices with their start and end apart: 7, of which 2 were waited for; matrix products, arithmetic and copies ran while one was open for 0% of the time, Pallas kernels for 15%

profile of v3, /device:TPU:8, one launch (start us, length us, event | category | flops | bytes accessed | tf_op | source)
XLA Modules:
  0.0 63.9 jit_solution(14394538281127302917)
XLA Ops:
  0.6 3.0 %pack.1 = (bf16[128,1024]{1,0:T(8,128)(2,1)}, bf16[272,1024]{1,0:T(8,128)(2,1)}, bf16[272,1024]{1,0:T(8,128)(2,1)}) custom-call(bf16[512,1024]{1,0:T(8,128)(2,1)} %grid_hbm.3, bf16[128,1024]{1,0:T(8,128)(2,1)} %cot_hbm.5, s32[2,128]{1,0:T(2,128)} %window_hbm.3, s32[32,128]{1,0:T(8,128)} %bitcast.11, s32[32,128]{1,0:T(8,128)} %bitcast.12, s32[1,2]{1,0:T(1,128)} %bitcast.15, ...), custom_call_target="tpu_custom_call" | custom-call | tf_op jit(solution)/shard_map/pack/pallas_call | solution.py:40
  3.6 1.9 %collective-permute-start = (bf16[272,1024]{1,0:T(8,128)(2,1)}, bf16[272,1024]{1,0:T(8,128)(2,1)S(1)}, u32[]{:S(2)}, u32[]{:S(2)}) collective-permute-start(bf16[272,1024]{1,0:T(8,128)(2,1)} %get-tuple-element.25), channel_id=1, source_target_pairs={{0,1},{1,2},{2,3},{3,4},{4,5},{5,6},{6,7},{7,8},{8,9},{9,10},{10,1... | collective-permute-start | bytes 1671176 | tf_op jit(solution)/shard_map/ppermute | solution.py:65
  5.6 4.5 %collective-permute-start.1 = (bf16[272,1024]{1,0:T(8,128)(2,1)}, bf16[272,1024]{1,0:T(8,128)(2,1)S(1)}, u32[]{:S(2)}, u32[]{:S(2)}) collective-permute-start(bf16[272,1024]{1,0:T(8,128)(2,1)} %get-tuple-element.26), channel_id=1, source_target_pairs={{1,0},{2,1},{3,2},{4,3},{5,4},{6,5},{7,6},{8,7},{9,8},{10,9},{11,1... | collective-permute-start | bytes 1671176 | tf_op jit(solution)/shard_map/ppermute | solution.py:64
  10.1 5.4 %all-to-all-start = ((bf16[16,8,1024]{2,1,0:T(8,128)(2,1)}), bf16[16,8,1024]{2,1,0:T(8,128)(2,1)S(1)}, u32[]{:S(2)}, u32[]{:S(2)}) async-start(bf16[16,8,1024]{2,1,0:T(8,128)(2,1)} %bitcast.6), calls=%async_computation | async-start | bytes 524288 | tf_op jit(solution)/shard_map/all_to_all | solution.py:462
  15.5 4.6 %own.1 = (f32[128,1024]{1,0:T(8,128)S(1)}, bf16[128,1024]{1,0:T(8,128)(2,1)S(1)}, bf16[1024,1024]{1,0:T(8,128)(2,1)S(1)}, bf16[1024,1024]{1,0:T(8,128)(2,1)S(1)}, bf16[1024,3072]{1,0:T(8,128)(2,1)S(1)}) custom-call(bf16[512,1024]{1,0:T(8,128)(2,1)} %grid_hbm.3, bf16[128,1024]{1,0:T(8,128)(2,1)} %mesh_in_hbm.1, s32[8,128]{1,0:T(8,128)} %bitcast.13, ...), custom_call_target="tpu_custom_call" | custom-call | tf_op jit(solution)/shard_map/own/pallas_call | solution.py:40
  20.1 0.0 copy-start
  20.1 2.7 %copy-done = bf16[1024,3072]{1,0:T(8,128)(2,1)} copy-done((bf16[1024,3072]{1,0:T(8,128)(2,1)}, bf16[1024,3072]{1,0:T(8,128)(2,1)S(1)}, u32[]{:S(2)}) %copy-start) | copy-done | bytes 6291480
  22.8 0.0 copy-start.9
  22.8 0.7 %copy-done.9 = bf16[128,1024]{1,0:T(8,128)(2,1)} copy-done((bf16[128,1024]{1,0:T(8,128)(2,1)}, bf16[128,1024]{1,0:T(8,128)(2,1)S(1)}, u32[]{:S(2)}) %copy-start.9) | copy-done | bytes 262168
  23.5 0.0 collective-permute-done.low
  23.5 0.0 collective-permute-done.1.high
  23.5 2.1 %side.1 = (f32[128,1024]{1,0:T(8,128)S(1)}, bf16[256,1024]{1,0:T(8,128)(2,1)S(1)}, s32[8,256]{1,0:T(8,128)S(1)}) custom-call(bf16[272,1024]{1,0:T(8,128)(2,1)S(1)} %collective-permute-done.low, bf16[272,1024]{1,0:T(8,128)(2,1)S(1)} %collective-permute-done.1.high, bf16[1024,1024]{1,0:T(8,128)(2,1)S(1)} %get-tuple-element.24.w_edge, ...), custom_call_target="tpu_custom_call" | custom-call | tf_op jit(solution)/shard_map/side/pallas_call | solution.py:40
  25.6 0.0 copy-start.3
  25.6 1.4 %copy-done.3 = bf16[1024,1024]{1,0:T(8,128)(2,1)} copy-done((bf16[1024,1024]{1,0:T(8,128)(2,1)}, bf16[1024,1024]{1,0:T(8,128)(2,1)S(1)}, u32[]{:S(2)}) %copy-start.3) | copy-done | bytes 2097176
  27.0 0.0 copy-start.5
  27.0 0.9 %copy-done.5 = bf16[256,1024]{1,0:T(8,128)(2,1)} copy-done((bf16[256,1024]{1,0:T(8,128)(2,1)}, bf16[256,1024]{1,0:T(8,128)(2,1)S(1)}, u32[]{:S(2)}) %copy-start.5) | copy-done | bytes 524312
  27.8 0.0 copy-start.7
  27.8 0.8 %copy-done.7 = f32[128,1024]{1,0:T(8,128)} copy-done((f32[128,1024]{1,0:T(8,128)}, f32[128,1024]{1,0:T(8,128)S(1)}, u32[]{:S(2)}) %copy-start.7) | copy-done | bytes 524312
  28.6 0.0 all-to-all-done
  28.6 0.0 copy-start.8
  28.6 1.0 %copy-done.8 = f32[128,1024]{1,0:T(8,128)S(1)} copy-done((f32[128,1024]{1,0:T(8,128)S(1)}, f32[128,1024]{1,0:T(8,128)}, u32[]{:S(2)}) %copy-start.8) | copy-done | bytes 524312
  29.7 0.9 %latent.1 = (bf16[128,1024]{1,0:T(8,128)(2,1)S(1)}, bf16[128,1024]{1,0:T(8,128)(2,1)S(1)}) custom-call(bf16[128,1024]{1,0:T(8,128)(2,1)S(1)} %bitcast.10, bf16[1024,1024]{1,0:T(8,128)(2,1)S(1)} %get-tuple-element.24.w_edge, f32[128,1024]{1,0:T(8,128)S(1)} %copy-done.8), custom_call_target="tpu_custom_call" | custom-call | tf_op jit(solution)/shard_map/latent/pallas_call | solution.py:40
  30.6 3.1 %collective-permute-start.3 = (bf16[128,1024]{1,0:T(8,128)(2,1)S(1)}, bf16[128,1024]{1,0:T(8,128)(2,1)S(1)}, u32[]{:S(2)}, u32[]{:S(2)}) collective-permute-start(bf16[128,1024]{1,0:T(8,128)(2,1)S(1)} %get-tuple-element.31.normed), channel_id=1, source_target_pairs={{1,0},{2,1},{3,2},{4,3},{5,4},{6,5},{7,6},{8,7},{9,8},{10,9},{11,1... | collective-permute-start | bytes 786440 | tf_op jit(solution)/shard_map/ppermute | solution.py:64
  33.7 2.1 %collective-permute-start.2 = (bf16[128,1024]{1,0:T(8,128)(2,1)S(1)}, bf16[128,1024]{1,0:T(8,128)(2,1)S(1)}, u32[]{:S(2)}, u32[]{:S(2)}) collective-permute-start(bf16[128,1024]{1,0:T(8,128)(2,1)S(1)} %get-tuple-element.31.normed), channel_id=1, source_target_pairs={{0,1},{1,2},{2,3},{3,4},{4,5},{5,6},{6,7},{7,8},{8,9},{9,10},{10,1... | collective-permute-start | bytes 786440 | tf_op jit(solution)/shard_map/ppermute | solution.py:65
  35.8 0.0 copy-start.1
  35.8 2.8 %copy-done.1 = bf16[1024,3072]{1,0:T(8,128)(2,1)S(1)} copy-done((bf16[1024,3072]{1,0:T(8,128)(2,1)S(1)}, bf16[1024,3072]{1,0:T(8,128)(2,1)}, u32[]{:S(2)}) %copy-start.1) | copy-done | bytes 6291480
  38.6 0.0 copy-start.2
  38.6 0.0 copy-start.10
  38.6 1.0 %project.1.own_qkv = bf16[128,3072]{1,0:T(8,128)(2,1)S(1)} custom-call(bf16[128,1024]{1,0:T(8,128)(2,1)S(1)} %get-tuple-element.31.normed, bf16[1024,3072]{1,0:T(8,128)(2,1)S(1)} %copy-done.1), custom_call_target="tpu_custom_call" | custom-call | tf_op jit(solution)/shard_map/project/pallas_call | solution.py:40
  39.6 0.0 collective-permute-done.3.high_normed
  39.6 2.7 %collective-permute-done.2.low_normed = bf16[128,1024]{1,0:T(8,128)(2,1)S(1)} collective-permute-done((bf16[128,1024]{1,0:T(8,128)(2,1)S(1)}, bf16[128,1024]{1,0:T(8,128)(2,1)S(1)}, u32[]{:S(2)}, u32[]{:S(2)}) %collective-permute-start.2) | collective-permute-done | bytes 262176 | tf_op jit(solution)/shard_map/ppermute | solution.py:65
  42.3 0.0 copy-done.2
  42.3 0.0 copy-done.10
  42.3 0.0 copy-start.4
  42.3 6.6 %attend.1 = (f32[24,256]{1,0:T(8,128)S(1)}, bf16[128,1024]{1,0:T(8,128)(2,1)S(1)}, bf16[128,1024]{1,0:T(8,128)(2,1)S(1)}, f32[128,1024]{1,0:T(8,128)S(1)}, f32[1...) custom-call(bf16[128,1024]{1,0:T(8,128)(2,1)S(1)} %collective-permute-done.2.low_normed, ...), custom_call_target="tpu_custom_call" | custom-call | tf_op jit(solution)/shard_map/attend/pallas_call | solution.py:40
  49.0 3.6 %collective-permute-start.5 = (f32[24,256]{1,0:T(8,128)S(1)}, f32[24,256]{1,0:T(8,128)S(1)}, u32[]{:S(2)}, u32[]{:S(2)}) collective-permute-start(f32[24,256]{1,0:T(8,128)S(1)} %get-tuple-element.37), channel_id=1, source_target_pairs={{1,0},{2,1},{3,2},{4,3},{5,4},{6,5},{7,6},{8,7},{9,8},{10,9},{11,1... | collective-permute-start | bytes 73736 | tf_op jit(solution)/shard_map/ppermute | solution.py:64
  52.6 1.9 %collective-permute-start.4 = (f32[24,256]{1,0:T(8,128)S(1)}, f32[24,256]{1,0:T(8,128)S(1)}, u32[]{:S(2)}, u32[]{:S(2)}) collective-permute-start(f32[24,256]{1,0:T(8,128)S(1)} %get-tuple-element.37), channel_id=1, source_target_pairs={{0,1},{1,2},{2,3},{3,4},{4,5},{5,6},{6,7},{7,8},{8,9},{9,10},{10,1... | collective-permute-start | bytes 73736 | tf_op jit(solution)/shard_map/ppermute | solution.py:65
  54.5 0.0 copy-done.4
  54.6 0.0 copy-start.6
  54.6 1.6 %output.1 = (bf16[128,1024]{1,0:T(8,128)(2,1)}, f32[128,1024]{1,0:T(8,128)S(1)}) custom-call(bf16[128,1024]{1,0:T(8,128)(2,1)S(1)} %get-tuple-element.30.latent, bf16[128,1024]{1,0:T(8,128)(2,1)S(1)} %get-tuple-element.34.attention, bf16[1024,1024]{1,0:T(8,128)(2,1)S(1)} %copy-done.4, bf16[128,1024]{1,0:T(8,128)(2,1)S(1)} %get-tuple-element.35.grad_query, ...), custom_call_target="tpu_custom_call" | custom-call | tf_op jit(solution)/shard_map/output/pallas_call | solution.py:40
  56.2 0.0 collective-permute-done.5.high_stats
  56.2 2.5 %collective-permute-done.4.low_stats = f32[24,256]{1,0:T(8,128)S(1)} collective-permute-done((f32[24,256]{1,0:T(8,128)S(1)}, f32[24,256]{1,0:T(8,128)S(1)}, u32[]{:S(2)}, u32[]{:S(2)}) %collective-permute-start.4) | collective-permute-done | bytes 24608 | tf_op jit(solution)/shard_map/ppermute | solution.py:65
  58.7 0.0 copy-done.6
  58.7 5.1 %finish.1 = bf16[128,1024]{1,0:T(8,128)(2,1)} custom-call(f32[24,256]{1,0:T(8,128)S(1)} %collective-permute-done.4.low_stats, f32[24,256]{1,0:T(8,128)S(1)} %collective-permute-done.5.high_stats, s32[8,256]{1,0:T(8,128)S(1)} %get-tuple-element.38.near_window, bf16[256,1024]{1,0:T(8,128)(2,1)S(1)} %get-tuple-element.39.near_q, ...), custom_call_target="tpu_custom_call" | custom-call | tf_op jit(solution)/shard_map/finish/pallas_call | solution.py:40
Async XLA Ops:
  3.6 19.9 %collective-permute-start = (bf16[272,1024]{1,0:T(8,128)(2,1)}, bf16[272,1024]{1,0:T(8,128)(2,1)S(1)}, u32[]{:S(2)}, u32[]{:S(2)}) collective-permute-start(bf16[272,1024]{1,0:T(8,128)(2,1)} %get-tuple-element.25), channel_id=1, source_target_pairs={{0,1},{1,2},{2,3},{3,4},{4,5},{5,6},{6,7},{7,8},{8,9},{9,10},{10,1... | collective-permute-start | bytes 1671176 | tf_op jit(solution)/shard_map/ppermute | solution.py:65
  5.6 17.9 %collective-permute-start.1 = (bf16[272,1024]{1,0:T(8,128)(2,1)}, bf16[272,1024]{1,0:T(8,128)(2,1)S(1)}, u32[]{:S(2)}, u32[]{:S(2)}) collective-permute-start(bf16[272,1024]{1,0:T(8,128)(2,1)} %get-tuple-element.26), channel_id=1, source_target_pairs={{1,0},{2,1},{3,2},{4,3},{5,4},{6,5},{7,6},{8,7},{9,8},{10,9},{11,1... | collective-permute-start | bytes 1671176 | tf_op jit(solution)/shard_map/ppermute | solution.py:64
  10.1 18.5 %all-to-all-start = ((bf16[16,8,1024]{2,1,0:T(8,128)(2,1)}), bf16[16,8,1024]{2,1,0:T(8,128)(2,1)S(1)}, u32[]{:S(2)}, u32[]{:S(2)}) async-start(bf16[16,8,1024]{2,1,0:T(8,128)(2,1)} %bitcast.6), calls=%async_computation | async-start | bytes 524288 | tf_op jit(solution)/shard_map/all_to_all | solution.py:462
  20.1 2.7 %copy-start = (bf16[1024,3072]{1,0:T(8,128)(2,1)}, bf16[1024,3072]{1,0:T(8,128)(2,1)S(1)}, u32[]{:S(2)}) copy-start(bf16[1024,3072]{1,0:T(8,128)(2,1)S(1)} %get-tuple-element.32.w_qkv) | copy-start | bytes 18874372
  22.8 0.7 %copy-start.9 = (bf16[128,1024]{1,0:T(8,128)(2,1)}, bf16[128,1024]{1,0:T(8,128)(2,1)S(1)}, u32[]{:S(2)}) copy-start(bf16[128,1024]{1,0:T(8,128)(2,1)S(1)} %get-tuple-element.33.own_grad) | copy-start | bytes 786436
  25.6 1.4 %copy-start.3 = (bf16[1024,1024]{1,0:T(8,128)(2,1)}, bf16[1024,1024]{1,0:T(8,128)(2,1)S(1)}, u32[]{:S(2)}) copy-start(bf16[1024,1024]{1,0:T(8,128)(2,1)S(1)} %get-tuple-element.27.w_out) | copy-start | bytes 6291460
  27.0 0.9 %copy-start.5 = (bf16[256,1024]{1,0:T(8,128)(2,1)}, bf16[256,1024]{1,0:T(8,128)(2,1)S(1)}, u32[]{:S(2)}) copy-start(bf16[256,1024]{1,0:T(8,128)(2,1)S(1)} %get-tuple-element.40.near_grad) | copy-start | bytes 1572868
  27.8 0.8 %copy-start.7 = (f32[128,1024]{1,0:T(8,128)}, f32[128,1024]{1,0:T(8,128)S(1)}, u32[]{:S(2)}) copy-start(f32[128,1024]{1,0:T(8,128)S(1)} %get-tuple-element.29.partial) | copy-start | bytes 1572868
  28.6 1.0 %copy-start.8 = (f32[128,1024]{1,0:T(8,128)S(1)}, f32[128,1024]{1,0:T(8,128)}, u32[]{:S(2)}) copy-start(f32[128,1024]{1,0:T(8,128)} %copy-done.7) | copy-start | bytes 1572868
  30.6 9.0 %collective-permute-start.3 = (bf16[128,1024]{1,0:T(8,128)(2,1)S(1)}, bf16[128,1024]{1,0:T(8,128)(2,1)S(1)}, u32[]{:S(2)}, u32[]{:S(2)}) collective-permute-start(bf16[128,1024]{1,0:T(8,128)(2,1)S(1)} %get-tuple-element.31.normed), channel_id=1, source_target_pairs={{1,0},{2,1},{3,2},{4,3},{5,4},{6,5},{7,6},{8,7},{9,8},{10,9},{11,1... | collective-permute-start | bytes 786440 | tf_op jit(solution)/shard_map/ppermute | solution.py:64
  33.7 8.6 %collective-permute-start.2 = (bf16[128,1024]{1,0:T(8,128)(2,1)S(1)}, bf16[128,1024]{1,0:T(8,128)(2,1)S(1)}, u32[]{:S(2)}, u32[]{:S(2)}) collective-permute-start(bf16[128,1024]{1,0:T(8,128)(2,1)S(1)} %get-tuple-element.31.normed), channel_id=1, source_target_pairs={{0,1},{1,2},{2,3},{3,4},{4,5},{5,6},{6,7},{7,8},{8,9},{9,10},{10,1... | collective-permute-start | bytes 786440 | tf_op jit(solution)/shard_map/ppermute | solution.py:65
  35.8 2.8 %copy-start.1 = (bf16[1024,3072]{1,0:T(8,128)(2,1)S(1)}, bf16[1024,3072]{1,0:T(8,128)(2,1)}, u32[]{:S(2)}) copy-start(bf16[1024,3072]{1,0:T(8,128)(2,1)} %copy-done) | copy-start | bytes 18874372
  38.6 3.7 %copy-start.2 = (bf16[1024,3072]{1,0:T(8,128)(2,1)S(1)}, bf16[1024,3072]{1,0:T(8,128)(2,1)}, u32[]{:S(2)}) copy-start(bf16[1024,3072]{1,0:T(8,128)(2,1)} %copy-done) | copy-start | bytes 18874372
  38.6 3.7 %copy-start.10 = (bf16[128,1024]{1,0:T(8,128)(2,1)S(1)}, bf16[128,1024]{1,0:T(8,128)(2,1)}, u32[]{:S(2)}) copy-start(bf16[128,1024]{1,0:T(8,128)(2,1)} %copy-done.9) | copy-start | bytes 786436
  42.3 12.2 %copy-start.4 = (bf16[1024,1024]{1,0:T(8,128)(2,1)S(1)}, bf16[1024,1024]{1,0:T(8,128)(2,1)}, u32[]{:S(2)}) copy-start(bf16[1024,1024]{1,0:T(8,128)(2,1)} %copy-done.3) | copy-start | bytes 6291460
  49.0 7.2 %collective-permute-start.5 = (f32[24,256]{1,0:T(8,128)S(1)}, f32[24,256]{1,0:T(8,128)S(1)}, u32[]{:S(2)}, u32[]{:S(2)}) collective-permute-start(f32[24,256]{1,0:T(8,128)S(1)} %get-tuple-element.37), channel_id=1, source_target_pairs={{1,0},{2,1},{3,2},{4,3},{5,4},{6,5},{7,6},{8,7},{9,8},{10,9},{11,1... | collective-permute-start | bytes 73736 | tf_op jit(solution)/shard_map/ppermute | solution.py:64
  52.6 6.0 %collective-permute-start.4 = (f32[24,256]{1,0:T(8,128)S(1)}, f32[24,256]{1,0:T(8,128)S(1)}, u32[]{:S(2)}, u32[]{:S(2)}) collective-permute-start(f32[24,256]{1,0:T(8,128)S(1)} %get-tuple-element.37), channel_id=1, source_target_pairs={{0,1},{1,2},{2,3},{3,4},{4,5},{5,6},{6,7},{7,8},{8,9},{9,10},{10,1... | collective-permute-start | bytes 73736 | tf_op jit(solution)/shard_map/ppermute | solution.py:65
  54.6 4.1 %copy-start.6 = (bf16[256,1024]{1,0:T(8,128)(2,1)S(1)}, bf16[256,1024]{1,0:T(8,128)(2,1)}, u32[]{:S(2)}) copy-start(bf16[256,1024]{1,0:T(8,128)(2,1)} %copy-done.5) | copy-start | bytes 1572868

commit v4 on v3

--- a/solution.py
+++ b/solution.py
@@ -14,6 +14,7 @@
 BF16 = jnp.bfloat16
 I32 = jnp.int32
 VMEM_LIMIT = 28 * 2**20
+PARTS = 4
 
 
 def mm(a, b):
@@ -32,20 +33,33 @@
     return lax.broadcasted_iota(I32, shape, dim)
 
 
-def call(kernel, outs, args, hbm=(), scratch=(), name=None):
-    args = [pltpu.with_memory_space_constraint(a, pltpu.HBM) if i in hbm else a for i, a in enumerate(args)]
-    specs = [
-        pl.BlockSpec(memory_space=pltpu.HBM if i in hbm else pltpu.VMEM) for i in range(len(args))
+def call(kernel, outs, args, hbm=(), hbm_outs=(), scratch=(), name=None):
+    args = [
+        pltpu.with_memory_space_constraint(a, pltpu.HBM) if i in hbm else a
+        for i, a in enumerate(args)
     ]
+
+    def specs(count, far):
+        return [
+            pl.BlockSpec(memory_space=pltpu.HBM if i in far else pltpu.VMEM) for i in range(count)
+        ]
+
     return pl.pallas_call(
         kernel,
-        out_shape=[jax.ShapeDtypeStruct(shape, dtype) for shape, dtype in outs],
-        in_specs=specs,
-        out_specs=[pl.BlockSpec(memory_space=pltpu.VMEM) for _ in outs],
+        out_shape=[
+            (pltpu.HBM if i in hbm_outs else jax.ShapeDtypeStruct)(shape, dtype)
+            for i, (shape, dtype) in enumerate(outs)
+        ],
+        in_specs=specs(len(args), hbm),
+        out_specs=specs(len(outs), hbm_outs),
         scratch_shapes=list(scratch),
         compiler_params=pltpu.CompilerParams(vmem_limit_bytes=VMEM_LIMIT),
         name=name,
     )(*args)
+
+
+def dma(count):
+    return pltpu.SemaphoreType.DMA((count,))
 
 
 def start_all(pairs, sems):
@@ -64,6 +78,20 @@
     from_high = lax.ppermute(toward_low, axis, [(i + 1, i) for i in range(ends)])
     from_low = lax.ppermute(toward_high, axis, [(i, i + 1) for i in range(ends)])
     return from_low, from_high
+
+
+def pair_gather(rows, axis):
+    n = lax.axis_size(axis)
+    gathered = [
+        lax.all_gather(
+            rows,
+            axis,
+            axis_index_groups=[[(i + k) % n, (i + k + 1) % n] for i in range(0, n, 2)],
+            tiled=True,
+        )
+        for k in range(2)
+    ]
+    return gathered
 
 
 def gelu(projected):
@@ -91,7 +119,6 @@
 
 def pack_kernel(
     grid_hbm,
-    cot_hbm,
     window_hbm,
     side_src_hbm,
     side_dst_hbm,
@@ -110,57 +137,66 @@
     far_src,
     far_dst,
     far_count,
+    far,
+    meta,
     sems,
+    out_sems,
 ):
     grid_rows, channels = grid.shape
-    mesh_rows = cot_hbm.shape[0]
+    mesh_rows = window.shape[1]
     slots = far_src.shape[1]
     devices = far_count.shape[1]
     depth = slots // devices
     first = grid_rows - BAND
+    count = side_src.shape[0] // 2
     copies = start_all(
         [
             (far_src_hbm, far_src),
             (far_dst_hbm, far_dst),
             (far_count_hbm, far_count),
-            (grid_hbm, grid),
             (side_src_hbm, side_src),
             (side_dst_hbm, side_dst),
             (side_count_hbm, side_count),
             (window_hbm, window),
+            (grid_hbm, grid),
             (grid_hbm.at[pl.ds(0, BAND)], low_out.at[pl.ds(0, BAND)]),
             (grid_hbm.at[pl.ds(first, BAND)], high_out.at[pl.ds(0, BAND)]),
-            (cot_hbm, low_out.at[pl.ds(BAND, mesh_rows)]),
-            (cot_hbm, high_out.at[pl.ds(BAND, mesh_rows)]),
         ],
         sems,
     )
-    for copy in copies[:4]:
-        copy.wait()
-    slot = iota((1, slots), 1)
-    receiver = jnp.where(iota((devices, slots), 0) == iota((devices, slots), 1) // depth, 1.0, 0.0)
-    live = mm(far_count[...].astype(F32).astype(BF16), receiver.astype(BF16))
-    target = jnp.where((slot % depth).astype(F32) < live, far_dst[...].astype(F32), 1.0 * mesh_rows)
-    place = slot // depth * (2 * depth) + slot % depth
-    select = onehot_rows([far_src[...]], grid_rows)
-    spread = mm_nt(select, onehot_rows([place], 2 * slots)).astype(BF16)
-    rows = mm_tn(spread, grid[...])
-    column = jnp.sum(
-        jnp.where(iota((2 * slots, slots), 0) == place + depth, target, 0.0), 1, keepdims=True
-    )
-    far_out[...] = (rows + column).astype(BF16)
-    for copy in copies[4:]:
-        copy.wait()
-    count = side_src.shape[0] // 2
-    for k, out in ((0, low_out), (1, high_out)):
+    for copy in copies[:7]:
+        copy.wait()
+    for k in range(2):
         rank = iota((count, LANES), 0) * LANES + iota((count, LANES), 1)
         src = side_src[k * count : (k + 1) * count] - k * first
         live = rank < side_count[:, k : k + 1]
         dst = jnp.where(live, side_dst[k * count : (k + 1) * count], mesh_rows)
         reach = jnp.concatenate([window[...], jnp.zeros((count - 2, mesh_rows), I32)], 0)
         blank = jnp.zeros((count, channels - 2 * LANES - mesh_rows), I32)
-        meta = jnp.concatenate([src, dst, reach, blank], 1)
-        out[BAND + mesh_rows :] = meta.astype(F32).astype(BF16)
+        meta[k] = jnp.concatenate([src, dst, reach, blank], 1).astype(F32).astype(BF16)
+    outs = start_all(
+        [
+            (meta.at[0], low_out.at[pl.ds(BAND, count)]),
+            (meta.at[1], high_out.at[pl.ds(BAND, count)]),
+        ],
+        out_sems,
+    )
+    slot = iota((1, slots), 1)
+    receiver = jnp.where(iota((devices, slots), 0) == iota((devices, slots), 1) // depth, 1.0, 0.0)
+    live = mm(far_count[...].astype(F32).astype(BF16), receiver.astype(BF16))
+    target = jnp.where((slot % depth).astype(F32) < live, far_dst[...].astype(F32), 1.0 * mesh_rows)
+    place = slot // depth * (2 * depth) + slot % depth
+    row = iota((2 * slots, slots), 0)
+    source = far_src[...].astype(F32) + 1.0
+    source = jnp.sum(jnp.where(row == place, source, 0.0), 1, keepdims=True) - 1.0
+    column = jnp.sum(jnp.where(row == place + depth, target, 0.0), 1, keepdims=True)
+    pick = jnp.where(iota((2 * slots, grid_rows), 1).astype(F32) == source, 1.0, 0.0).astype(BF16)
+    copies[7].wait()
+    far[...] = (mm(pick, grid[...]) + column).astype(BF16)
+    last = pltpu.make_async_copy(far, far_out, out_sems.at[2])
+    last.start()
+    for copy in copies[8:] + outs + [last]:
+        copy.wait()
 
 
 def own_kernel(
@@ -168,34 +204,26 @@
     mesh_in_hbm,
     own_src_hbm,
     own_dst_hbm,
-    cot_hbm,
     w_edge_hbm,
-    w_out_hbm,
-    w_qkv_hbm,
-    partial_out,
-    grad_out,
+    partial_hbm,
     w_edge,
-    w_out,
-    w_qkv,
     grid,
     mesh_in,
     own_src,
     own_dst,
-    cot,
+    partial,
     sems,
+    out_sems,
 ):
-    grid_rows = grid.shape[0]
+    grid_rows, channels = grid.shape
     mesh_rows = mesh_in.shape[0]
     copies = start_all(
         [
             (own_src_hbm, own_src),
             (own_dst_hbm, own_dst),
+            (grid_hbm, grid),
             (w_edge_hbm, w_edge),
-            (grid_hbm, grid),
             (mesh_in_hbm, mesh_in),
-            (cot_hbm, cot),
-            (w_out_hbm, w_out),
-            (w_qkv_hbm, w_qkv),
         ],
         sems,
     )
@@ -205,22 +233,36 @@
     src = onehot_rows([own_src[r : r + 1] for r in range(rows)], grid_rows)
     dst = onehot_rows([own_dst[r : r + 1] for r in range(rows)], mesh_rows)
     counts = mm_nt(dst, src).astype(BF16)
-    for copy in copies[2:5]:
-        copy.wait()
-    active = gelu(mm(grid[...], w_edge[...]))
-    partial_out[...] = mesh_in[...].astype(F32) + mm(counts, active)
-    for copy in copies[5:7]:
-        copy.wait()
-    grad_out[...] = mm_nt(cot[...], w_out[...]).astype(BF16)
-    copies[7].wait()
-
-
-def side_kernel(low, high, w_edge, w_out, partial, partial_out, grad_out, window_out):
-    mesh_rows = partial.shape[0]
-    active = gelu(mm(jnp.concatenate([low[:BAND], high[:BAND]], 0), w_edge[...]))
+    for copy in copies[2:]:
+        copy.wait()
+    step = channels // PARTS
+    outs = []
+    for c in range(PARTS):
+        cols = slice(c * step, (c + 1) * step)
+        active = gelu(mm(grid[...], w_edge[:, cols]))
+        partial[c] = mesh_in[:, cols].astype(F32) + mm(counts, active)
+        outs.append(pltpu.make_async_copy(partial.at[c], partial_hbm.at[c], out_sems.at[c]))
+        outs[-1].start()
+    for copy in outs:
+        copy.wait()
+
+
+def side_kernel(low_hbm, high_hbm, w_edge, partial_hbm, low, high, partial, sems, out_sems):
+    mesh_rows, step = partial.shape[1:]
+    copies = start_all(
+        [
+            (low_hbm.at[pl.ds(BAND, low.shape[0] - BAND)], low.at[pl.ds(BAND, low.shape[0] - BAND)]),
+            (high_hbm.at[pl.ds(BAND, low.shape[0] - BAND)], high.at[pl.ds(BAND, low.shape[0] - BAND)]),
+            (low_hbm.at[pl.ds(0, BAND)], low.at[pl.ds(0, BAND)]),
+            (high_hbm.at[pl.ds(0, BAND)], high.at[pl.ds(0, BAND)]),
+        ],
+        sems,
+    )
+    for copy in copies[:2]:
+        copy.wait()
     uppers, lowers = [], []
     for side in (low, high):
-        meta = side[BAND + mesh_rows :].astype(F32).astype(I32)
+        meta = side[BAND:].astype(F32).astype(I32)
         count = meta.shape[0]
         src = onehot_rows([meta[r : r + 1, :LANES] for r in range(count)], BAND)
         dst = onehot_rows([meta[r : r + 1, LANES : 2 * LANES] for r in range(count)], mesh_rows)
@@ -228,17 +270,25 @@
         upper = counts.astype(BF16)
         uppers.append(upper)
         lowers.append((counts - upper.astype(F32)).astype(BF16))
-        reach = meta[:8, 2 * LANES : 2 * LANES + mesh_rows]
-        at = 0 if side is low else mesh_rows
-        window_out[:, at : at + mesh_rows] = reach
     counts = jnp.concatenate(uppers + lowers, 1)
-    partial_out[...] = partial[...] + mm(counts, jnp.concatenate([active, active], 0))
-    both = jnp.concatenate([low[BAND : BAND + mesh_rows], high[BAND : BAND + mesh_rows]], 0)
-    grad_out[...] = mm_nt(both, w_out[...]).astype(BF16)
-
-
-def latent_kernel(depth, far, w_edge, partial, latent_out, normed_out):
-    mesh_rows = partial.shape[0]
+    for copy in copies[2:]:
+        copy.wait()
+    bands = jnp.concatenate([low[:BAND], high[:BAND]], 0)
+    outs = []
+    for c in range(PARTS):
+        active = gelu(mm(bands, w_edge[:, c * step : (c + 1) * step]))
+        partial[c] = mm(counts, jnp.concatenate([active, active], 0))
+        outs.append(pltpu.make_async_copy(partial.at[c], partial_hbm.at[c], out_sems.at[c]))
+        outs[-1].start()
+    for copy in outs:
+        copy.wait()
+
+
+def latent_kernel(
+    depth, far, w_edge, own_hbm, side_hbm, latent_out, normed_out, own_part, side_part, sems
+):
+    copies = start_all([(own_hbm, own_part), (side_hbm, side_part)], sems)
+    mesh_rows = latent_out.shape[0]
     slots = far.shape[0]
     rows = far[...]
     active = gelu(mm(rows, w_edge[...]))
@@ -247,14 +297,35 @@
     is_row = iota((slots, mesh_rows), 0) % (2 * depth) < depth
     hit = (target == iota((slots, mesh_rows), 1).astype(F32)) & is_row
     landing = jnp.where(hit, 1.0, 0.0).astype(BF16)
-    latent = (partial[...] + mm_tn(landing, active)).astype(BF16)
+    landed = mm_tn(landing, active)
+    for copy in copies:
+        copy.wait()
+    total = jnp.concatenate([own_part[c] + side_part[c] for c in range(PARTS)], 1)
+    latent = (total + landed).astype(BF16)
     latent_out[...] = latent
     normal, _ = norm_stats(latent)
     normed_out[...] = normal.astype(BF16)
 
 
-def project_kernel(normed, w_qkv, qkv_out):
-    qkv_out[...] = mm(normed[...], w_qkv[...]).astype(BF16)
+def project_kernel(
+    normed, w_qkv_hbm, w_out_hbm, cot_hbm, qkv_out, w_qkv, w_out, cot_out, grad_out, sems
+):
+    step = normed.shape[1]
+    copies = start_all(
+        [
+            (w_qkv_hbm.at[:, pl.ds(c * step, step)], w_qkv.at[:, pl.ds(c * step, step)])
+            for c in range(3)
+        ]
+        + [(cot_hbm, cot_out), (w_out_hbm, w_out)],
+        sems,
+    )
+    for c in range(3):
+        copies[c].wait()
+        cols = slice(c * step, (c + 1) * step)
+        qkv_out[:, cols] = mm(normed[...], w_qkv[:, cols]).astype(BF16)
+    for copy in copies[3:]:
+        copy.wait()
+    grad_out[...] = mm_nt(cot_out[...], w_out[...]).astype(BF16)
 
 
 def halves(rows, scale=None):
@@ -285,7 +356,6 @@
     gq_out,
     gk_out,
     gv_out,
-    near_q_out,
     kv,
     window,
     sems,
@@ -294,11 +364,11 @@
     m, channels = low_normed.shape
     devices = lax.axis_size("node")
     me = lax.axis_index("node")
-    near = mm(jnp.concatenate([low_normed[...], high_normed[...]], 0), w_qkv[...]).astype(BF16)
-    near_q_out[...] = near[:, :channels] * jnp.asarray(scale, BF16)
-    kv[:m] = near[:m, channels:]
+    near = mm(jnp.concatenate([low_normed[...], high_normed[...]], 0), w_qkv[:, channels:])
+    near = near.astype(BF16)
+    kv[:m] = near[:m]
     kv[m : 2 * m] = own_qkv[:, channels:]
-    kv[2 * m :] = near[m:, channels:]
+    kv[2 * m :] = near[m:]
     fetch[0].wait()
     key_at = iota((3 * m, m), 0)
     query_at = iota((3 * m, m), 1) + m
@@ -335,17 +405,54 @@
         gv_out[:, cols] = mm(weights[m : 2 * m], g2)
 
 
-def output_kernel(latent, attention, w_out, grad_query, w_qkv, mesh_out, grad_normed):
-    channels = latent.shape[1]
+def output_kernel(
+    scale,
+    latent,
+    attention,
+    w_out,
+    grad_query,
+    w_qkv,
+    low_normed,
+    high_normed,
+    first_cot_hbm,
+    second_cot_hbm,
+    mesh_out,
+    grad_normed,
+    near_q_out,
+    near_grad,
+    near_cot,
+    sems,
+):
+    m, channels = latent.shape
+    low, high = near_cot.at[pl.ds(0, m)], near_cot.at[pl.ds(m, m)]
+    odd = lax.axis_index("node") % 2 == 1
+
+    def fetch(before, after):
+        return start_all([(before.at[pl.ds(0, m)], low), (after.at[pl.ds(m, m)], high)], sems)
+
+    @pl.when(odd)
+    def _():
+        fetch(first_cot_hbm, second_cot_hbm)
+
+    @pl.when(jnp.logical_not(odd))
+    def _():
+        fetch(second_cot_hbm, first_cot_hbm)
+
+    near = mm(jnp.concatenate([low_normed[...], high_normed[...]], 0), w_qkv[:, :channels])
+    near_q_out[...] = near.astype(BF16) * jnp.asarray(scale, BF16)
+    grad_normed[...] = mm_nt(grad_query[...], w_qkv[:, :channels])
     mesh_out[...] = (latent[...].astype(F32) + mm(attention[...], w_out[...])).astype(BF16)
-    grad_normed[...] = mm_nt(grad_query[...], w_qkv[:, :channels])
+    pltpu.make_async_copy(first_cot_hbm.at[pl.ds(0, m)], low, sems.at[0]).wait()
+    pltpu.make_async_copy(first_cot_hbm.at[pl.ds(m, m)], high, sems.at[1]).wait()
+    near_grad[...] = mm_nt(near_cot[...], w_out[...]).astype(BF16)
 
 
 def finish_kernel(
     pair,
     low_stats,
     high_stats,
-    near_window,
+    low_hbm,
+    high_hbm,
     near_q,
     near_grad,
     own_qkv,
@@ -354,14 +461,26 @@
     grad_normed,
     w_qkv,
     latent,
-    cot_hbm,
+    cot,
     grad_out,
     grad_kv,
-    cot,
+    metas,
     sems,
 ):
-    fetch = start_all([(cot_hbm, cot)], sems)
     m, channels = latent.shape
+    count = metas.shape[1]
+    fetch = start_all(
+        [
+            (low_hbm.at[pl.ds(BAND, count)], metas.at[0]),
+            (high_hbm.at[pl.ds(BAND, count)], metas.at[1]),
+        ],
+        sems,
+    )
+    for copy in fetch:
+        copy.wait()
+    near_window = jnp.concatenate(
+        [metas[k][:8, 2 * LANES : 2 * LANES + m].astype(F32).astype(I32) for k in range(2)], 1
+    )
     key_at = iota((m, 2 * m), 0) + m
     lane = iota((m, 2 * m), 1)
     query_at = jnp.where(lane < m, lane, lane + m)
@@ -398,7 +517,6 @@
         - jnp.mean(total, -1, keepdims=True)
         - normal * jnp.mean(total * normal, -1, keepdims=True)
     )
-    fetch[0].wait()
     grad_out[...] = (cot[...].astype(F32) + inv_std * centred).astype(BF16)
 
 
@@ -434,29 +552,20 @@
     own_src, own_dst = own_src.reshape(-1, LANES), own_dst.reshape(-1, LANES)
     far_src, far_dst = far_src.reshape(1, -1), far_dst.reshape(1, -1)
     side_count, far_count = side_count.reshape(1, -1), far_count.reshape(1, -1)
+    message = ((BAND + meta_rows, channels), BF16)
     far_message, toward_low, toward_high = call(
         pack_kernel,
-        [
-            ((2 * far_slots, channels), BF16),
-            ((BAND + m + meta_rows, channels), BF16),
-            ((BAND + m + meta_rows, channels), BF16),
-        ],
-        [
-            grid_in,
-            cotangent,
-            window,
-            side_src,
-            side_dst,
-            side_count,
-            far_src,
-            far_dst,
-            far_count,
-        ],
-        hbm=range(9),
-        scratch=like(
-            grid_in, window, side_src, side_dst, side_count, far_src, far_dst, far_count
-        )
-        + [pltpu.SemaphoreType.DMA((12,))],
+        [((2 * far_slots, channels), BF16), message, message],
+        [grid_in, window, side_src, side_dst, side_count, far_src, far_dst, far_count],
+        hbm=range(8),
+        hbm_outs=range(3),
+        scratch=like(grid_in, window, side_src, side_dst, side_count, far_src, far_dst, far_count)
+        + [
+            pltpu.VMEM((2 * far_slots, channels), BF16),
+            pltpu.VMEM((2, meta_rows, channels), BF16),
+            dma(10),
+            dma(3),
+        ],
         name="pack",
     )
     got_far = lax.all_to_all(
@@ -468,37 +577,54 @@
     ).reshape(2 * far_slots, channels)
     from_low, from_high = exchange(toward_low, toward_high, "node")
 
-    partial, own_grad, w_edge, w_out, w_qkv = call(
+    part = (PARTS, m, channels // PARTS)
+    own_part, w_edge = call(
         own_kernel,
-        [
-            ((m, channels), F32),
-            ((m, channels), BF16),
-            (w_edge.shape, BF16),
-            (w_out.shape, BF16),
-            (w_qkv.shape, BF16),
-        ],
-        [grid_in, mesh_in, own_src, own_dst, cotangent, w_edge, w_out, w_qkv],
-        hbm=range(8),
-        scratch=like(grid_in, mesh_in, own_src, own_dst, cotangent)
-        + [pltpu.SemaphoreType.DMA((8,))],
+        [(part, F32), (w_edge.shape, BF16)],
+        [grid_in, mesh_in, own_src, own_dst, w_edge],
+        hbm=range(5),
+        hbm_outs=(0,),
+        scratch=like(grid_in, mesh_in, own_src, own_dst) + [pltpu.VMEM(part, F32), dma(5), dma(PARTS)],
         name="own",
     )
-    partial, near_grad, near_window = call(
+    (side_part,) = call(
         side_kernel,
-        [((m, channels), F32), ((2 * m, channels), BF16), ((8, 2 * m), I32)],
-        [from_low, from_high, w_edge, w_out, partial],
+        [(part, F32)],
+        [from_low, from_high, w_edge],
+        hbm=(0, 1),
+        hbm_outs=(0,),
+        scratch=like(from_low, from_high) + [pltpu.VMEM(part, F32), dma(4), dma(PARTS)],
         name="side",
     )
     latent, normed = call(
         functools.partial(latent_kernel, far_depth),
         [((m, channels), BF16), ((m, channels), BF16)],
-        [got_far, w_edge, partial],
+        [got_far, w_edge, own_part, side_part],
+        hbm=(2, 3),
+        scratch=[pltpu.VMEM(part, F32), pltpu.VMEM(part, F32), dma(2)],
         name="latent",
     )
     low_normed, high_normed = exchange(normed, normed, "node")
-    (own_qkv,) = call(project_kernel, [((m, 3 * channels), BF16)], [normed, w_qkv], name="project")
-
-    stats, attention, grad_query, grad_key, grad_value, near_q = call(
+    own_qkv, w_qkv, w_out, own_cot, own_grad = call(
+        project_kernel,
+        [
+            ((m, 3 * channels), BF16),
+            (w_qkv.shape, BF16),
+            (w_out.shape, BF16),
+            ((m, channels), BF16),
+            ((m, channels), BF16),
+        ],
+        [normed, w_qkv, w_out, cotangent],
+        hbm=(1, 2, 3),
+        scratch=[dma(5)],
+        name="project",
+    )
+    low_normed, high_normed, late_cot = lax.optimization_barrier(
+        (low_normed, high_normed, cotangent)
+    )
+    first_cot, second_cot = pair_gather(late_cot, "node")
+
+    stats, attention, grad_query, grad_key, grad_value = call(
         functools.partial(attend_kernel, scale, pair),
         [
             ((3 * pairs, 2 * m), F32),
@@ -506,21 +632,35 @@
             ((m, channels), BF16),
             ((m, channels), F32),
             ((m, channels), F32),
-            ((2 * m, channels), BF16),
         ],
         [low_normed, high_normed, w_qkv, own_qkv, own_grad, window],
         hbm=(5,),
-        scratch=[pltpu.VMEM((3 * m, 2 * channels), BF16)]
-        + like(window)
-        + [pltpu.SemaphoreType.DMA((1,))],
+        scratch=[pltpu.VMEM((3 * m, 2 * channels), BF16)] + like(window) + [dma(1)],
         name="attend",
     )
     low_stats, high_stats = exchange(stats, stats, "node")
 
-    mesh_out, grad_normed = call(
-        output_kernel,
-        [((m, channels), BF16), ((m, channels), F32)],
-        [latent, attention, w_out, grad_query, w_qkv],
+    mesh_out, grad_normed, near_q, near_grad = call(
+        functools.partial(output_kernel, scale),
+        [
+            ((m, channels), BF16),
+            ((m, channels), F32),
+            ((2 * m, channels), BF16),
+            ((2 * m, channels), BF16),
+        ],
+        [
+            latent,
+            attention,
+            w_out,
+            grad_query,
+            w_qkv,
+            low_normed,
+            high_normed,
+            first_cot,
+            second_cot,
+        ],
+        hbm=(7, 8),
+        scratch=[pltpu.VMEM((2 * m, channels), BF16), dma(2)],
         name="output",
     )
     (mesh_grad,) = call(
@@ -529,7 +669,8 @@
         [
             low_stats,
             high_stats,
-            near_window,
+            from_low,
+            from_high,
             near_q,
             near_grad,
             own_qkv,
@@ -538,12 +679,14 @@
             grad_normed,
             w_qkv,
             latent,
-            cotangent,
-        ],
-        hbm=(11,),
-        scratch=[pltpu.VMEM((m, 2 * channels), BF16)]
-        + like(cotangent)
-        + [pltpu.SemaphoreType.DMA((1,))],
+            own_cot,
+        ],
+        hbm=(2, 3),
+        scratch=[
+            pltpu.VMEM((m, 2 * channels), BF16),
+            pltpu.VMEM((2, meta_rows, channels), BF16),
+            dma(2),
+        ],
         name="finish",
     )
     return (mesh_out, mesh_grad)

time: 64.4 us -> 88.7 us (1.38)
  the two profiles are of different devices: /device:TPU:8 before, /device:TPU:1 now
where the time goes in v4:
time: 88.7 us; the launch traced here: 88.1 us
  Pallas kernels  48 us (54%)
  starting transfers between devices  24.9 us (28%)
  blocking collectives  11.7 us (13%)
  waiting for transfers between devices  1.81 us (2%)
  between operations  0.96 us (1%)
    pallas_call x8, Pallas kernels, call(): pl.pallas_call(kernel, out_shape=[(pltpu.HBM if i in hbm_outs else jax.Sh...  48 us
    ppermute x3, starting transfers between devices, exchange(): lax.ppermute(toward_high, axis, [(i, i + 1) for i in range(ends)])  11.7 us
    all_gather x2, blocking collectives, pair_gather(): lax.all_gather(rows, axis, axis_index_groups=[[(i + k) % n, (i + k + 1) %...  11.7 us
    all_to_all x1, starting transfers between devices, body(): lax.all_to_all(far_message.reshape(devices, 2 * far_depth, channels), 'no...  7.36 us
    ppermute x3, starting transfers between devices, exchange(): lax.ppermute(toward_low, axis, [(i + 1, i) for i in range(ends)])  5.76 us
  transfers between devices with their start and end apart: 7, of which 2 were waited for; matrix products, arithmetic and copies ran while one was open for 0% of the time, Pallas kernels for 20%

profile of v4, /device:TPU:1, one launch (start us, length us, event | category | flops | bytes accessed | tf_op | source)
XLA Modules:
  0.0 88.1 jit_solution(12546791978688306663)
XLA Ops:
  0.6 17.1 %pack.1 = (bf16[128,1024]{1,0:T(8,128)(2,1)}, bf16[144,1024]{1,0:T(8,128)(2,1)}, bf16[144,1024]{1,0:T(8,128)(2,1)}) custom-call(bf16[512,1024]{1,0:T(8,128)(2,1)} %grid_hbm.3, s32[2,128]{1,0:T(2,128)} %window_hbm.3, s32[32,128]{1,0:T(8,128)} %bitcast.12, s32[32,128]{1,0:T(8,128)} %bitcast.13, s32[1,2]{1,0:T(1,128)} %bitcast.16, s32[1,64]{1,0:T(1,128)} %bitcast.17, ...), custom_call_target="tpu_custom_call" | custom-call | tf_op jit(solution)/shard_map/pack/pallas_call | solution.py:47
  17.8 7.4 %all-to-all-start = ((bf16[16,8,1024]{2,1,0:T(8,128)(2,1)}), bf16[16,8,1024]{2,1,0:T(8,128)(2,1)S(1)}, u32[]{:S(2)}, u32[]{:S(2)}) async-start(bf16[16,8,1024]{2,1,0:T(8,128)(2,1)} %bitcast.11), calls=%async_computation | async-start | bytes 524288 | tf_op jit(solution)/shard_map/all_to_all | solution.py:571
  25.1 3.5 %collective-permute-start = (bf16[144,1024]{1,0:T(8,128)(2,1)}, bf16[144,1024]{1,0:T(8,128)(2,1)S(1)}, u32[]{:S(2)}, u32[]{:S(2)}) collective-permute-start(bf16[144,1024]{1,0:T(8,128)(2,1)} %get-tuple-element.29), channel_id=1, source_target_pairs={{0,1},{1,2},{2,3},{3,4},{4,5},{5,6},{6,7},{7,8},{8,9},{9,10},{10,1... | collective-permute-start | bytes 884744 | tf_op jit(solution)/shard_map/ppermute | solution.py:79
  28.7 1.9 %collective-permute-start.1 = (bf16[144,1024]{1,0:T(8,128)(2,1)}, bf16[144,1024]{1,0:T(8,128)(2,1)S(1)}, u32[]{:S(2)}, u32[]{:S(2)}) collective-permute-start(bf16[144,1024]{1,0:T(8,128)(2,1)} %get-tuple-element.30), channel_id=1, source_target_pairs={{1,0},{2,1},{3,2},{4,3},{5,4},{6,5},{7,6},{8,7},{9,8},{10,9},{11,1... | collective-permute-start | bytes 884744 | tf_op jit(solution)/shard_map/ppermute | solution.py:78
  30.6 5.9 %own.1 = (f32[4,128,256]{2,1,0:T(8,128)}, bf16[1024,1024]{1,0:T(8,128)(2,1)S(1)}) custom-call(bf16[512,1024]{1,0:T(8,128)(2,1)} %grid_hbm.3, bf16[128,1024]{1,0:T(8,128)(2,1)} %mesh_in_hbm.1, s32[8,128]{1,0:T(8,128)} %bitcast.14, s32[8,128]{1,0:T(8,128)} %bitcast.15, bf16[1024,1024]{1,0:T(8,128)(2,1)} %w_edge_hbm.1), custom_call_target="tpu_custom_call" | custom-call | tf_op jit(solution)/shard_map/own/pallas_call | solution.py:47
  36.5 0.0 collective-permute-done.low_hbm
  36.5 0.0 copy-start.1
  36.5 0.9 %collective-permute-done.1.high_hbm = bf16[144,1024]{1,0:T(8,128)(2,1)S(1)} collective-permute-done((bf16[144,1024]{1,0:T(8,128)(2,1)}, bf16[144,1024]{1,0:T(8,128)(2,1)S(1)}, u32[]{:S(2)}, u32[]{:S(2)}) %collective-permute-start.1) | collective-permute-done | bytes 294944 | tf_op jit(solution)/shard_map/ppermute | solution.py:78
  37.4 0.0 copy-start.2
  37.4 0.0 copy-done.1
  37.4 0.7 copy-done.2
  38.1 4.1 %side.1.side_hbm = f32[4,128,256]{2,1,0:T(8,128)} custom-call(bf16[144,1024]{1,0:T(8,128)(2,1)} %copy-done.1, bf16[144,1024]{1,0:T(8,128)(2,1)} %copy-done.2, bf16[1024,1024]{1,0:T(8,128)(2,1)S(1)} %get-tuple-element.27.w_edge), custom_call_target="tpu_custom_call" | custom-call | tf_op jit(solution)/shard_map/side/pallas_call | solution.py:47
  42.2 0.0 all-to-all-done
  42.2 1.9 %latent.1 = (bf16[128,1024]{1,0:T(8,128)(2,1)S(1)}, bf16[128,1024]{1,0:T(8,128)(2,1)S(1)}) custom-call(bf16[128,1024]{1,0:T(8,128)(2,1)S(1)} %bitcast.10, bf16[1024,1024]{1,0:T(8,128)(2,1)S(1)} %get-tuple-element.27.w_edge, f32[4,128,256]{2,1,0:T(8,128)} %get-tuple-element.28.own_hbm, f32[4,128,256]{2,1,0:T(8,128)} %side.1.side_hbm), custom_call_target="tpu_custom_call" | custom-call | tf_op jit(solution)/shard_map/latent/pallas_call | solution.py:47
  44.1 1.9 %collective-permute-start.3 = (bf16[128,1024]{1,0:T(8,128)(2,1)S(1)}, bf16[128,1024]{1,0:T(8,128)(2,1)S(1)}, u32[]{:S(2)}, u32[]{:S(2)}) collective-permute-start(bf16[128,1024]{1,0:T(8,128)(2,1)S(1)} %get-tuple-element.32.normed), channel_id=1, source_target_pairs={{1,0},{2,1},{3,2},{4,3},{5,4},{6,5},{7,6},{8,7},{9,8},{10,9},{11,1... | collective-permute-start | bytes 786440 | tf_op jit(solution)/shard_map/ppermute | solution.py:78
  46.0 3.8 %collective-permute-start.2 = (bf16[128,1024]{1,0:T(8,128)(2,1)S(1)}, bf16[128,1024]{1,0:T(8,128)(2,1)S(1)}, u32[]{:S(2)}, u32[]{:S(2)}) collective-permute-start(bf16[128,1024]{1,0:T(8,128)(2,1)S(1)} %get-tuple-element.32.normed), channel_id=1, source_target_pairs={{0,1},{1,2},{2,3},{3,4},{4,5},{5,6},{6,7},{7,8},{8,9},{9,10},{10,1... | collective-permute-start | bytes 786440 | tf_op jit(solution)/shard_map/ppermute | solution.py:79
  49.8 4.4 %project.1 = (bf16[128,3072]{1,0:T(8,128)(2,1)S(1)}, bf16[1024,3072]{1,0:T(8,128)(2,1)S(1)}, bf16[1024,1024]{1,0:T(8,128)(2,1)S(1)}, bf16[128,1024]{1,0:T(8,128)(2,1)S(1)}, bf16[128,1024]{1,0:T(8,128)(2,1)S(1)}) custom-call(bf16[128,1024]{1,0:T(8,128)(2,1)S(1)} %get-tuple-element.32.normed, bf16[1024,3072]{1,0:T(8,128)(2,1)} %w_qkv_hbm.1, ...), custom_call_target="tpu_custom_call" | custom-call | tf_op jit(solution)/shard_map/project/pallas_call | solution.py:47
  54.3 0.0 collective-permute-done.3.high_normed
  54.3 0.9 collective-permute-done.2.low_normed
  55.2 0.0 copy-start
  55.2 6.0 %attend.1 = (f32[24,256]{1,0:T(8,128)S(1)}, bf16[128,1024]{1,0:T(8,128)(2,1)S(1)}, bf16[128,1024]{1,0:T(8,128)(2,1)S(1)}, f32[128,1024]{1,0:T(8,128)S(1)}, f32[128,1024]{1,0:T(8,128)S(1)}) custom-call(bf16[128,1024]{1,0:T(8,128)(2,1)S(1)} %collective-permute-done.2.low_normed, bf16[128,1024]{1,0:T(8,128)(2,1)S(1)} %collective-permute-done.3.high_normed, ...), custom_call_target="tpu_custom_call" | custom-call | tf_op jit(solution)/shard_map/attend/pallas_call | solution.py:47
  61.2 1.9 %collective-permute-start.5 = (f32[24,256]{1,0:T(8,128)S(1)}, f32[24,256]{1,0:T(8,128)S(1)}, u32[]{:S(2)}, u32[]{:S(2)}) collective-permute-start(f32[24,256]{1,0:T(8,128)S(1)} %get-tuple-element.43), channel_id=1, source_target_pairs={{1,0},{2,1},{3,2},{4,3},{5,4},{6,5},{7,6},{8,7},{9,8},{10,9},{11,1... | collective-permute-start | bytes 73736 | tf_op jit(solution)/shard_map/ppermute | solution.py:78
  63.2 4.4 %collective-permute-start.4 = (f32[24,256]{1,0:T(8,128)S(1)}, f32[24,256]{1,0:T(8,128)S(1)}, u32[]{:S(2)}, u32[]{:S(2)}) collective-permute-start(f32[24,256]{1,0:T(8,128)S(1)} %get-tuple-element.43), channel_id=1, source_target_pairs={{0,1},{1,2},{2,3},{3,4},{4,5},{5,6},{6,7},{7,8},{8,9},{9,10},{10,1... | collective-permute-start | bytes 73736 | tf_op jit(solution)/shard_map/ppermute | solution.py:79
  67.5 0.0 copy-done
  67.6 9.4 %all_gather.7.second_cot_hbm = bf16[256,1024]{1,0:T(8,128)(2,1)} all-gather(bf16[128,1024]{1,0:T(8,128)(2,1)S(1)} %copy-done), channel_id=1, replica_groups={{1,2},{3,4},{5,6},{7,8},{9,10},{11,12},{13,14},{15,0},{17,18},{19,20},{..., dimensions={0}, use_global_device_ids=true | all-gather | bytes 786432 | tf_op jit(solution)/shard_map/all_gather | solution.py:86
  76.9 2.3 %all_gather.6.first_cot_hbm = bf16[256,1024]{1,0:T(8,128)(2,1)} all-gather(bf16[128,1024]{1,0:T(8,128)(2,1)S(1)} %copy-done), channel_id=1, replica_groups={{0,1},{2,3},{4,5},{6,7},{8,9},{10,11},{12,13},{14,15},{16,17},{18,19},{..., dimensions={0}, use_global_device_ids=true | all-gather | bytes 786432 | tf_op jit(solution)/shard_map/all_gather | solution.py:86
  79.2 3.6 %output.1 = (bf16[128,1024]{1,0:T(8,128)(2,1)}, f32[128,1024]{1,0:T(8,128)S(1)}, bf16[256,1024]{1,0:T(8,128)(2,1)S(1)}, bf16[256,1024]{1,0:T(8,128)(2,1)S(1)}) custom-call(bf16[128,1024]{1,0:T(8,128)(2,1)S(1)} %get-tuple-element.31.latent, bf16[128,1024]{1,0:T(8,128)(2,1)S(1)} %get-tuple-element.38.attention, ...), custom_call_target="tpu_custom_call" | custom-call | tf_op jit(solution)/shard_map/output/pallas_call | solution.py:47
  82.9 0.0 collective-permute-done.5.high_stats
  82.9 0.0 collective-permute-done.4.low_stats
  82.9 5.0 %finish.1 = bf16[128,1024]{1,0:T(8,128)(2,1)} custom-call(f32[24,256]{1,0:T(8,128)S(1)} %collective-permute-done.4.low_stats, f32[24,256]{1,0:T(8,128)S(1)} %collective-permute-done.5.high_stats, bf16[144,1024]{1,0:T(8,128)(2,1)} %copy-done.1, bf16[144,1024]{1,0:T(8,128)(2,1)} %copy-done.2, bf16[256,1024]{1,0:T(8,128)(2,1)S(1)} %get-tuple-element.44.near_q, ...), custom_call_target="tpu_custom_call" | custom-call | tf_op jit(solution)/shard_map/finish/pallas_call | solution.py:47
Async XLA Ops:
  17.8 24.4 %all-to-all-start = ((bf16[16,8,1024]{2,1,0:T(8,128)(2,1)}), bf16[16,8,1024]{2,1,0:T(8,128)(2,1)S(1)}, u32[]{:S(2)}, u32[]{:S(2)}) async-start(bf16[16,8,1024]{2,1,0:T(8,128)(2,1)} %bitcast.11), calls=%async_computation | async-start | bytes 524288 | tf_op jit(solution)/shard_map/all_to_all | solution.py:571
  25.1 11.3 %collective-permute-start = (bf16[144,1024]{1,0:T(8,128)(2,1)}, bf16[144,1024]{1,0:T(8,128)(2,1)S(1)}, u32[]{:S(2)}, u32[]{:S(2)}) collective-permute-start(bf16[144,1024]{1,0:T(8,128)(2,1)} %get-tuple-element.29), channel_id=1, source_target_pairs={{0,1},{1,2},{2,3},{3,4},{4,5},{5,6},{6,7},{7,8},{8,9},{9,10},{10,1... | collective-permute-start | bytes 884744 | tf_op jit(solution)/shard_map/ppermute | solution.py:79
  28.7 8.7 %collective-permute-start.1 = (bf16[144,1024]{1,0:T(8,128)(2,1)}, bf16[144,1024]{1,0:T(8,128)(2,1)S(1)}, u32[]{:S(2)}, u32[]{:S(2)}) collective-permute-start(bf16[144,1024]{1,0:T(8,128)(2,1)} %get-tuple-element.30), channel_id=1, source_target_pairs={{1,0},{2,1},{3,2},{4,3},{5,4},{6,5},{7,6},{8,7},{9,8},{10,9},{11,1... | collective-permute-start | bytes 884744 | tf_op jit(solution)/shard_map/ppermute | solution.py:78
  36.5 0.9 %copy-start.1 = (bf16[144,1024]{1,0:T(8,128)(2,1)}, bf16[144,1024]{1,0:T(8,128)(2,1)S(1)}, u32[]{:S(2)}) copy-start(bf16[144,1024]{1,0:T(8,128)(2,1)S(1)} %collective-permute-done.low_hbm) | copy-start | bytes 884740
  37.4 0.7 copy-start.2
  44.1 10.2 %collective-permute-start.3 = (bf16[128,1024]{1,0:T(8,128)(2,1)S(1)}, bf16[128,1024]{1,0:T(8,128)(2,1)S(1)}, u32[]{:S(2)}, u32[]{:S(2)}) collective-permute-start(bf16[128,1024]{1,0:T(8,128)(2,1)S(1)} %get-tuple-element.32.normed), channel_id=1, source_target_pairs={{1,0},{2,1},{3,2},{4,3},{5,4},{6,5},{7,6},{8,7},{9,8},{10,9},{11,1... | collective-permute-start | bytes 786440 | tf_op jit(solution)/shard_map/ppermute | solution.py:78
  46.0 9.2 %collective-permute-start.2 = (bf16[128,1024]{1,0:T(8,128)(2,1)S(1)}, bf16[128,1024]{1,0:T(8,128)(2,1)S(1)}, u32[]{:S(2)}, u32[]{:S(2)}) collective-permute-start(bf16[128,1024]{1,0:T(8,128)(2,1)S(1)} %get-tuple-element.32.normed), channel_id=1, source_target_pairs={{0,1},{1,2},{2,3},{3,4},{4,5},{5,6},{6,7},{7,8},{8,9},{9,10},{10,1... | collective-permute-start | bytes 786440 | tf_op jit(solution)/shard_map/ppermute | solution.py:79
  55.2 12.4 %copy-start = (bf16[128,1024]{1,0:T(8,128)(2,1)S(1)}, bf16[128,1024]{1,0:T(8,128)(2,1)}, u32[]{:S(2)}) copy-start(bf16[128,1024]{1,0:T(8,128)(2,1)} %cot_hbm.1) | copy-start | bytes 786436
  61.2 21.6 %collective-permute-start.5 = (f32[24,256]{1,0:T(8,128)S(1)}, f32[24,256]{1,0:T(8,128)S(1)}, u32[]{:S(2)}, u32[]{:S(2)}) collective-permute-start(f32[24,256]{1,0:T(8,128)S(1)} %get-tuple-element.43), channel_id=1, source_target_pairs={{1,0},{2,1},{3,2},{4,3},{5,4},{6,5},{7,6},{8,7},{9,8},{10,9},{11,1... | collective-permute-start | bytes 73736 | tf_op jit(solution)/shard_map/ppermute | solution.py:78
  63.2 19.7 %collective-permute-start.4 = (f32[24,256]{1,0:T(8,128)S(1)}, f32[24,256]{1,0:T(8,128)S(1)}, u32[]{:S(2)}, u32[]{:S(2)}) collective-permute-start(f32[24,256]{1,0:T(8,128)S(1)} %get-tuple-element.43), channel_id=1, source_target_pairs={{0,1},{1,2},{2,3},{3,4},{4,5},{5,6},{6,7},{7,8},{8,9},{9,10},{10,1... | collective-permute-start | bytes 73736 | tf_op jit(solution)/shard_map/ppermute | solution.py:79

commit v5 on v4

v5 whole, which is shorter than its diff:
```python
import functools

import jax
import jax.numpy as jnp
from jax import lax
from jax.experimental import pallas as pl
from jax.experimental.pallas import tpu as pltpu
from jax.sharding import PartitionSpec as P

HEADS = 16
BAND = 128
LANES = 128
F32 = jnp.float32
BF16 = jnp.bfloat16
I32 = jnp.int32
VMEM_LIMIT = 28 * 2**20
EARLY = 32


def mm(a, b):
    return lax.dot_general(a, b, (((1,), (0,)), ((), ())), preferred_element_type=F32)


def mm_nt(a, b):
    return lax.dot_general(a, b, (((1,), (1,)), ((), ())), preferred_element_type=F32)


def mm_tn(a, b):
    return lax.dot_general(a, b, (((0,), (0,)), ((), ())), preferred_element_type=F32)


def iota(shape, dim):
    return lax.broadcasted_iota(I32, shape, dim)


def call(kernel, outs, args, hbm=(), hbm_outs=(), scratch=(), name=None):
    args = [
        pltpu.with_memory_space_constraint(a, pltpu.HBM) if i in hbm else a
        for i, a in enumerate(args)
    ]

    def specs(count, far):
        return [
            pl.BlockSpec(memory_space=pltpu.HBM if i in far else pltpu.VMEM) for i in range(count)
        ]

    return pl.pallas_call(
        kernel,
        out_shape=[
            (pltpu.HBM if i in hbm_outs else jax.ShapeDtypeStruct)(shape, dtype)
            for i, (shape, dtype) in enumerate(outs)
        ],
        in_specs=specs(len(args), hbm),
        out_specs=specs(len(outs), hbm_outs),
        scratch_shapes=list(scratch),
        compiler_params=pltpu.CompilerParams(vmem_limit_bytes=VMEM_LIMIT),
        name=name,
    )(*args)


def dma(count):
    return pltpu.SemaphoreType.DMA((count,))


def start_all(pairs, sems):
    copies = [pltpu.make_async_copy(src, dst, sems.at[i]) for i, (src, dst) in enumerate(pairs)]
    for copy in copies:
        copy.start()
    return copies


def like(*arrays):
    return [pltpu.VMEM(a.shape, a.dtype) for a in arrays]


def exchange(toward_low, toward_high, axis):
    ends = lax.axis_size(axis) - 1
    from_high = lax.ppermute(toward_low, axis, [(i + 1, i) for i in range(ends)])
    from_low = lax.ppermute(toward_high, axis, [(i, i + 1) for i in range(ends)])
    return from_low, from_high


def gelu(projected):
    x = projected.astype(BF16).astype(F32)
    inner = (2.0 / jnp.pi) ** 0.5 * (x + 0.044715 * (x * x * x))
    return (0.5 * x * (1.0 + jnp.tanh(inner))).astype(BF16)


def onehot_rows(index_rows, count):
    parts = [
        jnp.where(iota((count, row.shape[1]), 0) == row, 1.0, 0.0).astype(BF16)
        for row in index_rows
    ]
    return parts[0] if len(parts) == 1 else jnp.concatenate(parts, 1)


def norm_stats(latent):
    values = latent.astype(F32)
    row_mean = jnp.mean(values, -1, keepdims=True)
    centred = values - row_mean
    variance = jnp.mean(centred * centred, -1, keepdims=True)
    inv_std = lax.rsqrt(variance + 1e-05)
    return centred * inv_std, inv_std


def pack_kernel(
    grid_hbm,
    cot_hbm,
    window_hbm,
    side_src_hbm,
    side_dst_hbm,
    side_count_hbm,
    far_src_hbm,
    far_dst_hbm,
    far_count_hbm,
    far_out,
    low_out,
    high_out,
    grid,
    cot,
    window,
    side_src,
    side_dst,
    side_count,
    far_src,
    far_dst,
    far_count,
    far,
    meta,
    sems,
    out_sems,
):
    grid_rows, channels = grid.shape
    mesh_rows = window.shape[1]
    slots = far_src.shape[1]
    devices = far_count.shape[1]
    depth = slots // devices
    first = grid_rows - BAND
    count = side_src.shape[0] // 2
    copies = start_all(
        [
            (side_src_hbm, side_src),
            (side_dst_hbm, side_dst),
            (side_count_hbm, side_count),
            (window_hbm, window),
            (grid_hbm, grid),
            (cot_hbm.at[pl.ds(0, EARLY)], cot),
            (far_src_hbm, far_src),
            (far_dst_hbm, far_dst),
            (far_count_hbm, far_count),
        ],
        sems,
    )
    for copy in copies[:4]:
        copy.wait()
    for k in range(2):
        rank = iota((count, LANES), 0) * LANES + iota((count, LANES), 1)
        src = side_src[k * count : (k + 1) * count] - k * first
        live = rank < side_count[:, k : k + 1]
        dst = jnp.where(live, side_dst[k * count : (k + 1) * count], mesh_rows)
        reach = jnp.concatenate([window[...], jnp.zeros((count - 2, mesh_rows), I32)], 0)
        blank = jnp.zeros((count, channels - 2 * LANES - mesh_rows), I32)
        meta[k] = jnp.concatenate([src, dst, reach, blank], 1).astype(F32).astype(BF16)
    for copy in copies[4:6]:
        copy.wait()
    outs = start_all(
        [
            pair
            for k, out in ((0, low_out), (1, high_out))
            for pair in (
                (grid.at[pl.ds(k * first, BAND)], out.at[pl.ds(0, BAND)]),
                (meta.at[k], out.at[pl.ds(BAND, count)]),
                (cot, out.at[pl.ds(BAND + count, EARLY)]),
            )
        ],
        out_sems,
    )
    for copy in copies[6:]:
        copy.wait()
    slot = iota((1, slots), 1)
    receiver = jnp.where(iota((devices, slots), 0) == iota((devices, slots), 1) // depth, 1.0, 0.0)
    live = mm(far_count[...].astype(F32).astype(BF16), receiver.astype(BF16))
    target = jnp.where((slot % depth).astype(F32) < live, far_dst[...].astype(F32), 1.0 * mesh_rows)
    row = iota((2 * slots, slots), 0)
    mine = slot == row // (2 * depth) * depth + row % depth
    source = jnp.sum(jnp.where(mine, far_src[...].astype(F32), 0.0), 1, keepdims=True)
    column = jnp.sum(jnp.where(mine, target, 0.0), 1, keepdims=True)
    pick = jnp.where(iota((2 * slots, grid_rows), 1).astype(F32) == source, 1.0, 0.0).astype(BF16)
    rows = mm(pick, grid[...])
    half = channels // 2
    is_first = iota((2 * slots, half), 0) % (2 * depth) < depth
    far[:, :half] = jnp.where(is_first, rows[:, :half], rows[:, half:]).astype(BF16)
    far[:, half:] = jnp.broadcast_to(column, (2 * slots, LANES)).astype(BF16)
    last = pltpu.make_async_copy(far, far_out, out_sems.at[6])
    last.start()
    for copy in outs + [last]:
        copy.wait()


def own_kernel(
    grid_hbm,
    mesh_in_hbm,
    own_src_hbm,
    own_dst_hbm,
    w_edge_hbm,
    partial_out,
    grid,
    mesh_in,
    own_src,
    own_dst,
    w_edge,
    sems,
):
    grid_rows = grid.shape[0]
    mesh_rows = mesh_in.shape[0]
    copies = start_all(
        [
            (own_src_hbm, own_src),
            (own_dst_hbm, own_dst),
            (grid_hbm, grid),
            (w_edge_hbm, w_edge),
            (mesh_in_hbm, mesh_in),
        ],
        sems,
    )
    for copy in copies[:2]:
        copy.wait()
    rows = own_src.shape[0]
    src = onehot_rows([own_src[r : r + 1] for r in range(rows)], grid_rows)
    dst = onehot_rows([own_dst[r : r + 1] for r in range(rows)], mesh_rows)
    counts = mm_nt(dst, src).astype(BF16)
    for copy in copies[2:]:
        copy.wait()
    active = gelu(mm(grid[...], w_edge[...]))
    partial_out[...] = mesh_in[...].astype(F32) + mm(counts, active)


def mesh_kernel(
    depth,
    low_hbm,
    high_hbm,
    far_hbm,
    w_edge_hbm,
    partial,
    latent_out,
    normed_out,
    window_out,
    cot_out,
    metas,
    bands,
    far,
    w_edge,
    sems,
):
    mesh_rows, channels = partial.shape
    count = metas.shape[1]
    ends = (low_hbm, high_hbm)
    copies = start_all(
        [(ends[k].at[pl.ds(BAND, count)], metas.at[k]) for k in range(2)]
        + [(far_hbm, far)]
        + [(ends[k].at[pl.ds(0, BAND)], bands.at[pl.ds(k * BAND, BAND)]) for k in range(2)]
        + [(w_edge_hbm, w_edge)]
        + [
            (ends[k].at[pl.ds(BAND + count, EARLY)], cot_out.at[pl.ds(k * EARLY, EARLY)])
            for k in range(2)
        ],
        sems,
    )
    for copy in copies[:2]:
        copy.wait()
    uppers, lowers = [], []
    for k in range(2):
        meta = metas[k].astype(F32).astype(I32)
        src = onehot_rows([meta[r : r + 1, :LANES] for r in range(count)], BAND)
        dst = onehot_rows([meta[r : r + 1, LANES : 2 * LANES] for r in range(count)], mesh_rows)
        counts = mm_nt(dst, src)
        upper = counts.astype(BF16)
        uppers.append(upper)
        lowers.append((counts - upper.astype(F32)).astype(BF16))
        window_out[:, k * mesh_rows : (k + 1) * mesh_rows] = meta[:8, 2 * LANES : 2 * LANES + mesh_rows]
    copies[2].wait()
    slots = far.shape[0]
    half = channels // 2
    first = far[:, :half]
    second = pltpu.roll(first.astype(F32), slots - depth, 0).astype(BF16)
    far_rows = jnp.concatenate([first, second], 1)
    target = jnp.transpose(far[:, half:].astype(F32))
    if mesh_rows != LANES:
        target = jnp.broadcast_to(target[:1], (mesh_rows, slots))
    is_row = iota((mesh_rows, slots), 1) % (2 * depth) < depth
    hit = (target == iota((mesh_rows, slots), 0).astype(F32)) & is_row
    landing = jnp.concatenate(uppers + [jnp.where(hit, 1.0, 0.0).astype(BF16)] + lowers, 1)
    for copy in copies[3:6]:
        copy.wait()
    active = gelu(mm(jnp.concatenate([bands[...], far_rows], 0), w_edge[...]))
    active = jnp.concatenate([active, active[: 2 * BAND]], 0)
    latent = (partial[...] + mm(landing, active)).astype(BF16)
    latent_out[...] = latent
    normal, _ = norm_stats(latent)
    normed_out[...] = normal.astype(BF16)
    for copy in copies[6:]:
        copy.wait()


def project_kernel(
    normed, near_cot, w_qkv_hbm, w_out_hbm, cot_hbm, qkv_out, w_qkv, w_out, cot_out, grad_out, near_out, sems
):
    m, step = normed.shape
    copies = start_all(
        [
            (w_qkv_hbm.at[:, pl.ds(c * step, step)], w_qkv.at[:, pl.ds(c * step, step)])
            for c in range(3)
        ]
        + [(cot_hbm, cot_out), (w_out_hbm, w_out)],
        sems,
    )
    for c in range(3):
        copies[c].wait()
        cols = slice(c * step, (c + 1) * step)
        qkv_out[:, cols] = mm(normed[...], w_qkv[:, cols]).astype(BF16)
    for copy in copies[3:]:
        copy.wait()
    grads = mm_nt(jnp.concatenate([cot_out[...], near_cot[...]], 0), w_out[...]).astype(BF16)
    grad_out[...] = grads[:m]
    near_out[...] = grads[m:]


def halves(rows, scale=None):
    first = iota(rows.shape, 1) < rows.shape[1] // 2
    if scale is not None:
        rows = rows * jnp.asarray(scale, rows.dtype)
    zero = jnp.zeros_like(rows)
    return jnp.concatenate([jnp.where(first, rows, zero), jnp.where(first, zero, rows)], 0)


def merge(stacked):
    m = stacked.shape[0] // 2
    first = iota((m, stacked.shape[1]), 1) < stacked.shape[1] // 2
    return jnp.where(first, stacked[:m], stacked[m:])


def attend_kernel(
    scale,
    pair,
    low_normed,
    high_normed,
    w_qkv,
    own_qkv,
    own_grad,
    window_hbm,
    message_out,
    kv,
    weights_out,
    scores_out,
    window,
    sems,
):
    fetch = start_all([(window_hbm, window)], sems)
    m, channels = low_normed.shape
    pairs = channels // pair
    rows = message_out.shape[0] - (m - EARLY)
    message_out[rows:] = own_grad[EARLY:]
    devices = lax.axis_size("node")
    me = lax.axis_index("node")
    near = mm(jnp.concatenate([low_normed[...], high_normed[...]], 0), w_qkv[:, channels:])
    near = near.astype(BF16)
    kv[:m] = near[:m]
    kv[m : 2 * m] = own_qkv[:, channels:]
    kv[2 * m :] = near[m:]
    fetch[0].wait()
    key_at = iota((3 * m, m), 0)
    query_at = iota((3 * m, m), 1) + m
    inside = (key_at >= jnp.where(me == 0, m, 0)) & (
        key_at < jnp.where(me == devices - 1, 2 * m, 3 * m)
    )
    keep = (
        inside & (key_at >= query_at - window[0:1, :]) & (key_at <= query_at + window[1:2, :])
    )
    bias = jnp.transpose(jnp.where(keep, 0.0, -jnp.inf).astype(F32))
    bias = jnp.concatenate([bias, bias], 0)
    lane = iota((2 * m, LANES), 1)
    stats = jnp.zeros((2 * m, LANES), F32)
    for p in range(pairs):
        cols = slice(p * pair, (p + 1) * pair)
        q2 = halves(own_qkv[:, cols], scale)
        g2 = halves(own_grad[:, cols])
        scores = mm_nt(q2, kv[:, cols]) + bias
        top = jnp.max(scores, 1, keepdims=True)
        shifted = jnp.exp(scores - top)
        inv_sum = 1.0 / jnp.sum(shifted, 1, keepdims=True)
        probs = shifted * inv_sum
        weights_out[p] = probs.astype(BF16)
        grad_prob = mm_nt(g2, kv[:, channels + p * pair : channels + (p + 1) * pair])
        delta = jnp.sum(probs * grad_prob, 1, keepdims=True)
        scores_out[p] = (probs * (grad_prob - delta)).astype(BF16)
        stats = jnp.where(lane == p, top, stats)
        stats = jnp.where(lane == pairs + p, inv_sum, stats)
        stats = jnp.where(lane == 2 * pairs + p, delta, stats)
    rest = jnp.transpose(stats)[:rows]
    for part in range(3):
        piece = rest.astype(BF16)
        message_out[:rows, part * 2 * m : (part + 1) * 2 * m] = piece
        rest = rest - piece.astype(F32)
    message_out[:rows, 6 * m :] = jnp.zeros((rows, channels - 6 * m), BF16)


def product_kernel(
    scale,
    pair,
    weights,
    grad_scores,
    kv,
    own_qkv,
    own_grad,
    latent,
    w_out,
    w_qkv,
    low_normed,
    high_normed,
    mesh_out,
    grad_normed,
    grad_key,
    grad_value,
    near_q_out,
    attention,
    grad_query,
):
    m, channels = latent.shape
    for p in range(channels // pair):
        cols = slice(p * pair, (p + 1) * pair)
        key = kv[:, cols]
        value = kv[:, channels + p * pair : channels + (p + 1) * pair]
        attention[:, cols] = merge(mm(weights[p], value)).astype(BF16)
        grad_query[:, cols] = (merge(mm(grad_scores[p], key)) * scale).astype(BF16)
        grad_key[:, cols] = mm_tn(grad_scores[p, :, m : 2 * m], halves(own_qkv[:, cols], scale))
        grad_value[:, cols] = mm_tn(weights[p, :, m : 2 * m], halves(own_grad[:, cols]))
    mesh_out[...] = (latent[...].astype(F32) + mm(attention[...], w_out[...])).astype(BF16)
    grad_normed[...] = mm_nt(grad_query[...], w_qkv[:, :channels])
    near = mm(jnp.concatenate([low_normed[...], high_normed[...]], 0), w_qkv[:, :channels])
    near_q_out[...] = near.astype(BF16) * jnp.asarray(scale, BF16)


def finish_kernel(
    pair,
    low,
    high,
    near_window,
    near_q,
    early_grad,
    own_qkv,
    grad_key,
    grad_value,
    grad_normed,
    w_qkv,
    latent,
    cot,
    grad_out,
    grad_kv,
):
    m, channels = latent.shape
    rows = low.shape[0] - (m - EARLY)
    key_at = iota((m, 2 * m), 0) + m
    lane = iota((m, 2 * m), 1)
    query_at = jnp.where(lane < m, lane, lane + m)
    keep = (key_at >= query_at - near_window[0:1, :]) & (key_at <= query_at + near_window[1:2, :])
    bias = jnp.where(keep, 0.0, -jnp.inf).astype(F32)
    pairs = channels // pair

    def whole(side):
        return sum(side[:rows, k * 2 * m : (k + 1) * 2 * m].astype(F32) for k in (2, 1, 0))

    low_stats, high_stats = whole(low), whole(high)
    stats = [jnp.concatenate([low_stats[:, h * m : (h + 1) * m], high_stats[:, h * m : (h + 1) * m]], 1) for h in range(2)]
    for p in range(pairs):
        cols = slice(p * pair, (p + 1) * pair)
        key2 = halves(own_qkv[:, channels + p * pair : channels + (p + 1) * pair])
        value2 = halves(own_qkv[:, 2 * channels + p * pair : 2 * channels + (p + 1) * pair])
        query = near_q[:, cols]
        grad = jnp.concatenate(
            [early_grad[:EARLY, cols], low[rows:, cols], early_grad[EARLY:, cols], high[rows:, cols]], 0
        )
        scores = mm_nt(key2, query)
        grad_prob = mm_nt(value2, grad)
        weights, grad_scores = [], []
        for h in range(2):
            half = slice(h * m, (h + 1) * m)
            top, inv_sum, delta = (stats[h][k * pairs + p : k * pairs + p + 1] for k in range(3))
            probs = jnp.exp(scores[half] + bias - top) * inv_sum
            weights.append(probs.astype(BF16))
            grad_scores.append((probs * (grad_prob[half] - delta)).astype(BF16))
        gk = grad_key[:, cols] + merge(mm(jnp.concatenate(grad_scores, 0), query))
        gv = grad_value[:, cols] + merge(mm(jnp.concatenate(weights, 0), grad))
        grad_kv[:, cols] = gk.astype(BF16)
        grad_kv[:, channels + p * pair : channels + (p + 1) * pair] = gv.astype(BF16)
    total = grad_normed[...] + mm_nt(grad_kv[...], w_qkv[:, channels:])
    normal, inv_std = norm_stats(latent[...])
    centred = (
        total
        - jnp.mean(total, -1, keepdims=True)
        - normal * jnp.mean(total * normal, -1, keepdims=True)
    )
    grad_out[...] = (cot[...].astype(F32) + inv_std * centred).astype(BF16)


def body(
    grid_in,
    mesh_in,
    own_src,
    own_dst,
    side_src,
    side_dst,
    side_count,
    far_src,
    far_dst,
    far_count,
    window,
    cotangent,
    w_edge,
    w_qkv,
    w_out,
):
    devices = lax.axis_size("node")
    grid_rows, channels = grid_in.shape
    m = mesh_in.shape[0]
    far_slots = far_src.shape[0]
    far_depth = far_slots // devices
    head_dim = channels // HEADS
    pair = 2 * head_dim
    pairs = channels // pair
    scale = head_dim ** (-0.5)
    meta_rows = side_src.shape[0] // (2 * LANES)

    side_src, side_dst = side_src.reshape(-1, LANES), side_dst.reshape(-1, LANES)
    own_src, own_dst = own_src.reshape(-1, LANES), own_dst.reshape(-1, LANES)
    far_src, far_dst = far_src.reshape(1, -1), far_dst.reshape(1, -1)
    side_count, far_count = side_count.reshape(1, -1), far_count.reshape(1, -1)
    message = ((BAND + meta_rows + EARLY, channels), BF16)
    far_block = (2 * far_slots, channels // 2 + LANES)
    far_message, toward_low, toward_high = call(
        pack_kernel,
        [(far_block, BF16), message, message],
        [grid_in, cotangent, window, side_src, side_dst, side_count, far_src, far_dst, far_count],
        hbm=range(9),
        hbm_outs=range(3),
        scratch=like(grid_in, cotangent[:EARLY])
        + like(window, side_src, side_dst, side_count, far_src, far_dst, far_count)
        + [
            pltpu.VMEM(far_block, BF16),
            pltpu.VMEM((2, meta_rows, channels), BF16),
            dma(9),
            dma(7),
        ],
        name="pack",
    )
    from_low, from_high = exchange(toward_low, toward_high, "node")
    got_far = lax.all_to_all(
        far_message.reshape(devices, 2 * far_depth, far_block[1]),
        "node",
        split_axis=0,
        concat_axis=0,
        tiled=True,
    ).reshape(far_block)

    rows = ((m, channels), BF16)
    (own_part,) = call(
        own_kernel,
        [((m, channels), F32)],
        [grid_in, mesh_in, own_src, own_dst, w_edge],
        hbm=range(5),
        scratch=like(grid_in, mesh_in, own_src, own_dst, w_edge) + [dma(5)],
        name="own",
    )
    latent, normed, near_window, near_cot = call(
        functools.partial(mesh_kernel, far_depth),
        [rows, rows, ((8, 2 * m), I32), ((2 * EARLY, channels), BF16)],
        [from_low, from_high, got_far, w_edge, own_part],
        hbm=(0, 1, 2, 3),
        scratch=[
            pltpu.VMEM((2, meta_rows, channels), BF16),
            pltpu.VMEM((2 * BAND, channels), BF16),
            pltpu.VMEM(far_block, BF16),
            pltpu.VMEM(w_edge.shape, BF16),
            dma(8),
        ],
        name="mesh",
    )
    low_normed, high_normed = exchange(normed, normed, "node")
    own_qkv, w_qkv, w_out, own_cot, own_grad, early_grad = call(
        project_kernel,
        [
            ((m, 3 * channels), BF16),
            (w_qkv.shape, BF16),
            (w_out.shape, BF16),
            rows,
            rows,
            ((2 * EARLY, channels), BF16),
        ],
        [normed, near_cot, w_qkv, w_out, cotangent],
        hbm=(2, 3, 4),
        scratch=[dma(5)],
        name="project",
    )
    stat_rows = -(-3 * pairs // 16) * 16
    probs = ((pairs, 2 * m, 3 * m), BF16)
    message, kv, weights, grad_scores = call(
        functools.partial(attend_kernel, scale, pair),
        [((stat_rows + m - EARLY, channels), BF16), ((3 * m, 2 * channels), BF16), probs, probs],
        [low_normed, high_normed, w_qkv, own_qkv, own_grad, window],
        hbm=(5,),
        scratch=like(window) + [dma(1)],
        name="attend",
    )
    low_late, high_late = exchange(message, message, "node")
    mesh_out, grad_normed, grad_key, grad_value, near_q = call(
        functools.partial(product_kernel, scale, pair),
        [
            rows,
            ((m, channels), F32),
            ((m, channels), F32),
            ((m, channels), F32),
            ((2 * m, channels), BF16),
        ],
        [
            weights,
            grad_scores,
            kv,
            own_qkv,
            own_grad,
            latent,
            w_out,
            w_qkv,
            low_normed,
            high_normed,
        ],
        scratch=[pltpu.VMEM((m, channels), BF16)] * 2,
        name="product",
    )
    (mesh_grad,) = call(
        functools.partial(finish_kernel, pair),
        [rows],
        [
            low_late,
            high_late,
            near_window,
            near_q,
            early_grad,
            own_qkv,
            grad_key,
            grad_value,
            grad_normed,
            w_qkv,
            latent,
            own_cot,
        ],
        scratch=[pltpu.VMEM((m, 2 * channels), BF16)],
        name="finish",
    )
    return (mesh_out, mesh_grad)


def solution(mesh):
    rows = P(("groups", "node"), None)
    flat = P(("groups", "node"))
    placed = (rows, rows) + (flat,) * 8 + (P(None, ("groups", "node")), rows, P(), P(), P())
    return jax.shard_map(
        body, mesh=mesh, in_specs=placed, out_specs=(rows, rows), check_vma=False
    )
```

time: 88.7 us -> 57.7 us (0.65)
  Pallas kernels: 48 us -> 26 us
  blocking collectives: 11.7 us -> 0 us
  waiting for transfers between devices: 1.81 us -> 4.87 us
    pallas_call x8 -> x7, Pallas kernels: 48 us -> 26 us  [call(): pl.pallas_call(kernel, out_shape=[(pltpu.HBM if i in hbm_outs else jax.Sh...]
    all_gather x2 -> x0, blocking collectives: 11.7 us -> none  [pair_gather(): lax.all_gather(rows, axis, axis_index_groups=[[(i + k) % n, (i + k + 1) %...]
    all_to_all x1, waiting for transfers between devices: 0.01 us -> 3.67 us  [body(): lax.all_to_all(far_message.reshape(devices, 2 * far_depth, far_block[1]),...]
    ppermute x3, starting transfers between devices: 5.76 us -> 6.91 us  [exchange(): lax.ppermute(toward_low, axis, [(i + 1, i) for i in range(ends)])]
    ppermute x3, waiting for transfers between devices: 0.92 us -> 0.01 us  [exchange(): lax.ppermute(toward_low, axis, [(i + 1, i) for i in range(ends)])]
    all_to_all x1, starting transfers between devices: 7.36 us -> 6.46 us  [body(): lax.all_to_all(far_message.reshape(devices, 2 * far_depth, far_block[1]),...]
where the time goes in v5:
time: 57.7 us; the launch traced here: 57.2 us
  Pallas kernels  26 us (45%)
  starting transfers between devices  24.7 us (43%)
  waiting for transfers between devices  4.87 us (8%)
  local copies, waits for them, and re-layouts  0.88 us (2%)
  between operations  0.75 us (1%)
    pallas_call x7, Pallas kernels, call(): pl.pallas_call(kernel, out_shape=[(pltpu.HBM if i in hbm_outs else jax.Sh...  26 us
    ppermute x3, starting transfers between devices, exchange(): lax.ppermute(toward_high, axis, [(i, i + 1) for i in range(ends)])  11.3 us
    ppermute x3, starting transfers between devices, exchange(): lax.ppermute(toward_low, axis, [(i + 1, i) for i in range(ends)])  6.91 us
    all_to_all x1, starting transfers between devices, body(): lax.all_to_all(far_message.reshape(devices, 2 * far_depth, far_block[1]),...  6.46 us
    all_to_all x1, waiting for transfers between devices, body(): lax.all_to_all(far_message.reshape(devices, 2 * far_depth, far_block[1]),...  3.67 us
    ppermute x3, waiting for transfers between devices, exchange(): lax.ppermute(toward_high, axis, [(i, i + 1) for i in range(ends)])  1.19 us
  transfers between devices with their start and end apart: 7, of which 2 were waited for; matrix products, arithmetic and copies ran while one was open for 0% of the time, Pallas kernels for 20%

profile of v5, /device:TPU:1, one launch (start us, length us, event | category | flops | bytes accessed | tf_op | source)
XLA Modules:
  0.0 57.2 jit_solution(2472054278194428760)
XLA Ops:
  0.6 2.5 %pack.1 = (bf16[128,640]{1,0:T(8,128)(2,1)}, bf16[176,1024]{1,0:T(8,128)(2,1)}, bf16[176,1024]{1,0:T(8,128)(2,1)}) custom-call(bf16[512,1024]{1,0:T(8,128)(2,1)} %grid_hbm.3, bf16[128,1024]{1,0:T(8,128)(2,1)} %cot_hbm.3, s32[2,128]{1,0:T(2,128)} %window_hbm.3, s32[32,128]{1,0:T(8,128)} %bitcast.12, s32[32,128]{1,0:T(8,128)} %bitcast.13, s32[1,2]{1,0:T(1,128)} %bitcast.16, ...), custom_call_target="tpu_custom_call" | custom-call | tf_op jit(solution)/shard_map/pack/pallas_call | solution.py:47
  3.1 4.5 %collective-permute-start = (bf16[176,1024]{1,0:T(8,128)(2,1)}, bf16[176,1024]{1,0:T(8,128)(2,1)S(1)}, u32[]{:S(2)}, u32[]{:S(2)}) collective-permute-start(bf16[176,1024]{1,0:T(8,128)(2,1)} %get-tuple-element.24), channel_id=1, source_target_pairs={{0,1},{1,2},{2,3},{3,4},{4,5},{5,6},{6,7},{7,8},{8,9},{9,10},{10,1... | collective-permute-start | bytes 1081352 | tf_op jit(solution)/shard_map/ppermute | solution.py:79
  7.7 1.9 %collective-permute-start.1 = (bf16[176,1024]{1,0:T(8,128)(2,1)}, bf16[176,1024]{1,0:T(8,128)(2,1)S(1)}, u32[]{:S(2)}, u32[]{:S(2)}) collective-permute-start(bf16[176,1024]{1,0:T(8,128)(2,1)} %get-tuple-element.25), channel_id=1, source_target_pairs={{1,0},{2,1},{3,2},{4,3},{5,4},{6,5},{7,6},{8,7},{9,8},{10,9},{11,1... | collective-permute-start | bytes 1081352 | tf_op jit(solution)/shard_map/ppermute | solution.py:78
  9.6 6.5 %all-to-all-start = ((bf16[16,8,640]{2,1,0:T(8,128)(2,1)}), bf16[16,8,640]{2,1,0:T(8,128)(2,1)S(1)}, u32[]{:S(2)}, u32[]{:S(2)}) async-start(bf16[16,8,640]{2,1,0:T(8,128)(2,1)} %bitcast.11), calls=%async_computation | async-start | bytes 327680 | tf_op jit(solution)/shard_map/all_to_all | solution.py:556
  16.1 3.7 %own.1.partial = f32[128,1024]{1,0:T(8,128)S(1)} custom-call(bf16[512,1024]{1,0:T(8,128)(2,1)} %grid_hbm.3, bf16[128,1024]{1,0:T(8,128)(2,1)} %mesh_in_hbm.1, s32[8,128]{1,0:T(8,128)} %bitcast.14, s32[8,128]{1,0:T(8,128)} %bitcast.15, bf16[1024,1024]{1,0:T(8,128)(2,1)} %w_edge_hbm.3), custom_call_target="tpu_custom_call" | custom-call | tf_op jit(solution)/shard_map/own/pallas_call | solution.py:47
  19.8 3.7 %all-to-all-done = bf16[16,8,640]{2,1,0:T(8,128)(2,1)S(1)} async-done(((bf16[16,8,640]{2,1,0:T(8,128)(2,1)}), bf16[16,8,640]{2,1,0:T(8,128)(2,1)S(1)}, u32[]{:S(2)}, u32[]{:S(2)}) %all-to-all-start) | async-done | bytes 163872 | tf_op jit(solution)/shard_map/all_to_all | solution.py:556
  23.5 0.0 copy-start
  23.5 0.0 collective-permute-done.low_hbm
  23.5 0.0 copy-start.1
  23.5 0.0 collective-permute-done.1.high_hbm
  23.5 0.0 copy-start.2
  23.5 0.6 %copy-done = bf16[16,8,640]{2,1,0:T(8,128)(2,1)} copy-done((bf16[16,8,640]{2,1,0:T(8,128)(2,1)}, bf16[16,8,640]{2,1,0:T(8,128)(2,1)S(1)}, u32[]{:S(2)}) %copy-start) | copy-done | bytes 163864
  24.1 0.1 copy-done.1
  24.2 0.1 copy-done.2
  24.4 3.7 %mesh.1 = (bf16[128,1024]{1,0:T(8,128)(2,1)S(1)}, bf16[128,1024]{1,0:T(8,128)(2,1)S(1)}, s32[8,256]{1,0:T(8,128)S(1)}, bf16[64,1024]{1,0:T(8,128)(2,1)S(1)}) custom-call(bf16[176,1024]{1,0:T(8,128)(2,1)} %copy-done.1, bf16[176,1024]{1,0:T(8,128)(2,1)} %copy-done.2, bf16[128,640]{1,0:T(8,128)(2,1)} %bitcast.10, bf16[1024,1024]{1,0:T(8,128)(2,1)} %w_edge_hbm.3, ...), custom_call_target="tpu_custom_call" | custom-call | tf_op jit(solution)/shard_map/mesh/pallas_call | solution.py:47
  28.0 3.1 %collective-permute-start.3 = (bf16[128,1024]{1,0:T(8,128)(2,1)S(1)}, bf16[128,1024]{1,0:T(8,128)(2,1)S(1)}, u32[]{:S(2)}, u32[]{:S(2)}) collective-permute-start(bf16[128,1024]{1,0:T(8,128)(2,1)S(1)} %get-tuple-element.27.normed), channel_id=1, source_target_pairs={{1,0},{2,1},{3,2},{4,3},{5,4},{6,5},{7,6},{8,7},{9,8},{10,9},{11,1... | collective-permute-start | bytes 786440 | tf_op jit(solution)/shard_map/ppermute | solution.py:78
  31.1 2.5 %collective-permute-start.2 = (bf16[128,1024]{1,0:T(8,128)(2,1)S(1)}, bf16[128,1024]{1,0:T(8,128)(2,1)S(1)}, u32[]{:S(2)}, u32[]{:S(2)}) collective-permute-start(bf16[128,1024]{1,0:T(8,128)(2,1)S(1)} %get-tuple-element.27.normed), channel_id=1, source_target_pairs={{0,1},{1,2},{2,3},{3,4},{4,5},{5,6},{6,7},{7,8},{8,9},{9,10},{10,1... | collective-permute-start | bytes 786440 | tf_op jit(solution)/shard_map/ppermute | solution.py:79
  33.6 4.5 %project.1 = (bf16[128,3072]{1,0:T(8,128)(2,1)S(1)}, bf16[1024,3072]{1,0:T(8,128)(2,1)S(1)}, bf16[1024,1024]{1,0:T(8,128)(2,1)S(1)}, bf16[128,1024]{1,0:T(8,128)...) custom-call(bf16[128,1024]{1,0:T(8,128)(2,1)S(1)} %get-tuple-element.27.normed, ...), custom_call_target="tpu_custom_call" | custom-call | tf_op jit(solution)/shard_map/project/pallas_call | solution.py:47
  38.1 0.0 collective-permute-done.3.high_normed
  38.1 0.0 collective-permute-done.2.low_normed
  38.1 4.1 %attend.1 = (bf16[128,1024]{1,0:T(8,128)(2,1)S(1)}, bf16[384,2048]{1,0:T(8,128)(2,1)S(1)}, bf16[8,256,384]{2,1,0:T(8,128)(2,1)S(1)}, bf16[8,256,384]{2,1,0:T(8,128)(2,1)S(1)}) custom-call(bf16[128,1024]{1,0:T(8,128)(2,1)S(1)} %collective-permute-done.2.low_normed, bf16[128,1024]{1,0:T(8,128)(2,1)S(1)} %collective-permute-done.3.high_normed, ...), custom_call_target="tpu_custom_call" | custom-call | tf_op jit(solution)/shard_map/attend/pallas_call | solution.py:47
  42.2 1.9 %collective-permute-start.5 = (bf16[128,1024]{1,0:T(8,128)(2,1)S(1)}, bf16[128,1024]{1,0:T(8,128)(2,1)S(1)}, u32[]{:S(2)}, u32[]{:S(2)}) collective-permute-start(bf16[128,1024]{1,0:T(8,128)(2,1)S(1)} %get-tuple-element.38), channel_id=1, source_target_pairs={{1,0},{2,1},{3,2},{4,3},{5,4},{6,5},{7,6},{8,7},{9,8},{10,9},{11,1... | collective-permute-start | bytes 786440 | tf_op jit(solution)/shard_map/ppermute | solution.py:78
  44.2 4.3 %collective-permute-start.4 = (bf16[128,1024]{1,0:T(8,128)(2,1)S(1)}, bf16[128,1024]{1,0:T(8,128)(2,1)S(1)}, u32[]{:S(2)}, u32[]{:S(2)}) collective-permute-start(bf16[128,1024]{1,0:T(8,128)(2,1)S(1)} %get-tuple-element.38), channel_id=1, source_target_pairs={{0,1},{1,2},{2,3},{3,4},{4,5},{5,6},{6,7},{7,8},{8,9},{9,10},{10,1... | collective-permute-start | bytes 786440 | tf_op jit(solution)/shard_map/ppermute | solution.py:79
  48.5 3.3 %product.1 = (bf16[128,1024]{1,0:T(8,128)(2,1)}, f32[128,1024]{1,0:T(8,128)S(1)}, f32[128,1024]{1,0:T(8,128)S(1)}, f32[128,1024]{1,0:T(8,128)S(1)}, bf16[256,1024]{1,0:T(8,128)(2,1)S(1)}) custom-call(bf16[8,256,384]{2,1,0:T(8,128)(2,1)S(1)} %get-tuple-element.32.weights, bf16[8,256,384]{2,1,0:T(8,128)(2,1)S(1)} %get-tuple-element.33.grad_scores, ...), custom_call_target="tpu_custom_call" | custom-call | tf_op jit(solution)/shard_map/product/pallas_call | solution.py:47
  51.8 0.0 collective-permute-done.5.high
  51.8 1.2 %collective-permute-done.4.low = bf16[128,1024]{1,0:T(8,128)(2,1)S(1)} collective-permute-done((bf16[128,1024]{1,0:T(8,128)(2,1)S(1)}, bf16[128,1024]{1,0:T(8,128)(2,1)S(1)}, u32[]{:S(2)}, u32[]{:S(2)}) %collective-permute-start.4) | collective-permute-done | bytes 262176 | tf_op jit(solution)/shard_map/ppermute | solution.py:79
  52.9 4.3 %finish.1 = bf16[128,1024]{1,0:T(8,128)(2,1)} custom-call(bf16[128,1024]{1,0:T(8,128)(2,1)S(1)} %collective-permute-done.4.low, bf16[128,1024]{1,0:T(8,128)(2,1)S(1)} %collective-permute-done.5.high, s32[8,256]{1,0:T(8,128)S(1)} %get-tuple-element.39.near_window, bf16[256,1024]{1,0:T(8,128)(2,1)S(1)} %get-tuple-element.40.near_q, ...), custom_call_target="tpu_custom_call" | custom-call | tf_op jit(solution)/shard_map/finish/pallas_call | solution.py:47
Async XLA Ops:
  3.1 20.3 %collective-permute-start = (bf16[176,1024]{1,0:T(8,128)(2,1)}, bf16[176,1024]{1,0:T(8,128)(2,1)S(1)}, u32[]{:S(2)}, u32[]{:S(2)}) collective-permute-start(bf16[176,1024]{1,0:T(8,128)(2,1)} %get-tuple-element.24), channel_id=1, source_target_pairs={{0,1},{1,2},{2,3},{3,4},{4,5},{5,6},{6,7},{7,8},{8,9},{9,10},{10,1... | collective-permute-start | bytes 1081352 | tf_op jit(solution)/shard_map/ppermute | solution.py:79
  7.7 15.8 %collective-permute-start.1 = (bf16[176,1024]{1,0:T(8,128)(2,1)}, bf16[176,1024]{1,0:T(8,128)(2,1)S(1)}, u32[]{:S(2)}, u32[]{:S(2)}) collective-permute-start(bf16[176,1024]{1,0:T(8,128)(2,1)} %get-tuple-element.25), channel_id=1, source_target_pairs={{1,0},{2,1},{3,2},{4,3},{5,4},{6,5},{7,6},{8,7},{9,8},{10,9},{11,1... | collective-permute-start | bytes 1081352 | tf_op jit(solution)/shard_map/ppermute | solution.py:78
  9.6 13.9 %all-to-all-start = ((bf16[16,8,640]{2,1,0:T(8,128)(2,1)}), bf16[16,8,640]{2,1,0:T(8,128)(2,1)S(1)}, u32[]{:S(2)}, u32[]{:S(2)}) async-start(bf16[16,8,640]{2,1,0:T(8,128)(2,1)} %bitcast.11), calls=%async_computation | async-start | bytes 327680 | tf_op jit(solution)/shard_map/all_to_all | solution.py:556
  23.5 0.7 %copy-start = (bf16[16,8,640]{2,1,0:T(8,128)(2,1)}, bf16[16,8,640]{2,1,0:T(8,128)(2,1)S(1)}, u32[]{:S(2)}) copy-start(bf16[16,8,640]{2,1,0:T(8,128)(2,1)S(1)} %all-to-all-done) | copy-start | bytes 491524
  23.5 0.8 %copy-start.1 = (bf16[176,1024]{1,0:T(8,128)(2,1)}, bf16[176,1024]{1,0:T(8,128)(2,1)S(1)}, u32[]{:S(2)}) copy-start(bf16[176,1024]{1,0:T(8,128)(2,1)S(1)} %collective-permute-done.low_hbm) | copy-start | bytes 1081348
  23.5 0.9 %copy-start.2 = (bf16[176,1024]{1,0:T(8,128)(2,1)}, bf16[176,1024]{1,0:T(8,128)(2,1)S(1)}, u32[]{:S(2)}) copy-start(bf16[176,1024]{1,0:T(8,128)(2,1)S(1)} %collective-permute-done.1.high_hbm) | copy-start | bytes 1081348
  28.0 10.0 %collective-permute-start.3 = (bf16[128,1024]{1,0:T(8,128)(2,1)S(1)}, bf16[128,1024]{1,0:T(8,128)(2,1)S(1)}, u32[]{:S(2)}, u32[]{:S(2)}) collective-permute-start(bf16[128,1024]{1,0:T(8,128)(2,1)S(1)} %get-tuple-element.27.normed), channel_id=1, source_target_pairs={{1,0},{2,1},{3,2},{4,3},{5,4},{6,5},{7,6},{8,7},{9,8},{10,9},{11,1... | collective-permute-start | bytes 786440 | tf_op jit(solution)/shard_map/ppermute | solution.py:78
  31.1 7.0 %collective-permute-start.2 = (bf16[128,1024]{1,0:T(8,128)(2,1)S(1)}, bf16[128,1024]{1,0:T(8,128)(2,1)S(1)}, u32[]{:S(2)}, u32[]{:S(2)}) collective-permute-start(bf16[128,1024]{1,0:T(8,128)(2,1)S(1)} %get-tuple-element.27.normed), channel_id=1, source_target_pairs={{0,1},{1,2},{2,3},{3,4},{4,5},{5,6},{6,7},{7,8},{8,9},{9,10},{10,1... | collective-permute-start | bytes 786440 | tf_op jit(solution)/shard_map/ppermute | solution.py:79
  42.2 9.5 %collective-permute-start.5 = (bf16[128,1024]{1,0:T(8,128)(2,1)S(1)}, bf16[128,1024]{1,0:T(8,128)(2,1)S(1)}, u32[]{:S(2)}, u32[]{:S(2)}) collective-permute-start(bf16[128,1024]{1,0:T(8,128)(2,1)S(1)} %get-tuple-element.38), channel_id=1, source_target_pairs={{1,0},{2,1},{3,2},{4,3},{5,4},{6,5},{7,6},{8,7},{9,8},{10,9},{11,1... | collective-permute-start | bytes 786440 | tf_op jit(solution)/shard_map/ppermute | solution.py:78
  44.2 8.8 %collective-permute-start.4 = (bf16[128,1024]{1,0:T(8,128)(2,1)S(1)}, bf16[128,1024]{1,0:T(8,128)(2,1)S(1)}, u32[]{:S(2)}, u32[]{:S(2)}) collective-permute-start(bf16[128,1024]{1,0:T(8,128)(2,1)S(1)} %get-tuple-element.38), channel_id=1, source_target_pairs={{0,1},{1,2},{2,3},{3,4},{4,5},{5,6},{6,7},{7,8},{8,9},{9,10},{10,1... | collective-permute-start | bytes 786440 | tf_op jit(solution)/shard_map/ppermute | solution.py:79

commit v6 on v5

--- a/solution.py
+++ b/solution.py
@@ -14,7 +14,7 @@
 BF16 = jnp.bfloat16
 I32 = jnp.int32
 VMEM_LIMIT = 28 * 2**20
-EARLY = 32
+EARLY = 64
 
 
 def mm(a, b):
@@ -73,11 +73,19 @@
     return [pltpu.VMEM(a.shape, a.dtype) for a in arrays]
 
 
-def exchange(toward_low, toward_high, axis):
-    ends = lax.axis_size(axis) - 1
-    from_high = lax.ppermute(toward_low, axis, [(i + 1, i) for i in range(ends)])
-    from_low = lax.ppermute(toward_high, axis, [(i, i + 1) for i in range(ends)])
-    return from_low, from_high
+def exchange(chip_message, off_message, axis):
+    n = lax.axis_size(axis)
+    from_off = lax.ppermute(
+        off_message, axis, [p for i in range(1, n - 1, 2) for p in ((i, i + 1), (i + 1, i))]
+    )
+    from_chip = lax.ppermute(
+        chip_message, axis, [p for i in range(0, n, 2) for p in ((i, i + 1), (i + 1, i))]
+    )
+    return from_chip, from_off
+
+
+def is_odd():
+    return lax.axis_index("node") % 2
 
 
 def gelu(projected):
@@ -113,9 +121,11 @@
     far_src_hbm,
     far_dst_hbm,
     far_count_hbm,
+    w_edge_hbm,
     far_out,
-    low_out,
-    high_out,
+    chip_out,
+    off_out,
+    w_edge,
     grid,
     cot,
     window,
@@ -148,6 +158,7 @@
             (far_src_hbm, far_src),
             (far_dst_hbm, far_dst),
             (far_count_hbm, far_count),
+            (w_edge_hbm, w_edge),
         ],
         sems,
     )
@@ -163,19 +174,20 @@
         meta[k] = jnp.concatenate([src, dst, reach, blank], 1).astype(F32).astype(BF16)
     for copy in copies[4:6]:
         copy.wait()
+    odd = is_odd()
     outs = start_all(
         [
             pair
-            for k, out in ((0, low_out), (1, high_out))
+            for k, out in ((1 - odd, chip_out), (odd, off_out))
             for pair in (
-                (grid.at[pl.ds(k * first, BAND)], out.at[pl.ds(0, BAND)]),
+                (grid.at[pl.ds(pl.multiple_of(k * first, BAND), BAND)], out.at[pl.ds(0, BAND)]),
                 (meta.at[k], out.at[pl.ds(BAND, count)]),
                 (cot, out.at[pl.ds(BAND + count, EARLY)]),
             )
         ],
         out_sems,
     )
-    for copy in copies[6:]:
+    for copy in copies[6:9]:
         copy.wait()
     slot = iota((1, slots), 1)
     receiver = jnp.where(iota((devices, slots), 0) == iota((devices, slots), 1) // depth, 1.0, 0.0)
@@ -186,10 +198,12 @@
     source = jnp.sum(jnp.where(mine, far_src[...].astype(F32), 0.0), 1, keepdims=True)
     column = jnp.sum(jnp.where(mine, target, 0.0), 1, keepdims=True)
     pick = jnp.where(iota((2 * slots, grid_rows), 1).astype(F32) == source, 1.0, 0.0).astype(BF16)
-    rows = mm(pick, grid[...])
+    rows = mm(pick, grid[...]).astype(BF16)
+    copies[9].wait()
+    rows = gelu(mm(rows, w_edge[...]))
     half = channels // 2
     is_first = iota((2 * slots, half), 0) % (2 * depth) < depth
-    far[:, :half] = jnp.where(is_first, rows[:, :half], rows[:, half:]).astype(BF16)
+    far[:, :half] = jnp.where(is_first, rows[:, :half], rows[:, half:])
     far[:, half:] = jnp.broadcast_to(column, (2 * slots, LANES)).astype(BF16)
     last = pltpu.make_async_copy(far, far_out, out_sems.at[6])
     last.start()
@@ -202,13 +216,12 @@
     mesh_in_hbm,
     own_src_hbm,
     own_dst_hbm,
-    w_edge_hbm,
+    w_edge,
     partial_out,
     grid,
     mesh_in,
     own_src,
     own_dst,
-    w_edge,
     sems,
 ):
     grid_rows = grid.shape[0]
@@ -218,7 +231,6 @@
             (own_src_hbm, own_src),
             (own_dst_hbm, own_dst),
             (grid_hbm, grid),
-            (w_edge_hbm, w_edge),
             (mesh_in_hbm, mesh_in),
         ],
         sems,
@@ -235,75 +247,47 @@
     partial_out[...] = mesh_in[...].astype(F32) + mm(counts, active)
 
 
-def mesh_kernel(
-    depth,
-    low_hbm,
-    high_hbm,
-    far_hbm,
-    w_edge_hbm,
-    partial,
-    latent_out,
-    normed_out,
-    window_out,
-    cot_out,
-    metas,
-    bands,
-    far,
-    w_edge,
-    sems,
-):
-    mesh_rows, channels = partial.shape
-    count = metas.shape[1]
-    ends = (low_hbm, high_hbm)
-    copies = start_all(
-        [(ends[k].at[pl.ds(BAND, count)], metas.at[k]) for k in range(2)]
-        + [(far_hbm, far)]
-        + [(ends[k].at[pl.ds(0, BAND)], bands.at[pl.ds(k * BAND, BAND)]) for k in range(2)]
-        + [(w_edge_hbm, w_edge)]
-        + [
-            (ends[k].at[pl.ds(BAND + count, EARLY)], cot_out.at[pl.ds(k * EARLY, EARLY)])
-            for k in range(2)
-        ],
-        sems,
-    )
-    for copy in copies[:2]:
-        copy.wait()
+def meta_of(message, count):
+    return message[BAND : BAND + count].astype(F32).astype(I32)
+
+
+def side_kernel(count, chip, off, w_edge, partial, partial_out):
+    mesh_rows = partial.shape[0]
     uppers, lowers = [], []
-    for k in range(2):
-        meta = metas[k].astype(F32).astype(I32)
+    for side in (chip, off):
+        meta = meta_of(side, count)
         src = onehot_rows([meta[r : r + 1, :LANES] for r in range(count)], BAND)
         dst = onehot_rows([meta[r : r + 1, LANES : 2 * LANES] for r in range(count)], mesh_rows)
         counts = mm_nt(dst, src)
         upper = counts.astype(BF16)
         uppers.append(upper)
         lowers.append((counts - upper.astype(F32)).astype(BF16))
-        window_out[:, k * mesh_rows : (k + 1) * mesh_rows] = meta[:8, 2 * LANES : 2 * LANES + mesh_rows]
-    copies[2].wait()
+    active = gelu(mm(jnp.concatenate([chip[:BAND], off[:BAND]], 0), w_edge[...]))
+    landing = jnp.concatenate(uppers + lowers, 1)
+    partial_out[...] = partial[...] + mm(landing, jnp.concatenate([active, active], 0))
+
+
+def latent_kernel(depth, far, partial, latent_out, normed_out):
+    mesh_rows, channels = partial.shape
     slots = far.shape[0]
     half = channels // 2
     first = far[:, :half]
     second = pltpu.roll(first.astype(F32), slots - depth, 0).astype(BF16)
-    far_rows = jnp.concatenate([first, second], 1)
     target = jnp.transpose(far[:, half:].astype(F32))
     if mesh_rows != LANES:
         target = jnp.broadcast_to(target[:1], (mesh_rows, slots))
     is_row = iota((mesh_rows, slots), 1) % (2 * depth) < depth
     hit = (target == iota((mesh_rows, slots), 0).astype(F32)) & is_row
-    landing = jnp.concatenate(uppers + [jnp.where(hit, 1.0, 0.0).astype(BF16)] + lowers, 1)
-    for copy in copies[3:6]:
-        copy.wait()
-    active = gelu(mm(jnp.concatenate([bands[...], far_rows], 0), w_edge[...]))
-    active = jnp.concatenate([active, active[: 2 * BAND]], 0)
-    latent = (partial[...] + mm(landing, active)).astype(BF16)
+    landing = jnp.where(hit, 1.0, 0.0).astype(BF16)
+    total = partial[...] + mm(landing, jnp.concatenate([first, second], 1))
+    latent = total.astype(BF16)
     latent_out[...] = latent
     normal, _ = norm_stats(latent)
     normed_out[...] = normal.astype(BF16)
-    for copy in copies[6:]:
-        copy.wait()
 
 
 def project_kernel(
-    normed, near_cot, w_qkv_hbm, w_out_hbm, cot_hbm, qkv_out, w_qkv, w_out, cot_out, grad_out, near_out, sems
+    normed, chip, off, w_qkv_hbm, w_out_hbm, cot_hbm, qkv_out, w_qkv, w_out, cot_out, grad_out, near_out, sems
 ):
     m, step = normed.shape
     copies = start_all(
@@ -320,7 +304,8 @@
         qkv_out[:, cols] = mm(normed[...], w_qkv[:, cols]).astype(BF16)
     for copy in copies[3:]:
         copy.wait()
-    grads = mm_nt(jnp.concatenate([cot_out[...], near_cot[...]], 0), w_out[...]).astype(BF16)
+    cots = jnp.concatenate([cot_out[...], chip[-EARLY:], off[-EARLY:]], 0)
+    grads = mm_nt(cots, w_out[...]).astype(BF16)
     grad_out[...] = grads[:m]
     near_out[...] = grads[m:]
 
@@ -339,11 +324,16 @@
     return jnp.where(first, stacked[:m], stacked[m:])
 
 
+def near_places(m):
+    odd = is_odd()
+    return (1 - odd) * 2 * m, odd * 2 * m
+
+
 def attend_kernel(
     scale,
     pair,
-    low_normed,
-    high_normed,
+    chip_normed,
+    off_normed,
     w_qkv,
     own_qkv,
     own_grad,
@@ -356,23 +346,23 @@
     sems,
 ):
     fetch = start_all([(window_hbm, window)], sems)
-    m, channels = low_normed.shape
+    m, channels = chip_normed.shape
     pairs = channels // pair
     rows = message_out.shape[0] - (m - EARLY)
     message_out[rows:] = own_grad[EARLY:]
     devices = lax.axis_size("node")
     me = lax.axis_index("node")
-    near = mm(jnp.concatenate([low_normed[...], high_normed[...]], 0), w_qkv[:, channels:])
+    near = mm(jnp.concatenate([chip_normed[...], off_normed[...]], 0), w_qkv[:, channels:])
     near = near.astype(BF16)
     kv[:m] = near[:m]
     kv[m : 2 * m] = own_qkv[:, channels:]
     kv[2 * m :] = near[m:]
     fetch[0].wait()
-    key_at = iota((3 * m, m), 0)
+    row = iota((3 * m, m), 0)
+    chip_at, off_at = near_places(m)
+    key_at = jnp.where(row < m, row + chip_at, jnp.where(row < 2 * m, row, row - 2 * m + off_at))
     query_at = iota((3 * m, m), 1) + m
-    inside = (key_at >= jnp.where(me == 0, m, 0)) & (
-        key_at < jnp.where(me == devices - 1, 2 * m, 3 * m)
-    )
+    inside = row < jnp.where((me == 0) | (me == devices - 1), 2 * m, 3 * m)
     keep = (
         inside & (key_at >= query_at - window[0:1, :]) & (key_at <= query_at + window[1:2, :])
     )
@@ -415,8 +405,8 @@
     latent,
     w_out,
     w_qkv,
-    low_normed,
-    high_normed,
+    chip_normed,
+    off_normed,
     mesh_out,
     grad_normed,
     grad_key,
@@ -436,15 +426,17 @@
         grad_value[:, cols] = mm_tn(weights[p, :, m : 2 * m], halves(own_grad[:, cols]))
     mesh_out[...] = (latent[...].astype(F32) + mm(attention[...], w_out[...])).astype(BF16)
     grad_normed[...] = mm_nt(grad_query[...], w_qkv[:, :channels])
-    near = mm(jnp.concatenate([low_normed[...], high_normed[...]], 0), w_qkv[:, :channels])
+    near = mm(jnp.concatenate([chip_normed[...], off_normed[...]], 0), w_qkv[:, :channels])
     near_q_out[...] = near.astype(BF16) * jnp.asarray(scale, BF16)
 
 
 def finish_kernel(
     pair,
-    low,
-    high,
-    near_window,
+    count,
+    chip,
+    off,
+    chip_first,
+    off_first,
     near_q,
     early_grad,
     own_qkv,
@@ -458,26 +450,32 @@
     grad_kv,
 ):
     m, channels = latent.shape
-    rows = low.shape[0] - (m - EARLY)
+    rows = chip.shape[0] - (m - EARLY)
+    reach = [meta_of(side, count)[:8, 2 * LANES : 2 * LANES + m] for side in (chip_first, off_first)]
+    reach = jnp.concatenate(reach, 1)
     key_at = iota((m, 2 * m), 0) + m
     lane = iota((m, 2 * m), 1)
-    query_at = jnp.where(lane < m, lane, lane + m)
-    keep = (key_at >= query_at - near_window[0:1, :]) & (key_at <= query_at + near_window[1:2, :])
+    chip_at, off_at = near_places(m)
+    query_at = jnp.where(lane < m, lane + chip_at, lane - m + off_at)
+    keep = (key_at >= query_at - reach[0:1, :]) & (key_at <= query_at + reach[1:2, :])
     bias = jnp.where(keep, 0.0, -jnp.inf).astype(F32)
     pairs = channels // pair
 
     def whole(side):
         return sum(side[:rows, k * 2 * m : (k + 1) * 2 * m].astype(F32) for k in (2, 1, 0))
 
-    low_stats, high_stats = whole(low), whole(high)
-    stats = [jnp.concatenate([low_stats[:, h * m : (h + 1) * m], high_stats[:, h * m : (h + 1) * m]], 1) for h in range(2)]
+    chip_stats, off_stats = whole(chip), whole(off)
+    stats = []
+    for h in range(2):
+        lanes = slice(h * m, (h + 1) * m)
+        stats.append(jnp.concatenate([chip_stats[:, lanes], off_stats[:, lanes]], 1))
     for p in range(pairs):
         cols = slice(p * pair, (p + 1) * pair)
         key2 = halves(own_qkv[:, channels + p * pair : channels + (p + 1) * pair])
         value2 = halves(own_qkv[:, 2 * channels + p * pair : 2 * channels + (p + 1) * pair])
         query = near_q[:, cols]
         grad = jnp.concatenate(
-            [early_grad[:EARLY, cols], low[rows:, cols], early_grad[EARLY:, cols], high[rows:, cols]], 0
+            [early_grad[:EARLY, cols], chip[rows:, cols], early_grad[EARLY:, cols], off[rows:, cols]], 0
         )
         scores = mm_nt(key2, query)
         grad_prob = mm_nt(value2, grad)
@@ -536,23 +534,24 @@
     side_count, far_count = side_count.reshape(1, -1), far_count.reshape(1, -1)
     message = ((BAND + meta_rows + EARLY, channels), BF16)
     far_block = (2 * far_slots, channels // 2 + LANES)
-    far_message, toward_low, toward_high = call(
+    far_message, chip_message, off_message, w_edge = call(
         pack_kernel,
-        [(far_block, BF16), message, message],
-        [grid_in, cotangent, window, side_src, side_dst, side_count, far_src, far_dst, far_count],
-        hbm=range(9),
+        [(far_block, BF16), message, message, (w_edge.shape, BF16)],
+        [grid_in, cotangent, window, side_src, side_dst, side_count, far_src, far_dst, far_count]
+        + [w_edge],
+        hbm=range(10),
         hbm_outs=range(3),
         scratch=like(grid_in, cotangent[:EARLY])
         + like(window, side_src, side_dst, side_count, far_src, far_dst, far_count)
         + [
             pltpu.VMEM(far_block, BF16),
             pltpu.VMEM((2, meta_rows, channels), BF16),
-            dma(9),
+            dma(10),
             dma(7),
         ],
         name="pack",
     )
-    from_low, from_high = exchange(toward_low, toward_high, "node")
+    from_chip, from_off = exchange(chip_message, off_message, "node")
     got_far = lax.all_to_all(
         far_message.reshape(devices, 2 * far_depth, far_block[1]),
         "node",
@@ -562,29 +561,24 @@
     ).reshape(far_block)
 
     rows = ((m, channels), BF16)
-    (own_part,) = call(
+    (partial,) = call(
         own_kernel,
         [((m, channels), F32)],
         [grid_in, mesh_in, own_src, own_dst, w_edge],
-        hbm=range(5),
-        scratch=like(grid_in, mesh_in, own_src, own_dst, w_edge) + [dma(5)],
+        hbm=range(4),
+        scratch=like(grid_in, mesh_in, own_src, own_dst) + [dma(4)],
         name="own",
     )
-    latent, normed, near_window, near_cot = call(
-        functools.partial(mesh_kernel, far_depth),
-        [rows, rows, ((8, 2 * m), I32), ((2 * EARLY, channels), BF16)],
-        [from_low, from_high, got_far, w_edge, own_part],
-        hbm=(0, 1, 2, 3),
-        scratch=[
-            pltpu.VMEM((2, meta_rows, channels), BF16),
-            pltpu.VMEM((2 * BAND, channels), BF16),
-            pltpu.VMEM(far_block, BF16),
-            pltpu.VMEM(w_edge.shape, BF16),
-            dma(8),
-        ],
-        name="mesh",
-    )
-    low_normed, high_normed = exchange(normed, normed, "node")
+    (partial,) = call(
+        functools.partial(side_kernel, meta_rows),
+        [((m, channels), F32)],
+        [from_chip, from_off, w_edge, partial],
+        name="side",
+    )
+    latent, normed = call(
+        functools.partial(latent_kernel, far_depth), [rows, rows], [got_far, partial], name="latent"
+    )
+    chip_normed, off_normed = exchange(normed, normed, "node")
     own_qkv, w_qkv, w_out, own_cot, own_grad, early_grad = call(
         project_kernel,
         [
@@ -595,8 +589,8 @@
             rows,
             ((2 * EARLY, channels), BF16),
         ],
-        [normed, near_cot, w_qkv, w_out, cotangent],
-        hbm=(2, 3, 4),
+        [normed, from_chip, from_off, w_qkv, w_out, cotangent],
+        hbm=(3, 4, 5),
         scratch=[dma(5)],
         name="project",
     )
@@ -605,12 +599,12 @@
     message, kv, weights, grad_scores = call(
         functools.partial(attend_kernel, scale, pair),
         [((stat_rows + m - EARLY, channels), BF16), ((3 * m, 2 * channels), BF16), probs, probs],
-        [low_normed, high_normed, w_qkv, own_qkv, own_grad, window],
+        [chip_normed, off_normed, w_qkv, own_qkv, own_grad, window],
         hbm=(5,),
         scratch=like(window) + [dma(1)],
         name="attend",
     )
-    low_late, high_late = exchange(message, message, "node")
+    chip_late, off_late = exchange(message, message, "node")
     mesh_out, grad_normed, grad_key, grad_value, near_q = call(
         functools.partial(product_kernel, scale, pair),
         [
@@ -629,19 +623,20 @@
             latent,
             w_out,
             w_qkv,
-            low_normed,
-            high_normed,
+            chip_normed,
+            off_normed,
         ],
         scratch=[pltpu.VMEM((m, channels), BF16)] * 2,
         name="product",
     )
     (mesh_grad,) = call(
-        functools.partial(finish_kernel, pair),
+        functools.partial(finish_kernel, pair, meta_rows),
         [rows],
         [
-            low_late,
-            high_late,
-            near_window,
+            chip_late,
+            off_late,
+            from_chip,
+            from_off,
             near_q,
             early_grad,
             own_qkv,

time: 57.7 us -> 50.3 us (0.87)
  starting transfers between devices: 24.7 us -> 19 us
  Pallas kernels: 26 us -> 25.1 us
  local copies, waits for them, and re-layouts: 0.88 us -> 0 us
    ppermute x6, starting transfers between devices: 18.3 us -> 13.7 us  [the longest x3 13.4 us: exchange(): lax.ppermute(off_message, axis, [p for i in range(1, n - 1, 2) for p in (...]
    all_to_all x1, waiting for transfers between devices: 3.67 us -> 0.04 us  [body(): lax.all_to_all(far_message.reshape(devices, 2 * far_depth, far_block[1]),...]
    ppermute x6, waiting for transfers between devices: 1.2 us -> 4.56 us  [the longest x3 4.56 us: exchange(): lax.ppermute(off_message, axis, [p for i in range(1, n - 1, 2) for p in (...]
    all_to_all x1, starting transfers between devices: 6.46 us -> 5.33 us  [body(): lax.all_to_all(far_message.reshape(devices, 2 * far_depth, far_block[1]),...]
    pallas_call x7 -> x8, Pallas kernels: 26 us -> 25.1 us  [call(): pl.pallas_call(kernel, out_shape=[(pltpu.HBM if i in hbm_outs else jax.Sh...]
    unnamed x6 -> x0, local copies, waits for them, and re-layouts: 0.88 us -> none
  transfers between devices with their start and end apart: 7 -> 7, of which waited for: 2 -> 2; matrix products, arithmetic and copies ran while one was open for 0% -> 0% of each run, Pallas kernels for 20% -> 24%
where the time goes in v6:
time: 50.3 us; the launch traced here: 49.4 us
  Pallas kernels  25.1 us (50%)
  starting transfers between devices  19 us (38%)
  waiting for transfers between devices  4.61 us (9%)
  between operations  0.73 us (1%)
    pallas_call x8, Pallas kernels, call(): pl.pallas_call(kernel, out_shape=[(pltpu.HBM if i in hbm_outs else jax.Sh...  25.1 us
    ppermute x3, starting transfers between devices, exchange(): lax.ppermute(off_message, axis, [p for i in range(1, n - 1, 2) for p in (...  13.4 us
    all_to_all x1, starting transfers between devices, body(): lax.all_to_all(far_message.reshape(devices, 2 * far_depth, far_block[1]),...  5.33 us
    ppermute x3, waiting for transfers between devices, exchange(): lax.ppermute(off_message, axis, [p for i in range(1, n - 1, 2) for p in (...  4.56 us
  transfers between devices with their start and end apart: 7, of which 2 were waited for; matrix products, arithmetic and copies ran while one was open for 0% of the time, Pallas kernels for 24%

profile of v6, /device:TPU:1, one launch (start us, length us, event | category | flops | bytes accessed | tf_op | source)
XLA Modules:
  0.0 49.4 jit_solution(9601069712928160640)
XLA Ops:
  0.6 3.4 %pack.1 = (bf16[128,640]{1,0:T(8,128)(2,1)}, bf16[208,1024]{1,0:T(8,128)(2,1)}, bf16[208,1024]{1,0:T(8,128)(2,1)}, bf16[1024,1024]{1,0:T(8,128)(2,1)S(1)}) custom-call(bf16[512,1024]{1,0:T(8,128)(2,1)} %grid_hbm.3, bf16[128,1024]{1,0:T(8,128)(2,1)} %cot_hbm.3, s32[2,128]{1,0:T(2,128)} %window_hbm.3, s32[32,128]{1,0:T(8,128)} %bitcast.11, ...), custom_call_target="tpu_custom_call" | custom-call | tf_op jit(solution)/shard_map/pack/pallas_call | solution.py:47
  4.0 0.1 collective-permute-start
  4.2 4.5 %collective-permute-start.1 = (bf16[208,1024]{1,0:T(8,128)(2,1)}, bf16[208,1024]{1,0:T(8,128)(2,1)S(1)}, u32[]{:S(2)}, u32[]{:S(2)}) collective-permute-start(bf16[208,1024]{1,0:T(8,128)(2,1)} %get-tuple-element.25), channel_id=1, source_target_pairs={{1,2},{2,1},{3,4},{4,3},{5,6},{6,5},{7,8},{8,7},{9,10},{10,9},{11,... | collective-permute-start | bytes 1277960 | tf_op jit(solution)/shard_map/ppermute | solution.py:78
  8.7 5.3 %all-to-all-start = ((bf16[16,8,640]{2,1,0:T(8,128)(2,1)}), bf16[16,8,640]{2,1,0:T(8,128)(2,1)}, u32[]{:S(2)}, u32[]{:S(2)}) async-start(bf16[16,8,640]{2,1,0:T(8,128)(2,1)} %bitcast.10), calls=%async_computation | async-start | bytes 327680 | tf_op jit(solution)/shard_map/all_to_all | solution.py:555
  14.0 3.1 %own.1.partial = f32[128,1024]{1,0:T(8,128)S(1)} custom-call(bf16[512,1024]{1,0:T(8,128)(2,1)} %grid_hbm.3, bf16[128,1024]{1,0:T(8,128)(2,1)} %mesh_in_hbm.1, s32[8,128]{1,0:T(8,128)} %bitcast.13, s32[8,128]{1,0:T(8,128)} %bitcast.14, bf16[1024,1024]{1,0:T(8,128)(2,1)S(1)} %get-tuple-element.26.w_edge), custom_call_target="tpu_custom_call" | custom-call | tf_op jit(solution)/shard_map/own/pallas_call | solution.py:47
  17.1 0.0 collective-permute-done.chip.chip_first
  17.1 2.9 %collective-permute-done.1.off.off_first = bf16[208,1024]{1,0:T(8,128)(2,1)S(1)} collective-permute-done((bf16[208,1024]{1,0:T(8,128)(2,1)}, bf16[208,1024]{1,0:T(8,128)(2,1)S(1)}, u32[]{:S(2)}, u32[]{:S(2)}) %collective-permute-start.1) | collective-permute-done | bytes 426016 | tf_op jit(solution)/shard_map/ppermute | solution.py:78
  20.0 1.4 %side.1.partial = f32[128,1024]{1,0:T(8,128)S(1)} custom-call(bf16[208,1024]{1,0:T(8,128)(2,1)S(1)} %collective-permute-done.chip.chip_first, bf16[208,1024]{1,0:T(8,128)(2,1)S(1)} %collective-permute-done.1.off.off_first, bf16[1024,1024]{1,0:T(8,128)(2,1)S(1)} %get-tuple-element.26.w_edge, f32[128,1024]{1,0:T(8,128)S(1)} %own.1.partial), custom_call_target="tpu_custom_call" | custom-call | tf_op jit(solution)/shard_map/side/pallas_call | solution.py:47
  21.5 0.0 all-to-all-done
  21.5 1.4 %latent.1 = (bf16[128,1024]{1,0:T(8,128)(2,1)S(1)}, bf16[128,1024]{1,0:T(8,128)(2,1)S(1)}) custom-call(bf16[128,640]{1,0:T(8,128)(2,1)} %bitcast.7.far, f32[128,1024]{1,0:T(8,128)S(1)} %side.1.partial), custom_call_target="tpu_custom_call" | custom-call | tf_op jit(solution)/shard_map/latent/pallas_call | solution.py:47
  22.9 4.4 %collective-permute-start.3 = (bf16[128,1024]{1,0:T(8,128)(2,1)S(1)}, bf16[128,1024]{1,0:T(8,128)(2,1)S(1)}, u32[]{:S(2)}, u32[]{:S(2)}) collective-permute-start(bf16[128,1024]{1,0:T(8,128)(2,1)S(1)} %get-tuple-element.27.normed), channel_id=1, source_target_pairs={{1,2},{2,1},{3,4},{4,3},{5,6},{6,5},{7,8},{8,7},{9,10},{10,9},{11,... | collective-permute-start | bytes 786440 | tf_op jit(solution)/shard_map/ppermute | solution.py:78
  27.3 0.1 collective-permute-start.2
  27.4 4.4 %project.1 = (bf16[128,3072]{1,0:T(8,128)(2,1)S(1)}, bf16[1024,3072]{1,0:T(8,128)(2,1)S(1)}, bf16[1024,1024]{1,0:T(8,128)(2,1)S(1)}, bf16[128,1024]{1,0:T(8,128)...) custom-call(bf16[128,1024]{1,0:T(8,128)(2,1)S(1)} %get-tuple-element.27.normed, ...), custom_call_target="tpu_custom_call" | custom-call | tf_op jit(solution)/shard_map/project/pallas_call | solution.py:47
  31.7 1.6 %collective-permute-done.3.off_normed = bf16[128,1024]{1,0:T(8,128)(2,1)S(1)} collective-permute-done((bf16[128,1024]{1,0:T(8,128)(2,1)S(1)}, bf16[128,1024]{1,0:T(8,128)(2,1)S(1)}, u32[]{:S(2)}, u32[]{:S(2)}) %collective-permute-start.3) | collective-permute-done | bytes 262176 | tf_op jit(solution)/shard_map/ppermute | solution.py:78
  33.3 0.0 collective-permute-done.2.chip_normed
  33.3 3.9 %attend.1 = (bf16[96,1024]{1,0:T(8,128)(2,1)S(1)}, bf16[384,2048]{1,0:T(8,128)(2,1)S(1)}, bf16[8,256,384]{2,1,0:T(8,128)(2,1)S(1)}, bf16[8,256,384]{2,1,0:T(8,128)(2,1)S(1)}) custom-call(bf16[128,1024]{1,0:T(8,128)(2,1)S(1)} %collective-permute-done.2.chip_normed, bf16[128,1024]{1,0:T(8,128)(2,1)S(1)} %collective-permute-done.3.off_normed, ...), custom_call_target="tpu_custom_call" | custom-call | tf_op jit(solution)/shard_map/attend/pallas_call | solution.py:47
  37.3 4.6 %collective-permute-start.5 = (bf16[96,1024]{1,0:T(8,128)(2,1)S(1)}, bf16[96,1024]{1,0:T(8,128)(2,1)S(1)}, u32[]{:S(2)}, u32[]{:S(2)}) collective-permute-start(bf16[96,1024]{1,0:T(8,128)(2,1)S(1)} %get-tuple-element.37), channel_id=1, source_target_pairs={{1,2},{2,1},{3,4},{4,3},{5,6},{6,5},{7,8},{8,7},{9,10},{10,9},{11,... | collective-permute-start | bytes 589832 | tf_op jit(solution)/shard_map/ppermute | solution.py:78
  41.9 0.1 collective-permute-start.4
  42.0 3.2 %product.1 = (bf16[128,1024]{1,0:T(8,128)(2,1)}, f32[128,1024]{1,0:T(8,128)S(1)}, f32[128,1024]{1,0:T(8,128)S(1)}, f32[128,1024]{1,0:T(8,128)S(1)}, bf16[256,1024]{1,0:T(8,128)(2,1)S(1)}) custom-call(bf16[8,256,384]{2,1,0:T(8,128)(2,1)S(1)} %get-tuple-element.31.weights, bf16[8,256,384]{2,1,0:T(8,128)(2,1)S(1)} %get-tuple-element.32.grad_scores, ...), custom_call_target="tpu_custom_call" | custom-call | tf_op jit(solution)/shard_map/product/pallas_call | solution.py:47
  45.2 0.0 collective-permute-done.5.off
  45.2 0.0 collective-permute-done.4.chip
  45.2 4.2 %finish.1 = bf16[128,1024]{1,0:T(8,128)(2,1)} custom-call(bf16[96,1024]{1,0:T(8,128)(2,1)S(1)} %collective-permute-done.4.chip, bf16[96,1024]{1,0:T(8,128)(2,1)S(1)} %collective-permute-done.5.off, bf16[208,1024]{1,0:T(8,128)(2,1)S(1)} %collective-permute-done.chip.chip_first, bf16[208,1024]{1,0:T(8,128)(2,1)S(1)} %collective-permute-done.1.off.off_first, ...), custom_call_target="tpu_custom_call" | custom-call | tf_op jit(solution)/shard_map/finish/pallas_call | solution.py:47
Async XLA Ops:
  4.0 13.0 %collective-permute-start = (bf16[208,1024]{1,0:T(8,128)(2,1)}, bf16[208,1024]{1,0:T(8,128)(2,1)S(1)}, u32[]{:S(2)}, u32[]{:S(2)}) collective-permute-start(bf16[208,1024]{1,0:T(8,128)(2,1)} %get-tuple-element.24), channel_id=1, source_target_pairs={{0,1},{1,0},{2,3},{3,2},{4,5},{5,4},{6,7},{7,6},{8,9},{9,8},{10,11... | collective-permute-start | bytes 1277960 | tf_op jit(solution)/shard_map/ppermute | solution.py:81
  4.2 15.9 %collective-permute-start.1 = (bf16[208,1024]{1,0:T(8,128)(2,1)}, bf16[208,1024]{1,0:T(8,128)(2,1)S(1)}, u32[]{:S(2)}, u32[]{:S(2)}) collective-permute-start(bf16[208,1024]{1,0:T(8,128)(2,1)} %get-tuple-element.25), channel_id=1, source_target_pairs={{1,2},{2,1},{3,4},{4,3},{5,6},{6,5},{7,8},{8,7},{9,10},{10,9},{11,... | collective-permute-start | bytes 1277960 | tf_op jit(solution)/shard_map/ppermute | solution.py:78
  8.7 12.8 %all-to-all-start = ((bf16[16,8,640]{2,1,0:T(8,128)(2,1)}), bf16[16,8,640]{2,1,0:T(8,128)(2,1)}, u32[]{:S(2)}, u32[]{:S(2)}) async-start(bf16[16,8,640]{2,1,0:T(8,128)(2,1)} %bitcast.10), calls=%async_computation | async-start | bytes 327680 | tf_op jit(solution)/shard_map/all_to_all | solution.py:555
  22.9 10.4 %collective-permute-start.3 = (bf16[128,1024]{1,0:T(8,128)(2,1)S(1)}, bf16[128,1024]{1,0:T(8,128)(2,1)S(1)}, u32[]{:S(2)}, u32[]{:S(2)}) collective-permute-start(bf16[128,1024]{1,0:T(8,128)(2,1)S(1)} %get-tuple-element.27.normed), channel_id=1, source_target_pairs={{1,2},{2,1},{3,4},{4,3},{5,6},{6,5},{7,8},{8,7},{9,10},{10,9},{11,... | collective-permute-start | bytes 786440 | tf_op jit(solution)/shard_map/ppermute | solution.py:78
  27.3 6.1 %collective-permute-start.2 = (bf16[128,1024]{1,0:T(8,128)(2,1)S(1)}, bf16[128,1024]{1,0:T(8,128)(2,1)S(1)}, u32[]{:S(2)}, u32[]{:S(2)}) collective-permute-start(bf16[128,1024]{1,0:T(8,128)(2,1)S(1)} %get-tuple-element.27.normed), channel_id=1, source_target_pairs={{0,1},{1,0},{2,3},{3,2},{4,5},{5,4},{6,7},{7,6},{8,9},{9,8},{10,11... | collective-permute-start | bytes 786440 | tf_op jit(solution)/shard_map/ppermute | solution.py:81
  37.3 7.9 %collective-permute-start.5 = (bf16[96,1024]{1,0:T(8,128)(2,1)S(1)}, bf16[96,1024]{1,0:T(8,128)(2,1)S(1)}, u32[]{:S(2)}, u32[]{:S(2)}) collective-permute-start(bf16[96,1024]{1,0:T(8,128)(2,1)S(1)} %get-tuple-element.37), channel_id=1, source_target_pairs={{1,2},{2,1},{3,4},{4,3},{5,6},{6,5},{7,8},{8,7},{9,10},{10,9},{11,... | collective-permute-start | bytes 589832 | tf_op jit(solution)/shard_map/ppermute | solution.py:78
  41.9 3.3 %collective-permute-start.4 = (bf16[96,1024]{1,0:T(8,128)(2,1)S(1)}, bf16[96,1024]{1,0:T(8,128)(2,1)S(1)}, u32[]{:S(2)}, u32[]{:S(2)}) collective-permute-start(bf16[96,1024]{1,0:T(8,128)(2,1)S(1)} %get-tuple-element.37), channel_id=1, source_target_pairs={{0,1},{1,0},{2,3},{3,2},{4,5},{5,4},{6,7},{7,6},{8,9},{9,8},{10,11... | collective-permute-start | bytes 589832 | tf_op jit(solution)/shard_map/ppermute | solution.py:81

commit v7 on v6

--- a/solution.py
+++ b/solution.py
@@ -14,7 +14,7 @@
 BF16 = jnp.bfloat16
 I32 = jnp.int32
 VMEM_LIMIT = 28 * 2**20
-EARLY = 64
+PIECES = 6
 
 
 def mm(a, b):
@@ -113,7 +113,6 @@
 
 def pack_kernel(
     grid_hbm,
-    cot_hbm,
     window_hbm,
     side_src_hbm,
     side_dst_hbm,
@@ -127,7 +126,6 @@
     off_out,
     w_edge,
     grid,
-    cot,
     window,
     side_src,
     side_dst,
@@ -154,7 +152,6 @@
             (side_count_hbm, side_count),
             (window_hbm, window),
             (grid_hbm, grid),
-            (cot_hbm.at[pl.ds(0, EARLY)], cot),
             (far_src_hbm, far_src),
             (far_dst_hbm, far_dst),
             (far_count_hbm, far_count),
@@ -172,8 +169,7 @@
         reach = jnp.concatenate([window[...], jnp.zeros((count - 2, mesh_rows), I32)], 0)
         blank = jnp.zeros((count, channels - 2 * LANES - mesh_rows), I32)
         meta[k] = jnp.concatenate([src, dst, reach, blank], 1).astype(F32).astype(BF16)
-    for copy in copies[4:6]:
-        copy.wait()
+    copies[4].wait()
     odd = is_odd()
     outs = start_all(
         [
@@ -182,12 +178,11 @@
             for pair in (
                 (grid.at[pl.ds(pl.multiple_of(k * first, BAND), BAND)], out.at[pl.ds(0, BAND)]),
                 (meta.at[k], out.at[pl.ds(BAND, count)]),
-                (cot, out.at[pl.ds(BAND + count, EARLY)]),
             )
         ],
         out_sems,
     )
-    for copy in copies[6:9]:
+    for copy in copies[5:8]:
         copy.wait()
     slot = iota((1, slots), 1)
     receiver = jnp.where(iota((devices, slots), 0) == iota((devices, slots), 1) // depth, 1.0, 0.0)
@@ -199,13 +194,13 @@
     column = jnp.sum(jnp.where(mine, target, 0.0), 1, keepdims=True)
     pick = jnp.where(iota((2 * slots, grid_rows), 1).astype(F32) == source, 1.0, 0.0).astype(BF16)
     rows = mm(pick, grid[...]).astype(BF16)
-    copies[9].wait()
+    copies[8].wait()
     rows = gelu(mm(rows, w_edge[...]))
     half = channels // 2
     is_first = iota((2 * slots, half), 0) % (2 * depth) < depth
     far[:, :half] = jnp.where(is_first, rows[:, :half], rows[:, half:])
     far[:, half:] = jnp.broadcast_to(column, (2 * slots, LANES)).astype(BF16)
-    last = pltpu.make_async_copy(far, far_out, out_sems.at[6])
+    last = pltpu.make_async_copy(far, far_out, out_sems.at[4])
     last.start()
     for copy in outs + [last]:
         copy.wait()
@@ -287,27 +282,30 @@
 
 
 def project_kernel(
-    normed, chip, off, w_qkv_hbm, w_out_hbm, cot_hbm, qkv_out, w_qkv, w_out, cot_out, grad_out, near_out, sems
+    normed, w_qkv_hbm, w_out_hbm, cot_hbm, qkv_out, w_qkv, w_out, cot_out, grad_out, sems
 ):
-    m, step = normed.shape
-    copies = start_all(
-        [
-            (w_qkv_hbm.at[:, pl.ds(c * step, step)], w_qkv.at[:, pl.ds(c * step, step)])
-            for c in range(3)
-        ]
-        + [(cot_hbm, cot_out), (w_out_hbm, w_out)],
-        sems,
-    )
-    for c in range(3):
-        copies[c].wait()
-        cols = slice(c * step, (c + 1) * step)
+    width = w_qkv.shape[1] // PIECES
+    pieces = [pl.ds(c * width, width) for c in range(PIECES)]
+    copies = [
+        pltpu.make_async_copy(src, dst, sems.at[i])
+        for i, (src, dst) in enumerate(
+            [(cot_hbm, cot_out), (w_out_hbm, w_out)]
+            + [(w_qkv_hbm.at[:, piece], w_qkv.at[:, piece]) for piece in pieces]
+        )
+    ]
+    for copy in copies[:4]:
+        copy.start()
+    copies[0].wait()
+    copies[1].wait()
+    copies[4].start()
+    copies[5].start()
+    grad_out[...] = mm_nt(cot_out[...], w_out[...]).astype(BF16)
+    for c in range(PIECES):
+        copies[2 + c].wait()
+        if c + 6 < len(copies):
+            copies[c + 6].start()
+        cols = slice(c * width, (c + 1) * width)
         qkv_out[:, cols] = mm(normed[...], w_qkv[:, cols]).astype(BF16)
-    for copy in copies[3:]:
-        copy.wait()
-    cots = jnp.concatenate([cot_out[...], chip[-EARLY:], off[-EARLY:]], 0)
-    grads = mm_nt(cots, w_out[...]).astype(BF16)
-    grad_out[...] = grads[:m]
-    near_out[...] = grads[m:]
 
 
 def halves(rows, scale=None):
@@ -338,7 +336,7 @@
     own_qkv,
     own_grad,
     window_hbm,
-    message_out,
+    stats_out,
     kv,
     weights_out,
     scores_out,
@@ -348,8 +346,6 @@
     fetch = start_all([(window_hbm, window)], sems)
     m, channels = chip_normed.shape
     pairs = channels // pair
-    rows = message_out.shape[0] - (m - EARLY)
-    message_out[rows:] = own_grad[EARLY:]
     devices = lax.axis_size("node")
     me = lax.axis_index("node")
     near = mm(jnp.concatenate([chip_normed[...], off_normed[...]], 0), w_qkv[:, channels:])
@@ -386,12 +382,7 @@
         stats = jnp.where(lane == p, top, stats)
         stats = jnp.where(lane == pairs + p, inv_sum, stats)
         stats = jnp.where(lane == 2 * pairs + p, delta, stats)
-    rest = jnp.transpose(stats)[:rows]
-    for part in range(3):
-        piece = rest.astype(BF16)
-        message_out[:rows, part * 2 * m : (part + 1) * 2 * m] = piece
-        rest = rest - piece.astype(F32)
-    message_out[:rows, 6 * m :] = jnp.zeros((rows, channels - 6 * m), BF16)
+    stats_out[...] = jnp.transpose(stats)[: 3 * pairs]
 
 
 def product_kernel(
@@ -433,12 +424,13 @@
 def finish_kernel(
     pair,
     count,
-    chip,
-    off,
+    chip_stats,
+    off_stats,
     chip_first,
     off_first,
     near_q,
-    early_grad,
+    chip_grad,
+    off_grad,
     own_qkv,
     grad_key,
     grad_value,
@@ -450,7 +442,6 @@
     grad_kv,
 ):
     m, channels = latent.shape
-    rows = chip.shape[0] - (m - EARLY)
     reach = [meta_of(side, count)[:8, 2 * LANES : 2 * LANES + m] for side in (chip_first, off_first)]
     reach = jnp.concatenate(reach, 1)
     key_at = iota((m, 2 * m), 0) + m
@@ -461,10 +452,6 @@
     bias = jnp.where(keep, 0.0, -jnp.inf).astype(F32)
     pairs = channels // pair
 
-    def whole(side):
-        return sum(side[:rows, k * 2 * m : (k + 1) * 2 * m].astype(F32) for k in (2, 1, 0))
-
-    chip_stats, off_stats = whole(chip), whole(off)
     stats = []
     for h in range(2):
         lanes = slice(h * m, (h + 1) * m)
@@ -474,9 +461,7 @@
         key2 = halves(own_qkv[:, channels + p * pair : channels + (p + 1) * pair])
         value2 = halves(own_qkv[:, 2 * channels + p * pair : 2 * channels + (p + 1) * pair])
         query = near_q[:, cols]
-        grad = jnp.concatenate(
-            [early_grad[:EARLY, cols], chip[rows:, cols], early_grad[EARLY:, cols], off[rows:, cols]], 0
-        )
+        grad = jnp.concatenate([chip_grad[:, cols], off_grad[:, cols]], 0)
         scores = mm_nt(key2, query)
         grad_prob = mm_nt(value2, grad)
         weights, grad_scores = [], []
@@ -532,22 +517,20 @@
     own_src, own_dst = own_src.reshape(-1, LANES), own_dst.reshape(-1, LANES)
     far_src, far_dst = far_src.reshape(1, -1), far_dst.reshape(1, -1)
     side_count, far_count = side_count.reshape(1, -1), far_count.reshape(1, -1)
-    message = ((BAND + meta_rows + EARLY, channels), BF16)
+    message = ((BAND + meta_rows, channels), BF16)
     far_block = (2 * far_slots, channels // 2 + LANES)
     far_message, chip_message, off_message, w_edge = call(
         pack_kernel,
         [(far_block, BF16), message, message, (w_edge.shape, BF16)],
-        [grid_in, cotangent, window, side_src, side_dst, side_count, far_src, far_dst, far_count]
-        + [w_edge],
-        hbm=range(10),
+        [grid_in, window, side_src, side_dst, side_count, far_src, far_dst, far_count, w_edge],
+        hbm=range(9),
         hbm_outs=range(3),
-        scratch=like(grid_in, cotangent[:EARLY])
-        + like(window, side_src, side_dst, side_count, far_src, far_dst, far_count)
+        scratch=like(grid_in, window, side_src, side_dst, side_count, far_src, far_dst, far_count)
         + [
             pltpu.VMEM(far_block, BF16),
             pltpu.VMEM((2, meta_rows, channels), BF16),
-            dma(10),
-            dma(7),
+            dma(9),
+            dma(5),
         ],
         name="pack",
     )
@@ -579,32 +562,25 @@
         functools.partial(latent_kernel, far_depth), [rows, rows], [got_far, partial], name="latent"
     )
     chip_normed, off_normed = exchange(normed, normed, "node")
-    own_qkv, w_qkv, w_out, own_cot, own_grad, early_grad = call(
+    own_qkv, w_qkv, w_out, own_cot, own_grad = call(
         project_kernel,
-        [
-            ((m, 3 * channels), BF16),
-            (w_qkv.shape, BF16),
-            (w_out.shape, BF16),
-            rows,
-            rows,
-            ((2 * EARLY, channels), BF16),
-        ],
-        [normed, from_chip, from_off, w_qkv, w_out, cotangent],
-        hbm=(3, 4, 5),
-        scratch=[dma(5)],
+        [((m, 3 * channels), BF16), (w_qkv.shape, BF16), (w_out.shape, BF16), rows, rows],
+        [normed, w_qkv, w_out, cotangent],
+        hbm=(1, 2, 3),
+        scratch=[dma(PIECES + 2)],
         name="project",
     )
-    stat_rows = -(-3 * pairs // 16) * 16
+    chip_grad, off_grad = exchange(own_grad, own_grad, "node")
     probs = ((pairs, 2 * m, 3 * m), BF16)
-    message, kv, weights, grad_scores = call(
+    stats, kv, weights, grad_scores = call(
         functools.partial(attend_kernel, scale, pair),
-        [((stat_rows + m - EARLY, channels), BF16), ((3 * m, 2 * channels), BF16), probs, probs],
+        [((3 * pairs, 2 * m), F32), ((3 * m, 2 * channels), BF16), probs, probs],
         [chip_normed, off_normed, w_qkv, own_qkv, own_grad, window],
         hbm=(5,),
         scratch=like(window) + [dma(1)],
         name="attend",
     )
-    chip_late, off_late = exchange(message, message, "node")
+    chip_stats, off_stats = exchange(stats, stats, "node")
     mesh_out, grad_normed, grad_key, grad_value, near_q = call(
         functools.partial(product_kernel, scale, pair),
         [
@@ -633,12 +609,13 @@
         functools.partial(finish_kernel, pair, meta_rows),
         [rows],
         [
-            chip_late,
-            off_late,
+            chip_stats,
+            off_stats,
             from_chip,
             from_off,
             near_q,
-            early_grad,
+            chip_grad,
+            off_grad,
             own_qkv,
             grad_key,
             grad_value,

time: 50.3 us -> 52.8 us (1.050)
  starting transfers between devices: 19 us -> 22.6 us
  Pallas kernels: 25.1 us -> 24.5 us
    all_to_all x1, starting transfers between devices: 5.33 us -> 7.36 us  [body(): lax.all_to_all(far_message.reshape(devices, 2 * far_depth, far_block[1]),...]
    ppermute x3 -> x4, starting transfers between devices: 13.4 us -> 14.9 us  [exchange(): lax.ppermute(off_message, axis, [p for i in range(1, n - 1, 2) for p in (...]
    pallas_call x8, Pallas kernels: 25.1 us -> 24.5 us  [call(): pl.pallas_call(kernel, out_shape=[(pltpu.HBM if i in hbm_outs else jax.Sh...]
    ppermute x3 -> x4, waiting for transfers between devices: 4.56 us -> 4.45 us  [exchange(): lax.ppermute(off_message, axis, [p for i in range(1, n - 1, 2) for p in (...]
  transfers between devices with their start and end apart: 7 -> 9, of which waited for: 2 -> 1; matrix products, arithmetic and copies ran while one was open for 0% -> 0% of each run, Pallas kernels for 24% -> 31%
where the time goes in v7:
time: 52.8 us; the launch traced here: 52.4 us
  Pallas kernels  24.5 us (46%)
  starting transfers between devices  22.6 us (43%)
  waiting for transfers between devices  4.46 us (8%)
  between operations  0.78 us (1%)
    pallas_call x8, Pallas kernels, call(): pl.pallas_call(kernel, out_shape=[(pltpu.HBM if i in hbm_outs else jax.Sh...  24.5 us
    ppermute x4, starting transfers between devices, exchange(): lax.ppermute(off_message, axis, [p for i in range(1, n - 1, 2) for p in (...  14.9 us
    all_to_all x1, starting transfers between devices, body(): lax.all_to_all(far_message.reshape(devices, 2 * far_depth, far_block[1]),...  7.36 us
    ppermute x4, waiting for transfers between devices, exchange(): lax.ppermute(off_message, axis, [p for i in range(1, n - 1, 2) for p in (...  4.45 us
  transfers between devices with their start and end apart: 9, of which 1 were waited for; matrix products, arithmetic and copies ran while one was open for 0% of the time, Pallas kernels for 31%

profile of v7, /device:TPU:1, one launch (start us, length us, event | category | flops | bytes accessed | tf_op | source)
XLA Modules:
  0.0 52.4 jit_solution(9768018803327901354)
XLA Ops:
  0.6 3.4 %pack.1 = (bf16[128,640]{1,0:T(8,128)(2,1)}, bf16[144,1024]{1,0:T(8,128)(2,1)}, bf16[144,1024]{1,0:T(8,128)(2,1)}, bf16[1024,1024]{1,0:T(8,128)(2,1)S(1)}) custom-call(bf16[512,1024]{1,0:T(8,128)(2,1)} %grid_hbm.3, s32[2,128]{1,0:T(2,128)} %window_hbm.3, s32[32,128]{1,0:T(8,128)} %bitcast.12, s32[32,128]{1,0:T(8,128)} %bitcast.13, s32[1,2]{1,0:T(1,128)} %bitcast.16, ...), custom_call_target="tpu_custom_call" | custom-call | tf_op jit(solution)/shard_map/pack/pallas_call | solution.py:47
  4.0 7.4 %all-to-all-start = ((bf16[16,8,640]{2,1,0:T(8,128)(2,1)}), bf16[16,8,640]{2,1,0:T(8,128)(2,1)S(1)}, u32[]{:S(2)}, u32[]{:S(2)}) async-start(bf16[16,8,640]{2,1,0:T(8,128)(2,1)} %bitcast.11), calls=%async_computation | async-start | bytes 327680 | tf_op jit(solution)/shard_map/all_to_all | solution.py:538
  11.4 0.2 collective-permute-start
  11.5 3.5 %collective-permute-start.1 = (bf16[144,1024]{1,0:T(8,128)(2,1)}, bf16[144,1024]{1,0:T(8,128)(2,1)S(1)}, u32[]{:S(2)}, u32[]{:S(2)}) collective-permute-start(bf16[144,1024]{1,0:T(8,128)(2,1)} %get-tuple-element.24), channel_id=1, source_target_pairs={{1,2},{2,1},{3,4},{4,3},{5,6},{6,5},{7,8},{8,7},{9,10},{10,9},{11,... | collective-permute-start | bytes 884744 | tf_op jit(solution)/shard_map/ppermute | solution.py:78
  15.0 3.1 %own.1.partial = f32[128,1024]{1,0:T(8,128)S(1)} custom-call(bf16[512,1024]{1,0:T(8,128)(2,1)} %grid_hbm.3, bf16[128,1024]{1,0:T(8,128)(2,1)} %mesh_in_hbm.1, s32[8,128]{1,0:T(8,128)} %bitcast.14, s32[8,128]{1,0:T(8,128)} %bitcast.15, bf16[1024,1024]{1,0:T(8,128)(2,1)S(1)} %get-tuple-element.25.w_edge), custom_call_target="tpu_custom_call" | custom-call | tf_op jit(solution)/shard_map/own/pallas_call | solution.py:47
  18.1 0.0 collective-permute-done.chip.chip_first
  18.1 4.4 %collective-permute-done.1.off.off_first = bf16[144,1024]{1,0:T(8,128)(2,1)S(1)} collective-permute-done((bf16[144,1024]{1,0:T(8,128)(2,1)}, bf16[144,1024]{1,0:T(8,128)(2,1)S(1)}, u32[]{:S(2)}, u32[]{:S(2)}) %collective-permute-start.1) | collective-permute-done | bytes 294944 | tf_op jit(solution)/shard_map/ppermute | solution.py:78
  22.6 1.4 %side.1.partial = f32[128,1024]{1,0:T(8,128)S(1)} custom-call(bf16[144,1024]{1,0:T(8,128)(2,1)S(1)} %collective-permute-done.chip.chip_first, bf16[144,1024]{1,0:T(8,128)(2,1)S(1)} %collective-permute-done.1.off.off_first, bf16[1024,1024]{1,0:T(8,128)(2,1)S(1)} %get-tuple-element.25.w_edge, f32[128,1024]{1,0:T(8,128)S(1)} %own.1.partial), custom_call_target="tpu_custom_call" | custom-call | tf_op jit(solution)/shard_map/side/pallas_call | solution.py:47
  24.0 0.0 all-to-all-done
  24.0 0.5 latent.1
  24.5 0.1 collective-permute-start.2
  24.6 4.3 %collective-permute-start.3 = (bf16[128,1024]{1,0:T(8,128)(2,1)S(1)}, bf16[128,1024]{1,0:T(8,128)(2,1)S(1)}, u32[]{:S(2)}, u32[]{:S(2)}) collective-permute-start(bf16[128,1024]{1,0:T(8,128)(2,1)S(1)} %get-tuple-element.26.normed), channel_id=1, source_target_pairs={{1,2},{2,1},{3,4},{4,3},{5,6},{6,5},{7,8},{8,7},{9,10},{10,9},{11,... | collective-permute-start | bytes 786440 | tf_op jit(solution)/shard_map/ppermute | solution.py:78
  28.9 4.6 %project.1 = (bf16[128,3072]{1,0:T(8,128)(2,1)S(1)}, bf16[1024,3072]{1,0:T(8,128)(2,1)S(1)}, bf16[1024,1024]{1,0:T(8,128)(2,1)S(1)}, bf16[128,1024]{1,0:T(8,128)(2,1)S(1)}, bf16[128,1024]{1,0:T(8,128)(2,1)S(1)}) custom-call(bf16[128,1024]{1,0:T(8,128)(2,1)S(1)} %get-tuple-element.26.normed, bf16[1024,3072]{1,0:T(8,128)(2,1)} %w_qkv_hbm.1, ...), custom_call_target="tpu_custom_call" | custom-call | tf_op jit(solution)/shard_map/project/pallas_call | solution.py:47
  33.5 0.1 collective-permute-start.6
  33.6 3.6 %collective-permute-start.7 = (bf16[128,1024]{1,0:T(8,128)(2,1)S(1)}, bf16[128,1024]{1,0:T(8,128)(2,1)S(1)}, u32[]{:S(2)}, u32[]{:S(2)}) collective-permute-start(bf16[128,1024]{1,0:T(8,128)(2,1)S(1)} %get-tuple-element.29.own_grad), channel_id=1, source_target_pairs={{1,2},{2,1},{3,4},{4,3},{5,6},{6,5},{7,8},{8,7},{9,10},{10,9},{11,... | collective-permute-start | bytes 786440 | tf_op jit(solution)/shard_map/ppermute | solution.py:78
  37.2 0.0 collective-permute-done.2.chip_normed
  37.2 0.0 collective-permute-done.3.off_normed
  37.2 4.0 %attend.1 = (f32[24,256]{1,0:T(8,128)S(1)}, bf16[384,2048]{1,0:T(8,128)(2,1)S(1)}, bf16[8,256,384]{2,1,0:T(8,128)(2,1)S(1)}, bf16[8,256,384]{2,1,0:T(8,128)(2,1)S(1)}) custom-call(bf16[128,1024]{1,0:T(8,128)(2,1)S(1)} %collective-permute-done.2.chip_normed, bf16[128,1024]{1,0:T(8,128)(2,1)S(1)} %collective-permute-done.3.off_normed, ...), custom_call_target="tpu_custom_call" | custom-call | tf_op jit(solution)/shard_map/attend/pallas_call | solution.py:47
  41.3 0.1 collective-permute-start.4
  41.4 3.5 %collective-permute-start.5 = (f32[24,256]{1,0:T(8,128)S(1)}, f32[24,256]{1,0:T(8,128)S(1)}, u32[]{:S(2)}, u32[]{:S(2)}) collective-permute-start(f32[24,256]{1,0:T(8,128)S(1)} %get-tuple-element.36), channel_id=1, source_target_pairs={{1,2},{2,1},{3,4},{4,3},{5,6},{6,5},{7,8},{8,7},{9,10},{10,9},{11,... | collective-permute-start | bytes 73736 | tf_op jit(solution)/shard_map/ppermute | solution.py:78
  44.9 3.3 %product.1 = (bf16[128,1024]{1,0:T(8,128)(2,1)}, f32[128,1024]{1,0:T(8,128)S(1)}, f32[128,1024]{1,0:T(8,128)S(1)}, f32[128,1024]{1,0:T(8,128)S(1)}, bf16[256,1024]{1,0:T(8,128)(2,1)S(1)}) custom-call(bf16[8,256,384]{2,1,0:T(8,128)(2,1)S(1)} %get-tuple-element.30.weights, bf16[8,256,384]{2,1,0:T(8,128)(2,1)S(1)} %get-tuple-element.31.grad_scores, ...), custom_call_target="tpu_custom_call" | custom-call | tf_op jit(solution)/shard_map/product/pallas_call | solution.py:47
  48.1 0.0 collective-permute-done.6.chip_grad
  48.1 0.0 collective-permute-done.7.off_grad
  48.1 0.0 collective-permute-done.4.chip_stats
  48.1 0.0 collective-permute-done.5.off_stats
  48.1 4.3 %finish.1 = bf16[128,1024]{1,0:T(8,128)(2,1)} custom-call(f32[24,256]{1,0:T(8,128)S(1)} %collective-permute-done.4.chip_stats, f32[24,256]{1,0:T(8,128)S(1)} %collective-permute-done.5.off_stats, bf16[144,1024]{1,0:T(8,128)(2,1)S(1)} %collective-permute-done.chip.chip_first, bf16[144,1024]{1,0:T(8,128)(2,1)S(1)} %collective-permute-done.1.off.off_first, ...), custom_call_target="tpu_custom_call" | custom-call | tf_op jit(solution)/shard_map/finish/pallas_call | solution.py:47
Async XLA Ops:
  4.0 20.0 %all-to-all-start = ((bf16[16,8,640]{2,1,0:T(8,128)(2,1)}), bf16[16,8,640]{2,1,0:T(8,128)(2,1)S(1)}, u32[]{:S(2)}, u32[]{:S(2)}) async-start(bf16[16,8,640]{2,1,0:T(8,128)(2,1)} %bitcast.11), calls=%async_computation | async-start | bytes 327680 | tf_op jit(solution)/shard_map/all_to_all | solution.py:538
  11.4 6.8 %collective-permute-start = (bf16[144,1024]{1,0:T(8,128)(2,1)}, bf16[144,1024]{1,0:T(8,128)(2,1)S(1)}, u32[]{:S(2)}, u32[]{:S(2)}) collective-permute-start(bf16[144,1024]{1,0:T(8,128)(2,1)} %get-tuple-element.23), channel_id=1, source_target_pairs={{0,1},{1,0},{2,3},{3,2},{4,5},{5,4},{6,7},{7,6},{8,9},{9,8},{10,11... | collective-permute-start | bytes 884744 | tf_op jit(solution)/shard_map/ppermute | solution.py:81
  11.5 11.0 %collective-permute-start.1 = (bf16[144,1024]{1,0:T(8,128)(2,1)}, bf16[144,1024]{1,0:T(8,128)(2,1)S(1)}, u32[]{:S(2)}, u32[]{:S(2)}) collective-permute-start(bf16[144,1024]{1,0:T(8,128)(2,1)} %get-tuple-element.24), channel_id=1, source_target_pairs={{1,2},{2,1},{3,4},{4,3},{5,6},{6,5},{7,8},{8,7},{9,10},{10,9},{11,... | collective-permute-start | bytes 884744 | tf_op jit(solution)/shard_map/ppermute | solution.py:78
  24.5 12.7 %collective-permute-start.2 = (bf16[128,1024]{1,0:T(8,128)(2,1)S(1)}, bf16[128,1024]{1,0:T(8,128)(2,1)S(1)}, u32[]{:S(2)}, u32[]{:S(2)}) collective-permute-start(bf16[128,1024]{1,0:T(8,128)(2,1)S(1)} %get-tuple-element.26.normed), channel_id=1, source_target_pairs={{0,1},{1,0},{2,3},{3,2},{4,5},{5,4},{6,7},{7,6},{8,9},{9,8},{10,11... | collective-permute-start | bytes 786440 | tf_op jit(solution)/shard_map/ppermute | solution.py:81
  24.6 12.6 %collective-permute-start.3 = (bf16[128,1024]{1,0:T(8,128)(2,1)S(1)}, bf16[128,1024]{1,0:T(8,128)(2,1)S(1)}, u32[]{:S(2)}, u32[]{:S(2)}) collective-permute-start(bf16[128,1024]{1,0:T(8,128)(2,1)S(1)} %get-tuple-element.26.normed), channel_id=1, source_target_pairs={{1,2},{2,1},{3,4},{4,3},{5,6},{6,5},{7,8},{8,7},{9,10},{10,9},{11,... | collective-permute-start | bytes 786440 | tf_op jit(solution)/shard_map/ppermute | solution.py:78
  33.5 14.6 %collective-permute-start.6 = (bf16[128,1024]{1,0:T(8,128)(2,1)S(1)}, bf16[128,1024]{1,0:T(8,128)(2,1)S(1)}, u32[]{:S(2)}, u32[]{:S(2)}) collective-permute-start(bf16[128,1024]{1,0:T(8,128)(2,1)S(1)} %get-tuple-element.29.own_grad), channel_id=1, source_target_pairs={{0,1},{1,0},{2,3},{3,2},{4,5},{5,4},{6,7},{7,6},{8,9},{9,8},{10,11... | collective-permute-start | bytes 786440 | tf_op jit(solution)/shard_map/ppermute | solution.py:81
  33.6 14.5 %collective-permute-start.7 = (bf16[128,1024]{1,0:T(8,128)(2,1)S(1)}, bf16[128,1024]{1,0:T(8,128)(2,1)S(1)}, u32[]{:S(2)}, u32[]{:S(2)}) collective-permute-start(bf16[128,1024]{1,0:T(8,128)(2,1)S(1)} %get-tuple-element.29.own_grad), channel_id=1, source_target_pairs={{1,2},{2,1},{3,4},{4,3},{5,6},{6,5},{7,8},{8,7},{9,10},{10,9},{11,... | collective-permute-start | bytes 786440 | tf_op jit(solution)/shard_map/ppermute | solution.py:78
  41.3 6.8 %collective-permute-start.4 = (f32[24,256]{1,0:T(8,128)S(1)}, f32[24,256]{1,0:T(8,128)S(1)}, u32[]{:S(2)}, u32[]{:S(2)}) collective-permute-start(f32[24,256]{1,0:T(8,128)S(1)} %get-tuple-element.36), channel_id=1, source_target_pairs={{0,1},{1,0},{2,3},{3,2},{4,5},{5,4},{6,7},{7,6},{8,9},{9,8},{10,11... | collective-permute-start | bytes 73736 | tf_op jit(solution)/shard_map/ppermute | solution.py:81
  41.4 6.8 %collective-permute-start.5 = (f32[24,256]{1,0:T(8,128)S(1)}, f32[24,256]{1,0:T(8,128)S(1)}, u32[]{:S(2)}, u32[]{:S(2)}) collective-permute-start(f32[24,256]{1,0:T(8,128)S(1)} %get-tuple-element.36), channel_id=1, source_target_pairs={{1,2},{2,1},{3,4},{4,3},{5,6},{6,5},{7,8},{8,7},{9,10},{10,9},{11,... | collective-permute-start | bytes 73736 | tf_op jit(solution)/shard_map/ppermute | solution.py:78

commit v8 on v7

--- a/solution.py
+++ b/solution.py
@@ -33,15 +33,18 @@
     return lax.broadcasted_iota(I32, shape, dim)
 
 
-def call(kernel, outs, args, hbm=(), hbm_outs=(), scratch=(), name=None):
+def call(kernel, outs, args, hbm=(), hbm_outs=(), anywhere=(), scratch=(), name=None):
     args = [
         pltpu.with_memory_space_constraint(a, pltpu.HBM) if i in hbm else a
         for i, a in enumerate(args)
     ]
 
-    def specs(count, far):
+    def specs(count, far, free=()):
         return [
-            pl.BlockSpec(memory_space=pltpu.HBM if i in far else pltpu.VMEM) for i in range(count)
+            pl.BlockSpec(
+                memory_space=pltpu.HBM if i in far else pl.ANY if i in free else pltpu.VMEM
+            )
+            for i in range(count)
         ]
 
     return pl.pallas_call(
@@ -50,7 +53,7 @@
             (pltpu.HBM if i in hbm_outs else jax.ShapeDtypeStruct)(shape, dtype)
             for i, (shape, dtype) in enumerate(outs)
         ],
-        in_specs=specs(len(args), hbm),
+        in_specs=specs(len(args), hbm, anywhere),
         out_specs=specs(len(outs), hbm_outs),
         scratch_shapes=list(scratch),
         compiler_params=pltpu.CompilerParams(vmem_limit_bytes=VMEM_LIMIT),
@@ -111,38 +114,25 @@
     return centred * inv_std, inv_std
 
 
-def pack_kernel(
+def band_kernel(
     grid_hbm,
     window_hbm,
     side_src_hbm,
     side_dst_hbm,
     side_count_hbm,
-    far_src_hbm,
-    far_dst_hbm,
-    far_count_hbm,
-    w_edge_hbm,
-    far_out,
     chip_out,
     off_out,
-    w_edge,
-    grid,
+    bands,
     window,
     side_src,
     side_dst,
     side_count,
-    far_src,
-    far_dst,
-    far_count,
-    far,
     meta,
     sems,
     out_sems,
 ):
-    grid_rows, channels = grid.shape
+    grid_rows, channels = grid_hbm.shape
     mesh_rows = window.shape[1]
-    slots = far_src.shape[1]
-    devices = far_count.shape[1]
-    depth = slots // devices
     first = grid_rows - BAND
     count = side_src.shape[0] // 2
     copies = start_all(
@@ -151,11 +141,8 @@
             (side_dst_hbm, side_dst),
             (side_count_hbm, side_count),
             (window_hbm, window),
-            (grid_hbm, grid),
-            (far_src_hbm, far_src),
-            (far_dst_hbm, far_dst),
-            (far_count_hbm, far_count),
-            (w_edge_hbm, w_edge),
+            (grid_hbm.at[pl.ds(0, BAND)], bands.at[0]),
+            (grid_hbm.at[pl.ds(first, BAND)], bands.at[1]),
         ],
         sems,
     )
@@ -169,20 +156,57 @@
         reach = jnp.concatenate([window[...], jnp.zeros((count - 2, mesh_rows), I32)], 0)
         blank = jnp.zeros((count, channels - 2 * LANES - mesh_rows), I32)
         meta[k] = jnp.concatenate([src, dst, reach, blank], 1).astype(F32).astype(BF16)
-    copies[4].wait()
+    for copy in copies[4:]:
+        copy.wait()
     odd = is_odd()
     outs = start_all(
         [
             pair
             for k, out in ((1 - odd, chip_out), (odd, off_out))
             for pair in (
-                (grid.at[pl.ds(pl.multiple_of(k * first, BAND), BAND)], out.at[pl.ds(0, BAND)]),
+                (bands.at[k], out.at[pl.ds(0, BAND)]),
                 (meta.at[k], out.at[pl.ds(BAND, count)]),
             )
         ],
         out_sems,
     )
-    for copy in copies[5:8]:
+    for copy in outs:
+        copy.wait()
+
+
+def far_kernel(
+    mesh_rows,
+    grid_hbm,
+    far_src_hbm,
+    far_dst_hbm,
+    far_count_hbm,
+    w_edge_hbm,
+    chip_message,
+    far_out,
+    w_edge,
+    grid,
+    far_src,
+    far_dst,
+    far_count,
+    far,
+    sems,
+    out_sems,
+):
+    grid_rows, channels = grid.shape
+    slots = far_src.shape[1]
+    devices = far_count.shape[1]
+    depth = slots // devices
+    copies = start_all(
+        [
+            (far_src_hbm, far_src),
+            (far_dst_hbm, far_dst),
+            (far_count_hbm, far_count),
+            (grid_hbm, grid),
+            (w_edge_hbm, w_edge),
+        ],
+        sems,
+    )
+    for copy in copies[:3]:
         copy.wait()
     slot = iota((1, slots), 1)
     receiver = jnp.where(iota((devices, slots), 0) == iota((devices, slots), 1) // depth, 1.0, 0.0)
@@ -193,17 +217,17 @@
     source = jnp.sum(jnp.where(mine, far_src[...].astype(F32), 0.0), 1, keepdims=True)
     column = jnp.sum(jnp.where(mine, target, 0.0), 1, keepdims=True)
     pick = jnp.where(iota((2 * slots, grid_rows), 1).astype(F32) == source, 1.0, 0.0).astype(BF16)
+    half = channels // 2
+    far[:, half:] = jnp.broadcast_to(column, (2 * slots, LANES)).astype(BF16)
+    copies[3].wait()
     rows = mm(pick, grid[...]).astype(BF16)
-    copies[8].wait()
+    copies[4].wait()
     rows = gelu(mm(rows, w_edge[...]))
-    half = channels // 2
     is_first = iota((2 * slots, half), 0) % (2 * depth) < depth
     far[:, :half] = jnp.where(is_first, rows[:, :half], rows[:, half:])
-    far[:, half:] = jnp.broadcast_to(column, (2 * slots, LANES)).astype(BF16)
-    last = pltpu.make_async_copy(far, far_out, out_sems.at[4])
+    last = pltpu.make_async_copy(far, far_out, out_sems.at[0])
     last.start()
-    for copy in outs + [last]:
-        copy.wait()
+    last.wait()
 
 
 def own_kernel(
@@ -211,12 +235,17 @@
     mesh_in_hbm,
     own_src_hbm,
     own_dst_hbm,
+    cot_hbm,
+    w_out_hbm,
     w_edge,
     partial_out,
+    grad_out,
     grid,
     mesh_in,
     own_src,
     own_dst,
+    cot,
+    w_out,
     sems,
 ):
     grid_rows = grid.shape[0]
@@ -227,6 +256,8 @@
             (own_dst_hbm, own_dst),
             (grid_hbm, grid),
             (mesh_in_hbm, mesh_in),
+            (cot_hbm, cot),
+            (w_out_hbm, w_out),
         ],
         sems,
     )
@@ -236,10 +267,13 @@
     src = onehot_rows([own_src[r : r + 1] for r in range(rows)], grid_rows)
     dst = onehot_rows([own_dst[r : r + 1] for r in range(rows)], mesh_rows)
     counts = mm_nt(dst, src).astype(BF16)
-    for copy in copies[2:]:
+    for copy in copies[2:4]:
         copy.wait()
     active = gelu(mm(grid[...], w_edge[...]))
     partial_out[...] = mesh_in[...].astype(F32) + mm(counts, active)
+    for copy in copies[4:]:
+        copy.wait()
+    grad_out[...] = mm_nt(cot[...], w_out[...]).astype(BF16)
 
 
 def meta_of(message, count):
@@ -281,29 +315,13 @@
     normed_out[...] = normal.astype(BF16)
 
 
-def project_kernel(
-    normed, w_qkv_hbm, w_out_hbm, cot_hbm, qkv_out, w_qkv, w_out, cot_out, grad_out, sems
-):
+def project_kernel(normed, own_grad, w_qkv_hbm, qkv_out, w_qkv, grad_out, sems):
+    grad_out[...] = own_grad[...]
     width = w_qkv.shape[1] // PIECES
     pieces = [pl.ds(c * width, width) for c in range(PIECES)]
-    copies = [
-        pltpu.make_async_copy(src, dst, sems.at[i])
-        for i, (src, dst) in enumerate(
-            [(cot_hbm, cot_out), (w_out_hbm, w_out)]
-            + [(w_qkv_hbm.at[:, piece], w_qkv.at[:, piece]) for piece in pieces]
-        )
-    ]
-    for copy in copies[:4]:
-        copy.start()
-    copies[0].wait()
-    copies[1].wait()
-    copies[4].start()
-    copies[5].start()
-    grad_out[...] = mm_nt(cot_out[...], w_out[...]).astype(BF16)
+    copies = start_all([(w_qkv_hbm.at[:, piece], w_qkv.at[:, piece]) for piece in pieces], sems)
     for c in range(PIECES):
-        copies[2 + c].wait()
-        if c + 6 < len(copies):
-            copies[c + 6].start()
+        copies[c].wait()
         cols = slice(c * width, (c + 1) * width)
         qkv_out[:, cols] = mm(normed[...], w_qkv[:, cols]).astype(BF16)
 
@@ -394,7 +412,7 @@
     own_qkv,
     own_grad,
     latent,
-    w_out,
+    w_out_hbm,
     w_qkv,
     chip_normed,
     off_normed,
@@ -405,7 +423,10 @@
     near_q_out,
     attention,
     grad_query,
+    w_out,
+    sems,
 ):
+    fetch = start_all([(w_out_hbm, w_out)], sems)
     m, channels = latent.shape
     for p in range(channels // pair):
         cols = slice(p * pair, (p + 1) * pair)
@@ -415,10 +436,11 @@
         grad_query[:, cols] = (merge(mm(grad_scores[p], key)) * scale).astype(BF16)
         grad_key[:, cols] = mm_tn(grad_scores[p, :, m : 2 * m], halves(own_qkv[:, cols], scale))
         grad_value[:, cols] = mm_tn(weights[p, :, m : 2 * m], halves(own_grad[:, cols]))
-    mesh_out[...] = (latent[...].astype(F32) + mm(attention[...], w_out[...])).astype(BF16)
-    grad_normed[...] = mm_nt(grad_query[...], w_qkv[:, :channels])
     near = mm(jnp.concatenate([chip_normed[...], off_normed[...]], 0), w_qkv[:, :channels])
     near_q_out[...] = near.astype(BF16) * jnp.asarray(scale, BF16)
+    grad_normed[...] = mm_nt(grad_query[...], w_qkv[:, :channels])
+    fetch[0].wait()
+    mesh_out[...] = (latent[...].astype(F32) + mm(attention[...], w_out[...])).astype(BF16)
 
 
 def finish_kernel(
@@ -437,10 +459,13 @@
     grad_normed,
     w_qkv,
     latent,
-    cot,
+    cot_hbm,
     grad_out,
     grad_kv,
+    cot,
+    sems,
 ):
+    fetch = start_all([(cot_hbm, cot)], sems)
     m, channels = latent.shape
     reach = [meta_of(side, count)[:8, 2 * LANES : 2 * LANES + m] for side in (chip_first, off_first)]
     reach = jnp.concatenate(reach, 1)
@@ -482,6 +507,7 @@
         - jnp.mean(total, -1, keepdims=True)
         - normal * jnp.mean(total * normal, -1, keepdims=True)
     )
+    fetch[0].wait()
     grad_out[...] = (cot[...].astype(F32) + inv_std * centred).astype(BF16)
 
 
@@ -519,22 +545,29 @@
     side_count, far_count = side_count.reshape(1, -1), far_count.reshape(1, -1)
     message = ((BAND + meta_rows, channels), BF16)
     far_block = (2 * far_slots, channels // 2 + LANES)
-    far_message, chip_message, off_message, w_edge = call(
-        pack_kernel,
-        [(far_block, BF16), message, message, (w_edge.shape, BF16)],
-        [grid_in, window, side_src, side_dst, side_count, far_src, far_dst, far_count, w_edge],
-        hbm=range(9),
-        hbm_outs=range(3),
-        scratch=like(grid_in, window, side_src, side_dst, side_count, far_src, far_dst, far_count)
-        + [
-            pltpu.VMEM(far_block, BF16),
-            pltpu.VMEM((2, meta_rows, channels), BF16),
-            dma(9),
-            dma(5),
-        ],
-        name="pack",
+    chip_message, off_message = call(
+        band_kernel,
+        [message, message],
+        [grid_in, window, side_src, side_dst, side_count],
+        hbm=range(5),
+        hbm_outs=range(2),
+        scratch=[pltpu.VMEM((2, BAND, channels), BF16)]
+        + like(window, side_src, side_dst, side_count)
+        + [pltpu.VMEM((2, meta_rows, channels), BF16), dma(6), dma(4)],
+        name="bands",
     )
     from_chip, from_off = exchange(chip_message, off_message, "node")
+    far_message, w_edge = call(
+        functools.partial(far_kernel, m),
+        [(far_block, BF16), (w_edge.shape, BF16)],
+        [grid_in, far_src, far_dst, far_count, w_edge, from_chip],
+        hbm=range(5),
+        anywhere=(5,),
+        hbm_outs=(0,),
+        scratch=like(grid_in, far_src, far_dst, far_count)
+        + [pltpu.VMEM(far_block, BF16), dma(5), dma(1)],
+        name="far",
+    )
     got_far = lax.all_to_all(
         far_message.reshape(devices, 2 * far_depth, far_block[1]),
         "node",
@@ -544,12 +577,12 @@
     ).reshape(far_block)
 
     rows = ((m, channels), BF16)
-    (partial,) = call(
+    partial, own_grad = call(
         own_kernel,
-        [((m, channels), F32)],
-        [grid_in, mesh_in, own_src, own_dst, w_edge],
-        hbm=range(4),
-        scratch=like(grid_in, mesh_in, own_src, own_dst) + [dma(4)],
+        [((m, channels), F32), rows],
+        [grid_in, mesh_in, own_src, own_dst, cotangent, w_out, w_edge],
+        hbm=range(6),
+        scratch=like(grid_in, mesh_in, own_src, own_dst, cotangent, w_out) + [dma(6)],
         name="own",
     )
     (partial,) = call(
@@ -562,12 +595,12 @@
         functools.partial(latent_kernel, far_depth), [rows, rows], [got_far, partial], name="latent"
     )
     chip_normed, off_normed = exchange(normed, normed, "node")
-    own_qkv, w_qkv, w_out, own_cot, own_grad = call(
+    own_qkv, w_qkv, own_grad = call(
         project_kernel,
-        [((m, 3 * channels), BF16), (w_qkv.shape, BF16), (w_out.shape, BF16), rows, rows],
-        [normed, w_qkv, w_out, cotangent],
-        hbm=(1, 2, 3),
-        scratch=[dma(PIECES + 2)],
+        [((m, 3 * channels), BF16), (w_qkv.shape, BF16), rows],
+        [normed, own_grad, w_qkv],
+        hbm=(2,),
+        scratch=[dma(PIECES)],
         name="project",
     )
     chip_grad, off_grad = exchange(own_grad, own_grad, "node")
@@ -602,7 +635,8 @@
             chip_normed,
             off_normed,
         ],
-        scratch=[pltpu.VMEM((m, channels), BF16)] * 2,
+        hbm=(6,),
+        scratch=[pltpu.VMEM((m, channels), BF16)] * 2 + like(w_out) + [dma(1)],
         name="product",
     )
     (mesh_grad,) = call(
@@ -622,9 +656,10 @@
             grad_normed,
             w_qkv,
             latent,
-            own_cot,
-        ],
-        scratch=[pltpu.VMEM((m, 2 * channels), BF16)],
+            cotangent,
+        ],
+        hbm=(13,),
+        scratch=[pltpu.VMEM((m, 2 * channels), BF16)] + like(cotangent) + [dma(1)],
         name="finish",
     )
     return (mesh_out, mesh_grad)

time: 52.8 us -> 58.7 us (1.11)
  Pallas kernels: 24.5 us -> 28.4 us
  local copies, waits for them, and re-layouts: 0 us -> 1.65 us
    pallas_call x8 -> x9, Pallas kernels: 24.5 us -> 28.4 us  [call(): pl.pallas_call(kernel, out_shape=[(pltpu.HBM if i in hbm_outs else jax.Sh...]
    ppermute x4, waiting for transfers between devices: 4.45 us -> 2.63 us  [exchange(): lax.ppermute(off_message, axis, [p for i in range(1, n - 1, 2) for p in (...]
    ppermute x4, waiting for transfers between devices: 0.01 us -> 1.74 us  [exchange(): lax.ppermute(chip_message, axis, [p for i in range(0, n, 2) for p in ((i,...]
    unnamed x0 -> x6, local copies, waits for them, and re-layouts: none -> 1.65 us
  transfers between devices with their start and end apart: 9 -> 9, of which waited for: 1 -> 2; matrix products, arithmetic and copies ran while one was open for 0% -> 0% of each run, Pallas kernels for 31% -> 30%
where the time goes in v8:
time: 58.7 us; the launch traced here: 58.3 us
  Pallas kernels  28.4 us (48%)
  starting transfers between devices  22.8 us (39%)
  waiting for transfers between devices  4.38 us (7%)
  local copies, waits for them, and re-layouts  1.65 us (3%)
  between operations  0.99 us (2%)
    pallas_call x9, Pallas kernels, call(): pl.pallas_call(kernel, out_shape=[(pltpu.HBM if i in hbm_outs else jax.Sh...  28.4 us
    ppermute x4, starting transfers between devices, exchange(): lax.ppermute(off_message, axis, [p for i in range(1, n - 1, 2) for p in (...  15.1 us
    all_to_all x1, starting transfers between devices, body(): lax.all_to_all(far_message.reshape(devices, 2 * far_depth, far_block[1]),...  7.36 us
    ppermute x4, waiting for transfers between devices, exchange(): lax.ppermute(off_message, axis, [p for i in range(1, n - 1, 2) for p in (...  2.63 us
    ppermute x4, waiting for transfers between devices, exchange(): lax.ppermute(chip_message, axis, [p for i in range(0, n, 2) for p in ((i,...  1.74 us
    unnamed x6, local copies, waits for them, and re-layouts  1.65 us
  transfers between devices with their start and end apart: 9, of which 2 were waited for; matrix products, arithmetic and copies ran while one was open for 0% of the time, Pallas kernels for 30%

profile of v8, /device:TPU:1, one launch (start us, length us, event | category | flops | bytes accessed | tf_op | source)
XLA Modules:
  0.0 58.3 jit_solution(1865060739880518572)
XLA Ops:
  0.6 2.0 %bands.1 = (bf16[144,1024]{1,0:T(8,128)(2,1)}, bf16[144,1024]{1,0:T(8,128)(2,1)}) custom-call(bf16[512,1024]{1,0:T(8,128)(2,1)} %grid_hbm.5, s32[2,128]{1,0:T(2,128)} %window_hbm.3, s32[32,128]{1,0:T(8,128)} %bitcast.12, s32[32,128]{1,0:T(8,128)} %bitcast.13, s32[1,2]{1,0:T(1,128)} %bitcast.16), custom_call_target="tpu_custom_call" | custom-call | tf_op jit(solution)/shard_map/bands/pallas_call | solution.py:50
  2.6 0.0 copy-start.2
  2.7 0.1 collective-permute-start
  2.8 1.7 %collective-permute-done.chip_message.chip.chip_first = bf16[144,1024]{1,0:T(8,128)(2,1)S(1)} collective-permute-done((bf16[144,1024]{1,0:T(8,128)(2,1)}, bf16[144,1024]{1,0:T(8,128)(2,1)S(1)}, u32[]{:S(2)}, u32[]{:S(2)}) %collective-permute-start) | collective-permute-done | bytes 294944 | tf_op jit(solution)/shard_map/ppermute | solution.py:84
  4.5 3.2 %far.1 = (bf16[128,640]{1,0:T(8,128)(2,1)}, bf16[1024,1024]{1,0:T(8,128)(2,1)S(1)}) custom-call(bf16[512,1024]{1,0:T(8,128)(2,1)} %grid_hbm.5, s32[1,64]{1,0:T(1,128)} %bitcast.17, s32[1,64]{1,0:T(1,128)} %bitcast.18, s32[1,16]{1,0:T(1,128)} %bitcast.19, bf16[1024,1024]{1,0:T(8,128)(2,1)} %w_edge_hbm.1, ...), custom_call_target="tpu_custom_call" | custom-call | tf_op jit(solution)/shard_map/far/pallas_call | solution.py:50
  7.7 7.4 %all-to-all-start = ((bf16[16,8,640]{2,1,0:T(8,128)(2,1)}), bf16[16,8,640]{2,1,0:T(8,128)(2,1)S(1)}, u32[]{:S(2)}, u32[]{:S(2)}) async-start(bf16[16,8,640]{2,1,0:T(8,128)(2,1)} %bitcast.11), calls=%async_computation | async-start | bytes 327680 | tf_op jit(solution)/shard_map/all_to_all | solution.py:571
  15.1 0.0 copy-done.2
  15.1 3.5 %collective-permute-start.1 = (bf16[144,1024]{1,0:T(8,128)(2,1)S(1)}, bf16[144,1024]{1,0:T(8,128)(2,1)S(1)}, u32[]{:S(2)}, u32[]{:S(2)}) collective-permute-start(bf16[144,1024]{1,0:T(8,128)(2,1)S(1)} %copy-done.2), channel_id=1, source_target_pairs={{1,2},{2,1},{3,4},{4,3},{5,6},{6,5},{7,8},{8,7},{9,10},{10,9},{11,... | collective-permute-start | bytes 884744 | tf_op jit(solution)/shard_map/ppermute | solution.py:81
  18.6 3.9 %own.1 = (f32[128,1024]{1,0:T(8,128)S(1)}, bf16[128,1024]{1,0:T(8,128)(2,1)S(1)}) custom-call(bf16[512,1024]{1,0:T(8,128)(2,1)} %grid_hbm.5, bf16[128,1024]{1,0:T(8,128)(2,1)} %mesh_in_hbm.1, s32[8,128]{1,0:T(8,128)} %bitcast.14, s32[8,128]{1,0:T(8,128)} %bitcast.15, bf16[128,1024]{1,0:T(8,128)(2,1)} %cot_hbm.3, bf16[1024,1024]{1,0:T(8,128)(2,1)} %w_out_hbm.3, ...), custom_call_target="tpu_custom_call" | custom-call | tf_op jit(solution)/shard_map/own/pallas_call | solution.py:50
  22.6 0.0 copy-start
  22.6 0.7 %copy-done = bf16[128,1024]{1,0:T(8,128)(2,1)} copy-done((bf16[128,1024]{1,0:T(8,128)(2,1)}, bf16[128,1024]{1,0:T(8,128)(2,1)S(1)}, u32[]{:S(2)}) %copy-start) | copy-done | bytes 262168
  23.3 2.6 %collective-permute-done.1.off.off_first = bf16[144,1024]{1,0:T(8,128)(2,1)S(1)} collective-permute-done((bf16[144,1024]{1,0:T(8,128)(2,1)S(1)}, bf16[144,1024]{1,0:T(8,128)(2,1)S(1)}, u32[]{:S(2)}, u32[]{:S(2)}) %collective-permute-start.1) | collective-permute-done | bytes 294944 | tf_op jit(solution)/shard_map/ppermute | solution.py:81
  25.9 1.4 %side.1.partial = f32[128,1024]{1,0:T(8,128)S(1)} custom-call(bf16[144,1024]{1,0:T(8,128)(2,1)S(1)} %collective-permute-done.chip_message.chip.chip_first, bf16[144,1024]{1,0:T(8,128)(2,1)S(1)} %collective-permute-done.1.off.off_first, bf16[1024,1024]{1,0:T(8,128)(2,1)S(1)} %get-tuple-element.25.w_edge, f32[128,1024]{1,0:T(8,128)S(1)} %get-tuple-element.26.partial), custom_call_target="tpu_custom_call" | custom-call | tf_op jit(solution)/shard_map/side/pallas_call | solution.py:50
  27.3 0.0 all-to-all-done
  27.3 0.5 latent.1
  27.8 0.1 collective-permute-start.2
  27.9 4.4 %collective-permute-start.3 = (bf16[128,1024]{1,0:T(8,128)(2,1)S(1)}, bf16[128,1024]{1,0:T(8,128)(2,1)S(1)}, u32[]{:S(2)}, u32[]{:S(2)}) collective-permute-start(bf16[128,1024]{1,0:T(8,128)(2,1)S(1)} %get-tuple-element.27.normed), channel_id=1, source_target_pairs={{1,2},{2,1},{3,4},{4,3},{5,6},{6,5},{7,8},{8,7},{9,10},{10,9},{11,... | collective-permute-start | bytes 786440 | tf_op jit(solution)/shard_map/ppermute | solution.py:81
  32.3 0.0 copy-start.1
  32.3 0.9 %copy-done.1 = bf16[128,1024]{1,0:T(8,128)(2,1)S(1)} copy-done((bf16[128,1024]{1,0:T(8,128)(2,1)S(1)}, bf16[128,1024]{1,0:T(8,128)(2,1)}, u32[]{:S(2)}) %copy-start.1) | copy-done | bytes 262168
  33.3 3.2 %project.1 = (bf16[128,3072]{1,0:T(8,128)(2,1)S(1)}, bf16[1024,3072]{1,0:T(8,128)(2,1)S(1)}, bf16[128,1024]{1,0:T(8,128)(2,1)S(1)}) custom-call(bf16[128,1024]{1,0:T(8,128)(2,1)S(1)} %get-tuple-element.27.normed, bf16[128,1024]{1,0:T(8,128)(2,1)S(1)} %copy-done.1, bf16[1024,3072]{1,0:T(8,128)(2,1)} %w_qkv_hbm.1), custom_call_target="tpu_custom_call" | custom-call | tf_op jit(solution)/shard_map/project/pallas_call | solution.py:50
  36.5 0.1 collective-permute-start.6
  36.6 3.7 %collective-permute-start.7 = (bf16[128,1024]{1,0:T(8,128)(2,1)S(1)}, bf16[128,1024]{1,0:T(8,128)(2,1)S(1)}, u32[]{:S(2)}, u32[]{:S(2)}) collective-permute-start(bf16[128,1024]{1,0:T(8,128)(2,1)S(1)} %get-tuple-element.31.own_grad), channel_id=1, source_target_pairs={{1,2},{2,1},{3,4},{4,3},{5,6},{6,5},{7,8},{8,7},{9,10},{10,9},{11,... | collective-permute-start | bytes 786440 | tf_op jit(solution)/shard_map/ppermute | solution.py:81
  40.2 0.0 collective-permute-done.2.chip_normed
  40.2 0.0 collective-permute-done.3.off_normed
  40.3 4.0 %attend.1 = (f32[24,256]{1,0:T(8,128)S(1)}, bf16[384,2048]{1,0:T(8,128)(2,1)S(1)}, bf16[8,256,384]{2,1,0:T(8,128)(2,1)S(1)}, bf16[8,256,384]{2,1,0:T(8,128)(2,1)S(1)}) custom-call(bf16[128,1024]{1,0:T(8,128)(2,1)S(1)} %collective-permute-done.2.chip_normed, bf16[128,1024]{1,0:T(8,128)(2,1)S(1)} %collective-permute-done.3.off_normed, ...), custom_call_target="tpu_custom_call" | custom-call | tf_op jit(solution)/shard_map/attend/pallas_call | solution.py:50
  44.3 0.1 collective-permute-start.4
  44.4 3.5 %collective-permute-start.5 = (f32[24,256]{1,0:T(8,128)S(1)}, f32[24,256]{1,0:T(8,128)S(1)}, u32[]{:S(2)}, u32[]{:S(2)}) collective-permute-start(f32[24,256]{1,0:T(8,128)S(1)} %get-tuple-element.37), channel_id=1, source_target_pairs={{1,2},{2,1},{3,4},{4,3},{5,6},{6,5},{7,8},{8,7},{9,10},{10,9},{11,... | collective-permute-start | bytes 73736 | tf_op jit(solution)/shard_map/ppermute | solution.py:81
  47.9 5.0 %product.1 = (bf16[128,1024]{1,0:T(8,128)(2,1)}, f32[128,1024]{1,0:T(8,128)S(1)}, f32[128,1024]{1,0:T(8,128)S(1)}, f32[128,1024]{1,0:T(8,128)S(1)}, bf16[256,1024]{1,0:T(8,128)(2,1)S(1)}) custom-call(bf16[8,256,384]{2,1,0:T(8,128)(2,1)S(1)} %get-tuple-element.32.weights, bf16[8,256,384]{2,1,0:T(8,128)(2,1)S(1)} %get-tuple-element.33.grad_scores, ...), custom_call_target="tpu_custom_call" | custom-call | tf_op jit(solution)/shard_map/product/pallas_call | solution.py:50
  52.9 0.0 collective-permute-done.6.chip_grad
  53.0 0.0 collective-permute-done.7.off_grad
  53.0 0.0 collective-permute-done.4.chip_stats
  53.0 0.0 collective-permute-done.5.off_stats
  53.0 5.1 %finish.1 = bf16[128,1024]{1,0:T(8,128)(2,1)} custom-call(f32[24,256]{1,0:T(8,128)S(1)} %collective-permute-done.4.chip_stats, f32[24,256]{1,0:T(8,128)S(1)} %collective-permute-done.5.off_stats, bf16[144,1024]{1,0:T(8,128)(2,1)S(1)} %collective-permute-done.chip_message.chip.chip_first, bf16[144,1024]{1,0:T(8,128)(2,1)S(1)} %collective-permute-done.1.off.off_first, ...), custom_call_target="tpu_custom_call" | custom-call | tf_op jit(solution)/shard_map/finish/pallas_call | solution.py:50
Async XLA Ops:
  2.6 12.5 %copy-start.2 = (bf16[144,1024]{1,0:T(8,128)(2,1)S(1)}, bf16[144,1024]{1,0:T(8,128)(2,1)}, u32[]{:S(2)}) copy-start(bf16[144,1024]{1,0:T(8,128)(2,1)} %get-tuple-element.24) | copy-start | bytes 884740
  2.7 1.9 %collective-permute-start = (bf16[144,1024]{1,0:T(8,128)(2,1)}, bf16[144,1024]{1,0:T(8,128)(2,1)S(1)}, u32[]{:S(2)}, u32[]{:S(2)}) collective-permute-start(bf16[144,1024]{1,0:T(8,128)(2,1)} %get-tuple-element.22), channel_id=1, source_target_pairs={{0,1},{1,0},{2,3},{3,2},{4,5},{5,4},{6,7},{7,6},{8,9},{9,8},{10,11... | collective-permute-start | bytes 884744 | tf_op jit(solution)/shard_map/ppermute | solution.py:84
  7.7 19.6 %all-to-all-start = ((bf16[16,8,640]{2,1,0:T(8,128)(2,1)}), bf16[16,8,640]{2,1,0:T(8,128)(2,1)S(1)}, u32[]{:S(2)}, u32[]{:S(2)}) async-start(bf16[16,8,640]{2,1,0:T(8,128)(2,1)} %bitcast.11), calls=%async_computation | async-start | bytes 327680 | tf_op jit(solution)/shard_map/all_to_all | solution.py:571
  15.1 10.8 %collective-permute-start.1 = (bf16[144,1024]{1,0:T(8,128)(2,1)S(1)}, bf16[144,1024]{1,0:T(8,128)(2,1)S(1)}, u32[]{:S(2)}, u32[]{:S(2)}) collective-permute-start(bf16[144,1024]{1,0:T(8,128)(2,1)S(1)} %copy-done.2), channel_id=1, source_target_pairs={{1,2},{2,1},{3,4},{4,3},{5,6},{6,5},{7,8},{8,7},{9,10},{10,9},{11,... | collective-permute-start | bytes 884744 | tf_op jit(solution)/shard_map/ppermute | solution.py:81
  22.6 0.7 %copy-start = (bf16[128,1024]{1,0:T(8,128)(2,1)}, bf16[128,1024]{1,0:T(8,128)(2,1)S(1)}, u32[]{:S(2)}) copy-start(bf16[128,1024]{1,0:T(8,128)(2,1)S(1)} %get-tuple-element.28.own_grad) | copy-start | bytes 786436
  27.8 12.4 %collective-permute-start.2 = (bf16[128,1024]{1,0:T(8,128)(2,1)S(1)}, bf16[128,1024]{1,0:T(8,128)(2,1)S(1)}, u32[]{:S(2)}, u32[]{:S(2)}) collective-permute-start(bf16[128,1024]{1,0:T(8,128)(2,1)S(1)} %get-tuple-element.27.normed), channel_id=1, source_target_pairs={{0,1},{1,0},{2,3},{3,2},{4,5},{5,4},{6,7},{7,6},{8,9},{9,8},{10,11... | collective-permute-start | bytes 786440 | tf_op jit(solution)/shard_map/ppermute | solution.py:84
  27.9 12.3 %collective-permute-start.3 = (bf16[128,1024]{1,0:T(8,128)(2,1)S(1)}, bf16[128,1024]{1,0:T(8,128)(2,1)S(1)}, u32[]{:S(2)}, u32[]{:S(2)}) collective-permute-start(bf16[128,1024]{1,0:T(8,128)(2,1)S(1)} %get-tuple-element.27.normed), channel_id=1, source_target_pairs={{1,2},{2,1},{3,4},{4,3},{5,6},{6,5},{7,8},{8,7},{9,10},{10,9},{11,... | collective-permute-start | bytes 786440 | tf_op jit(solution)/shard_map/ppermute | solution.py:81
  32.3 1.0 %copy-start.1 = (bf16[128,1024]{1,0:T(8,128)(2,1)S(1)}, bf16[128,1024]{1,0:T(8,128)(2,1)}, u32[]{:S(2)}) copy-start(bf16[128,1024]{1,0:T(8,128)(2,1)} %copy-done) | copy-start | bytes 786436
  36.5 16.5 %collective-permute-start.6 = (bf16[128,1024]{1,0:T(8,128)(2,1)S(1)}, bf16[128,1024]{1,0:T(8,128)(2,1)S(1)}, u32[]{:S(2)}, u32[]{:S(2)}) collective-permute-start(bf16[128,1024]{1,0:T(8,128)(2,1)S(1)} %get-tuple-element.31.own_grad), channel_id=1, source_target_pairs={{0,1},{1,0},{2,3},{3,2},{4,5},{5,4},{6,7},{7,6},{8,9},{9,8},{10,11... | collective-permute-start | bytes 786440 | tf_op jit(solution)/shard_map/ppermute | solution.py:84
  36.6 16.4 %collective-permute-start.7 = (bf16[128,1024]{1,0:T(8,128)(2,1)S(1)}, bf16[128,1024]{1,0:T(8,128)(2,1)S(1)}, u32[]{:S(2)}, u32[]{:S(2)}) collective-permute-start(bf16[128,1024]{1,0:T(8,128)(2,1)S(1)} %get-tuple-element.31.own_grad), channel_id=1, source_target_pairs={{1,2},{2,1},{3,4},{4,3},{5,6},{6,5},{7,8},{8,7},{9,10},{10,9},{11,... | collective-permute-start | bytes 786440 | tf_op jit(solution)/shard_map/ppermute | solution.py:81
  44.3 8.7 %collective-permute-start.4 = (f32[24,256]{1,0:T(8,128)S(1)}, f32[24,256]{1,0:T(8,128)S(1)}, u32[]{:S(2)}, u32[]{:S(2)}) collective-permute-start(f32[24,256]{1,0:T(8,128)S(1)} %get-tuple-element.37), channel_id=1, source_target_pairs={{0,1},{1,0},{2,3},{3,2},{4,5},{5,4},{6,7},{7,6},{8,9},{9,8},{10,11... | collective-permute-start | bytes 73736 | tf_op jit(solution)/shard_map/ppermute | solution.py:84
  44.4 8.6 %collective-permute-start.5 = (f32[24,256]{1,0:T(8,128)S(1)}, f32[24,256]{1,0:T(8,128)S(1)}, u32[]{:S(2)}, u32[]{:S(2)}) collective-permute-start(f32[24,256]{1,0:T(8,128)S(1)} %get-tuple-element.37), channel_id=1, source_target_pairs={{1,2},{2,1},{3,4},{4,3},{5,6},{6,5},{7,8},{8,7},{9,10},{10,9},{11,... | collective-permute-start | bytes 73736 | tf_op jit(solution)/shard_map/ppermute | solution.py:81

commit v9 on v7

--- a/solution.py
+++ b/solution.py
@@ -33,7 +33,7 @@
     return lax.broadcasted_iota(I32, shape, dim)
 
 
-def call(kernel, outs, args, hbm=(), hbm_outs=(), scratch=(), name=None):
+def call(kernel, outs, args, hbm=(), hbm_outs=(), scratch=(), name=None, flops=None):
     args = [
         pltpu.with_memory_space_constraint(a, pltpu.HBM) if i in hbm else a
         for i, a in enumerate(args)
@@ -54,6 +54,7 @@
         out_specs=specs(len(outs), hbm_outs),
         scratch_shapes=list(scratch),
         compiler_params=pltpu.CompilerParams(vmem_limit_bytes=VMEM_LIMIT),
+        cost_estimate=flops and pl.CostEstimate(flops=flops, transcendentals=0, bytes_accessed=0),
         name=name,
     )(*args)
 
@@ -211,12 +212,18 @@
     mesh_in_hbm,
     own_src_hbm,
     own_dst_hbm,
+    cot_hbm,
+    w_out_hbm,
     w_edge,
     partial_out,
+    grad_hbm,
     grid,
     mesh_in,
     own_src,
     own_dst,
+    cot,
+    w_out,
+    grad,
     sems,
 ):
     grid_rows = grid.shape[0]
@@ -225,6 +232,8 @@
         [
             (own_src_hbm, own_src),
             (own_dst_hbm, own_dst),
+            (cot_hbm, cot),
+            (w_out_hbm, w_out),
             (grid_hbm, grid),
             (mesh_in_hbm, mesh_in),
         ],
@@ -236,10 +245,16 @@
     src = onehot_rows([own_src[r : r + 1] for r in range(rows)], grid_rows)
     dst = onehot_rows([own_dst[r : r + 1] for r in range(rows)], mesh_rows)
     counts = mm_nt(dst, src).astype(BF16)
-    for copy in copies[2:]:
+    for copy in copies[2:4]:
+        copy.wait()
+    grad[...] = mm_nt(cot[...], w_out[...]).astype(BF16)
+    out = pltpu.make_async_copy(grad, grad_hbm, sems.at[6])
+    out.start()
+    for copy in copies[4:]:
         copy.wait()
     active = gelu(mm(grid[...], w_edge[...]))
     partial_out[...] = mesh_in[...].astype(F32) + mm(counts, active)
+    out.wait()
 
 
 def meta_of(message, count):
@@ -281,31 +296,18 @@
     normed_out[...] = normal.astype(BF16)
 
 
-def project_kernel(
-    normed, w_qkv_hbm, w_out_hbm, cot_hbm, qkv_out, w_qkv, w_out, cot_out, grad_out, sems
-):
+def project_kernel(normed, grad_hbm, w_qkv_hbm, qkv_out, w_qkv, grad_out, sems):
     width = w_qkv.shape[1] // PIECES
     pieces = [pl.ds(c * width, width) for c in range(PIECES)]
-    copies = [
-        pltpu.make_async_copy(src, dst, sems.at[i])
-        for i, (src, dst) in enumerate(
-            [(cot_hbm, cot_out), (w_out_hbm, w_out)]
-            + [(w_qkv_hbm.at[:, piece], w_qkv.at[:, piece]) for piece in pieces]
-        )
-    ]
-    for copy in copies[:4]:
-        copy.start()
-    copies[0].wait()
-    copies[1].wait()
-    copies[4].start()
-    copies[5].start()
-    grad_out[...] = mm_nt(cot_out[...], w_out[...]).astype(BF16)
+    copies = start_all(
+        [(w_qkv_hbm.at[:, piece], w_qkv.at[:, piece]) for piece in pieces] + [(grad_hbm, grad_out)],
+        sems,
+    )
     for c in range(PIECES):
-        copies[2 + c].wait()
-        if c + 6 < len(copies):
-            copies[c + 6].start()
+        copies[c].wait()
         cols = slice(c * width, (c + 1) * width)
         qkv_out[:, cols] = mm(normed[...], w_qkv[:, cols]).astype(BF16)
+    copies[PIECES].wait()
 
 
 def halves(rows, scale=None):
@@ -336,14 +338,18 @@
     own_qkv,
     own_grad,
     window_hbm,
+    w_out_hbm,
+    cot_hbm,
     stats_out,
     kv,
     weights_out,
     scores_out,
+    w_out,
+    cot,
     window,
     sems,
 ):
-    fetch = start_all([(window_hbm, window)], sems)
+    fetch = start_all([(window_hbm, window), (w_out_hbm, w_out), (cot_hbm, cot)], sems)
     m, channels = chip_normed.shape
     pairs = channels // pair
     devices = lax.axis_size("node")
@@ -383,6 +389,8 @@
         stats = jnp.where(lane == pairs + p, inv_sum, stats)
         stats = jnp.where(lane == 2 * pairs + p, delta, stats)
     stats_out[...] = jnp.transpose(stats)[: 3 * pairs]
+    for copy in fetch[1:]:
+        copy.wait()
 
 
 def product_kernel(
@@ -544,12 +552,13 @@
     ).reshape(far_block)
 
     rows = ((m, channels), BF16)
-    (partial,) = call(
+    partial, own_grad = call(
         own_kernel,
-        [((m, channels), F32)],
-        [grid_in, mesh_in, own_src, own_dst, w_edge],
-        hbm=range(4),
-        scratch=like(grid_in, mesh_in, own_src, own_dst) + [dma(4)],
+        [((m, channels), F32), rows],
+        [grid_in, mesh_in, own_src, own_dst, cotangent, w_out, w_edge],
+        hbm=range(6),
+        hbm_outs=(1,),
+        scratch=like(grid_in, mesh_in, own_src, own_dst, cotangent, w_out, cotangent) + [dma(7)],
         name="own",
     )
     (partial,) = call(
@@ -557,27 +566,35 @@
         [((m, channels), F32)],
         [from_chip, from_off, w_edge, partial],
         name="side",
+        flops=8 * 10**9,
     )
     latent, normed = call(
         functools.partial(latent_kernel, far_depth), [rows, rows], [got_far, partial], name="latent"
     )
     chip_normed, off_normed = exchange(normed, normed, "node")
-    own_qkv, w_qkv, w_out, own_cot, own_grad = call(
+    own_qkv, w_qkv, own_grad = call(
         project_kernel,
-        [((m, 3 * channels), BF16), (w_qkv.shape, BF16), (w_out.shape, BF16), rows, rows],
-        [normed, w_qkv, w_out, cotangent],
-        hbm=(1, 2, 3),
-        scratch=[dma(PIECES + 2)],
+        [((m, 3 * channels), BF16), (w_qkv.shape, BF16), rows],
+        [normed, own_grad, w_qkv],
+        hbm=(1, 2),
+        scratch=[dma(PIECES + 1)],
         name="project",
     )
     chip_grad, off_grad = exchange(own_grad, own_grad, "node")
     probs = ((pairs, 2 * m, 3 * m), BF16)
-    stats, kv, weights, grad_scores = call(
+    stats, kv, weights, grad_scores, w_out, cotangent = call(
         functools.partial(attend_kernel, scale, pair),
-        [((3 * pairs, 2 * m), F32), ((3 * m, 2 * channels), BF16), probs, probs],
-        [chip_normed, off_normed, w_qkv, own_qkv, own_grad, window],
-        hbm=(5,),
-        scratch=like(window) + [dma(1)],
+        [
+            ((3 * pairs, 2 * m), F32),
+            ((3 * m, 2 * channels), BF16),
+            probs,
+            probs,
+            (w_out.shape, BF16),
+            rows,
+        ],
+        [chip_normed, off_normed, w_qkv, own_qkv, own_grad, window, w_out, cotangent],
+        hbm=(5, 6, 7),
+        scratch=like(window) + [dma(3)],
         name="attend",
     )
     chip_stats, off_stats = exchange(stats, stats, "node")
@@ -622,7 +639,7 @@
             grad_normed,
             w_qkv,
             latent,
-            own_cot,
+            cotangent,
         ],
         scratch=[pltpu.VMEM((m, 2 * channels), BF16)],
         name="finish",

time: 52.8 us -> 47.8 us (0.905)
  waiting for transfers between devices: 4.46 us -> 1.62 us
  starting transfers between devices: 22.6 us -> 20.6 us
    ppermute x4, waiting for transfers between devices: 4.45 us -> 0.01 us  [exchange(): lax.ppermute(off_message, axis, [p for i in range(1, n - 1, 2) for p in (...]
    all_to_all x1, starting transfers between devices: 7.36 us -> 5.33 us  [body(): lax.all_to_all(far_message.reshape(devices, 2 * far_depth, far_block[1]),...]
    all_to_all x1, waiting for transfers between devices: 0.01 us -> 1.6 us  [body(): lax.all_to_all(far_message.reshape(devices, 2 * far_depth, far_block[1]),...]
    ppermute x4, starting transfers between devices: 14.9 us -> 13.7 us  [exchange(): lax.ppermute(off_message, axis, [p for i in range(1, n - 1, 2) for p in (...]
    ppermute x4, starting transfers between devices: 0.38 us -> 1.49 us  [exchange(): lax.ppermute(chip_message, axis, [p for i in range(0, n, 2) for p in ((i,...]
  transfers between devices with their start and end apart: 9 -> 9, of which waited for: 1 -> 1; matrix products, arithmetic and copies ran while one was open for 0% -> 0% of each run, Pallas kernels for 31% -> 34%
where the time goes in v9:
time: 47.8 us; the launch traced here: 47.4 us
  Pallas kernels  24.4 us (51%)
  starting transfers between devices  20.6 us (43%)
  waiting for transfers between devices  1.62 us (3%)
  between operations  0.77 us (2%)
    pallas_call x8, Pallas kernels, call(): pl.pallas_call(kernel, out_shape=[(pltpu.HBM if i in hbm_outs else jax.Sh...  24.4 us
    ppermute x4, starting transfers between devices, exchange(): lax.ppermute(off_message, axis, [p for i in range(1, n - 1, 2) for p in (...  13.7 us
    all_to_all x1, starting transfers between devices, body(): lax.all_to_all(far_message.reshape(devices, 2 * far_depth, far_block[1]),...  5.33 us
    all_to_all x1, waiting for transfers between devices, body(): lax.all_to_all(far_message.reshape(devices, 2 * far_depth, far_block[1]),...  1.6 us
    ppermute x4, starting transfers between devices, exchange(): lax.ppermute(chip_message, axis, [p for i in range(0, n, 2) for p in ((i,...  1.49 us
  transfers between devices with their start and end apart: 9, of which 1 were waited for; matrix products, arithmetic and copies ran while one was open for 0% of the time, Pallas kernels for 34%

profile of v9, /device:TPU:1, one launch (start us, length us, event | category | flops | bytes accessed | tf_op | source)
XLA Modules:
  0.0 47.4 jit_solution(16949092098524217282)
XLA Ops:
  0.6 3.4 %pack.1 = (bf16[128,640]{1,0:T(8,128)(2,1)}, bf16[144,1024]{1,0:T(8,128)(2,1)}, bf16[144,1024]{1,0:T(8,128)(2,1)}, bf16[1024,1024]{1,0:T(8,128)(2,1)S(1)}) custom-call(bf16[512,1024]{1,0:T(8,128)(2,1)} %grid_hbm.3, s32[2,128]{1,0:T(2,128)} %window_hbm.3, s32[32,128]{1,0:T(8,128)} %bitcast.12, s32[32,128]{1,0:T(8,128)} %bitcast.13, s32[1,2]{1,0:T(1,128)} %bitcast.16, ...), custom_call_target="tpu_custom_call" | custom-call | tf_op jit(solution)/shard_map/pack/pallas_call | solution.py:47
  4.0 0.1 collective-permute-start
  4.1 4.5 %collective-permute-start.1 = (bf16[144,1024]{1,0:T(8,128)(2,1)}, bf16[144,1024]{1,0:T(8,128)(2,1)S(1)}, u32[]{:S(2)}, u32[]{:S(2)}) collective-permute-start(bf16[144,1024]{1,0:T(8,128)(2,1)} %get-tuple-element.26), channel_id=1, source_target_pairs={{1,2},{2,1},{3,4},{4,3},{5,6},{6,5},{7,8},{8,7},{9,10},{10,9},{11,... | collective-permute-start | bytes 884744 | tf_op jit(solution)/shard_map/ppermute | solution.py:79
  8.6 5.3 %all-to-all-start = ((bf16[16,8,640]{2,1,0:T(8,128)(2,1)}), bf16[16,8,640]{2,1,0:T(8,128)(2,1)S(1)}, u32[]{:S(2)}, u32[]{:S(2)}) async-start(bf16[16,8,640]{2,1,0:T(8,128)(2,1)} %bitcast.11), calls=%async_computation | async-start | bytes 327680 | tf_op jit(solution)/shard_map/all_to_all | solution.py:546
  13.9 4.3 %own.1 = (f32[128,1024]{1,0:T(8,128)S(1)}, bf16[128,1024]{1,0:T(8,128)(2,1)}) custom-call(bf16[512,1024]{1,0:T(8,128)(2,1)} %grid_hbm.3, bf16[128,1024]{1,0:T(8,128)(2,1)} %mesh_in_hbm.1, s32[8,128]{1,0:T(8,128)} %bitcast.14, s32[8,128]{1,0:T(8,128)} %bitcast.15, bf16[128,1024]{1,0:T(8,128)(2,1)} %cot_hbm.3, bf16[1024,1024]{1,0:T(8,128)(2,1)} %w_out_hbm.3, ...), custom_call_target="tpu_custom_call" | custom-call | tf_op jit(solution)/shard_map/own/pallas_call | solution.py:47
  18.3 0.0 collective-permute-done.chip.chip_first
  18.3 0.0 collective-permute-done.1.off.off_first
  18.3 1.4 %side.1.partial = f32[128,1024]{1,0:T(8,128)S(1)} custom-call(bf16[144,1024]{1,0:T(8,128)(2,1)S(1)} %collective-permute-done.chip.chip_first, bf16[144,1024]{1,0:T(8,128)(2,1)S(1)} %collective-permute-done.1.off.off_first, bf16[1024,1024]{1,0:T(8,128)(2,1)S(1)} %get-tuple-element.27.w_edge, f32[128,1024]{1,0:T(8,128)S(1)} %get-tuple-element.28.partial), custom_call_target="tpu_custom_call" | custom-call | flops 8000000000 | tf_op jit(solution)/shard_map/side/pallas_call | solution.py:47
  19.7 1.6 %all-to-all-done = bf16[16,8,640]{2,1,0:T(8,128)(2,1)S(1)} async-done(((bf16[16,8,640]{2,1,0:T(8,128)(2,1)}), bf16[16,8,640]{2,1,0:T(8,128)(2,1)S(1)}, u32[]{:S(2)}, u32[]{:S(2)}) %all-to-all-start) | async-done | bytes 163872 | tf_op jit(solution)/shard_map/all_to_all | solution.py:546
  21.3 0.5 %latent.1 = (bf16[128,1024]{1,0:T(8,128)(2,1)S(1)}, bf16[128,1024]{1,0:T(8,128)(2,1)S(1)}) custom-call(bf16[128,640]{1,0:T(8,128)(2,1)S(1)} %bitcast.10, f32[128,1024]{1,0:T(8,128)S(1)} %side.1.partial), custom_call_target="tpu_custom_call" | custom-call | tf_op jit(solution)/shard_map/latent/pallas_call | solution.py:47
  21.8 1.2 %collective-permute-start.2 = (bf16[128,1024]{1,0:T(8,128)(2,1)S(1)}, bf16[128,1024]{1,0:T(8,128)(2,1)S(1)}, u32[]{:S(2)}, u32[]{:S(2)}) collective-permute-start(bf16[128,1024]{1,0:T(8,128)(2,1)S(1)} %get-tuple-element.29.normed), channel_id=1, source_target_pairs={{0,1},{1,0},{2,3},{3,2},{4,5},{5,4},{6,7},{7,6},{8,9},{9,8},{10,11... | collective-permute-start | bytes 786440 | tf_op jit(solution)/shard_map/ppermute | solution.py:82
  23.1 1.9 %collective-permute-start.3 = (bf16[128,1024]{1,0:T(8,128)(2,1)S(1)}, bf16[128,1024]{1,0:T(8,128)(2,1)S(1)}, u32[]{:S(2)}, u32[]{:S(2)}) collective-permute-start(bf16[128,1024]{1,0:T(8,128)(2,1)S(1)} %get-tuple-element.29.normed), channel_id=1, source_target_pairs={{1,2},{2,1},{3,4},{4,3},{5,6},{6,5},{7,8},{8,7},{9,10},{10,9},{11,... | collective-permute-start | bytes 786440 | tf_op jit(solution)/shard_map/ppermute | solution.py:79
  25.0 3.2 %project.1 = (bf16[128,3072]{1,0:T(8,128)(2,1)S(1)}, bf16[1024,3072]{1,0:T(8,128)(2,1)S(1)}, bf16[128,1024]{1,0:T(8,128)(2,1)S(1)}) custom-call(bf16[128,1024]{1,0:T(8,128)(2,1)S(1)} %get-tuple-element.29.normed, bf16[128,1024]{1,0:T(8,128)(2,1)} %get-tuple-element.30.grad_hbm, bf16[1024,3072]{1,0:T(8,128)(2,1)} %w_qkv_hbm.1), custom_call_target="tpu_custom_call" | custom-call | tf_op jit(solution)/shard_map/project/pallas_call | solution.py:47
  28.2 0.1 collective-permute-start.6
  28.3 3.6 %collective-permute-start.7 = (bf16[128,1024]{1,0:T(8,128)(2,1)S(1)}, bf16[128,1024]{1,0:T(8,128)(2,1)S(1)}, u32[]{:S(2)}, u32[]{:S(2)}) collective-permute-start(bf16[128,1024]{1,0:T(8,128)(2,1)S(1)} %get-tuple-element.33.own_grad), channel_id=1, source_target_pairs={{1,2},{2,1},{3,4},{4,3},{5,6},{6,5},{7,8},{8,7},{9,10},{10,9},{11,... | collective-permute-start | bytes 786440 | tf_op jit(solution)/shard_map/ppermute | solution.py:79
  31.9 0.0 collective-permute-done.2.chip_normed
  32.0 0.0 collective-permute-done.3.off_normed
  32.0 4.1 %attend.1 = (f32[24,256]{1,0:T(8,128)S(1)}, bf16[384,2048]{1,0:T(8,128)(2,1)S(1)}, bf16[8,256,384]{2,1,0:T(8,128)(2,1)S(1)}, bf16[8,256,384]{2,1,0:T(8,128)(2,1)...) custom-call(bf16[128,1024]{1,0:T(8,128)(2,1)S(1)} %collective-permute-done.2.chip_normed, ...), custom_call_target="tpu_custom_call" | custom-call | tf_op jit(solution)/shard_map/attend/pallas_call | solution.py:47
  36.0 0.1 collective-permute-start.4
  36.1 3.7 %collective-permute-start.5 = (f32[24,256]{1,0:T(8,128)S(1)}, f32[24,256]{1,0:T(8,128)S(1)}, u32[]{:S(2)}, u32[]{:S(2)}) collective-permute-start(f32[24,256]{1,0:T(8,128)S(1)} %get-tuple-element.40), channel_id=1, source_target_pairs={{1,2},{2,1},{3,4},{4,3},{5,6},{6,5},{7,8},{8,7},{9,10},{10,9},{11,... | collective-permute-start | bytes 73736 | tf_op jit(solution)/shard_map/ppermute | solution.py:79
  39.8 3.3 %product.1 = (bf16[128,1024]{1,0:T(8,128)(2,1)}, f32[128,1024]{1,0:T(8,128)S(1)}, f32[128,1024]{1,0:T(8,128)S(1)}, f32[128,1024]{1,0:T(8,128)S(1)}, bf16[256,1024]{1,0:T(8,128)(2,1)S(1)}) custom-call(bf16[8,256,384]{2,1,0:T(8,128)(2,1)S(1)} %get-tuple-element.34.weights, bf16[8,256,384]{2,1,0:T(8,128)(2,1)S(1)} %get-tuple-element.35.grad_scores, ...), custom_call_target="tpu_custom_call" | custom-call | tf_op jit(solution)/shard_map/product/pallas_call | solution.py:47
  43.1 0.0 collective-permute-done.6.chip_grad
  43.1 0.0 collective-permute-done.7.off_grad
  43.1 0.0 collective-permute-done.4.chip_stats
  43.1 0.0 collective-permute-done.5.off_stats
  43.1 4.3 %finish.1 = bf16[128,1024]{1,0:T(8,128)(2,1)} custom-call(f32[24,256]{1,0:T(8,128)S(1)} %collective-permute-done.4.chip_stats, f32[24,256]{1,0:T(8,128)S(1)} %collective-permute-done.5.off_stats, bf16[144,1024]{1,0:T(8,128)(2,1)S(1)} %collective-permute-done.chip.chip_first, bf16[144,1024]{1,0:T(8,128)(2,1)S(1)} %collective-permute-done.1.off.off_first, ...), custom_call_target="tpu_custom_call" | custom-call | tf_op jit(solution)/shard_map/finish/pallas_call | solution.py:47
Async XLA Ops:
  4.0 14.3 %collective-permute-start = (bf16[144,1024]{1,0:T(8,128)(2,1)}, bf16[144,1024]{1,0:T(8,128)(2,1)S(1)}, u32[]{:S(2)}, u32[]{:S(2)}) collective-permute-start(bf16[144,1024]{1,0:T(8,128)(2,1)} %get-tuple-element.25), channel_id=1, source_target_pairs={{0,1},{1,0},{2,3},{3,2},{4,5},{5,4},{6,7},{7,6},{8,9},{9,8},{10,11... | collective-permute-start | bytes 884744 | tf_op jit(solution)/shard_map/ppermute | solution.py:82
  4.1 14.2 %collective-permute-start.1 = (bf16[144,1024]{1,0:T(8,128)(2,1)}, bf16[144,1024]{1,0:T(8,128)(2,1)S(1)}, u32[]{:S(2)}, u32[]{:S(2)}) collective-permute-start(bf16[144,1024]{1,0:T(8,128)(2,1)} %get-tuple-element.26), channel_id=1, source_target_pairs={{1,2},{2,1},{3,4},{4,3},{5,6},{6,5},{7,8},{8,7},{9,10},{10,9},{11,... | collective-permute-start | bytes 884744 | tf_op jit(solution)/shard_map/ppermute | solution.py:79
  8.6 12.7 %all-to-all-start = ((bf16[16,8,640]{2,1,0:T(8,128)(2,1)}), bf16[16,8,640]{2,1,0:T(8,128)(2,1)S(1)}, u32[]{:S(2)}, u32[]{:S(2)}) async-start(bf16[16,8,640]{2,1,0:T(8,128)(2,1)} %bitcast.11), calls=%async_computation | async-start | bytes 327680 | tf_op jit(solution)/shard_map/all_to_all | solution.py:546
  21.8 10.1 %collective-permute-start.2 = (bf16[128,1024]{1,0:T(8,128)(2,1)S(1)}, bf16[128,1024]{1,0:T(8,128)(2,1)S(1)}, u32[]{:S(2)}, u32[]{:S(2)}) collective-permute-start(bf16[128,1024]{1,0:T(8,128)(2,1)S(1)} %get-tuple-element.29.normed), channel_id=1, source_target_pairs={{0,1},{1,0},{2,3},{3,2},{4,5},{5,4},{6,7},{7,6},{8,9},{9,8},{10,11... | collective-permute-start | bytes 786440 | tf_op jit(solution)/shard_map/ppermute | solution.py:82
  23.1 8.9 %collective-permute-start.3 = (bf16[128,1024]{1,0:T(8,128)(2,1)S(1)}, bf16[128,1024]{1,0:T(8,128)(2,1)S(1)}, u32[]{:S(2)}, u32[]{:S(2)}) collective-permute-start(bf16[128,1024]{1,0:T(8,128)(2,1)S(1)} %get-tuple-element.29.normed), channel_id=1, source_target_pairs={{1,2},{2,1},{3,4},{4,3},{5,6},{6,5},{7,8},{8,7},{9,10},{10,9},{11,... | collective-permute-start | bytes 786440 | tf_op jit(solution)/shard_map/ppermute | solution.py:79
  28.2 14.9 %collective-permute-start.6 = (bf16[128,1024]{1,0:T(8,128)(2,1)S(1)}, bf16[128,1024]{1,0:T(8,128)(2,1)S(1)}, u32[]{:S(2)}, u32[]{:S(2)}) collective-permute-start(bf16[128,1024]{1,0:T(8,128)(2,1)S(1)} %get-tuple-element.33.own_grad), channel_id=1, source_target_pairs={{0,1},{1,0},{2,3},{3,2},{4,5},{5,4},{6,7},{7,6},{8,9},{9,8},{10,11... | collective-permute-start | bytes 786440 | tf_op jit(solution)/shard_map/ppermute | solution.py:82
  28.3 14.8 %collective-permute-start.7 = (bf16[128,1024]{1,0:T(8,128)(2,1)S(1)}, bf16[128,1024]{1,0:T(8,128)(2,1)S(1)}, u32[]{:S(2)}, u32[]{:S(2)}) collective-permute-start(bf16[128,1024]{1,0:T(8,128)(2,1)S(1)} %get-tuple-element.33.own_grad), channel_id=1, source_target_pairs={{1,2},{2,1},{3,4},{4,3},{5,6},{6,5},{7,8},{8,7},{9,10},{10,9},{11,... | collective-permute-start | bytes 786440 | tf_op jit(solution)/shard_map/ppermute | solution.py:79
  36.0 7.0 %collective-permute-start.4 = (f32[24,256]{1,0:T(8,128)S(1)}, f32[24,256]{1,0:T(8,128)S(1)}, u32[]{:S(2)}, u32[]{:S(2)}) collective-permute-start(f32[24,256]{1,0:T(8,128)S(1)} %get-tuple-element.40), channel_id=1, source_target_pairs={{0,1},{1,0},{2,3},{3,2},{4,5},{5,4},{6,7},{7,6},{8,9},{9,8},{10,11... | collective-permute-start | bytes 73736 | tf_op jit(solution)/shard_map/ppermute | solution.py:82
  36.1 7.0 %collective-permute-start.5 = (f32[24,256]{1,0:T(8,128)S(1)}, f32[24,256]{1,0:T(8,128)S(1)}, u32[]{:S(2)}, u32[]{:S(2)}) collective-permute-start(f32[24,256]{1,0:T(8,128)S(1)} %get-tuple-element.40), channel_id=1, source_target_pairs={{1,2},{2,1},{3,4},{4,3},{5,6},{6,5},{7,8},{8,7},{9,10},{10,9},{11,... | collective-permute-start | bytes 73736 | tf_op jit(solution)/shard_map/ppermute | solution.py:79

commit v10 on v9

--- a/solution.py
+++ b/solution.py
@@ -14,7 +14,7 @@
 BF16 = jnp.bfloat16
 I32 = jnp.int32
 VMEM_LIMIT = 28 * 2**20
-PIECES = 6
+PIECES = 2
 
 
 def mm(a, b):
@@ -277,7 +277,7 @@
     partial_out[...] = partial[...] + mm(landing, jnp.concatenate([active, active], 0))
 
 
-def latent_kernel(depth, far, partial, latent_out, normed_out):
+def latent_kernel(depth, far, partial, latent_out, normed_out, normal_out, inv_std_out):
     mesh_rows, channels = partial.shape
     slots = far.shape[0]
     half = channels // 2
@@ -292,22 +292,10 @@
     total = partial[...] + mm(landing, jnp.concatenate([first, second], 1))
     latent = total.astype(BF16)
     latent_out[...] = latent
-    normal, _ = norm_stats(latent)
+    normal, inv_std = norm_stats(latent)
     normed_out[...] = normal.astype(BF16)
-
-
-def project_kernel(normed, grad_hbm, w_qkv_hbm, qkv_out, w_qkv, grad_out, sems):
-    width = w_qkv.shape[1] // PIECES
-    pieces = [pl.ds(c * width, width) for c in range(PIECES)]
-    copies = start_all(
-        [(w_qkv_hbm.at[:, piece], w_qkv.at[:, piece]) for piece in pieces] + [(grad_hbm, grad_out)],
-        sems,
-    )
-    for c in range(PIECES):
-        copies[c].wait()
-        cols = slice(c * width, (c + 1) * width)
-        qkv_out[:, cols] = mm(normed[...], w_qkv[:, cols]).astype(BF16)
-    copies[PIECES].wait()
+    normal_out[...] = normal
+    inv_std_out[...] = jnp.broadcast_to(inv_std, inv_std_out.shape)
 
 
 def halves(rows, scale=None):
@@ -322,6 +310,34 @@
     m = stacked.shape[0] // 2
     first = iota((m, stacked.shape[1]), 1) < stacked.shape[1] // 2
     return jnp.where(first, stacked[:m], stacked[m:])
+
+
+def project_kernel(
+    scale, pair, normed, grad_hbm, w_qkv_hbm, qkv_out, w_qkv, grad_out, scores_out, products_out, sems
+):
+    m, channels = normed.shape
+    width = channels // PIECES
+    starts = [part * channels + c * width for c in range(PIECES) for part in range(3)]
+    copies = start_all(
+        [(grad_hbm, grad_out)]
+        + [(w_qkv_hbm.at[:, pl.ds(at, width)], w_qkv.at[:, pl.ds(at, width)]) for at in starts],
+        sems,
+    )
+    for i, at in enumerate(starts):
+        copies[1 + i].wait()
+        cols = slice(at, at + width)
+        qkv_out[:, cols] = mm(normed[...], w_qkv[:, cols]).astype(BF16)
+        if i % 3 < 2:
+            continue
+        if i == 2:
+            copies[0].wait()
+        for p in range(i // 3 * width // pair, (i // 3 + 1) * width // pair):
+            q, k, v = (
+                slice(part * channels + p * pair, part * channels + (p + 1) * pair)
+                for part in range(3)
+            )
+            scores_out[p] = mm_nt(halves(qkv_out[:, q], scale), qkv_out[:, k])
+            products_out[p] = mm_nt(halves(grad_out[:, q]), qkv_out[:, v])
 
 
 def near_places(m):
@@ -337,6 +353,8 @@
     w_qkv,
     own_qkv,
     own_grad,
+    own_scores,
+    own_products,
     window_hbm,
     w_out_hbm,
     cot_hbm,
@@ -355,34 +373,40 @@
     devices = lax.axis_size("node")
     me = lax.axis_index("node")
     near = mm(jnp.concatenate([chip_normed[...], off_normed[...]], 0), w_qkv[:, channels:])
-    near = near.astype(BF16)
-    kv[:m] = near[:m]
-    kv[m : 2 * m] = own_qkv[:, channels:]
-    kv[2 * m :] = near[m:]
+    kv[: 2 * m] = near.astype(BF16)
+    kv[2 * m :] = own_qkv[:, channels:]
     fetch[0].wait()
     row = iota((3 * m, m), 0)
     chip_at, off_at = near_places(m)
-    key_at = jnp.where(row < m, row + chip_at, jnp.where(row < 2 * m, row, row - 2 * m + off_at))
+    key_at = jnp.where(row < m, row + chip_at, jnp.where(row < 2 * m, row - m + off_at, row - m))
     query_at = iota((3 * m, m), 1) + m
-    inside = row < jnp.where((me == 0) | (me == devices - 1), 2 * m, 3 * m)
-    keep = (
-        inside & (key_at >= query_at - window[0:1, :]) & (key_at <= query_at + window[1:2, :])
-    )
-    bias = jnp.transpose(jnp.where(keep, 0.0, -jnp.inf).astype(F32))
+    missing = (row >= m) & (row < 2 * m) & ((me == 0) | (me == devices - 1))
+    keep = (key_at >= query_at - window[0:1, :]) & (key_at <= query_at + window[1:2, :])
+    bias = jnp.transpose(jnp.where(keep & jnp.logical_not(missing), 0.0, -jnp.inf).astype(F32))
     bias = jnp.concatenate([bias, bias], 0)
     lane = iota((2 * m, LANES), 1)
     stats = jnp.zeros((2 * m, LANES), F32)
+
+    def multiply(p):
+        cols = slice(p * pair, (p + 1) * pair)
+        value_cols = slice(channels + p * pair, channels + (p + 1) * pair)
+        return (
+            mm_nt(halves(own_qkv[:, cols], scale), kv[: 2 * m, cols]),
+            mm_nt(halves(own_grad[:, cols]), kv[: 2 * m, value_cols]),
+        )
+
+    ahead = multiply(0)
     for p in range(pairs):
-        cols = slice(p * pair, (p + 1) * pair)
-        q2 = halves(own_qkv[:, cols], scale)
-        g2 = halves(own_grad[:, cols])
-        scores = mm_nt(q2, kv[:, cols]) + bias
+        scores, grad_prob = ahead
+        if p + 1 < pairs:
+            ahead = multiply(p + 1)
+        scores = jnp.concatenate([scores, own_scores[p]], 1) + bias
+        grad_prob = jnp.concatenate([grad_prob, own_products[p]], 1)
         top = jnp.max(scores, 1, keepdims=True)
         shifted = jnp.exp(scores - top)
         inv_sum = 1.0 / jnp.sum(shifted, 1, keepdims=True)
         probs = shifted * inv_sum
         weights_out[p] = probs.astype(BF16)
-        grad_prob = mm_nt(g2, kv[:, channels + p * pair : channels + (p + 1) * pair])
         delta = jnp.sum(probs * grad_prob, 1, keepdims=True)
         scores_out[p] = (probs * (grad_prob - delta)).astype(BF16)
         stats = jnp.where(lane == p, top, stats)
@@ -421,8 +445,8 @@
         value = kv[:, channels + p * pair : channels + (p + 1) * pair]
         attention[:, cols] = merge(mm(weights[p], value)).astype(BF16)
         grad_query[:, cols] = (merge(mm(grad_scores[p], key)) * scale).astype(BF16)
-        grad_key[:, cols] = mm_tn(grad_scores[p, :, m : 2 * m], halves(own_qkv[:, cols], scale))
-        grad_value[:, cols] = mm_tn(weights[p, :, m : 2 * m], halves(own_grad[:, cols]))
+        grad_key[:, cols] = mm_tn(grad_scores[p, :, 2 * m :], halves(own_qkv[:, cols], scale))
+        grad_value[:, cols] = mm_tn(weights[p, :, 2 * m :], halves(own_grad[:, cols]))
     mesh_out[...] = (latent[...].astype(F32) + mm(attention[...], w_out[...])).astype(BF16)
     grad_normed[...] = mm_nt(grad_query[...], w_qkv[:, :channels])
     near = mm(jnp.concatenate([chip_normed[...], off_normed[...]], 0), w_qkv[:, :channels])
@@ -444,12 +468,12 @@
     grad_value,
     grad_normed,
     w_qkv,
-    latent,
+    normal,
+    inv_std,
     cot,
     grad_out,
-    grad_kv,
 ):
-    m, channels = latent.shape
+    m, channels = normal.shape
     reach = [meta_of(side, count)[:8, 2 * LANES : 2 * LANES + m] for side in (chip_first, off_first)]
     reach = jnp.concatenate(reach, 1)
     key_at = iota((m, 2 * m), 0) + m
@@ -464,14 +488,24 @@
     for h in range(2):
         lanes = slice(h * m, (h + 1) * m)
         stats.append(jnp.concatenate([chip_stats[:, lanes], off_stats[:, lanes]], 1))
-    for p in range(pairs):
+
+    def multiply(p):
         cols = slice(p * pair, (p + 1) * pair)
         key2 = halves(own_qkv[:, channels + p * pair : channels + (p + 1) * pair])
         value2 = halves(own_qkv[:, 2 * channels + p * pair : 2 * channels + (p + 1) * pair])
         query = near_q[:, cols]
         grad = jnp.concatenate([chip_grad[:, cols], off_grad[:, cols]], 0)
-        scores = mm_nt(key2, query)
-        grad_prob = mm_nt(value2, grad)
+        return query, grad, mm_nt(key2, query), mm_nt(value2, grad)
+
+    total = grad_normed[...]
+    group = pairs // 2
+    gks, gvs = [], []
+    ahead = multiply(0)
+    for p in range(pairs):
+        cols = slice(p * pair, (p + 1) * pair)
+        query, grad, scores, grad_prob = ahead
+        if p + 1 < pairs:
+            ahead = multiply(p + 1)
         weights, grad_scores = [], []
         for h in range(2):
             half = slice(h * m, (h + 1) * m)
@@ -481,16 +515,21 @@
             grad_scores.append((probs * (grad_prob[half] - delta)).astype(BF16))
         gk = grad_key[:, cols] + merge(mm(jnp.concatenate(grad_scores, 0), query))
         gv = grad_value[:, cols] + merge(mm(jnp.concatenate(weights, 0), grad))
-        grad_kv[:, cols] = gk.astype(BF16)
-        grad_kv[:, channels + p * pair : channels + (p + 1) * pair] = gv.astype(BF16)
-    total = grad_normed[...] + mm_nt(grad_kv[...], w_qkv[:, channels:])
-    normal, inv_std = norm_stats(latent[...])
+        gks.append(gk.astype(BF16))
+        gvs.append(gv.astype(BF16))
+        if len(gks) == group:
+            at = channels + (p + 1 - group) * pair
+            width = group * pair
+            total = total + mm_nt(jnp.concatenate(gks, 1), w_qkv[:, at : at + width])
+            at = at + channels
+            total = total + mm_nt(jnp.concatenate(gvs, 1), w_qkv[:, at : at + width])
+            gks, gvs = [], []
     centred = (
         total
         - jnp.mean(total, -1, keepdims=True)
-        - normal * jnp.mean(total * normal, -1, keepdims=True)
-    )
-    grad_out[...] = (cot[...].astype(F32) + inv_std * centred).astype(BF16)
+        - normal[...] * jnp.mean(total * normal[...], -1, keepdims=True)
+    )
+    grad_out[...] = (cot[...].astype(F32) + inv_std[:, :1] * centred).astype(BF16)
 
 
 def body(
@@ -568,16 +607,20 @@
         name="side",
         flops=8 * 10**9,
     )
-    latent, normed = call(
-        functools.partial(latent_kernel, far_depth), [rows, rows], [got_far, partial], name="latent"
+    latent, normed, normal, inv_std = call(
+        functools.partial(latent_kernel, far_depth),
+        [rows, rows, ((m, channels), F32), ((m, LANES), F32)],
+        [got_far, partial],
+        name="latent",
     )
     chip_normed, off_normed = exchange(normed, normed, "node")
-    own_qkv, w_qkv, own_grad = call(
-        project_kernel,
-        [((m, 3 * channels), BF16), (w_qkv.shape, BF16), rows],
+    own_block = ((pairs, 2 * m, m), F32)
+    own_qkv, w_qkv, own_grad, own_scores, own_products = call(
+        functools.partial(project_kernel, scale, pair),
+        [((m, 3 * channels), BF16), (w_qkv.shape, BF16), rows, own_block, own_block],
         [normed, own_grad, w_qkv],
         hbm=(1, 2),
-        scratch=[dma(PIECES + 1)],
+        scratch=[dma(3 * PIECES + 1)],
         name="project",
     )
     chip_grad, off_grad = exchange(own_grad, own_grad, "node")
@@ -592,8 +635,9 @@
             (w_out.shape, BF16),
             rows,
         ],
-        [chip_normed, off_normed, w_qkv, own_qkv, own_grad, window, w_out, cotangent],
-        hbm=(5, 6, 7),
+        [chip_normed, off_normed, w_qkv, own_qkv, own_grad, own_scores, own_products]
+        + [window, w_out, cotangent],
+        hbm=(7, 8, 9),
         scratch=like(window) + [dma(3)],
         name="attend",
     )
@@ -638,10 +682,10 @@
             grad_value,
             grad_normed,
             w_qkv,
-            latent,
+            normal,
+            inv_std,
             cotangent,
         ],
-        scratch=[pltpu.VMEM((m, 2 * channels), BF16)],
         name="finish",
     )
     return (mesh_out, mesh_grad)

time: 47.8 us -> 47.2 us (0.987)
  starting transfers between devices: 20.6 us -> 19.9 us
    ppermute x4, starting transfers between devices: 13.7 us -> 13.1 us  [exchange(): lax.ppermute(off_message, axis, [p for i in range(1, n - 1, 2) for p in (...]
  transfers between devices with their start and end apart: 9 -> 9, of which waited for: 1 -> 1; matrix products, arithmetic and copies ran while one was open for 0% -> 0% of each run, Pallas kernels for 34% -> 36%
where the time goes in v10:
time: 47.2 us; the launch traced here: 46.8 us
  Pallas kernels  24.5 us (52%)
  starting transfers between devices  19.9 us (42%)
  waiting for transfers between devices  1.62 us (3%)
  between operations  0.77 us (2%)
    pallas_call x8, Pallas kernels, call(): pl.pallas_call(kernel, out_shape=[(pltpu.HBM if i in hbm_outs else jax.Sh...  24.5 us
    ppermute x4, starting transfers between devices, exchange(): lax.ppermute(off_message, axis, [p for i in range(1, n - 1, 2) for p in (...  13.1 us
    all_to_all x1, starting transfers between devices, body(): lax.all_to_all(far_message.reshape(devices, 2 * far_depth, far_block[1]),...  5.33 us
    all_to_all x1, waiting for transfers between devices, body(): lax.all_to_all(far_message.reshape(devices, 2 * far_depth, far_block[1]),...  1.6 us
    ppermute x4, starting transfers between devices, exchange(): lax.ppermute(chip_message, axis, [p for i in range(0, n, 2) for p in ((i,...  1.49 us
  transfers between devices with their start and end apart: 9, of which 1 were waited for; matrix products, arithmetic and copies ran while one was open for 0% of the time, Pallas kernels for 36%

profile of v10, /device:TPU:1, one launch (start us, length us, event | category | flops | bytes accessed | tf_op | source)
XLA Modules:
  0.0 46.8 jit_solution(7608610243189861169)
XLA Ops:
  0.6 3.4 %pack.1 = (bf16[128,640]{1,0:T(8,128)(2,1)}, bf16[144,1024]{1,0:T(8,128)(2,1)}, bf16[144,1024]{1,0:T(8,128)(2,1)}, bf16[1024,1024]{1,0:T(8,128)(2,1)S(1)}) custom-call(bf16[512,1024]{1,0:T(8,128)(2,1)} %grid_hbm.3, s32[2,128]{1,0:T(2,128)} %window_hbm.3, s32[32,128]{1,0:T(8,128)} %bitcast.12, s32[32,128]{1,0:T(8,128)} %bitcast.13, s32[1,2]{1,0:T(1,128)} %bitcast.16, ...), custom_call_target="tpu_custom_call" | custom-call | tf_op jit(solution)/shard_map/pack/pallas_call | solution.py:47
  4.0 0.1 collective-permute-start
  4.1 4.5 %collective-permute-start.1 = (bf16[144,1024]{1,0:T(8,128)(2,1)}, bf16[144,1024]{1,0:T(8,128)(2,1)S(1)}, u32[]{:S(2)}, u32[]{:S(2)}) collective-permute-start(bf16[144,1024]{1,0:T(8,128)(2,1)} %get-tuple-element.30), channel_id=1, source_target_pairs={{1,2},{2,1},{3,4},{4,3},{5,6},{6,5},{7,8},{8,7},{9,10},{10,9},{11,... | collective-permute-start | bytes 884744 | tf_op jit(solution)/shard_map/ppermute | solution.py:79
  8.6 5.3 %all-to-all-start = ((bf16[16,8,640]{2,1,0:T(8,128)(2,1)}), bf16[16,8,640]{2,1,0:T(8,128)(2,1)S(1)}, u32[]{:S(2)}, u32[]{:S(2)}) async-start(bf16[16,8,640]{2,1,0:T(8,128)(2,1)} %bitcast.11), calls=%async_computation | async-start | bytes 327680 | tf_op jit(solution)/shard_map/all_to_all | solution.py:585
  13.9 4.3 %own.1 = (f32[128,1024]{1,0:T(8,128)S(1)}, bf16[128,1024]{1,0:T(8,128)(2,1)}) custom-call(bf16[512,1024]{1,0:T(8,128)(2,1)} %grid_hbm.3, bf16[128,1024]{1,0:T(8,128)(2,1)} %mesh_in_hbm.1, s32[8,128]{1,0:T(8,128)} %bitcast.14, s32[8,128]{1,0:T(8,128)} %bitcast.15, bf16[128,1024]{1,0:T(8,128)(2,1)} %cot_hbm.3, bf16[1024,1024]{1,0:T(8,128)(2,1)} %w_out_hbm.3, ...), custom_call_target="tpu_custom_call" | custom-call | tf_op jit(solution)/shard_map/own/pallas_call | solution.py:47
  18.3 0.0 collective-permute-done.chip.chip_first
  18.3 0.0 collective-permute-done.1.off.off_first
  18.3 1.4 %side.1.partial = f32[128,1024]{1,0:T(8,128)S(1)} custom-call(bf16[144,1024]{1,0:T(8,128)(2,1)S(1)} %collective-permute-done.chip.chip_first, bf16[144,1024]{1,0:T(8,128)(2,1)S(1)} %collective-permute-done.1.off.off_first, bf16[1024,1024]{1,0:T(8,128)(2,1)S(1)} %get-tuple-element.31.w_edge, f32[128,1024]{1,0:T(8,128)S(1)} %get-tuple-element.32.partial), custom_call_target="tpu_custom_call" | custom-call | flops 8000000000 | tf_op jit(solution)/shard_map/side/pallas_call | solution.py:47
  19.7 1.6 %all-to-all-done = bf16[16,8,640]{2,1,0:T(8,128)(2,1)S(1)} async-done(((bf16[16,8,640]{2,1,0:T(8,128)(2,1)}), bf16[16,8,640]{2,1,0:T(8,128)(2,1)S(1)}, u32[]{:S(2)}, u32[]{:S(2)}) %all-to-all-start) | async-done | bytes 163872 | tf_op jit(solution)/shard_map/all_to_all | solution.py:585
  21.3 0.5 %latent.1 = (bf16[128,1024]{1,0:T(8,128)(2,1)S(1)}, bf16[128,1024]{1,0:T(8,128)(2,1)S(1)}, f32[128,1024]{1,0:T(8,128)S(1)}, f32[128,128]{1,0:T(8,128)S(1)}) custom-call(bf16[128,640]{1,0:T(8,128)(2,1)S(1)} %bitcast.10, f32[128,1024]{1,0:T(8,128)S(1)} %side.1.partial), custom_call_target="tpu_custom_call" | custom-call | tf_op jit(solution)/shard_map/latent/pallas_call | solution.py:47
  21.8 1.2 %collective-permute-start.2 = (bf16[128,1024]{1,0:T(8,128)(2,1)S(1)}, bf16[128,1024]{1,0:T(8,128)(2,1)S(1)}, u32[]{:S(2)}, u32[]{:S(2)}) collective-permute-start(bf16[128,1024]{1,0:T(8,128)(2,1)S(1)} %get-tuple-element.33.normed), channel_id=1, source_target_pairs={{0,1},{1,0},{2,3},{3,2},{4,5},{5,4},{6,7},{7,6},{8,9},{9,8},{10,11... | collective-permute-start | bytes 786440 | tf_op jit(solution)/shard_map/ppermute | solution.py:82
  23.1 1.9 %collective-permute-start.3 = (bf16[128,1024]{1,0:T(8,128)(2,1)S(1)}, bf16[128,1024]{1,0:T(8,128)(2,1)S(1)}, u32[]{:S(2)}, u32[]{:S(2)}) collective-permute-start(bf16[128,1024]{1,0:T(8,128)(2,1)S(1)} %get-tuple-element.33.normed), channel_id=1, source_target_pairs={{1,2},{2,1},{3,4},{4,3},{5,6},{6,5},{7,8},{8,7},{9,10},{10,9},{11,... | collective-permute-start | bytes 786440 | tf_op jit(solution)/shard_map/ppermute | solution.py:79
  25.0 3.9 %project.1 = (bf16[128,3072]{1,0:T(8,128)(2,1)S(1)}, bf16[1024,3072]{1,0:T(8,128)(2,1)S(1)}, bf16[128,1024]{1,0:T(8,128)(2,1)S(1)}, f32[8,256,128]{2,1,0:T(8,128)S(1)}, f32[8,256,128]{2,1,0:T(8,128)S(1)}) custom-call(bf16[128,1024]{1,0:T(8,128)(2,1)S(1)} %get-tuple-element.33.normed, bf16[128,1024]{1,0:T(8,128)(2,1)} %get-tuple-element.34.grad_hbm, ...), custom_call_target="tpu_custom_call" | custom-call | tf_op jit(solution)/shard_map/project/pallas_call | solution.py:47
  28.9 0.1 collective-permute-start.6
  29.0 3.6 %collective-permute-start.7 = (bf16[128,1024]{1,0:T(8,128)(2,1)S(1)}, bf16[128,1024]{1,0:T(8,128)(2,1)S(1)}, u32[]{:S(2)}, u32[]{:S(2)}) collective-permute-start(bf16[128,1024]{1,0:T(8,128)(2,1)S(1)} %get-tuple-element.37.own_grad), channel_id=1, source_target_pairs={{1,2},{2,1},{3,4},{4,3},{5,6},{6,5},{7,8},{8,7},{9,10},{10,9},{11,... | collective-permute-start | bytes 786440 | tf_op jit(solution)/shard_map/ppermute | solution.py:79
  32.6 0.0 collective-permute-done.2.chip_normed
  32.6 0.0 collective-permute-done.3.off_normed
  32.6 4.1 %attend.1 = (f32[24,256]{1,0:T(8,128)S(1)}, bf16[384,2048]{1,0:T(8,128)(2,1)S(1)}, bf16[8,256,384]{2,1,0:T(8,128)(2,1)S(1)}, bf16[8,256,384]{2,1,0:T(8,128)(2,1)...) custom-call(bf16[128,1024]{1,0:T(8,128)(2,1)S(1)} %collective-permute-done.2.chip_normed, ...), custom_call_target="tpu_custom_call" | custom-call | tf_op jit(solution)/shard_map/attend/pallas_call | solution.py:47
  36.8 0.1 collective-permute-start.4
  36.8 3.0 %collective-permute-start.5 = (f32[24,256]{1,0:T(8,128)S(1)}, f32[24,256]{1,0:T(8,128)S(1)}, u32[]{:S(2)}, u32[]{:S(2)}) collective-permute-start(f32[24,256]{1,0:T(8,128)S(1)} %get-tuple-element.46), channel_id=1, source_target_pairs={{1,2},{2,1},{3,4},{4,3},{5,6},{6,5},{7,8},{8,7},{9,10},{10,9},{11,... | collective-permute-start | bytes 73736 | tf_op jit(solution)/shard_map/ppermute | solution.py:79
  39.9 3.3 %product.1 = (bf16[128,1024]{1,0:T(8,128)(2,1)}, f32[128,1024]{1,0:T(8,128)S(1)}, f32[128,1024]{1,0:T(8,128)S(1)}, f32[128,1024]{1,0:T(8,128)S(1)}, bf16[256,1024]{1,0:T(8,128)(2,1)S(1)}) custom-call(bf16[8,256,384]{2,1,0:T(8,128)(2,1)S(1)} %get-tuple-element.40.weights, bf16[8,256,384]{2,1,0:T(8,128)(2,1)S(1)} %get-tuple-element.41.grad_scores, ...), custom_call_target="tpu_custom_call" | custom-call | tf_op jit(solution)/shard_map/product/pallas_call | solution.py:47
  43.1 0.0 collective-permute-done.6.chip_grad
  43.1 0.0 collective-permute-done.7.off_grad
  43.2 0.0 collective-permute-done.4.chip_stats
  43.2 0.0 collective-permute-done.5.off_stats
  43.2 3.6 %finish.1 = bf16[128,1024]{1,0:T(8,128)(2,1)} custom-call(f32[24,256]{1,0:T(8,128)S(1)} %collective-permute-done.4.chip_stats, f32[24,256]{1,0:T(8,128)S(1)} %collective-permute-done.5.off_stats, bf16[144,1024]{1,0:T(8,128)(2,1)S(1)} %collective-permute-done.chip.chip_first, bf16[144,1024]{1,0:T(8,128)(2,1)S(1)} %collective-permute-done.1.off.off_first, ...), custom_call_target="tpu_custom_call" | custom-call | tf_op jit(solution)/shard_map/finish/pallas_call | solution.py:47
Async XLA Ops:
  4.0 14.3 %collective-permute-start = (bf16[144,1024]{1,0:T(8,128)(2,1)}, bf16[144,1024]{1,0:T(8,128)(2,1)S(1)}, u32[]{:S(2)}, u32[]{:S(2)}) collective-permute-start(bf16[144,1024]{1,0:T(8,128)(2,1)} %get-tuple-element.29), channel_id=1, source_target_pairs={{0,1},{1,0},{2,3},{3,2},{4,5},{5,4},{6,7},{7,6},{8,9},{9,8},{10,11... | collective-permute-start | bytes 884744 | tf_op jit(solution)/shard_map/ppermute | solution.py:82
  4.1 14.2 %collective-permute-start.1 = (bf16[144,1024]{1,0:T(8,128)(2,1)}, bf16[144,1024]{1,0:T(8,128)(2,1)S(1)}, u32[]{:S(2)}, u32[]{:S(2)}) collective-permute-start(bf16[144,1024]{1,0:T(8,128)(2,1)} %get-tuple-element.30), channel_id=1, source_target_pairs={{1,2},{2,1},{3,4},{4,3},{5,6},{6,5},{7,8},{8,7},{9,10},{10,9},{11,... | collective-permute-start | bytes 884744 | tf_op jit(solution)/shard_map/ppermute | solution.py:79
  8.6 12.7 %all-to-all-start = ((bf16[16,8,640]{2,1,0:T(8,128)(2,1)}), bf16[16,8,640]{2,1,0:T(8,128)(2,1)S(1)}, u32[]{:S(2)}, u32[]{:S(2)}) async-start(bf16[16,8,640]{2,1,0:T(8,128)(2,1)} %bitcast.11), calls=%async_computation | async-start | bytes 327680 | tf_op jit(solution)/shard_map/all_to_all | solution.py:585
  21.8 10.8 %collective-permute-start.2 = (bf16[128,1024]{1,0:T(8,128)(2,1)S(1)}, bf16[128,1024]{1,0:T(8,128)(2,1)S(1)}, u32[]{:S(2)}, u32[]{:S(2)}) collective-permute-start(bf16[128,1024]{1,0:T(8,128)(2,1)S(1)} %get-tuple-element.33.normed), channel_id=1, source_target_pairs={{0,1},{1,0},{2,3},{3,2},{4,5},{5,4},{6,7},{7,6},{8,9},{9,8},{10,11... | collective-permute-start | bytes 786440 | tf_op jit(solution)/shard_map/ppermute | solution.py:82
  23.1 9.6 %collective-permute-start.3 = (bf16[128,1024]{1,0:T(8,128)(2,1)S(1)}, bf16[128,1024]{1,0:T(8,128)(2,1)S(1)}, u32[]{:S(2)}, u32[]{:S(2)}) collective-permute-start(bf16[128,1024]{1,0:T(8,128)(2,1)S(1)} %get-tuple-element.33.normed), channel_id=1, source_target_pairs={{1,2},{2,1},{3,4},{4,3},{5,6},{6,5},{7,8},{8,7},{9,10},{10,9},{11,... | collective-permute-start | bytes 786440 | tf_op jit(solution)/shard_map/ppermute | solution.py:79
  28.9 14.3 %collective-permute-start.6 = (bf16[128,1024]{1,0:T(8,128)(2,1)S(1)}, bf16[128,1024]{1,0:T(8,128)(2,1)S(1)}, u32[]{:S(2)}, u32[]{:S(2)}) collective-permute-start(bf16[128,1024]{1,0:T(8,128)(2,1)S(1)} %get-tuple-element.37.own_grad), channel_id=1, source_target_pairs={{0,1},{1,0},{2,3},{3,2},{4,5},{5,4},{6,7},{7,6},{8,9},{9,8},{10,11... | collective-permute-start | bytes 786440 | tf_op jit(solution)/shard_map/ppermute | solution.py:82
  29.0 14.2 %collective-permute-start.7 = (bf16[128,1024]{1,0:T(8,128)(2,1)S(1)}, bf16[128,1024]{1,0:T(8,128)(2,1)S(1)}, u32[]{:S(2)}, u32[]{:S(2)}) collective-permute-start(bf16[128,1024]{1,0:T(8,128)(2,1)S(1)} %get-tuple-element.37.own_grad), channel_id=1, source_target_pairs={{1,2},{2,1},{3,4},{4,3},{5,6},{6,5},{7,8},{8,7},{9,10},{10,9},{11,... | collective-permute-start | bytes 786440 | tf_op jit(solution)/shard_map/ppermute | solution.py:79
  36.8 6.4 %collective-permute-start.4 = (f32[24,256]{1,0:T(8,128)S(1)}, f32[24,256]{1,0:T(8,128)S(1)}, u32[]{:S(2)}, u32[]{:S(2)}) collective-permute-start(f32[24,256]{1,0:T(8,128)S(1)} %get-tuple-element.46), channel_id=1, source_target_pairs={{0,1},{1,0},{2,3},{3,2},{4,5},{5,4},{6,7},{7,6},{8,9},{9,8},{10,11... | collective-permute-start | bytes 73736 | tf_op jit(solution)/shard_map/ppermute | solution.py:82
  36.8 6.3 %collective-permute-start.5 = (f32[24,256]{1,0:T(8,128)S(1)}, f32[24,256]{1,0:T(8,128)S(1)}, u32[]{:S(2)}, u32[]{:S(2)}) collective-permute-start(f32[24,256]{1,0:T(8,128)S(1)} %get-tuple-element.46), channel_id=1, source_target_pairs={{1,2},{2,1},{3,4},{4,3},{5,6},{6,5},{7,8},{8,7},{9,10},{10,9},{11,... | collective-permute-start | bytes 73736 | tf_op jit(solution)/shard_map/ppermute | solution.py:79

commit v11 on v10

--- a/solution.py
+++ b/solution.py
@@ -372,8 +372,18 @@
     pairs = channels // pair
     devices = lax.axis_size("node")
     me = lax.axis_index("node")
-    near = mm(jnp.concatenate([chip_normed[...], off_normed[...]], 0), w_qkv[:, channels:])
-    kv[: 2 * m] = near.astype(BF16)
+    near = jnp.concatenate([chip_normed[...], off_normed[...]], 0)
+
+    def bring(group):
+        blocks = []
+        for part in range(2):
+            at = part * channels + group * 2 * pair
+            block = mm(near, w_qkv[:, channels + at : channels + at + 2 * pair]).astype(BF16)
+            kv[: 2 * m, at : at + 2 * pair] = block
+            blocks.append(block)
+        return blocks
+
+    brought = {0: bring(0)}
     kv[2 * m :] = own_qkv[:, channels:]
     fetch[0].wait()
     row = iota((3 * m, m), 0)
@@ -389,16 +399,18 @@
 
     def multiply(p):
         cols = slice(p * pair, (p + 1) * pair)
-        value_cols = slice(channels + p * pair, channels + (p + 1) * pair)
+        keys, values = (b[:, p % 2 * pair : (p % 2 + 1) * pair] for b in brought[p // 2])
         return (
-            mm_nt(halves(own_qkv[:, cols], scale), kv[: 2 * m, cols]),
-            mm_nt(halves(own_grad[:, cols]), kv[: 2 * m, value_cols]),
+            mm_nt(halves(own_qkv[:, cols], scale), keys),
+            mm_nt(halves(own_grad[:, cols]), values),
         )
 
     ahead = multiply(0)
     for p in range(pairs):
         scores, grad_prob = ahead
         if p + 1 < pairs:
+            if p % 2 == 0 and p + 2 < pairs:
+                brought[p // 2 + 1] = bring(p // 2 + 1)
             ahead = multiply(p + 1)
         scores = jnp.concatenate([scores, own_scores[p]], 1) + bias
         grad_prob = jnp.concatenate([grad_prob, own_products[p]], 1)
@@ -430,27 +442,36 @@
     w_qkv,
     chip_normed,
     off_normed,
-    mesh_out,
+    mesh_out_hbm,
     grad_normed,
     grad_key,
     grad_value,
     near_q_out,
     attention,
     grad_query,
+    mesh_out,
+    sems,
 ):
     m, channels = latent.shape
-    for p in range(channels // pair):
+    pairs = channels // pair
+    for p in range(pairs):
         cols = slice(p * pair, (p + 1) * pair)
-        key = kv[:, cols]
         value = kv[:, channels + p * pair : channels + (p + 1) * pair]
         attention[:, cols] = merge(mm(weights[p], value)).astype(BF16)
-        grad_query[:, cols] = (merge(mm(grad_scores[p], key)) * scale).astype(BF16)
+    mesh_out[...] = (latent[...].astype(F32) + mm(attention[...], w_out[...])).astype(BF16)
+    out = pltpu.make_async_copy(mesh_out, mesh_out_hbm, sems.at[0])
+    out.start()
+    for p in range(pairs):
+        cols = slice(p * pair, (p + 1) * pair)
+        grad_query[:, cols] = (merge(mm(grad_scores[p], kv[:, cols])) * scale).astype(BF16)
+    for p in range(pairs):
+        cols = slice(p * pair, (p + 1) * pair)
         grad_key[:, cols] = mm_tn(grad_scores[p, :, 2 * m :], halves(own_qkv[:, cols], scale))
         grad_value[:, cols] = mm_tn(weights[p, :, 2 * m :], halves(own_grad[:, cols]))
-    mesh_out[...] = (latent[...].astype(F32) + mm(attention[...], w_out[...])).astype(BF16)
     grad_normed[...] = mm_nt(grad_query[...], w_qkv[:, :channels])
     near = mm(jnp.concatenate([chip_normed[...], off_normed[...]], 0), w_qkv[:, :channels])
     near_q_out[...] = near.astype(BF16) * jnp.asarray(scale, BF16)
+    out.wait()
 
 
 def finish_kernel(
@@ -663,7 +684,8 @@
             chip_normed,
             off_normed,
         ],
-        scratch=[pltpu.VMEM((m, channels), BF16)] * 2,
+        hbm_outs=(0,),
+        scratch=[pltpu.VMEM((m, channels), BF16)] * 3 + [dma(1)],
         name="product",
     )
     (mesh_grad,) = call(

time: 47.2 us -> 46.9 us (level)
  no operation moved by 1% of the time
where the time goes in v11:
time: 46.9 us; the launch traced here: 46.4 us
  Pallas kernels  24.1 us (51%)
  starting transfers between devices  19.9 us (42%)
  waiting for transfers between devices  1.62 us (3%)
  between operations  0.8 us (2%)
    pallas_call x8, Pallas kernels, call(): pl.pallas_call(kernel, out_shape=[(pltpu.HBM if i in hbm_outs else jax.Sh...  24.1 us
    ppermute x4, starting transfers between devices, exchange(): lax.ppermute(off_message, axis, [p for i in range(1, n - 1, 2) for p in (...  13.1 us
    all_to_all x1, starting transfers between devices, body(): lax.all_to_all(far_message.reshape(devices, 2 * far_depth, far_block[1]),...  5.33 us
    all_to_all x1, waiting for transfers between devices, body(): lax.all_to_all(far_message.reshape(devices, 2 * far_depth, far_block[1]),...  1.6 us
    ppermute x4, starting transfers between devices, exchange(): lax.ppermute(chip_message, axis, [p for i in range(0, n, 2) for p in ((i,...  1.49 us
  transfers between devices with their start and end apart: 9, of which 1 were waited for; matrix products, arithmetic and copies ran while one was open for 0% of the time, Pallas kernels for 36%

profile of v11, /device:TPU:1, one launch (start us, length us, event | category | flops | bytes accessed | tf_op | source)
XLA Modules:
  0.0 46.4 jit_solution(3977983541485672925)
XLA Ops:
  0.6 3.4 %pack.1 = (bf16[128,640]{1,0:T(8,128)(2,1)}, bf16[144,1024]{1,0:T(8,128)(2,1)}, bf16[144,1024]{1,0:T(8,128)(2,1)}, bf16[1024,1024]{1,0:T(8,128)(2,1)S(1)}) custom-call(bf16[512,1024]{1,0:T(8,128)(2,1)} %grid_hbm.3, s32[2,128]{1,0:T(2,128)} %window_hbm.3, s32[32,128]{1,0:T(8,128)} %bitcast.12, s32[32,128]{1,0:T(8,128)} %bitcast.13, s32[1,2]{1,0:T(1,128)} %bitcast.16, ...), custom_call_target="tpu_custom_call" | custom-call | tf_op jit(solution)/shard_map/pack/pallas_call | solution.py:47
  4.0 0.1 collective-permute-start
  4.1 4.5 %collective-permute-start.1 = (bf16[144,1024]{1,0:T(8,128)(2,1)}, bf16[144,1024]{1,0:T(8,128)(2,1)S(1)}, u32[]{:S(2)}, u32[]{:S(2)}) collective-permute-start(bf16[144,1024]{1,0:T(8,128)(2,1)} %get-tuple-element.30), channel_id=1, source_target_pairs={{1,2},{2,1},{3,4},{4,3},{5,6},{6,5},{7,8},{8,7},{9,10},{10,9},{11,... | collective-permute-start | bytes 884744 | tf_op jit(solution)/shard_map/ppermute | solution.py:79
  8.6 5.3 %all-to-all-start = ((bf16[16,8,640]{2,1,0:T(8,128)(2,1)}), bf16[16,8,640]{2,1,0:T(8,128)(2,1)S(1)}, u32[]{:S(2)}, u32[]{:S(2)}) async-start(bf16[16,8,640]{2,1,0:T(8,128)(2,1)} %bitcast.11), calls=%async_computation | async-start | bytes 327680 | tf_op jit(solution)/shard_map/all_to_all | solution.py:606
  13.9 4.3 %own.1 = (f32[128,1024]{1,0:T(8,128)S(1)}, bf16[128,1024]{1,0:T(8,128)(2,1)}) custom-call(bf16[512,1024]{1,0:T(8,128)(2,1)} %grid_hbm.3, bf16[128,1024]{1,0:T(8,128)(2,1)} %mesh_in_hbm.1, s32[8,128]{1,0:T(8,128)} %bitcast.14, s32[8,128]{1,0:T(8,128)} %bitcast.15, bf16[128,1024]{1,0:T(8,128)(2,1)} %cot_hbm.3, bf16[1024,1024]{1,0:T(8,128)(2,1)} %w_out_hbm.3, ...), custom_call_target="tpu_custom_call" | custom-call | tf_op jit(solution)/shard_map/own/pallas_call | solution.py:47
  18.3 0.0 collective-permute-done.chip.chip_first
  18.3 0.0 collective-permute-done.1.off.off_first
  18.3 1.4 %side.1.partial = f32[128,1024]{1,0:T(8,128)S(1)} custom-call(bf16[144,1024]{1,0:T(8,128)(2,1)S(1)} %collective-permute-done.chip.chip_first, bf16[144,1024]{1,0:T(8,128)(2,1)S(1)} %collective-permute-done.1.off.off_first, bf16[1024,1024]{1,0:T(8,128)(2,1)S(1)} %get-tuple-element.31.w_edge, f32[128,1024]{1,0:T(8,128)S(1)} %get-tuple-element.32.partial), custom_call_target="tpu_custom_call" | custom-call | flops 8000000000 | tf_op jit(solution)/shard_map/side/pallas_call | solution.py:47
  19.7 1.6 %all-to-all-done = bf16[16,8,640]{2,1,0:T(8,128)(2,1)S(1)} async-done(((bf16[16,8,640]{2,1,0:T(8,128)(2,1)}), bf16[16,8,640]{2,1,0:T(8,128)(2,1)S(1)}, u32[]{:S(2)}, u32[]{:S(2)}) %all-to-all-start) | async-done | bytes 163872 | tf_op jit(solution)/shard_map/all_to_all | solution.py:606
  21.3 0.5 %latent.1 = (bf16[128,1024]{1,0:T(8,128)(2,1)S(1)}, bf16[128,1024]{1,0:T(8,128)(2,1)S(1)}, f32[128,1024]{1,0:T(8,128)S(1)}, f32[128,128]{1,0:T(8,128)S(1)}) custom-call(bf16[128,640]{1,0:T(8,128)(2,1)S(1)} %bitcast.10, f32[128,1024]{1,0:T(8,128)S(1)} %side.1.partial), custom_call_target="tpu_custom_call" | custom-call | tf_op jit(solution)/shard_map/latent/pallas_call | solution.py:47
  21.8 1.2 %collective-permute-start.2 = (bf16[128,1024]{1,0:T(8,128)(2,1)S(1)}, bf16[128,1024]{1,0:T(8,128)(2,1)S(1)}, u32[]{:S(2)}, u32[]{:S(2)}) collective-permute-start(bf16[128,1024]{1,0:T(8,128)(2,1)S(1)} %get-tuple-element.33.normed), channel_id=1, source_target_pairs={{0,1},{1,0},{2,3},{3,2},{4,5},{5,4},{6,7},{7,6},{8,9},{9,8},{10,11... | collective-permute-start | bytes 786440 | tf_op jit(solution)/shard_map/ppermute | solution.py:82
  23.1 1.9 %collective-permute-start.3 = (bf16[128,1024]{1,0:T(8,128)(2,1)S(1)}, bf16[128,1024]{1,0:T(8,128)(2,1)S(1)}, u32[]{:S(2)}, u32[]{:S(2)}) collective-permute-start(bf16[128,1024]{1,0:T(8,128)(2,1)S(1)} %get-tuple-element.33.normed), channel_id=1, source_target_pairs={{1,2},{2,1},{3,4},{4,3},{5,6},{6,5},{7,8},{8,7},{9,10},{10,9},{11,... | collective-permute-start | bytes 786440 | tf_op jit(solution)/shard_map/ppermute | solution.py:79
  25.0 3.9 %project.1 = (bf16[128,3072]{1,0:T(8,128)(2,1)S(1)}, bf16[1024,3072]{1,0:T(8,128)(2,1)S(1)}, bf16[128,1024]{1,0:T(8,128)(2,1)S(1)}, f32[8,256,128]{2,1,0:T(8,128)S(1)}, f32[8,256,128]{2,1,0:T(8,128)S(1)}) custom-call(bf16[128,1024]{1,0:T(8,128)(2,1)S(1)} %get-tuple-element.33.normed, bf16[128,1024]{1,0:T(8,128)(2,1)} %get-tuple-element.34.grad_hbm, ...), custom_call_target="tpu_custom_call" | custom-call | tf_op jit(solution)/shard_map/project/pallas_call | solution.py:47
  28.9 0.1 collective-permute-start.6
  29.0 3.6 %collective-permute-start.7 = (bf16[128,1024]{1,0:T(8,128)(2,1)S(1)}, bf16[128,1024]{1,0:T(8,128)(2,1)S(1)}, u32[]{:S(2)}, u32[]{:S(2)}) collective-permute-start(bf16[128,1024]{1,0:T(8,128)(2,1)S(1)} %get-tuple-element.37.own_grad), channel_id=1, source_target_pairs={{1,2},{2,1},{3,4},{4,3},{5,6},{6,5},{7,8},{8,7},{9,10},{10,9},{11,... | collective-permute-start | bytes 786440 | tf_op jit(solution)/shard_map/ppermute | solution.py:79
  32.6 0.0 collective-permute-done.2.chip_normed
  32.6 0.0 collective-permute-done.3.off_normed
  32.6 3.8 %attend.1 = (f32[24,256]{1,0:T(8,128)S(1)}, bf16[384,2048]{1,0:T(8,128)(2,1)S(1)}, bf16[8,256,384]{2,1,0:T(8,128)(2,1)S(1)}, bf16[8,256,384]{2,1,0:T(8,128)(2,1)...) custom-call(bf16[128,1024]{1,0:T(8,128)(2,1)S(1)} %collective-permute-done.2.chip_normed, ...), custom_call_target="tpu_custom_call" | custom-call | tf_op jit(solution)/shard_map/attend/pallas_call | solution.py:47
  36.4 0.1 collective-permute-start.4
  36.5 3.0 %collective-permute-start.5 = (f32[24,256]{1,0:T(8,128)S(1)}, f32[24,256]{1,0:T(8,128)S(1)}, u32[]{:S(2)}, u32[]{:S(2)}) collective-permute-start(f32[24,256]{1,0:T(8,128)S(1)} %get-tuple-element.46), channel_id=1, source_target_pairs={{1,2},{2,1},{3,4},{4,3},{5,6},{6,5},{7,8},{8,7},{9,10},{10,9},{11,... | collective-permute-start | bytes 73736 | tf_op jit(solution)/shard_map/ppermute | solution.py:79
  39.5 3.3 %product.1 = (bf16[128,1024]{1,0:T(8,128)(2,1)}, f32[128,1024]{1,0:T(8,128)S(1)}, f32[128,1024]{1,0:T(8,128)S(1)}, f32[128,1024]{1,0:T(8,128)S(1)}, bf16[256,1024]{1,0:T(8,128)(2,1)S(1)}) custom-call(bf16[8,256,384]{2,1,0:T(8,128)(2,1)S(1)} %get-tuple-element.40.weights, bf16[8,256,384]{2,1,0:T(8,128)(2,1)S(1)} %get-tuple-element.41.grad_scores, ...), custom_call_target="tpu_custom_call" | custom-call | tf_op jit(solution)/shard_map/product/pallas_call | solution.py:47
  42.8 0.0 collective-permute-done.6.chip_grad
  42.8 0.0 collective-permute-done.7.off_grad
  42.8 0.0 collective-permute-done.4.chip_stats
  42.9 0.0 collective-permute-done.5.off_stats
  42.9 3.6 %finish.1 = bf16[128,1024]{1,0:T(8,128)(2,1)} custom-call(f32[24,256]{1,0:T(8,128)S(1)} %collective-permute-done.4.chip_stats, f32[24,256]{1,0:T(8,128)S(1)} %collective-permute-done.5.off_stats, bf16[144,1024]{1,0:T(8,128)(2,1)S(1)} %collective-permute-done.chip.chip_first, bf16[144,1024]{1,0:T(8,128)(2,1)S(1)} %collective-permute-done.1.off.off_first, ...), custom_call_target="tpu_custom_call" | custom-call | tf_op jit(solution)/shard_map/finish/pallas_call | solution.py:47
Async XLA Ops:
  4.0 14.3 %collective-permute-start = (bf16[144,1024]{1,0:T(8,128)(2,1)}, bf16[144,1024]{1,0:T(8,128)(2,1)S(1)}, u32[]{:S(2)}, u32[]{:S(2)}) collective-permute-start(bf16[144,1024]{1,0:T(8,128)(2,1)} %get-tuple-element.29), channel_id=1, source_target_pairs={{0,1},{1,0},{2,3},{3,2},{4,5},{5,4},{6,7},{7,6},{8,9},{9,8},{10,11... | collective-permute-start | bytes 884744 | tf_op jit(solution)/shard_map/ppermute | solution.py:82
  4.1 14.2 %collective-permute-start.1 = (bf16[144,1024]{1,0:T(8,128)(2,1)}, bf16[144,1024]{1,0:T(8,128)(2,1)S(1)}, u32[]{:S(2)}, u32[]{:S(2)}) collective-permute-start(bf16[144,1024]{1,0:T(8,128)(2,1)} %get-tuple-element.30), channel_id=1, source_target_pairs={{1,2},{2,1},{3,4},{4,3},{5,6},{6,5},{7,8},{8,7},{9,10},{10,9},{11,... | collective-permute-start | bytes 884744 | tf_op jit(solution)/shard_map/ppermute | solution.py:79
  8.6 12.7 %all-to-all-start = ((bf16[16,8,640]{2,1,0:T(8,128)(2,1)}), bf16[16,8,640]{2,1,0:T(8,128)(2,1)S(1)}, u32[]{:S(2)}, u32[]{:S(2)}) async-start(bf16[16,8,640]{2,1,0:T(8,128)(2,1)} %bitcast.11), calls=%async_computation | async-start | bytes 327680 | tf_op jit(solution)/shard_map/all_to_all | solution.py:606
  21.8 10.8 %collective-permute-start.2 = (bf16[128,1024]{1,0:T(8,128)(2,1)S(1)}, bf16[128,1024]{1,0:T(8,128)(2,1)S(1)}, u32[]{:S(2)}, u32[]{:S(2)}) collective-permute-start(bf16[128,1024]{1,0:T(8,128)(2,1)S(1)} %get-tuple-element.33.normed), channel_id=1, source_target_pairs={{0,1},{1,0},{2,3},{3,2},{4,5},{5,4},{6,7},{7,6},{8,9},{9,8},{10,11... | collective-permute-start | bytes 786440 | tf_op jit(solution)/shard_map/ppermute | solution.py:82
  23.1 9.6 %collective-permute-start.3 = (bf16[128,1024]{1,0:T(8,128)(2,1)S(1)}, bf16[128,1024]{1,0:T(8,128)(2,1)S(1)}, u32[]{:S(2)}, u32[]{:S(2)}) collective-permute-start(bf16[128,1024]{1,0:T(8,128)(2,1)S(1)} %get-tuple-element.33.normed), channel_id=1, source_target_pairs={{1,2},{2,1},{3,4},{4,3},{5,6},{6,5},{7,8},{8,7},{9,10},{10,9},{11,... | collective-permute-start | bytes 786440 | tf_op jit(solution)/shard_map/ppermute | solution.py:79
  28.9 13.9 %collective-permute-start.6 = (bf16[128,1024]{1,0:T(8,128)(2,1)S(1)}, bf16[128,1024]{1,0:T(8,128)(2,1)S(1)}, u32[]{:S(2)}, u32[]{:S(2)}) collective-permute-start(bf16[128,1024]{1,0:T(8,128)(2,1)S(1)} %get-tuple-element.37.own_grad), channel_id=1, source_target_pairs={{0,1},{1,0},{2,3},{3,2},{4,5},{5,4},{6,7},{7,6},{8,9},{9,8},{10,11... | collective-permute-start | bytes 786440 | tf_op jit(solution)/shard_map/ppermute | solution.py:82
  29.0 13.9 %collective-permute-start.7 = (bf16[128,1024]{1,0:T(8,128)(2,1)S(1)}, bf16[128,1024]{1,0:T(8,128)(2,1)S(1)}, u32[]{:S(2)}, u32[]{:S(2)}) collective-permute-start(bf16[128,1024]{1,0:T(8,128)(2,1)S(1)} %get-tuple-element.37.own_grad), channel_id=1, source_target_pairs={{1,2},{2,1},{3,4},{4,3},{5,6},{6,5},{7,8},{8,7},{9,10},{10,9},{11,... | collective-permute-start | bytes 786440 | tf_op jit(solution)/shard_map/ppermute | solution.py:79
  36.4 6.5 %collective-permute-start.4 = (f32[24,256]{1,0:T(8,128)S(1)}, f32[24,256]{1,0:T(8,128)S(1)}, u32[]{:S(2)}, u32[]{:S(2)}) collective-permute-start(f32[24,256]{1,0:T(8,128)S(1)} %get-tuple-element.46), channel_id=1, source_target_pairs={{0,1},{1,0},{2,3},{3,2},{4,5},{5,4},{6,7},{7,6},{8,9},{9,8},{10,11... | collective-permute-start | bytes 73736 | tf_op jit(solution)/shard_map/ppermute | solution.py:82
  36.5 6.4 %collective-permute-start.5 = (f32[24,256]{1,0:T(8,128)S(1)}, f32[24,256]{1,0:T(8,128)S(1)}, u32[]{:S(2)}, u32[]{:S(2)}) collective-permute-start(f32[24,256]{1,0:T(8,128)S(1)} %get-tuple-element.46), channel_id=1, source_target_pairs={{1,2},{2,1},{3,4},{4,3},{5,6},{6,5},{7,8},{8,7},{9,10},{10,9},{11,... | collective-permute-start | bytes 73736 | tf_op jit(solution)/shard_map/ppermute | solution.py:79

commit v12 on v11

--- a/solution.py
+++ b/solution.py
@@ -362,6 +362,7 @@
     kv,
     weights_out,
     scores_out,
+    near_q,
     w_out,
     cot,
     window,
@@ -375,6 +376,8 @@
     near = jnp.concatenate([chip_normed[...], off_normed[...]], 0)
 
     def bring(group):
+        cols = slice(group * 2 * pair, (group + 1) * 2 * pair)
+        near_q[:, cols] = mm(near, w_qkv[:, cols]).astype(BF16) * jnp.asarray(scale, BF16)
         blocks = []
         for part in range(2):
             at = part * channels + group * 2 * pair
@@ -440,13 +443,10 @@
     latent,
     w_out,
     w_qkv,
-    chip_normed,
-    off_normed,
     mesh_out_hbm,
     grad_normed,
     grad_key,
     grad_value,
-    near_q_out,
     attention,
     grad_query,
     mesh_out,
@@ -469,8 +469,6 @@
         grad_key[:, cols] = mm_tn(grad_scores[p, :, 2 * m :], halves(own_qkv[:, cols], scale))
         grad_value[:, cols] = mm_tn(weights[p, :, 2 * m :], halves(own_grad[:, cols]))
     grad_normed[...] = mm_nt(grad_query[...], w_qkv[:, :channels])
-    near = mm(jnp.concatenate([chip_normed[...], off_normed[...]], 0), w_qkv[:, :channels])
-    near_q_out[...] = near.astype(BF16) * jnp.asarray(scale, BF16)
     out.wait()
 
 
@@ -519,7 +517,7 @@
         return query, grad, mm_nt(key2, query), mm_nt(value2, grad)
 
     total = grad_normed[...]
-    group = pairs // 2
+    group = 2
     gks, gvs = [], []
     ahead = multiply(0)
     for p in range(pairs):
@@ -646,13 +644,14 @@
     )
     chip_grad, off_grad = exchange(own_grad, own_grad, "node")
     probs = ((pairs, 2 * m, 3 * m), BF16)
-    stats, kv, weights, grad_scores, w_out, cotangent = call(
+    stats, kv, weights, grad_scores, near_q, w_out, cotangent = call(
         functools.partial(attend_kernel, scale, pair),
         [
             ((3 * pairs, 2 * m), F32),
             ((3 * m, 2 * channels), BF16),
             probs,
             probs,
+            ((2 * m, channels), BF16),
             (w_out.shape, BF16),
             rows,
         ],
@@ -663,14 +662,13 @@
         name="attend",
     )
     chip_stats, off_stats = exchange(stats, stats, "node")
-    mesh_out, grad_normed, grad_key, grad_value, near_q = call(
+    mesh_out, grad_normed, grad_key, grad_value = call(
         functools.partial(product_kernel, scale, pair),
         [
             rows,
             ((m, channels), F32),
             ((m, channels), F32),
             ((m, channels), F32),
-            ((2 * m, channels), BF16),
         ],
         [
             weights,
@@ -681,8 +679,6 @@
             latent,
             w_out,
             w_qkv,
-            chip_normed,
-            off_normed,
         ],
         hbm_outs=(0,),
         scratch=[pltpu.VMEM((m, channels), BF16)] * 3 + [dma(1)],

time: 46.9 us -> 46.5 us (level)
  transfers between devices with their start and end apart: 9 -> 9, of which waited for: 1 -> 1; matrix products, arithmetic and copies ran while one was open for 0% -> 0% of each run, Pallas kernels for 36% -> 35%
where the time goes in v12:
time: 46.5 us; the launch traced here: 46.1 us
  Pallas kernels  23.8 us (51%)
  starting transfers between devices  19.9 us (43%)
  waiting for transfers between devices  1.62 us (3%)
  between operations  0.8 us (2%)
    pallas_call x8, Pallas kernels, call(): pl.pallas_call(kernel, out_shape=[(pltpu.HBM if i in hbm_outs else jax.Sh...  23.8 us
    ppermute x4, starting transfers between devices, exchange(): lax.ppermute(off_message, axis, [p for i in range(1, n - 1, 2) for p in (...  13.1 us
    all_to_all x1, starting transfers between devices, body(): lax.all_to_all(far_message.reshape(devices, 2 * far_depth, far_block[1]),...  5.33 us
    all_to_all x1, waiting for transfers between devices, body(): lax.all_to_all(far_message.reshape(devices, 2 * far_depth, far_block[1]),...  1.6 us
    ppermute x4, starting transfers between devices, exchange(): lax.ppermute(chip_message, axis, [p for i in range(0, n, 2) for p in ((i,...  1.49 us
  transfers between devices with their start and end apart: 9, of which 1 were waited for; matrix products, arithmetic and copies ran while one was open for 0% of the time, Pallas kernels for 35%

profile of v12, /device:TPU:1, one launch (start us, length us, event | category | flops | bytes accessed | tf_op | source)
XLA Modules:
  0.0 46.1 jit_solution(14629300782636601290)
XLA Ops:
  0.6 3.4 %pack.1 = (bf16[128,640]{1,0:T(8,128)(2,1)}, bf16[144,1024]{1,0:T(8,128)(2,1)}, bf16[144,1024]{1,0:T(8,128)(2,1)}, bf16[1024,1024]{1,0:T(8,128)(2,1)S(1)}) custom-call(bf16[512,1024]{1,0:T(8,128)(2,1)} %grid_hbm.3, s32[2,128]{1,0:T(2,128)} %window_hbm.3, s32[32,128]{1,0:T(8,128)} %bitcast.12, s32[32,128]{1,0:T(8,128)} %bitcast.13, s32[1,2]{1,0:T(1,128)} %bitcast.16, ...), custom_call_target="tpu_custom_call" | custom-call | tf_op jit(solution)/shard_map/pack/pallas_call | solution.py:47
  4.0 0.1 collective-permute-start
  4.1 4.5 %collective-permute-start.1 = (bf16[144,1024]{1,0:T(8,128)(2,1)}, bf16[144,1024]{1,0:T(8,128)(2,1)S(1)}, u32[]{:S(2)}, u32[]{:S(2)}) collective-permute-start(bf16[144,1024]{1,0:T(8,128)(2,1)} %get-tuple-element.30), channel_id=1, source_target_pairs={{1,2},{2,1},{3,4},{4,3},{5,6},{6,5},{7,8},{8,7},{9,10},{10,9},{11,... | collective-permute-start | bytes 884744 | tf_op jit(solution)/shard_map/ppermute | solution.py:79
  8.6 5.3 %all-to-all-start = ((bf16[16,8,640]{2,1,0:T(8,128)(2,1)}), bf16[16,8,640]{2,1,0:T(8,128)(2,1)S(1)}, u32[]{:S(2)}, u32[]{:S(2)}) async-start(bf16[16,8,640]{2,1,0:T(8,128)(2,1)} %bitcast.11), calls=%async_computation | async-start | bytes 327680 | tf_op jit(solution)/shard_map/all_to_all | solution.py:604
  13.9 4.3 %own.1 = (f32[128,1024]{1,0:T(8,128)S(1)}, bf16[128,1024]{1,0:T(8,128)(2,1)}) custom-call(bf16[512,1024]{1,0:T(8,128)(2,1)} %grid_hbm.3, bf16[128,1024]{1,0:T(8,128)(2,1)} %mesh_in_hbm.1, s32[8,128]{1,0:T(8,128)} %bitcast.14, s32[8,128]{1,0:T(8,128)} %bitcast.15, bf16[128,1024]{1,0:T(8,128)(2,1)} %cot_hbm.3, bf16[1024,1024]{1,0:T(8,128)(2,1)} %w_out_hbm.3, ...), custom_call_target="tpu_custom_call" | custom-call | tf_op jit(solution)/shard_map/own/pallas_call | solution.py:47
  18.3 0.0 collective-permute-done.chip.chip_first
  18.3 0.0 collective-permute-done.1.off.off_first
  18.3 1.4 %side.1.partial = f32[128,1024]{1,0:T(8,128)S(1)} custom-call(bf16[144,1024]{1,0:T(8,128)(2,1)S(1)} %collective-permute-done.chip.chip_first, bf16[144,1024]{1,0:T(8,128)(2,1)S(1)} %collective-permute-done.1.off.off_first, bf16[1024,1024]{1,0:T(8,128)(2,1)S(1)} %get-tuple-element.31.w_edge, f32[128,1024]{1,0:T(8,128)S(1)} %get-tuple-element.32.partial), custom_call_target="tpu_custom_call" | custom-call | flops 8000000000 | tf_op jit(solution)/shard_map/side/pallas_call | solution.py:47
  19.7 1.6 %all-to-all-done = bf16[16,8,640]{2,1,0:T(8,128)(2,1)S(1)} async-done(((bf16[16,8,640]{2,1,0:T(8,128)(2,1)}), bf16[16,8,640]{2,1,0:T(8,128)(2,1)S(1)}, u32[]{:S(2)}, u32[]{:S(2)}) %all-to-all-start) | async-done | bytes 163872 | tf_op jit(solution)/shard_map/all_to_all | solution.py:604
  21.3 0.5 %latent.1 = (bf16[128,1024]{1,0:T(8,128)(2,1)S(1)}, bf16[128,1024]{1,0:T(8,128)(2,1)S(1)}, f32[128,1024]{1,0:T(8,128)S(1)}, f32[128,128]{1,0:T(8,128)S(1)}) custom-call(bf16[128,640]{1,0:T(8,128)(2,1)S(1)} %bitcast.10, f32[128,1024]{1,0:T(8,128)S(1)} %side.1.partial), custom_call_target="tpu_custom_call" | custom-call | tf_op jit(solution)/shard_map/latent/pallas_call | solution.py:47
  21.8 1.2 %collective-permute-start.2 = (bf16[128,1024]{1,0:T(8,128)(2,1)S(1)}, bf16[128,1024]{1,0:T(8,128)(2,1)S(1)}, u32[]{:S(2)}, u32[]{:S(2)}) collective-permute-start(bf16[128,1024]{1,0:T(8,128)(2,1)S(1)} %get-tuple-element.33.normed), channel_id=1, source_target_pairs={{0,1},{1,0},{2,3},{3,2},{4,5},{5,4},{6,7},{7,6},{8,9},{9,8},{10,11... | collective-permute-start | bytes 786440 | tf_op jit(solution)/shard_map/ppermute | solution.py:82
  23.1 1.9 %collective-permute-start.3 = (bf16[128,1024]{1,0:T(8,128)(2,1)S(1)}, bf16[128,1024]{1,0:T(8,128)(2,1)S(1)}, u32[]{:S(2)}, u32[]{:S(2)}) collective-permute-start(bf16[128,1024]{1,0:T(8,128)(2,1)S(1)} %get-tuple-element.33.normed), channel_id=1, source_target_pairs={{1,2},{2,1},{3,4},{4,3},{5,6},{6,5},{7,8},{8,7},{9,10},{10,9},{11,... | collective-permute-start | bytes 786440 | tf_op jit(solution)/shard_map/ppermute | solution.py:79
  25.0 3.9 %project.1 = (bf16[128,3072]{1,0:T(8,128)(2,1)S(1)}, bf16[1024,3072]{1,0:T(8,128)(2,1)S(1)}, bf16[128,1024]{1,0:T(8,128)(2,1)S(1)}, f32[8,256,128]{2,1,0:T(8,128)S(1)}, f32[8,256,128]{2,1,0:T(8,128)S(1)}) custom-call(bf16[128,1024]{1,0:T(8,128)(2,1)S(1)} %get-tuple-element.33.normed, bf16[128,1024]{1,0:T(8,128)(2,1)} %get-tuple-element.34.grad_hbm, ...), custom_call_target="tpu_custom_call" | custom-call | tf_op jit(solution)/shard_map/project/pallas_call | solution.py:47
  28.9 0.1 collective-permute-start.6
  29.0 3.6 %collective-permute-start.7 = (bf16[128,1024]{1,0:T(8,128)(2,1)S(1)}, bf16[128,1024]{1,0:T(8,128)(2,1)S(1)}, u32[]{:S(2)}, u32[]{:S(2)}) collective-permute-start(bf16[128,1024]{1,0:T(8,128)(2,1)S(1)} %get-tuple-element.37.own_grad), channel_id=1, source_target_pairs={{1,2},{2,1},{3,4},{4,3},{5,6},{6,5},{7,8},{8,7},{9,10},{10,9},{11,... | collective-permute-start | bytes 786440 | tf_op jit(solution)/shard_map/ppermute | solution.py:79
  32.6 0.0 collective-permute-done.2.chip_normed
  32.6 0.0 collective-permute-done.3.off_normed
  32.6 3.8 %attend.1 = (f32[24,256]{1,0:T(8,128)S(1)}, bf16[384,2048]{1,0:T(8,128)(2,1)S(1)}, bf16[8,256,384]{2,1,0:T(8,128)(2,1)S(1)}, bf16[8,256,384]{2,1,0:T(8,128)(2,1)...) custom-call(bf16[128,1024]{1,0:T(8,128)(2,1)S(1)} %collective-permute-done.2.chip, ...), custom_call_target="tpu_custom_call" | custom-call | tf_op jit(solution)/shard_map/attend/pallas_call | solution.py:47
  36.4 0.1 collective-permute-start.4
  36.5 3.0 %collective-permute-start.5 = (f32[24,256]{1,0:T(8,128)S(1)}, f32[24,256]{1,0:T(8,128)S(1)}, u32[]{:S(2)}, u32[]{:S(2)}) collective-permute-start(f32[24,256]{1,0:T(8,128)S(1)} %get-tuple-element.46), channel_id=1, source_target_pairs={{1,2},{2,1},{3,4},{4,3},{5,6},{6,5},{7,8},{8,7},{9,10},{10,9},{11,... | collective-permute-start | bytes 73736 | tf_op jit(solution)/shard_map/ppermute | solution.py:79
  39.5 2.8 %product.1 = (bf16[128,1024]{1,0:T(8,128)(2,1)}, f32[128,1024]{1,0:T(8,128)S(1)}, f32[128,1024]{1,0:T(8,128)S(1)}, f32[128,1024]{1,0:T(8,128)S(1)}) custom-call(bf16[8,256,384]{2,1,0:T(8,128)(2,1)S(1)} %get-tuple-element.40.weights, bf16[8,256,384]{2,1,0:T(8,128)(2,1)S(1)} %get-tuple-element.41.grad_scores, bf16[384,2048]{1,0:T(8,128)(2,1)S(1)} %get-tuple-element.42.kv, ...), custom_call_target="tpu_custom_call" | custom-call | tf_op jit(solution)/shard_map/product/pallas_call | solution.py:47
  42.3 0.0 collective-permute-done.6.chip_grad
  42.3 0.0 collective-permute-done.7.off_grad
  42.3 0.0 collective-permute-done.4.chip_stats
  42.3 0.0 collective-permute-done.5.off_stats
  42.3 3.8 %finish.1 = bf16[128,1024]{1,0:T(8,128)(2,1)} custom-call(f32[24,256]{1,0:T(8,128)S(1)} %collective-permute-done.4.chip_stats, f32[24,256]{1,0:T(8,128)S(1)} %collective-permute-done.5.off_stats, bf16[144,1024]{1,0:T(8,128)(2,1)S(1)} %collective-permute-done.chip.chip_first, bf16[144,1024]{1,0:T(8,128)(2,1)S(1)} %collective-permute-done.1.off.off_first, ...), custom_call_target="tpu_custom_call" | custom-call | tf_op jit(solution)/shard_map/finish/pallas_call | solution.py:47
Async XLA Ops:
  4.0 14.3 %collective-permute-start = (bf16[144,1024]{1,0:T(8,128)(2,1)}, bf16[144,1024]{1,0:T(8,128)(2,1)S(1)}, u32[]{:S(2)}, u32[]{:S(2)}) collective-permute-start(bf16[144,1024]{1,0:T(8,128)(2,1)} %get-tuple-element.29), channel_id=1, source_target_pairs={{0,1},{1,0},{2,3},{3,2},{4,5},{5,4},{6,7},{7,6},{8,9},{9,8},{10,11... | collective-permute-start | bytes 884744 | tf_op jit(solution)/shard_map/ppermute | solution.py:82
  4.1 14.2 %collective-permute-start.1 = (bf16[144,1024]{1,0:T(8,128)(2,1)}, bf16[144,1024]{1,0:T(8,128)(2,1)S(1)}, u32[]{:S(2)}, u32[]{:S(2)}) collective-permute-start(bf16[144,1024]{1,0:T(8,128)(2,1)} %get-tuple-element.30), channel_id=1, source_target_pairs={{1,2},{2,1},{3,4},{4,3},{5,6},{6,5},{7,8},{8,7},{9,10},{10,9},{11,... | collective-permute-start | bytes 884744 | tf_op jit(solution)/shard_map/ppermute | solution.py:79
  8.6 12.7 %all-to-all-start = ((bf16[16,8,640]{2,1,0:T(8,128)(2,1)}), bf16[16,8,640]{2,1,0:T(8,128)(2,1)S(1)}, u32[]{:S(2)}, u32[]{:S(2)}) async-start(bf16[16,8,640]{2,1,0:T(8,128)(2,1)} %bitcast.11), calls=%async_computation | async-start | bytes 327680 | tf_op jit(solution)/shard_map/all_to_all | solution.py:604
  21.8 10.8 %collective-permute-start.2 = (bf16[128,1024]{1,0:T(8,128)(2,1)S(1)}, bf16[128,1024]{1,0:T(8,128)(2,1)S(1)}, u32[]{:S(2)}, u32[]{:S(2)}) collective-permute-start(bf16[128,1024]{1,0:T(8,128)(2,1)S(1)} %get-tuple-element.33.normed), channel_id=1, source_target_pairs={{0,1},{1,0},{2,3},{3,2},{4,5},{5,4},{6,7},{7,6},{8,9},{9,8},{10,11... | collective-permute-start | bytes 786440 | tf_op jit(solution)/shard_map/ppermute | solution.py:82
  23.1 9.6 %collective-permute-start.3 = (bf16[128,1024]{1,0:T(8,128)(2,1)S(1)}, bf16[128,1024]{1,0:T(8,128)(2,1)S(1)}, u32[]{:S(2)}, u32[]{:S(2)}) collective-permute-start(bf16[128,1024]{1,0:T(8,128)(2,1)S(1)} %get-tuple-element.33.normed), channel_id=1, source_target_pairs={{1,2},{2,1},{3,4},{4,3},{5,6},{6,5},{7,8},{8,7},{9,10},{10,9},{11,... | collective-permute-start | bytes 786440 | tf_op jit(solution)/shard_map/ppermute | solution.py:79
  28.9 13.4 %collective-permute-start.6 = (bf16[128,1024]{1,0:T(8,128)(2,1)S(1)}, bf16[128,1024]{1,0:T(8,128)(2,1)S(1)}, u32[]{:S(2)}, u32[]{:S(2)}) collective-permute-start(bf16[128,1024]{1,0:T(8,128)(2,1)S(1)} %get-tuple-element.37.own_grad), channel_id=1, source_target_pairs={{0,1},{1,0},{2,3},{3,2},{4,5},{5,4},{6,7},{7,6},{8,9},{9,8},{10,11... | collective-permute-start | bytes 786440 | tf_op jit(solution)/shard_map/ppermute | solution.py:82
  29.0 13.4 %collective-permute-start.7 = (bf16[128,1024]{1,0:T(8,128)(2,1)S(1)}, bf16[128,1024]{1,0:T(8,128)(2,1)S(1)}, u32[]{:S(2)}, u32[]{:S(2)}) collective-permute-start(bf16[128,1024]{1,0:T(8,128)(2,1)S(1)} %get-tuple-element.37.own_grad), channel_id=1, source_target_pairs={{1,2},{2,1},{3,4},{4,3},{5,6},{6,5},{7,8},{8,7},{9,10},{10,9},{11,... | collective-permute-start | bytes 786440 | tf_op jit(solution)/shard_map/ppermute | solution.py:79
  36.4 5.9 %collective-permute-start.4 = (f32[24,256]{1,0:T(8,128)S(1)}, f32[24,256]{1,0:T(8,128)S(1)}, u32[]{:S(2)}, u32[]{:S(2)}) collective-permute-start(f32[24,256]{1,0:T(8,128)S(1)} %get-tuple-element.46), channel_id=1, source_target_pairs={{0,1},{1,0},{2,3},{3,2},{4,5},{5,4},{6,7},{7,6},{8,9},{9,8},{10,11... | collective-permute-start | bytes 73736 | tf_op jit(solution)/shard_map/ppermute | solution.py:82
  36.5 5.9 %collective-permute-start.5 = (f32[24,256]{1,0:T(8,128)S(1)}, f32[24,256]{1,0:T(8,128)S(1)}, u32[]{:S(2)}, u32[]{:S(2)}) collective-permute-start(f32[24,256]{1,0:T(8,128)S(1)} %get-tuple-element.46), channel_id=1, source_target_pairs={{1,2},{2,1},{3,4},{4,3},{5,6},{6,5},{7,8},{8,7},{9,10},{10,9},{11,... | collective-permute-start | bytes 73736 | tf_op jit(solution)/shard_map/ppermute | solution.py:79

commit v13 on v12

--- a/solution.py
+++ b/solution.py
@@ -359,7 +359,8 @@
     w_out_hbm,
     cot_hbm,
     stats_out,
-    kv,
+    attention,
+    grad_query,
     weights_out,
     scores_out,
     near_q,
@@ -379,15 +380,12 @@
         cols = slice(group * 2 * pair, (group + 1) * 2 * pair)
         near_q[:, cols] = mm(near, w_qkv[:, cols]).astype(BF16) * jnp.asarray(scale, BF16)
         blocks = []
-        for part in range(2):
+        for part in range(1, 3):
             at = part * channels + group * 2 * pair
-            block = mm(near, w_qkv[:, channels + at : channels + at + 2 * pair]).astype(BF16)
-            kv[: 2 * m, at : at + 2 * pair] = block
-            blocks.append(block)
+            blocks.append(mm(near, w_qkv[:, at : at + 2 * pair]).astype(BF16))
         return blocks
 
     brought = {0: bring(0)}
-    kv[2 * m :] = own_qkv[:, channels:]
     fetch[0].wait()
     row = iota((3 * m, m), 0)
     chip_at, off_at = near_places(m)
@@ -400,9 +398,12 @@
     lane = iota((2 * m, LANES), 1)
     stats = jnp.zeros((2 * m, LANES), F32)
 
+    def near_of(p):
+        return [b[:, p % 2 * pair : (p % 2 + 1) * pair] for b in brought[p // 2]]
+
     def multiply(p):
         cols = slice(p * pair, (p + 1) * pair)
-        keys, values = (b[:, p % 2 * pair : (p % 2 + 1) * pair] for b in brought[p // 2])
+        keys, values = near_of(p)
         return (
             mm_nt(halves(own_qkv[:, cols], scale), keys),
             mm_nt(halves(own_grad[:, cols]), values),
@@ -421,9 +422,18 @@
         shifted = jnp.exp(scores - top)
         inv_sum = 1.0 / jnp.sum(shifted, 1, keepdims=True)
         probs = shifted * inv_sum
-        weights_out[p] = probs.astype(BF16)
+        weights = probs.astype(BF16)
         delta = jnp.sum(probs * grad_prob, 1, keepdims=True)
-        scores_out[p] = (probs * (grad_prob - delta)).astype(BF16)
+        grad_scores = (probs * (grad_prob - delta)).astype(BF16)
+        weights_out[p] = weights[:, 2 * m :]
+        scores_out[p] = grad_scores[:, 2 * m :]
+        keys, values = (
+            jnp.concatenate([block, own_qkv[:, at + p * pair : at + (p + 1) * pair]], 0)
+            for block, at in zip(near_of(p), (channels, 2 * channels))
+        )
+        cols = slice(p * pair, (p + 1) * pair)
+        attention[:, cols] = merge(mm(weights, values)).astype(BF16)
+        grad_query[:, cols] = (merge(mm(grad_scores, keys)) * scale).astype(BF16)
         stats = jnp.where(lane == p, top, stats)
         stats = jnp.where(lane == pairs + p, inv_sum, stats)
         stats = jnp.where(lane == 2 * pairs + p, delta, stats)
@@ -437,7 +447,8 @@
     pair,
     weights,
     grad_scores,
-    kv,
+    attention,
+    grad_query,
     own_qkv,
     own_grad,
     latent,
@@ -447,27 +458,17 @@
     grad_normed,
     grad_key,
     grad_value,
-    attention,
-    grad_query,
     mesh_out,
     sems,
 ):
     m, channels = latent.shape
-    pairs = channels // pair
-    for p in range(pairs):
-        cols = slice(p * pair, (p + 1) * pair)
-        value = kv[:, channels + p * pair : channels + (p + 1) * pair]
-        attention[:, cols] = merge(mm(weights[p], value)).astype(BF16)
     mesh_out[...] = (latent[...].astype(F32) + mm(attention[...], w_out[...])).astype(BF16)
     out = pltpu.make_async_copy(mesh_out, mesh_out_hbm, sems.at[0])
     out.start()
-    for p in range(pairs):
+    for p in range(channels // pair):
         cols = slice(p * pair, (p + 1) * pair)
-        grad_query[:, cols] = (merge(mm(grad_scores[p], kv[:, cols])) * scale).astype(BF16)
-    for p in range(pairs):
-        cols = slice(p * pair, (p + 1) * pair)
-        grad_key[:, cols] = mm_tn(grad_scores[p, :, 2 * m :], halves(own_qkv[:, cols], scale))
-        grad_value[:, cols] = mm_tn(weights[p, :, 2 * m :], halves(own_grad[:, cols]))
+        grad_key[:, cols] = mm_tn(grad_scores[p], halves(own_qkv[:, cols], scale))
+        grad_value[:, cols] = mm_tn(weights[p], halves(own_grad[:, cols]))
     grad_normed[...] = mm_nt(grad_query[...], w_qkv[:, :channels])
     out.wait()
 
@@ -643,12 +644,13 @@
         name="project",
     )
     chip_grad, off_grad = exchange(own_grad, own_grad, "node")
-    probs = ((pairs, 2 * m, 3 * m), BF16)
-    stats, kv, weights, grad_scores, near_q, w_out, cotangent = call(
+    probs = ((pairs, 2 * m, m), BF16)
+    stats, attention, grad_query, weights, grad_scores, near_q, w_out, cotangent = call(
         functools.partial(attend_kernel, scale, pair),
         [
             ((3 * pairs, 2 * m), F32),
-            ((3 * m, 2 * channels), BF16),
+            rows,
+            rows,
             probs,
             probs,
             ((2 * m, channels), BF16),
@@ -673,7 +675,8 @@
         [
             weights,
             grad_scores,
-            kv,
+            attention,
+            grad_query,
             own_qkv,
             own_grad,
             latent,
@@ -681,7 +684,7 @@
             w_qkv,
         ],
         hbm_outs=(0,),
-        scratch=[pltpu.VMEM((m, channels), BF16)] * 3 + [dma(1)],
+        scratch=[pltpu.VMEM((m, channels), BF16), dma(1)],
         name="product",
     )
     (mesh_grad,) = call(

time: 46.5 us -> 46.5 us (level)
  transfers between devices with their start and end apart: 9 -> 9, of which waited for: 1 -> 2; matrix products, arithmetic and copies ran while one was open for 0% -> 0% of each run, Pallas kernels for 35% -> 35%
where the time goes in v13:
time: 46.5 us; the launch traced here: 46.1 us
  Pallas kernels  23.7 us (51%)
  starting transfers between devices  19.9 us (43%)
  waiting for transfers between devices  1.75 us (4%)
  between operations  0.79 us (2%)
    pallas_call x8, Pallas kernels, call(): pl.pallas_call(kernel, out_shape=[(pltpu.HBM if i in hbm_outs else jax.Sh...  23.7 us
    ppermute x4, starting transfers between devices, exchange(): lax.ppermute(off_message, axis, [p for i in range(1, n - 1, 2) for p in (...  13.1 us
    all_to_all x1, starting transfers between devices, body(): lax.all_to_all(far_message.reshape(devices, 2 * far_depth, far_block[1]),...  5.33 us
    all_to_all x1, waiting for transfers between devices, body(): lax.all_to_all(far_message.reshape(devices, 2 * far_depth, far_block[1]),...  1.6 us
    ppermute x4, starting transfers between devices, exchange(): lax.ppermute(chip_message, axis, [p for i in range(0, n, 2) for p in ((i,...  1.49 us
  transfers between devices with their start and end apart: 9, of which 2 were waited for; matrix products, arithmetic and copies ran while one was open for 0% of the time, Pallas kernels for 35%

profile of v13, /device:TPU:1, one launch (start us, length us, event | category | flops | bytes accessed | tf_op | source)
XLA Modules:
  0.0 46.1 jit_solution(46511354603112098)
XLA Ops:
  0.6 3.4 %pack.1 = (bf16[128,640]{1,0:T(8,128)(2,1)}, bf16[144,1024]{1,0:T(8,128)(2,1)}, bf16[144,1024]{1,0:T(8,128)(2,1)}, bf16[1024,1024]{1,0:T(8,128)(2,1)S(1)}) custom-call(bf16[512,1024]{1,0:T(8,128)(2,1)} %grid_hbm.3, s32[2,128]{1,0:T(2,128)} %window_hbm.3, s32[32,128]{1,0:T(8,128)} %bitcast.12, s32[32,128]{1,0:T(8,128)} %bitcast.13, s32[1,2]{1,0:T(1,128)} %bitcast.16, ...), custom_call_target="tpu_custom_call" | custom-call | tf_op jit(solution)/shard_map/pack/pallas_call | solution.py:47
  4.0 0.1 collective-permute-start
  4.1 4.5 %collective-permute-start.1 = (bf16[144,1024]{1,0:T(8,128)(2,1)}, bf16[144,1024]{1,0:T(8,128)(2,1)S(1)}, u32[]{:S(2)}, u32[]{:S(2)}) collective-permute-start(bf16[144,1024]{1,0:T(8,128)(2,1)} %get-tuple-element.31), channel_id=1, source_target_pairs={{1,2},{2,1},{3,4},{4,3},{5,6},{6,5},{7,8},{8,7},{9,10},{10,9},{11,... | collective-permute-start | bytes 884744 | tf_op jit(solution)/shard_map/ppermute | solution.py:79
  8.6 5.3 %all-to-all-start = ((bf16[16,8,640]{2,1,0:T(8,128)(2,1)}), bf16[16,8,640]{2,1,0:T(8,128)(2,1)S(1)}, u32[]{:S(2)}, u32[]{:S(2)}) async-start(bf16[16,8,640]{2,1,0:T(8,128)(2,1)} %bitcast.11), calls=%async_computation | async-start | bytes 327680 | tf_op jit(solution)/shard_map/all_to_all | solution.py:605
  13.9 4.3 %own.1 = (f32[128,1024]{1,0:T(8,128)S(1)}, bf16[128,1024]{1,0:T(8,128)(2,1)}) custom-call(bf16[512,1024]{1,0:T(8,128)(2,1)} %grid_hbm.3, bf16[128,1024]{1,0:T(8,128)(2,1)} %mesh_in_hbm.1, s32[8,128]{1,0:T(8,128)} %bitcast.14, s32[8,128]{1,0:T(8,128)} %bitcast.15, bf16[128,1024]{1,0:T(8,128)(2,1)} %cot_hbm.3, bf16[1024,1024]{1,0:T(8,128)(2,1)} %w_out_hbm.3, ...), custom_call_target="tpu_custom_call" | custom-call | tf_op jit(solution)/shard_map/own/pallas_call | solution.py:47
  18.3 0.0 collective-permute-done.chip.chip_first
  18.3 0.0 collective-permute-done.1.off.off_first
  18.3 1.4 %side.1.partial = f32[128,1024]{1,0:T(8,128)S(1)} custom-call(bf16[144,1024]{1,0:T(8,128)(2,1)S(1)} %collective-permute-done.chip.chip_first, bf16[144,1024]{1,0:T(8,128)(2,1)S(1)} %collective-permute-done.1.off.off_first, bf16[1024,1024]{1,0:T(8,128)(2,1)S(1)} %get-tuple-element.32.w_edge, f32[128,1024]{1,0:T(8,128)S(1)} %get-tuple-element.33.partial), custom_call_target="tpu_custom_call" | custom-call | flops 8000000000 | tf_op jit(solution)/shard_map/side/pallas_call | solution.py:47
  19.7 1.6 %all-to-all-done = bf16[16,8,640]{2,1,0:T(8,128)(2,1)S(1)} async-done(((bf16[16,8,640]{2,1,0:T(8,128)(2,1)}), bf16[16,8,640]{2,1,0:T(8,128)(2,1)S(1)}, u32[]{:S(2)}, u32[]{:S(2)}) %all-to-all-start) | async-done | bytes 163872 | tf_op jit(solution)/shard_map/all_to_all | solution.py:605
  21.3 0.5 %latent.1 = (bf16[128,1024]{1,0:T(8,128)(2,1)S(1)}, bf16[128,1024]{1,0:T(8,128)(2,1)S(1)}, f32[128,1024]{1,0:T(8,128)S(1)}, f32[128,128]{1,0:T(8,128)S(1)}) custom-call(bf16[128,640]{1,0:T(8,128)(2,1)S(1)} %bitcast.10, f32[128,1024]{1,0:T(8,128)S(1)} %side.1.partial), custom_call_target="tpu_custom_call" | custom-call | tf_op jit(solution)/shard_map/latent/pallas_call | solution.py:47
  21.8 1.2 %collective-permute-start.2 = (bf16[128,1024]{1,0:T(8,128)(2,1)S(1)}, bf16[128,1024]{1,0:T(8,128)(2,1)S(1)}, u32[]{:S(2)}, u32[]{:S(2)}) collective-permute-start(bf16[128,1024]{1,0:T(8,128)(2,1)S(1)} %get-tuple-element.34.normed), channel_id=1, source_target_pairs={{0,1},{1,0},{2,3},{3,2},{4,5},{5,4},{6,7},{7,6},{8,9},{9,8},{10,11... | collective-permute-start | bytes 786440 | tf_op jit(solution)/shard_map/ppermute | solution.py:82
  23.1 1.9 %collective-permute-start.3 = (bf16[128,1024]{1,0:T(8,128)(2,1)S(1)}, bf16[128,1024]{1,0:T(8,128)(2,1)S(1)}, u32[]{:S(2)}, u32[]{:S(2)}) collective-permute-start(bf16[128,1024]{1,0:T(8,128)(2,1)S(1)} %get-tuple-element.34.normed), channel_id=1, source_target_pairs={{1,2},{2,1},{3,4},{4,3},{5,6},{6,5},{7,8},{8,7},{9,10},{10,9},{11,... | collective-permute-start | bytes 786440 | tf_op jit(solution)/shard_map/ppermute | solution.py:79
  25.0 3.9 %project.1 = (bf16[128,3072]{1,0:T(8,128)(2,1)S(1)}, bf16[1024,3072]{1,0:T(8,128)(2,1)S(1)}, bf16[128,1024]{1,0:T(8,128)(2,1)S(1)}, f32[8,256,128]{2,1,0:T(8,128)S(1)}, f32[8,256,128]{2,1,0:T(8,128)S(1)}) custom-call(bf16[128,1024]{1,0:T(8,128)(2,1)S(1)} %get-tuple-element.34.normed, bf16[128,1024]{1,0:T(8,128)(2,1)} %get-tuple-element.35.grad_hbm, ...), custom_call_target="tpu_custom_call" | custom-call | tf_op jit(solution)/shard_map/project/pallas_call | solution.py:47
  28.9 0.1 collective-permute-start.6
  29.0 3.6 %collective-permute-start.7 = (bf16[128,1024]{1,0:T(8,128)(2,1)S(1)}, bf16[128,1024]{1,0:T(8,128)(2,1)S(1)}, u32[]{:S(2)}, u32[]{:S(2)}) collective-permute-start(bf16[128,1024]{1,0:T(8,128)(2,1)S(1)} %get-tuple-element.38.own_grad), channel_id=1, source_target_pairs={{1,2},{2,1},{3,4},{4,3},{5,6},{6,5},{7,8},{8,7},{9,10},{10,9},{11,... | collective-permute-start | bytes 786440 | tf_op jit(solution)/shard_map/ppermute | solution.py:79
  32.6 0.0 collective-permute-done.2.chip_normed
  32.6 0.0 collective-permute-done.3.off_normed
  32.6 4.4 %attend.1 = (f32[24,256]{1,0:T(8,128)S(1)}, bf16[128,1024]{1,0:T(8,128)(2,1)S(1)}, bf16[128,1024]{1,0:T(8,128)(2,1)S(1)}, bf16[8,256,128]{2,1,0:T(8,128)(2,1)S(1...) custom-call(bf16[128,1024]{1,0:T(8,128)(2,1)S(1)} %collective-permut, ...), custom_call_target="tpu_custom_call" | custom-call | tf_op jit(solution)/shard_map/attend/pallas_call | solution.py:47
  37.1 0.1 collective-permute-start.4
  37.2 3.0 %collective-permute-start.5 = (f32[24,256]{1,0:T(8,128)S(1)}, f32[24,256]{1,0:T(8,128)S(1)}, u32[]{:S(2)}, u32[]{:S(2)}) collective-permute-start(f32[24,256]{1,0:T(8,128)S(1)} %get-tuple-element.48), channel_id=1, source_target_pairs={{1,2},{2,1},{3,4},{4,3},{5,6},{6,5},{7,8},{8,7},{9,10},{10,9},{11,... | collective-permute-start | bytes 73736 | tf_op jit(solution)/shard_map/ppermute | solution.py:79
  40.2 2.0 %product.1 = (bf16[128,1024]{1,0:T(8,128)(2,1)}, f32[128,1024]{1,0:T(8,128)S(1)}, f32[128,1024]{1,0:T(8,128)S(1)}, f32[128,1024]{1,0:T(8,128)S(1)}) custom-call(bf16[8,256,128]{2,1,0:T(8,128)(2,1)S(1)} %get-tuple-element.41.weights, bf16[8,256,128]{2,1,0:T(8,128)(2,1)S(1)} %get-tuple-element.42.grad_scores, ...), custom_call_target="tpu_custom_call" | custom-call | tf_op jit(solution)/shard_map/product/pallas_call | solution.py:47
  42.1 0.0 collective-permute-done.6.chip_grad
  42.1 0.0 collective-permute-done.7.off_grad
  42.1 0.0 collective-permute-done.4.chip_stats
  42.2 0.1 collective-permute-done.5.off_stats
  42.3 3.8 %finish.1 = bf16[128,1024]{1,0:T(8,128)(2,1)} custom-call(f32[24,256]{1,0:T(8,128)S(1)} %collective-permute-done.4.chip_stats, f32[24,256]{1,0:T(8,128)S(1)} %collective-permute-done.5.off_stats, bf16[144,1024]{1,0:T(8,128)(2,1)S(1)} %collective-permute-done.chip.chip_first, bf16[144,1024]{1,0:T(8,128)(2,1)S(1)} %collective-permute-done.1.off.off_first, ...), custom_call_target="tpu_custom_call" | custom-call | tf_op jit(solution)/shard_map/finish/pallas_call | solution.py:47
Async XLA Ops:
  4.0 14.3 %collective-permute-start = (bf16[144,1024]{1,0:T(8,128)(2,1)}, bf16[144,1024]{1,0:T(8,128)(2,1)S(1)}, u32[]{:S(2)}, u32[]{:S(2)}) collective-permute-start(bf16[144,1024]{1,0:T(8,128)(2,1)} %get-tuple-element.30), channel_id=1, source_target_pairs={{0,1},{1,0},{2,3},{3,2},{4,5},{5,4},{6,7},{7,6},{8,9},{9,8},{10,11... | collective-permute-start | bytes 884744 | tf_op jit(solution)/shard_map/ppermute | solution.py:82
  4.1 14.2 %collective-permute-start.1 = (bf16[144,1024]{1,0:T(8,128)(2,1)}, bf16[144,1024]{1,0:T(8,128)(2,1)S(1)}, u32[]{:S(2)}, u32[]{:S(2)}) collective-permute-start(bf16[144,1024]{1,0:T(8,128)(2,1)} %get-tuple-element.31), channel_id=1, source_target_pairs={{1,2},{2,1},{3,4},{4,3},{5,6},{6,5},{7,8},{8,7},{9,10},{10,9},{11,... | collective-permute-start | bytes 884744 | tf_op jit(solution)/shard_map/ppermute | solution.py:79
  8.6 12.7 %all-to-all-start = ((bf16[16,8,640]{2,1,0:T(8,128)(2,1)}), bf16[16,8,640]{2,1,0:T(8,128)(2,1)S(1)}, u32[]{:S(2)}, u32[]{:S(2)}) async-start(bf16[16,8,640]{2,1,0:T(8,128)(2,1)} %bitcast.11), calls=%async_computation | async-start | bytes 327680 | tf_op jit(solution)/shard_map/all_to_all | solution.py:605
  21.8 10.8 %collective-permute-start.2 = (bf16[128,1024]{1,0:T(8,128)(2,1)S(1)}, bf16[128,1024]{1,0:T(8,128)(2,1)S(1)}, u32[]{:S(2)}, u32[]{:S(2)}) collective-permute-start(bf16[128,1024]{1,0:T(8,128)(2,1)S(1)} %get-tuple-element.34.normed), channel_id=1, source_target_pairs={{0,1},{1,0},{2,3},{3,2},{4,5},{5,4},{6,7},{7,6},{8,9},{9,8},{10,11... | collective-permute-start | bytes 786440 | tf_op jit(solution)/shard_map/ppermute | solution.py:82
  23.1 9.6 %collective-permute-start.3 = (bf16[128,1024]{1,0:T(8,128)(2,1)S(1)}, bf16[128,1024]{1,0:T(8,128)(2,1)S(1)}, u32[]{:S(2)}, u32[]{:S(2)}) collective-permute-start(bf16[128,1024]{1,0:T(8,128)(2,1)S(1)} %get-tuple-element.34.normed), channel_id=1, source_target_pairs={{1,2},{2,1},{3,4},{4,3},{5,6},{6,5},{7,8},{8,7},{9,10},{10,9},{11,... | collective-permute-start | bytes 786440 | tf_op jit(solution)/shard_map/ppermute | solution.py:79
  28.9 13.2 %collective-permute-start.6 = (bf16[128,1024]{1,0:T(8,128)(2,1)S(1)}, bf16[128,1024]{1,0:T(8,128)(2,1)S(1)}, u32[]{:S(2)}, u32[]{:S(2)}) collective-permute-start(bf16[128,1024]{1,0:T(8,128)(2,1)S(1)} %get-tuple-element.38.own_grad), channel_id=1, source_target_pairs={{0,1},{1,0},{2,3},{3,2},{4,5},{5,4},{6,7},{7,6},{8,9},{9,8},{10,11... | collective-permute-start | bytes 786440 | tf_op jit(solution)/shard_map/ppermute | solution.py:82
  29.0 13.2 %collective-permute-start.7 = (bf16[128,1024]{1,0:T(8,128)(2,1)S(1)}, bf16[128,1024]{1,0:T(8,128)(2,1)S(1)}, u32[]{:S(2)}, u32[]{:S(2)}) collective-permute-start(bf16[128,1024]{1,0:T(8,128)(2,1)S(1)} %get-tuple-element.38.own_grad), channel_id=1, source_target_pairs={{1,2},{2,1},{3,4},{4,3},{5,6},{6,5},{7,8},{8,7},{9,10},{10,9},{11,... | collective-permute-start | bytes 786440 | tf_op jit(solution)/shard_map/ppermute | solution.py:79
  37.1 5.1 %collective-permute-start.4 = (f32[24,256]{1,0:T(8,128)S(1)}, f32[24,256]{1,0:T(8,128)S(1)}, u32[]{:S(2)}, u32[]{:S(2)}) collective-permute-start(f32[24,256]{1,0:T(8,128)S(1)} %get-tuple-element.48), channel_id=1, source_target_pairs={{0,1},{1,0},{2,3},{3,2},{4,5},{5,4},{6,7},{7,6},{8,9},{9,8},{10,11... | collective-permute-start | bytes 73736 | tf_op jit(solution)/shard_map/ppermute | solution.py:82
  37.2 5.1 %collective-permute-start.5 = (f32[24,256]{1,0:T(8,128)S(1)}, f32[24,256]{1,0:T(8,128)S(1)}, u32[]{:S(2)}, u32[]{:S(2)}) collective-permute-start(f32[24,256]{1,0:T(8,128)S(1)} %get-tuple-element.48), channel_id=1, source_target_pairs={{1,2},{2,1},{3,4},{4,3},{5,6},{6,5},{7,8},{8,7},{9,10},{10,9},{11,... | collective-permute-start | bytes 73736 | tf_op jit(solution)/shard_map/ppermute | solution.py:79

commit v14 on v13

--- a/solution.py
+++ b/solution.py
@@ -15,6 +15,7 @@
 I32 = jnp.int32
 VMEM_LIMIT = 28 * 2**20
 PIECES = 2
+CHUNK = 64
 
 
 def mm(a, b):
@@ -394,9 +395,8 @@
     missing = (row >= m) & (row < 2 * m) & ((me == 0) | (me == devices - 1))
     keep = (key_at >= query_at - window[0:1, :]) & (key_at <= query_at + window[1:2, :])
     bias = jnp.transpose(jnp.where(keep & jnp.logical_not(missing), 0.0, -jnp.inf).astype(F32))
-    bias = jnp.concatenate([bias, bias], 0)
-    lane = iota((2 * m, LANES), 1)
-    stats = jnp.zeros((2 * m, LANES), F32)
+    lane = iota((CHUNK, LANES), 1)
+    stats = [jnp.zeros((CHUNK, LANES), F32) for _ in range(2 * m // CHUNK)]
 
     def near_of(p):
         return [b[:, p % 2 * pair : (p % 2 + 1) * pair] for b in brought[p // 2]]
@@ -416,15 +416,23 @@
             if p % 2 == 0 and p + 2 < pairs:
                 brought[p // 2 + 1] = bring(p // 2 + 1)
             ahead = multiply(p + 1)
-        scores = jnp.concatenate([scores, own_scores[p]], 1) + bias
-        grad_prob = jnp.concatenate([grad_prob, own_products[p]], 1)
-        top = jnp.max(scores, 1, keepdims=True)
-        shifted = jnp.exp(scores - top)
-        inv_sum = 1.0 / jnp.sum(shifted, 1, keepdims=True)
-        probs = shifted * inv_sum
-        weights = probs.astype(BF16)
-        delta = jnp.sum(probs * grad_prob, 1, keepdims=True)
-        grad_scores = (probs * (grad_prob - delta)).astype(BF16)
+        weights, grad_scores = [], []
+        for at in range(0, 2 * m, CHUNK):
+            part = slice(at, at + CHUNK)
+            place = slice(at % m, at % m + CHUNK)
+            raw = jnp.concatenate([scores[part], own_scores[p, part]], 1) + bias[place]
+            top = jnp.max(raw, 1, keepdims=True)
+            shifted = jnp.exp(raw - top)
+            inv_sum = 1.0 / jnp.sum(shifted, 1, keepdims=True)
+            probs = shifted * inv_sum
+            product = jnp.concatenate([grad_prob[part], own_products[p, part]], 1)
+            delta = jnp.sum(probs * product, 1, keepdims=True)
+            weights.append(probs.astype(BF16))
+            grad_scores.append((probs * (product - delta)).astype(BF16))
+            for k, column in enumerate((top, inv_sum, delta)):
+                stats[at // CHUNK] = jnp.where(lane == k * pairs + p, column, stats[at // CHUNK])
+        weights = jnp.concatenate(weights, 0)
+        grad_scores = jnp.concatenate(grad_scores, 0)
         weights_out[p] = weights[:, 2 * m :]
         scores_out[p] = grad_scores[:, 2 * m :]
         keys, values = (
@@ -434,10 +442,7 @@
         cols = slice(p * pair, (p + 1) * pair)
         attention[:, cols] = merge(mm(weights, values)).astype(BF16)
         grad_query[:, cols] = (merge(mm(grad_scores, keys)) * scale).astype(BF16)
-        stats = jnp.where(lane == p, top, stats)
-        stats = jnp.where(lane == pairs + p, inv_sum, stats)
-        stats = jnp.where(lane == 2 * pairs + p, delta, stats)
-    stats_out[...] = jnp.transpose(stats)[: 3 * pairs]
+    stats_out[...] = jnp.transpose(jnp.concatenate(stats, 0))[: 3 * pairs]
     for copy in fetch[1:]:
         copy.wait()
 
@@ -527,12 +532,15 @@
         if p + 1 < pairs:
             ahead = multiply(p + 1)
         weights, grad_scores = [], []
-        for h in range(2):
-            half = slice(h * m, (h + 1) * m)
-            top, inv_sum, delta = (stats[h][k * pairs + p : k * pairs + p + 1] for k in range(3))
-            probs = jnp.exp(scores[half] + bias - top) * inv_sum
+        for at in range(0, 2 * m, CHUNK):
+            part = slice(at, at + CHUNK)
+            place = slice(at % m, at % m + CHUNK)
+            top, inv_sum, delta = (
+                stats[at // m][k * pairs + p : k * pairs + p + 1] for k in range(3)
+            )
+            probs = jnp.exp(scores[part] + bias[place] - top) * inv_sum
             weights.append(probs.astype(BF16))
-            grad_scores.append((probs * (grad_prob[half] - delta)).astype(BF16))
+            grad_scores.append((probs * (grad_prob[part] - delta)).astype(BF16))
         gk = grad_key[:, cols] + merge(mm(jnp.concatenate(grad_scores, 0), query))
         gv = grad_value[:, cols] + merge(mm(jnp.concatenate(weights, 0), grad))
         gks.append(gk.astype(BF16))

time: 46.5 us -> 46.5 us (level)
  no operation moved by 1% of the time
where the time goes in v14:
time: 46.5 us; the launch traced here: 46.1 us
  Pallas kernels  23.7 us (51%)
  starting transfers between devices  19.9 us (43%)
  waiting for transfers between devices  1.75 us (4%)
  between operations  0.79 us (2%)
    pallas_call x8, Pallas kernels, call(): pl.pallas_call(kernel, out_shape=[(pltpu.HBM if i in hbm_outs else jax.Sh...  23.7 us
    ppermute x4, starting transfers between devices, exchange(): lax.ppermute(off_message, axis, [p for i in range(1, n - 1, 2) for p in (...  13.1 us
    all_to_all x1, starting transfers between devices, body(): lax.all_to_all(far_message.reshape(devices, 2 * far_depth, far_block[1]),...  5.33 us
    all_to_all x1, waiting for transfers between devices, body(): lax.all_to_all(far_message.reshape(devices, 2 * far_depth, far_block[1]),...  1.6 us
    ppermute x4, starting transfers between devices, exchange(): lax.ppermute(chip_message, axis, [p for i in range(0, n, 2) for p in ((i,...  1.49 us
  transfers between devices with their start and end apart: 9, of which 2 were waited for; matrix products, arithmetic and copies ran while one was open for 0% of the time, Pallas kernels for 35%

profile of v14, /device:TPU:1, one launch (start us, length us, event | category | flops | bytes accessed | tf_op | source)
XLA Modules:
  0.0 46.1 jit_solution(12011560402239628140)
XLA Ops:
  0.6 3.4 %pack.1 = (bf16[128,640]{1,0:T(8,128)(2,1)}, bf16[144,1024]{1,0:T(8,128)(2,1)}, bf16[144,1024]{1,0:T(8,128)(2,1)}, bf16[1024,1024]{1,0:T(8,128)(2,1)S(1)}) custom-call(bf16[512,1024]{1,0:T(8,128)(2,1)} %grid_hbm.3, s32[2,128]{1,0:T(2,128)} %window_hbm.3, s32[32,128]{1,0:T(8,128)} %bitcast.12, s32[32,128]{1,0:T(8,128)} %bitcast.13, s32[1,2]{1,0:T(1,128)} %bitcast.16, ...), custom_call_target="tpu_custom_call" | custom-call | tf_op jit(solution)/shard_map/pack/pallas_call | solution.py:48
  4.0 0.1 collective-permute-start
  4.1 4.5 %collective-permute-start.1 = (bf16[144,1024]{1,0:T(8,128)(2,1)}, bf16[144,1024]{1,0:T(8,128)(2,1)S(1)}, u32[]{:S(2)}, u32[]{:S(2)}) collective-permute-start(bf16[144,1024]{1,0:T(8,128)(2,1)} %get-tuple-element.31), channel_id=1, source_target_pairs={{1,2},{2,1},{3,4},{4,3},{5,6},{6,5},{7,8},{8,7},{9,10},{10,9},{11,... | collective-permute-start | bytes 884744 | tf_op jit(solution)/shard_map/ppermute | solution.py:80
  8.6 5.3 %all-to-all-start = ((bf16[16,8,640]{2,1,0:T(8,128)(2,1)}), bf16[16,8,640]{2,1,0:T(8,128)(2,1)S(1)}, u32[]{:S(2)}, u32[]{:S(2)}) async-start(bf16[16,8,640]{2,1,0:T(8,128)(2,1)} %bitcast.11), calls=%async_computation | async-start | bytes 327680 | tf_op jit(solution)/shard_map/all_to_all | solution.py:613
  13.9 4.3 %own.1 = (f32[128,1024]{1,0:T(8,128)S(1)}, bf16[128,1024]{1,0:T(8,128)(2,1)}) custom-call(bf16[512,1024]{1,0:T(8,128)(2,1)} %grid_hbm.3, bf16[128,1024]{1,0:T(8,128)(2,1)} %mesh_in_hbm.1, s32[8,128]{1,0:T(8,128)} %bitcast.14, s32[8,128]{1,0:T(8,128)} %bitcast.15, bf16[128,1024]{1,0:T(8,128)(2,1)} %cot_hbm.3, bf16[1024,1024]{1,0:T(8,128)(2,1)} %w_out_hbm.3, ...), custom_call_target="tpu_custom_call" | custom-call | tf_op jit(solution)/shard_map/own/pallas_call | solution.py:48
  18.3 0.0 collective-permute-done.chip.chip_first
  18.3 0.0 collective-permute-done.1.off.off_first
  18.3 1.4 %side.1.partial = f32[128,1024]{1,0:T(8,128)S(1)} custom-call(bf16[144,1024]{1,0:T(8,128)(2,1)S(1)} %collective-permute-done.chip.chip_first, bf16[144,1024]{1,0:T(8,128)(2,1)S(1)} %collective-permute-done.1.off.off_first, bf16[1024,1024]{1,0:T(8,128)(2,1)S(1)} %get-tuple-element.32.w_edge, f32[128,1024]{1,0:T(8,128)S(1)} %get-tuple-element.33.partial), custom_call_target="tpu_custom_call" | custom-call | flops 8000000000 | tf_op jit(solution)/shard_map/side/pallas_call | solution.py:48
  19.7 1.6 %all-to-all-done = bf16[16,8,640]{2,1,0:T(8,128)(2,1)S(1)} async-done(((bf16[16,8,640]{2,1,0:T(8,128)(2,1)}), bf16[16,8,640]{2,1,0:T(8,128)(2,1)S(1)}, u32[]{:S(2)}, u32[]{:S(2)}) %all-to-all-start) | async-done | bytes 163872 | tf_op jit(solution)/shard_map/all_to_all | solution.py:613
  21.3 0.5 %latent.1 = (bf16[128,1024]{1,0:T(8,128)(2,1)S(1)}, bf16[128,1024]{1,0:T(8,128)(2,1)S(1)}, f32[128,1024]{1,0:T(8,128)S(1)}, f32[128,128]{1,0:T(8,128)S(1)}) custom-call(bf16[128,640]{1,0:T(8,128)(2,1)S(1)} %bitcast.10, f32[128,1024]{1,0:T(8,128)S(1)} %side.1.partial), custom_call_target="tpu_custom_call" | custom-call | tf_op jit(solution)/shard_map/latent/pallas_call | solution.py:48
  21.8 1.2 %collective-permute-start.2 = (bf16[128,1024]{1,0:T(8,128)(2,1)S(1)}, bf16[128,1024]{1,0:T(8,128)(2,1)S(1)}, u32[]{:S(2)}, u32[]{:S(2)}) collective-permute-start(bf16[128,1024]{1,0:T(8,128)(2,1)S(1)} %get-tuple-element.34.normed), channel_id=1, source_target_pairs={{0,1},{1,0},{2,3},{3,2},{4,5},{5,4},{6,7},{7,6},{8,9},{9,8},{10,11... | collective-permute-start | bytes 786440 | tf_op jit(solution)/shard_map/ppermute | solution.py:83
  23.1 1.9 %collective-permute-start.3 = (bf16[128,1024]{1,0:T(8,128)(2,1)S(1)}, bf16[128,1024]{1,0:T(8,128)(2,1)S(1)}, u32[]{:S(2)}, u32[]{:S(2)}) collective-permute-start(bf16[128,1024]{1,0:T(8,128)(2,1)S(1)} %get-tuple-element.34.normed), channel_id=1, source_target_pairs={{1,2},{2,1},{3,4},{4,3},{5,6},{6,5},{7,8},{8,7},{9,10},{10,9},{11,... | collective-permute-start | bytes 786440 | tf_op jit(solution)/shard_map/ppermute | solution.py:80
  25.0 3.9 %project.1 = (bf16[128,3072]{1,0:T(8,128)(2,1)S(1)}, bf16[1024,3072]{1,0:T(8,128)(2,1)S(1)}, bf16[128,1024]{1,0:T(8,128)(2,1)S(1)}, f32[8,256,128]{2,1,0:T(8,128)S(1)}, f32[8,256,128]{2,1,0:T(8,128)S(1)}) custom-call(bf16[128,1024]{1,0:T(8,128)(2,1)S(1)} %get-tuple-element.34.normed, bf16[128,1024]{1,0:T(8,128)(2,1)} %get-tuple-element.35.grad_hbm, ...), custom_call_target="tpu_custom_call" | custom-call | tf_op jit(solution)/shard_map/project/pallas_call | solution.py:48
  28.9 0.1 collective-permute-start.6
  29.0 3.6 %collective-permute-start.7 = (bf16[128,1024]{1,0:T(8,128)(2,1)S(1)}, bf16[128,1024]{1,0:T(8,128)(2,1)S(1)}, u32[]{:S(2)}, u32[]{:S(2)}) collective-permute-start(bf16[128,1024]{1,0:T(8,128)(2,1)S(1)} %get-tuple-element.38.own_grad), channel_id=1, source_target_pairs={{1,2},{2,1},{3,4},{4,3},{5,6},{6,5},{7,8},{8,7},{9,10},{10,9},{11,... | collective-permute-start | bytes 786440 | tf_op jit(solution)/shard_map/ppermute | solution.py:80
  32.6 0.0 collective-permute-done.2.chip_normed
  32.6 0.0 collective-permute-done.3.off_normed
  32.6 4.4 %attend.1 = (f32[24,256]{1,0:T(8,128)S(1)}, bf16[128,1024]{1,0:T(8,128)(2,1)S(1)}, bf16[128,1024]{1,0:T(8,128)(2,1)S(1)}, bf16[8,256,128]{2,1,0:T(8,128)(2,1)S(1...) custom-call(bf16[128,1024]{1,0:T(8,128)(2,1)S(1)} %collective-permut, ...), custom_call_target="tpu_custom_call" | custom-call | tf_op jit(solution)/shard_map/attend/pallas_call | solution.py:48
  37.1 0.1 collective-permute-start.4
  37.2 3.0 %collective-permute-start.5 = (f32[24,256]{1,0:T(8,128)S(1)}, f32[24,256]{1,0:T(8,128)S(1)}, u32[]{:S(2)}, u32[]{:S(2)}) collective-permute-start(f32[24,256]{1,0:T(8,128)S(1)} %get-tuple-element.48), channel_id=1, source_target_pairs={{1,2},{2,1},{3,4},{4,3},{5,6},{6,5},{7,8},{8,7},{9,10},{10,9},{11,... | collective-permute-start | bytes 73736 | tf_op jit(solution)/shard_map/ppermute | solution.py:80
  40.2 1.9 %product.1 = (bf16[128,1024]{1,0:T(8,128)(2,1)}, f32[128,1024]{1,0:T(8,128)S(1)}, f32[128,1024]{1,0:T(8,128)S(1)}, f32[128,1024]{1,0:T(8,128)S(1)}) custom-call(bf16[8,256,128]{2,1,0:T(8,128)(2,1)S(1)} %get-tuple-element.41.weights, bf16[8,256,128]{2,1,0:T(8,128)(2,1)S(1)} %get-tuple-element.42.grad_scores, ...), custom_call_target="tpu_custom_call" | custom-call | tf_op jit(solution)/shard_map/product/pallas_call | solution.py:48
  42.1 0.0 collective-permute-done.6.chip_grad
  42.1 0.0 collective-permute-done.7.off_grad
  42.1 0.0 collective-permute-done.4.chip_stats
  42.2 0.1 collective-permute-done.5.off_stats
  42.3 3.8 %finish.1 = bf16[128,1024]{1,0:T(8,128)(2,1)} custom-call(f32[24,256]{1,0:T(8,128)S(1)} %collective-permute-done.4.chip_stats, f32[24,256]{1,0:T(8,128)S(1)} %collective-permute-done.5.off_stats, bf16[144,1024]{1,0:T(8,128)(2,1)S(1)} %collective-permute-done.chip.chip_first, bf16[144,1024]{1,0:T(8,128)(2,1)S(1)} %collective-permute-done.1.off.off_first, ...), custom_call_target="tpu_custom_call" | custom-call | tf_op jit(solution)/shard_map/finish/pallas_call | solution.py:48
Async XLA Ops:
  4.0 14.3 %collective-permute-start = (bf16[144,1024]{1,0:T(8,128)(2,1)}, bf16[144,1024]{1,0:T(8,128)(2,1)S(1)}, u32[]{:S(2)}, u32[]{:S(2)}) collective-permute-start(bf16[144,1024]{1,0:T(8,128)(2,1)} %get-tuple-element.30), channel_id=1, source_target_pairs={{0,1},{1,0},{2,3},{3,2},{4,5},{5,4},{6,7},{7,6},{8,9},{9,8},{10,11... | collective-permute-start | bytes 884744 | tf_op jit(solution)/shard_map/ppermute | solution.py:83
  4.1 14.2 %collective-permute-start.1 = (bf16[144,1024]{1,0:T(8,128)(2,1)}, bf16[144,1024]{1,0:T(8,128)(2,1)S(1)}, u32[]{:S(2)}, u32[]{:S(2)}) collective-permute-start(bf16[144,1024]{1,0:T(8,128)(2,1)} %get-tuple-element.31), channel_id=1, source_target_pairs={{1,2},{2,1},{3,4},{4,3},{5,6},{6,5},{7,8},{8,7},{9,10},{10,9},{11,... | collective-permute-start | bytes 884744 | tf_op jit(solution)/shard_map/ppermute | solution.py:80
  8.6 12.7 %all-to-all-start = ((bf16[16,8,640]{2,1,0:T(8,128)(2,1)}), bf16[16,8,640]{2,1,0:T(8,128)(2,1)S(1)}, u32[]{:S(2)}, u32[]{:S(2)}) async-start(bf16[16,8,640]{2,1,0:T(8,128)(2,1)} %bitcast.11), calls=%async_computation | async-start | bytes 327680 | tf_op jit(solution)/shard_map/all_to_all | solution.py:613
  21.8 10.8 %collective-permute-start.2 = (bf16[128,1024]{1,0:T(8,128)(2,1)S(1)}, bf16[128,1024]{1,0:T(8,128)(2,1)S(1)}, u32[]{:S(2)}, u32[]{:S(2)}) collective-permute-start(bf16[128,1024]{1,0:T(8,128)(2,1)S(1)} %get-tuple-element.34.normed), channel_id=1, source_target_pairs={{0,1},{1,0},{2,3},{3,2},{4,5},{5,4},{6,7},{7,6},{8,9},{9,8},{10,11... | collective-permute-start | bytes 786440 | tf_op jit(solution)/shard_map/ppermute | solution.py:83
  23.1 9.6 %collective-permute-start.3 = (bf16[128,1024]{1,0:T(8,128)(2,1)S(1)}, bf16[128,1024]{1,0:T(8,128)(2,1)S(1)}, u32[]{:S(2)}, u32[]{:S(2)}) collective-permute-start(bf16[128,1024]{1,0:T(8,128)(2,1)S(1)} %get-tuple-element.34.normed), channel_id=1, source_target_pairs={{1,2},{2,1},{3,4},{4,3},{5,6},{6,5},{7,8},{8,7},{9,10},{10,9},{11,... | collective-permute-start | bytes 786440 | tf_op jit(solution)/shard_map/ppermute | solution.py:80
  28.9 13.2 %collective-permute-start.6 = (bf16[128,1024]{1,0:T(8,128)(2,1)S(1)}, bf16[128,1024]{1,0:T(8,128)(2,1)S(1)}, u32[]{:S(2)}, u32[]{:S(2)}) collective-permute-start(bf16[128,1024]{1,0:T(8,128)(2,1)S(1)} %get-tuple-element.38.own_grad), channel_id=1, source_target_pairs={{0,1},{1,0},{2,3},{3,2},{4,5},{5,4},{6,7},{7,6},{8,9},{9,8},{10,11... | collective-permute-start | bytes 786440 | tf_op jit(solution)/shard_map/ppermute | solution.py:83
  29.0 13.2 %collective-permute-start.7 = (bf16[128,1024]{1,0:T(8,128)(2,1)S(1)}, bf16[128,1024]{1,0:T(8,128)(2,1)S(1)}, u32[]{:S(2)}, u32[]{:S(2)}) collective-permute-start(bf16[128,1024]{1,0:T(8,128)(2,1)S(1)} %get-tuple-element.38.own_grad), channel_id=1, source_target_pairs={{1,2},{2,1},{3,4},{4,3},{5,6},{6,5},{7,8},{8,7},{9,10},{10,9},{11,... | collective-permute-start | bytes 786440 | tf_op jit(solution)/shard_map/ppermute | solution.py:80
  37.1 5.1 %collective-permute-start.4 = (f32[24,256]{1,0:T(8,128)S(1)}, f32[24,256]{1,0:T(8,128)S(1)}, u32[]{:S(2)}, u32[]{:S(2)}) collective-permute-start(f32[24,256]{1,0:T(8,128)S(1)} %get-tuple-element.48), channel_id=1, source_target_pairs={{0,1},{1,0},{2,3},{3,2},{4,5},{5,4},{6,7},{7,6},{8,9},{9,8},{10,11... | collective-permute-start | bytes 73736 | tf_op jit(solution)/shard_map/ppermute | solution.py:83
  37.2 5.1 %collective-permute-start.5 = (f32[24,256]{1,0:T(8,128)S(1)}, f32[24,256]{1,0:T(8,128)S(1)}, u32[]{:S(2)}, u32[]{:S(2)}) collective-permute-start(f32[24,256]{1,0:T(8,128)S(1)} %get-tuple-element.48), channel_id=1, source_target_pairs={{1,2},{2,1},{3,4},{4,3},{5,6},{6,5},{7,8},{8,7},{9,10},{10,9},{11,... | collective-permute-start | bytes 73736 | tf_op jit(solution)/shard_map/ppermute | solution.py:80

commit v15 on v14

--- a/solution.py
+++ b/solution.py
@@ -313,17 +313,58 @@
     return jnp.where(first, stacked[:m], stacked[m:])
 
 
+def near_places(m):
+    odd = is_odd()
+    return (1 - odd) * 2 * m, odd * 2 * m
+
+
 def project_kernel(
-    scale, pair, normed, grad_hbm, w_qkv_hbm, qkv_out, w_qkv, grad_out, scores_out, products_out, sems
+    scale,
+    pair,
+    count,
+    normed,
+    chip_first,
+    off_first,
+    window_hbm,
+    grad_hbm,
+    w_qkv_hbm,
+    qkv_out,
+    w_qkv,
+    grad_out,
+    scores_out,
+    products_out,
+    bias_out,
+    near_bias_out,
+    window,
+    sems,
 ):
     m, channels = normed.shape
     width = channels // PIECES
     starts = [part * channels + c * width for c in range(PIECES) for part in range(3)]
     copies = start_all(
         [(grad_hbm, grad_out)]
-        + [(w_qkv_hbm.at[:, pl.ds(at, width)], w_qkv.at[:, pl.ds(at, width)]) for at in starts],
+        + [(w_qkv_hbm.at[:, pl.ds(at, width)], w_qkv.at[:, pl.ds(at, width)]) for at in starts]
+        + [(window_hbm, window)],
         sems,
     )
+    chip_at, off_at = near_places(m)
+    reach = [meta_of(side, count)[:8, 2 * LANES : 2 * LANES + m] for side in (chip_first, off_first)]
+    reach = jnp.concatenate(reach, 1)
+    key_at = iota((m, 2 * m), 0) + m
+    lane = iota((m, 2 * m), 1)
+    query_at = jnp.where(lane < m, lane + chip_at, lane - m + off_at)
+    keep = (key_at >= query_at - reach[0:1, :]) & (key_at <= query_at + reach[1:2, :])
+    near_bias_out[...] = jnp.where(keep, 0.0, -jnp.inf).astype(F32)
+    copies[-1].wait()
+    me = lax.axis_index("node")
+    row = iota((3 * m, m), 0)
+    key_at = jnp.where(row < m, row + chip_at, jnp.where(row < 2 * m, row - m + off_at, row - m))
+    query_at = iota((3 * m, m), 1) + m
+    at_end = (me == 0) | (me == lax.axis_size("node") - 1)
+    missing = (row >= m) & (row < 2 * m) & at_end
+    keep = (key_at >= query_at - window[0:1, :]) & (key_at <= query_at + window[1:2, :])
+    bias = jnp.where(keep & jnp.logical_not(missing), 0.0, -jnp.inf).astype(F32)
+    bias_out[...] = jnp.transpose(bias)
     for i, at in enumerate(starts):
         copies[1 + i].wait()
         cols = slice(at, at + width)
@@ -341,11 +382,6 @@
             products_out[p] = mm_nt(halves(grad_out[:, q]), qkv_out[:, v])
 
 
-def near_places(m):
-    odd = is_odd()
-    return (1 - odd) * 2 * m, odd * 2 * m
-
-
 def attend_kernel(
     scale,
     pair,
@@ -356,7 +392,7 @@
     own_grad,
     own_scores,
     own_products,
-    window_hbm,
+    bias,
     w_out_hbm,
     cot_hbm,
     stats_out,
@@ -367,14 +403,11 @@
     near_q,
     w_out,
     cot,
-    window,
     sems,
 ):
-    fetch = start_all([(window_hbm, window), (w_out_hbm, w_out), (cot_hbm, cot)], sems)
+    fetch = start_all([(w_out_hbm, w_out), (cot_hbm, cot)], sems)
     m, channels = chip_normed.shape
     pairs = channels // pair
-    devices = lax.axis_size("node")
-    me = lax.axis_index("node")
     near = jnp.concatenate([chip_normed[...], off_normed[...]], 0)
 
     def bring(group):
@@ -387,14 +420,6 @@
         return blocks
 
     brought = {0: bring(0)}
-    fetch[0].wait()
-    row = iota((3 * m, m), 0)
-    chip_at, off_at = near_places(m)
-    key_at = jnp.where(row < m, row + chip_at, jnp.where(row < 2 * m, row - m + off_at, row - m))
-    query_at = iota((3 * m, m), 1) + m
-    missing = (row >= m) & (row < 2 * m) & ((me == 0) | (me == devices - 1))
-    keep = (key_at >= query_at - window[0:1, :]) & (key_at <= query_at + window[1:2, :])
-    bias = jnp.transpose(jnp.where(keep & jnp.logical_not(missing), 0.0, -jnp.inf).astype(F32))
     lane = iota((CHUNK, LANES), 1)
     stats = [jnp.zeros((CHUNK, LANES), F32) for _ in range(2 * m // CHUNK)]
 
@@ -443,7 +468,7 @@
         attention[:, cols] = merge(mm(weights, values)).astype(BF16)
         grad_query[:, cols] = (merge(mm(grad_scores, keys)) * scale).astype(BF16)
     stats_out[...] = jnp.transpose(jnp.concatenate(stats, 0))[: 3 * pairs]
-    for copy in fetch[1:]:
+    for copy in fetch:
         copy.wait()
 
 
@@ -480,11 +505,9 @@
 
 def finish_kernel(
     pair,
-    count,
     chip_stats,
     off_stats,
-    chip_first,
-    off_first,
+    bias,
     near_q,
     chip_grad,
     off_grad,
@@ -499,14 +522,6 @@
     grad_out,
 ):
     m, channels = normal.shape
-    reach = [meta_of(side, count)[:8, 2 * LANES : 2 * LANES + m] for side in (chip_first, off_first)]
-    reach = jnp.concatenate(reach, 1)
-    key_at = iota((m, 2 * m), 0) + m
-    lane = iota((m, 2 * m), 1)
-    chip_at, off_at = near_places(m)
-    query_at = jnp.where(lane < m, lane + chip_at, lane - m + off_at)
-    keep = (key_at >= query_at - reach[0:1, :]) & (key_at <= query_at + reach[1:2, :])
-    bias = jnp.where(keep, 0.0, -jnp.inf).astype(F32)
     pairs = channels // pair
 
     stats = []
@@ -522,7 +537,7 @@
         grad = jnp.concatenate([chip_grad[:, cols], off_grad[:, cols]], 0)
         return query, grad, mm_nt(key2, query), mm_nt(value2, grad)
 
-    total = grad_normed[...]
+    turned = None
     group = 2
     gks, gvs = [], []
     ahead = multiply(0)
@@ -548,10 +563,11 @@
         if len(gks) == group:
             at = channels + (p + 1 - group) * pair
             width = group * pair
-            total = total + mm_nt(jnp.concatenate(gks, 1), w_qkv[:, at : at + width])
-            at = at + channels
-            total = total + mm_nt(jnp.concatenate(gvs, 1), w_qkv[:, at : at + width])
+            for blocks, start in ((gks, at), (gvs, at + channels)):
+                piece = mm_nt(w_qkv[:, start : start + width], jnp.concatenate(blocks, 1))
+                turned = piece if turned is None else turned + piece
             gks, gvs = [], []
+    total = grad_normed[...] + jnp.transpose(turned)
     centred = (
         total
         - jnp.mean(total, -1, keepdims=True)
@@ -643,12 +659,13 @@
     )
     chip_normed, off_normed = exchange(normed, normed, "node")
     own_block = ((pairs, 2 * m, m), F32)
-    own_qkv, w_qkv, own_grad, own_scores, own_products = call(
-        functools.partial(project_kernel, scale, pair),
-        [((m, 3 * channels), BF16), (w_qkv.shape, BF16), rows, own_block, own_block],
-        [normed, own_grad, w_qkv],
-        hbm=(1, 2),
-        scratch=[dma(3 * PIECES + 1)],
+    own_qkv, w_qkv, own_grad, own_scores, own_products, bias, near_bias = call(
+        functools.partial(project_kernel, scale, pair, meta_rows),
+        [((m, 3 * channels), BF16), (w_qkv.shape, BF16), rows, own_block, own_block]
+        + [((m, 3 * m), F32), ((m, 2 * m), F32)],
+        [normed, from_chip, from_off, window, own_grad, w_qkv],
+        hbm=(3, 4, 5),
+        scratch=like(window) + [dma(3 * PIECES + 2)],
         name="project",
     )
     chip_grad, off_grad = exchange(own_grad, own_grad, "node")
@@ -666,9 +683,9 @@
             rows,
         ],
         [chip_normed, off_normed, w_qkv, own_qkv, own_grad, own_scores, own_products]
-        + [window, w_out, cotangent],
-        hbm=(7, 8, 9),
-        scratch=like(window) + [dma(3)],
+        + [bias, w_out, cotangent],
+        hbm=(8, 9),
+        scratch=[dma(2)],
         name="attend",
     )
     chip_stats, off_stats = exchange(stats, stats, "node")
@@ -696,13 +713,12 @@
         name="product",
     )
     (mesh_grad,) = call(
-        functools.partial(finish_kernel, pair, meta_rows),
+        functools.partial(finish_kernel, pair),
         [rows],
         [
             chip_stats,
             off_stats,
-            from_chip,
-            from_off,
+            near_bias,
             near_q,
             chip_grad,
             off_grad,

time: 46.5 us -> 49.6 us (1.067)
  Pallas kernels: 23.7 us -> 26.8 us
  starting transfers between devices: 19.9 us -> 19.4 us
    pallas_call x8, Pallas kernels: 23.7 us -> 26.8 us  [call(): pl.pallas_call(kernel, out_shape=[(pltpu.HBM if i in hbm_outs else jax.Sh...]
  transfers between devices with their start and end apart: 9 -> 9, of which waited for: 2 -> 2; matrix products, arithmetic and copies ran while one was open for 0% -> 0% of each run, Pallas kernels for 35% -> 38%
where the time goes in v15:
time: 49.6 us; the launch traced here: 49.2 us
  Pallas kernels  26.8 us (54%)
  starting transfers between devices  19.4 us (39%)
  waiting for transfers between devices  2.21 us (4%)
  between operations  0.79 us (2%)
    pallas_call x8, Pallas kernels, call(): pl.pallas_call(kernel, out_shape=[(pltpu.HBM if i in hbm_outs else jax.Sh...  26.8 us
    ppermute x4, starting transfers between devices, exchange(): lax.ppermute(off_message, axis, [p for i in range(1, n - 1, 2) for p in (...  12.6 us
    all_to_all x1, starting transfers between devices, body(): lax.all_to_all(far_message.reshape(devices, 2 * far_depth, far_block[1]),...  5.33 us
    all_to_all x1, waiting for transfers between devices, body(): lax.all_to_all(far_message.reshape(devices, 2 * far_depth, far_block[1]),...  1.6 us
    ppermute x4, starting transfers between devices, exchange(): lax.ppermute(chip_message, axis, [p for i in range(0, n, 2) for p in ((i,...  1.49 us
  transfers between devices with their start and end apart: 9, of which 2 were waited for; matrix products, arithmetic and copies ran while one was open for 0% of the time, Pallas kernels for 38%

profile of v15, /device:TPU:1, one launch (start us, length us, event | category | flops | bytes accessed | tf_op | source)
XLA Modules:
  0.0 49.2 jit_solution(17127339049327575604)
XLA Ops:
  0.6 3.4 %pack.1 = (bf16[128,640]{1,0:T(8,128)(2,1)}, bf16[144,1024]{1,0:T(8,128)(2,1)}, bf16[144,1024]{1,0:T(8,128)(2,1)}, bf16[1024,1024]{1,0:T(8,128)(2,1)S(1)}) custom-call(bf16[512,1024]{1,0:T(8,128)(2,1)} %grid_hbm.3, s32[2,128]{1,0:T(2,128)} %window_hbm.3, s32[32,128]{1,0:T(8,128)} %bitcast.12, s32[32,128]{1,0:T(8,128)} %bitcast.13, s32[1,2]{1,0:T(1,128)} %bitcast.16, ...), custom_call_target="tpu_custom_call" | custom-call | tf_op jit(solution)/shard_map/pack/pallas_call | solution.py:48
  4.0 0.1 collective-permute-start
  4.1 4.5 %collective-permute-start.1 = (bf16[144,1024]{1,0:T(8,128)(2,1)}, bf16[144,1024]{1,0:T(8,128)(2,1)S(1)}, u32[]{:S(2)}, u32[]{:S(2)}) collective-permute-start(bf16[144,1024]{1,0:T(8,128)(2,1)} %get-tuple-element.33), channel_id=1, source_target_pairs={{1,2},{2,1},{3,4},{4,3},{5,6},{6,5},{7,8},{8,7},{9,10},{10,9},{11,... | collective-permute-start | bytes 884744 | tf_op jit(solution)/shard_map/ppermute | solution.py:80
  8.6 5.3 %all-to-all-start = ((bf16[16,8,640]{2,1,0:T(8,128)(2,1)}), bf16[16,8,640]{2,1,0:T(8,128)(2,1)S(1)}, u32[]{:S(2)}, u32[]{:S(2)}) async-start(bf16[16,8,640]{2,1,0:T(8,128)(2,1)} %bitcast.11), calls=%async_computation | async-start | bytes 327680 | tf_op jit(solution)/shard_map/all_to_all | solution.py:629
  13.9 4.3 %own.1 = (f32[128,1024]{1,0:T(8,128)S(1)}, bf16[128,1024]{1,0:T(8,128)(2,1)}) custom-call(bf16[512,1024]{1,0:T(8,128)(2,1)} %grid_hbm.3, bf16[128,1024]{1,0:T(8,128)(2,1)} %mesh_in_hbm.1, s32[8,128]{1,0:T(8,128)} %bitcast.14, s32[8,128]{1,0:T(8,128)} %bitcast.15, bf16[128,1024]{1,0:T(8,128)(2,1)} %cot_hbm.3, bf16[1024,1024]{1,0:T(8,128)(2,1)} %w_out_hbm.3, ...), custom_call_target="tpu_custom_call" | custom-call | tf_op jit(solution)/shard_map/own/pallas_call | solution.py:48
  18.3 0.0 collective-permute-done.chip.chip_first
  18.3 0.0 collective-permute-done.1.off.off_first
  18.3 1.4 %side.1.partial = f32[128,1024]{1,0:T(8,128)S(1)} custom-call(bf16[144,1024]{1,0:T(8,128)(2,1)S(1)} %collective-permute-done.chip.chip_first, bf16[144,1024]{1,0:T(8,128)(2,1)S(1)} %collective-permute-done.1.off.off_first, bf16[1024,1024]{1,0:T(8,128)(2,1)S(1)} %get-tuple-element.34.w_edge, f32[128,1024]{1,0:T(8,128)S(1)} %get-tuple-element.35.partial), custom_call_target="tpu_custom_call" | custom-call | flops 8000000000 | tf_op jit(solution)/shard_map/side/pallas_call | solution.py:48
  19.7 1.6 %all-to-all-done = bf16[16,8,640]{2,1,0:T(8,128)(2,1)S(1)} async-done(((bf16[16,8,640]{2,1,0:T(8,128)(2,1)}), bf16[16,8,640]{2,1,0:T(8,128)(2,1)S(1)}, u32[]{:S(2)}, u32[]{:S(2)}) %all-to-all-start) | async-done | bytes 163872 | tf_op jit(solution)/shard_map/all_to_all | solution.py:629
  21.3 0.5 latent.1
  21.8 1.2 %collective-permute-start.2 = (bf16[128,1024]{1,0:T(8,128)(2,1)S(1)}, bf16[128,1024]{1,0:T(8,128)(2,1)S(1)}, u32[]{:S(2)}, u32[]{:S(2)}) collective-permute-start(bf16[128,1024]{1,0:T(8,128)(2,1)S(1)} %get-tuple-element.36.normed), channel_id=1, source_target_pairs={{0,1},{1,0},{2,3},{3,2},{4,5},{5,4},{6,7},{7,6},{8,9},{9,8},{10,11... | collective-permute-start | bytes 786440 | tf_op jit(solution)/shard_map/ppermute | solution.py:83
  23.1 1.9 %collective-permute-start.3 = (bf16[128,1024]{1,0:T(8,128)(2,1)S(1)}, bf16[128,1024]{1,0:T(8,128)(2,1)S(1)}, u32[]{:S(2)}, u32[]{:S(2)}) collective-permute-start(bf16[128,1024]{1,0:T(8,128)(2,1)S(1)} %get-tuple-element.36.normed), channel_id=1, source_target_pairs={{1,2},{2,1},{3,4},{4,3},{5,6},{6,5},{7,8},{8,7},{9,10},{10,9},{11,... | collective-permute-start | bytes 786440 | tf_op jit(solution)/shard_map/ppermute | solution.py:80
  25.0 5.4 %project.1 = (bf16[128,3072]{1,0:T(8,128)(2,1)S(1)}, bf16[1024,3072]{1,0:T(8,128)(2,1)S(1)}, bf16[128,1024]{1,0:T(8,128)(2,1)S(1)}, f32[8,256,128]{2,1,0:T(8,128...) custom-call(bf16[128,1024]{1,0:T(8,128)(2,1)S(1)} %get-tuple-element.36.normed, ...), custom_call_target="tpu_custom_call" | custom-call | tf_op jit(solution)/shard_map/project/pallas_call | solution.py:48
  30.4 0.1 collective-permute-start.6
  30.4 3.6 %collective-permute-start.7 = (bf16[128,1024]{1,0:T(8,128)(2,1)S(1)}, bf16[128,1024]{1,0:T(8,128)(2,1)S(1)}, u32[]{:S(2)}, u32[]{:S(2)}) collective-permute-start(bf16[128,1024]{1,0:T(8,128)(2,1)S(1)} %get-tuple-element.40.own_grad), channel_id=1, source_target_pairs={{1,2},{2,1},{3,4},{4,3},{5,6},{6,5},{7,8},{8,7},{9,10},{10,9},{11,... | collective-permute-start | bytes 786440 | tf_op jit(solution)/shard_map/ppermute | solution.py:80
  34.1 0.0 collective-permute-done.2.chip_normed
  34.1 0.0 collective-permute-done.3.off_normed
  34.1 5.7 %attend.1 = (f32[24,256]{1,0:T(8,128)S(1)}, bf16[128,1024]{1,0:T(8,128)(2,1)S(1)}, bf16[128,1024]{1,0:T(8,128)(2,1)S(1)}, bf16[8,256,128]{2,1,0:T(8,128)(2,1)S(1...) custom-call(bf16[128,1024]{1,0:T(8,128)(2,1)S(1)} %collective-permut, ...), custom_call_target="tpu_custom_call" | custom-call | tf_op jit(solution)/shard_map/attend/pallas_call | solution.py:48
  39.8 0.1 collective-permute-start.4
  39.9 2.6 %collective-permute-start.5 = (f32[24,256]{1,0:T(8,128)S(1)}, f32[24,256]{1,0:T(8,128)S(1)}, u32[]{:S(2)}, u32[]{:S(2)}) collective-permute-start(f32[24,256]{1,0:T(8,128)S(1)} %get-tuple-element.51), channel_id=1, source_target_pairs={{1,2},{2,1},{3,4},{4,3},{5,6},{6,5},{7,8},{8,7},{9,10},{10,9},{11,... | collective-permute-start | bytes 73736 | tf_op jit(solution)/shard_map/ppermute | solution.py:80
  42.4 2.0 %product.1 = (bf16[128,1024]{1,0:T(8,128)(2,1)}, f32[128,1024]{1,0:T(8,128)S(1)}, f32[128,1024]{1,0:T(8,128)S(1)}, f32[128,1024]{1,0:T(8,128)S(1)}) custom-call(bf16[8,256,128]{2,1,0:T(8,128)(2,1)S(1)} %get-tuple-element.44.weights, bf16[8,256,128]{2,1,0:T(8,128)(2,1)S(1)} %get-tuple-element.45.grad_scores, ...), custom_call_target="tpu_custom_call" | custom-call | tf_op jit(solution)/shard_map/product/pallas_call | solution.py:48
  44.4 0.0 collective-permute-done.6.chip_grad
  44.4 0.0 collective-permute-done.7.off_grad
  44.4 0.0 collective-permute-done.4.chip_stats
  44.4 0.6 %collective-permute-done.5.off_stats = f32[24,256]{1,0:T(8,128)S(1)} collective-permute-done((f32[24,256]{1,0:T(8,128)S(1)}, f32[24,256]{1,0:T(8,128)S(1)}, u32[]{:S(2)}, u32[]{:S(2)}) %collective-permute-start.5) | collective-permute-done | bytes 24608 | tf_op jit(solution)/shard_map/ppermute | solution.py:80
  45.0 4.2 %finish.1 = bf16[128,1024]{1,0:T(8,128)(2,1)} custom-call(f32[24,256]{1,0:T(8,128)S(1)} %collective-permute-done.4.chip_stats, f32[24,256]{1,0:T(8,128)S(1)} %collective-permute-done.5.off_stats, f32[128,256]{1,0:T(8,128)S(1)} %get-tuple-element.52.bias, bf16[256,1024]{1,0:T(8,128)(2,1)S(1)} %get-tuple-element.53.near_q, ...), custom_call_target="tpu_custom_call" | custom-call | tf_op jit(solution)/shard_map/finish/pallas_call | solution.py:48
Async XLA Ops:
  4.0 14.3 %collective-permute-start = (bf16[144,1024]{1,0:T(8,128)(2,1)}, bf16[144,1024]{1,0:T(8,128)(2,1)S(1)}, u32[]{:S(2)}, u32[]{:S(2)}) collective-permute-start(bf16[144,1024]{1,0:T(8,128)(2,1)} %get-tuple-element.32), channel_id=1, source_target_pairs={{0,1},{1,0},{2,3},{3,2},{4,5},{5,4},{6,7},{7,6},{8,9},{9,8},{10,11... | collective-permute-start | bytes 884744 | tf_op jit(solution)/shard_map/ppermute | solution.py:83
  4.1 14.2 %collective-permute-start.1 = (bf16[144,1024]{1,0:T(8,128)(2,1)}, bf16[144,1024]{1,0:T(8,128)(2,1)S(1)}, u32[]{:S(2)}, u32[]{:S(2)}) collective-permute-start(bf16[144,1024]{1,0:T(8,128)(2,1)} %get-tuple-element.33), channel_id=1, source_target_pairs={{1,2},{2,1},{3,4},{4,3},{5,6},{6,5},{7,8},{8,7},{9,10},{10,9},{11,... | collective-permute-start | bytes 884744 | tf_op jit(solution)/shard_map/ppermute | solution.py:80
  8.6 12.7 %all-to-all-start = ((bf16[16,8,640]{2,1,0:T(8,128)(2,1)}), bf16[16,8,640]{2,1,0:T(8,128)(2,1)S(1)}, u32[]{:S(2)}, u32[]{:S(2)}) async-start(bf16[16,8,640]{2,1,0:T(8,128)(2,1)} %bitcast.11), calls=%async_computation | async-start | bytes 327680 | tf_op jit(solution)/shard_map/all_to_all | solution.py:629
  21.8 12.3 %collective-permute-start.2 = (bf16[128,1024]{1,0:T(8,128)(2,1)S(1)}, bf16[128,1024]{1,0:T(8,128)(2,1)S(1)}, u32[]{:S(2)}, u32[]{:S(2)}) collective-permute-start(bf16[128,1024]{1,0:T(8,128)(2,1)S(1)} %get-tuple-element.36.normed), channel_id=1, source_target_pairs={{0,1},{1,0},{2,3},{3,2},{4,5},{5,4},{6,7},{7,6},{8,9},{9,8},{10,11... | collective-permute-start | bytes 786440 | tf_op jit(solution)/shard_map/ppermute | solution.py:83
  23.1 11.0 %collective-permute-start.3 = (bf16[128,1024]{1,0:T(8,128)(2,1)S(1)}, bf16[128,1024]{1,0:T(8,128)(2,1)S(1)}, u32[]{:S(2)}, u32[]{:S(2)}) collective-permute-start(bf16[128,1024]{1,0:T(8,128)(2,1)S(1)} %get-tuple-element.36.normed), channel_id=1, source_target_pairs={{1,2},{2,1},{3,4},{4,3},{5,6},{6,5},{7,8},{8,7},{9,10},{10,9},{11,... | collective-permute-start | bytes 786440 | tf_op jit(solution)/shard_map/ppermute | solution.py:80
  30.4 14.0 %collective-permute-start.6 = (bf16[128,1024]{1,0:T(8,128)(2,1)S(1)}, bf16[128,1024]{1,0:T(8,128)(2,1)S(1)}, u32[]{:S(2)}, u32[]{:S(2)}) collective-permute-start(bf16[128,1024]{1,0:T(8,128)(2,1)S(1)} %get-tuple-element.40.own_grad), channel_id=1, source_target_pairs={{0,1},{1,0},{2,3},{3,2},{4,5},{5,4},{6,7},{7,6},{8,9},{9,8},{10,11... | collective-permute-start | bytes 786440 | tf_op jit(solution)/shard_map/ppermute | solution.py:83
  30.4 14.0 %collective-permute-start.7 = (bf16[128,1024]{1,0:T(8,128)(2,1)S(1)}, bf16[128,1024]{1,0:T(8,128)(2,1)S(1)}, u32[]{:S(2)}, u32[]{:S(2)}) collective-permute-start(bf16[128,1024]{1,0:T(8,128)(2,1)S(1)} %get-tuple-element.40.own_grad), channel_id=1, source_target_pairs={{1,2},{2,1},{3,4},{4,3},{5,6},{6,5},{7,8},{8,7},{9,10},{10,9},{11,... | collective-permute-start | bytes 786440 | tf_op jit(solution)/shard_map/ppermute | solution.py:80
  39.8 4.6 %collective-permute-start.4 = (f32[24,256]{1,0:T(8,128)S(1)}, f32[24,256]{1,0:T(8,128)S(1)}, u32[]{:S(2)}, u32[]{:S(2)}) collective-permute-start(f32[24,256]{1,0:T(8,128)S(1)} %get-tuple-element.51), channel_id=1, source_target_pairs={{0,1},{1,0},{2,3},{3,2},{4,5},{5,4},{6,7},{7,6},{8,9},{9,8},{10,11... | collective-permute-start | bytes 73736 | tf_op jit(solution)/shard_map/ppermute | solution.py:83
  39.9 5.1 %collective-permute-start.5 = (f32[24,256]{1,0:T(8,128)S(1)}, f32[24,256]{1,0:T(8,128)S(1)}, u32[]{:S(2)}, u32[]{:S(2)}) collective-permute-start(f32[24,256]{1,0:T(8,128)S(1)} %get-tuple-element.51), channel_id=1, source_target_pairs={{1,2},{2,1},{3,4},{4,3},{5,6},{6,5},{7,8},{8,7},{9,10},{10,9},{11,... | collective-permute-start | bytes 73736 | tf_op jit(solution)/shard_map/ppermute | solution.py:80

commit v16 on v15

--- a/solution.py
+++ b/solution.py
@@ -88,6 +88,10 @@
 
 def is_odd():
     return lax.axis_index("node") % 2
+
+
+def everywhere():
+    return lax.axis_index("node") >= 0
 
 
 def gelu(projected):
@@ -347,28 +351,32 @@
         + [(window_hbm, window)],
         sems,
     )
-    chip_at, off_at = near_places(m)
-    reach = [meta_of(side, count)[:8, 2 * LANES : 2 * LANES + m] for side in (chip_first, off_first)]
-    reach = jnp.concatenate(reach, 1)
-    key_at = iota((m, 2 * m), 0) + m
-    lane = iota((m, 2 * m), 1)
-    query_at = jnp.where(lane < m, lane + chip_at, lane - m + off_at)
-    keep = (key_at >= query_at - reach[0:1, :]) & (key_at <= query_at + reach[1:2, :])
-    near_bias_out[...] = jnp.where(keep, 0.0, -jnp.inf).astype(F32)
-    copies[-1].wait()
-    me = lax.axis_index("node")
-    row = iota((3 * m, m), 0)
-    key_at = jnp.where(row < m, row + chip_at, jnp.where(row < 2 * m, row - m + off_at, row - m))
-    query_at = iota((3 * m, m), 1) + m
-    at_end = (me == 0) | (me == lax.axis_size("node") - 1)
-    missing = (row >= m) & (row < 2 * m) & at_end
-    keep = (key_at >= query_at - window[0:1, :]) & (key_at <= query_at + window[1:2, :])
-    bias = jnp.where(keep & jnp.logical_not(missing), 0.0, -jnp.inf).astype(F32)
-    bias_out[...] = jnp.transpose(bias)
+    def masks():
+        chip_at, off_at = near_places(m)
+        reach = [meta_of(side, count)[:8, 2 * LANES : 2 * LANES + m] for side in (chip_first, off_first)]
+        reach = jnp.concatenate(reach, 1)
+        key_at = iota((m, 2 * m), 0) + m
+        lane = iota((m, 2 * m), 1)
+        query_at = jnp.where(lane < m, lane + chip_at, lane - m + off_at)
+        keep = (key_at >= query_at - reach[0:1, :]) & (key_at <= query_at + reach[1:2, :])
+        near_bias_out[...] = jnp.where(keep, 0.0, -jnp.inf).astype(F32)
+        copies[-1].wait()
+        me = lax.axis_index("node")
+        row = iota((3 * m, m), 0)
+        key_at = jnp.where(row < m, row + chip_at, jnp.where(row < 2 * m, row - m + off_at, row - m))
+        query_at = iota((3 * m, m), 1) + m
+        at_end = (me == 0) | (me == lax.axis_size("node") - 1)
+        missing = (row >= m) & (row < 2 * m) & at_end
+        keep = (key_at >= query_at - window[0:1, :]) & (key_at <= query_at + window[1:2, :])
+        bias = jnp.where(keep & jnp.logical_not(missing), 0.0, -jnp.inf).astype(F32)
+        bias_out[...] = jnp.transpose(bias)
+
     for i, at in enumerate(starts):
         copies[1 + i].wait()
         cols = slice(at, at + width)
         qkv_out[:, cols] = mm(normed[...], w_qkv[:, cols]).astype(BF16)
+        if i == 0:
+            masks()
         if i % 3 < 2:
             continue
         if i == 2:
@@ -408,66 +416,70 @@
     fetch = start_all([(w_out_hbm, w_out), (cot_hbm, cot)], sems)
     m, channels = chip_normed.shape
     pairs = channels // pair
-    near = jnp.concatenate([chip_normed[...], off_normed[...]], 0)
-
-    def bring(group):
-        cols = slice(group * 2 * pair, (group + 1) * 2 * pair)
-        near_q[:, cols] = mm(near, w_qkv[:, cols]).astype(BF16) * jnp.asarray(scale, BF16)
-        blocks = []
-        for part in range(1, 3):
-            at = part * channels + group * 2 * pair
-            blocks.append(mm(near, w_qkv[:, at : at + 2 * pair]).astype(BF16))
-        return blocks
-
-    brought = {0: bring(0)}
-    lane = iota((CHUNK, LANES), 1)
-    stats = [jnp.zeros((CHUNK, LANES), F32) for _ in range(2 * m // CHUNK)]
-
-    def near_of(p):
-        return [b[:, p % 2 * pair : (p % 2 + 1) * pair] for b in brought[p // 2]]
-
-    def multiply(p):
-        cols = slice(p * pair, (p + 1) * pair)
-        keys, values = near_of(p)
-        return (
-            mm_nt(halves(own_qkv[:, cols], scale), keys),
-            mm_nt(halves(own_grad[:, cols]), values),
-        )
-
-    ahead = multiply(0)
-    for p in range(pairs):
-        scores, grad_prob = ahead
-        if p + 1 < pairs:
-            if p % 2 == 0 and p + 2 < pairs:
-                brought[p // 2 + 1] = bring(p // 2 + 1)
-            ahead = multiply(p + 1)
-        weights, grad_scores = [], []
-        for at in range(0, 2 * m, CHUNK):
-            part = slice(at, at + CHUNK)
-            place = slice(at % m, at % m + CHUNK)
-            raw = jnp.concatenate([scores[part], own_scores[p, part]], 1) + bias[place]
-            top = jnp.max(raw, 1, keepdims=True)
-            shifted = jnp.exp(raw - top)
-            inv_sum = 1.0 / jnp.sum(shifted, 1, keepdims=True)
-            probs = shifted * inv_sum
-            product = jnp.concatenate([grad_prob[part], own_products[p, part]], 1)
-            delta = jnp.sum(probs * product, 1, keepdims=True)
-            weights.append(probs.astype(BF16))
-            grad_scores.append((probs * (product - delta)).astype(BF16))
-            for k, column in enumerate((top, inv_sum, delta)):
-                stats[at // CHUNK] = jnp.where(lane == k * pairs + p, column, stats[at // CHUNK])
-        weights = jnp.concatenate(weights, 0)
-        grad_scores = jnp.concatenate(grad_scores, 0)
-        weights_out[p] = weights[:, 2 * m :]
-        scores_out[p] = grad_scores[:, 2 * m :]
-        keys, values = (
-            jnp.concatenate([block, own_qkv[:, at + p * pair : at + (p + 1) * pair]], 0)
-            for block, at in zip(near_of(p), (channels, 2 * channels))
-        )
-        cols = slice(p * pair, (p + 1) * pair)
-        attention[:, cols] = merge(mm(weights, values)).astype(BF16)
-        grad_query[:, cols] = (merge(mm(grad_scores, keys)) * scale).astype(BF16)
-    stats_out[...] = jnp.transpose(jnp.concatenate(stats, 0))[: 3 * pairs]
+
+    @pl.when(everywhere())
+    def _():
+        near = jnp.concatenate([chip_normed[...], off_normed[...]], 0)
+
+        def bring(group):
+            cols = slice(group * 2 * pair, (group + 1) * 2 * pair)
+            near_q[:, cols] = mm(near, w_qkv[:, cols]).astype(BF16) * jnp.asarray(scale, BF16)
+            blocks = []
+            for part in range(1, 3):
+                at = part * channels + group * 2 * pair
+                blocks.append(mm(near, w_qkv[:, at : at + 2 * pair]).astype(BF16))
+            return blocks
+
+        brought = {0: bring(0)}
+        lane = iota((CHUNK, LANES), 1)
+        stats = [jnp.zeros((CHUNK, LANES), F32) for _ in range(2 * m // CHUNK)]
+
+        def near_of(p):
+            return [b[:, p % 2 * pair : (p % 2 + 1) * pair] for b in brought[p // 2]]
+
+        def multiply(p):
+            cols = slice(p * pair, (p + 1) * pair)
+            keys, values = near_of(p)
+            return (
+                mm_nt(halves(own_qkv[:, cols], scale), keys),
+                mm_nt(halves(own_grad[:, cols]), values),
+            )
+
+        ahead = multiply(0)
+        for p in range(pairs):
+            scores, grad_prob = ahead
+            if p + 1 < pairs:
+                if p % 2 == 0 and p + 2 < pairs:
+                    brought[p // 2 + 1] = bring(p // 2 + 1)
+                ahead = multiply(p + 1)
+            weights, grad_scores = [], []
+            for at in range(0, 2 * m, CHUNK):
+                part = slice(at, at + CHUNK)
+                place = slice(at % m, at % m + CHUNK)
+                raw = jnp.concatenate([scores[part], own_scores[p, part]], 1) + bias[place]
+                top = jnp.max(raw, 1, keepdims=True)
+                shifted = jnp.exp(raw - top)
+                inv_sum = 1.0 / jnp.sum(shifted, 1, keepdims=True)
+                probs = shifted * inv_sum
+                product = jnp.concatenate([grad_prob[part], own_products[p, part]], 1)
+                delta = jnp.sum(probs * product, 1, keepdims=True)
+                weights.append(probs.astype(BF16))
+                grad_scores.append((probs * (product - delta)).astype(BF16))
+                for k, column in enumerate((top, inv_sum, delta)):
+                    stats[at // CHUNK] = jnp.where(lane == k * pairs + p, column, stats[at // CHUNK])
+            weights = jnp.concatenate(weights, 0)
+            grad_scores = jnp.concatenate(grad_scores, 0)
+            weights_out[p] = weights[:, 2 * m :]
+            scores_out[p] = grad_scores[:, 2 * m :]
+            keys, values = (
+                jnp.concatenate([block, own_qkv[:, at + p * pair : at + (p + 1) * pair]], 0)
+                for block, at in zip(near_of(p), (channels, 2 * channels))
+            )
+            cols = slice(p * pair, (p + 1) * pair)
+            attention[:, cols] = merge(mm(weights, values)).astype(BF16)
+            grad_query[:, cols] = (merge(mm(grad_scores, keys)) * scale).astype(BF16)
+        stats_out[...] = jnp.transpose(jnp.concatenate(stats, 0))[: 3 * pairs]
+
     for copy in fetch:
         copy.wait()
 
@@ -495,11 +507,15 @@
     mesh_out[...] = (latent[...].astype(F32) + mm(attention[...], w_out[...])).astype(BF16)
     out = pltpu.make_async_copy(mesh_out, mesh_out_hbm, sems.at[0])
     out.start()
-    for p in range(channels // pair):
-        cols = slice(p * pair, (p + 1) * pair)
-        grad_key[:, cols] = mm_tn(grad_scores[p], halves(own_qkv[:, cols], scale))
-        grad_value[:, cols] = mm_tn(weights[p], halves(own_grad[:, cols]))
-    grad_normed[...] = mm_nt(grad_query[...], w_qkv[:, :channels])
+
+    @pl.when(everywhere())
+    def _():
+        for p in range(channels // pair):
+            cols = slice(p * pair, (p + 1) * pair)
+            grad_key[:, cols] = mm_tn(grad_scores[p], halves(own_qkv[:, cols], scale))
+            grad_value[:, cols] = mm_tn(weights[p], halves(own_grad[:, cols]))
+        grad_normed[...] = mm_nt(grad_query[...], w_qkv[:, :channels])
+
     out.wait()
 
 
@@ -537,7 +553,7 @@
         grad = jnp.concatenate([chip_grad[:, cols], off_grad[:, cols]], 0)
         return query, grad, mm_nt(key2, query), mm_nt(value2, grad)
 
-    turned = None
+    total = grad_normed[...]
     group = 2
     gks, gvs = [], []
     ahead = multiply(0)
@@ -564,10 +580,10 @@
             at = channels + (p + 1 - group) * pair
             width = group * pair
             for blocks, start in ((gks, at), (gvs, at + channels)):
-                piece = mm_nt(w_qkv[:, start : start + width], jnp.concatenate(blocks, 1))
-                turned = piece if turned is None else turned + piece
+                total = total + mm_nt(
+                    jnp.concatenate(blocks, 1), w_qkv[:, start : start + width]
+                )
             gks, gvs = [], []
-    total = grad_normed[...] + jnp.transpose(turned)
     centred = (
         total
         - jnp.mean(total, -1, keepdims=True)

time: 49.6 us -> 47.4 us (0.956)
  Pallas kernels: 26.8 us -> 24.4 us
    pallas_call x8, Pallas kernels: 26.8 us -> 24.4 us  [call(): pl.pallas_call(kernel, out_shape=[(pltpu.HBM if i in hbm_outs else jax.Sh...]
  transfers between devices with their start and end apart: 9 -> 9, of which waited for: 2 -> 2; matrix products, arithmetic and copies ran while one was open for 0% -> 0% of each run, Pallas kernels for 38% -> 36%
where the time goes in v16:
time: 47.4 us; the launch traced here: 47 us
  Pallas kernels  24.4 us (51%)
  starting transfers between devices  19.2 us (41%)
  waiting for transfers between devices  2.53 us (5%)
  between operations  0.79 us (2%)
    pallas_call x8, Pallas kernels, call(): pl.pallas_call(kernel, out_shape=[(pltpu.HBM if i in hbm_outs else jax.Sh...  24.4 us
    ppermute x4, starting transfers between devices, exchange(): lax.ppermute(off_message, axis, [p for i in range(1, n - 1, 2) for p in (...  12.4 us
    all_to_all x1, starting transfers between devices, body(): lax.all_to_all(far_message.reshape(devices, 2 * far_depth, far_block[1]),...  5.33 us
    all_to_all x1, waiting for transfers between devices, body(): lax.all_to_all(far_message.reshape(devices, 2 * far_depth, far_block[1]),...  1.6 us
    ppermute x4, starting transfers between devices, exchange(): lax.ppermute(chip_message, axis, [p for i in range(0, n, 2) for p in ((i,...  1.49 us
  transfers between devices with their start and end apart: 9, of which 2 were waited for; matrix products, arithmetic and copies ran while one was open for 0% of the time, Pallas kernels for 36%

profile of v16, /device:TPU:1, one launch (start us, length us, event | category | flops | bytes accessed | tf_op | source)
XLA Modules:
  0.0 47.0 jit_solution(17370438464092633742)
XLA Ops:
  0.6 3.4 %pack.1 = (bf16[128,640]{1,0:T(8,128)(2,1)}, bf16[144,1024]{1,0:T(8,128)(2,1)}, bf16[144,1024]{1,0:T(8,128)(2,1)}, bf16[1024,1024]{1,0:T(8,128)(2,1)S(1)}) custom-call(bf16[512,1024]{1,0:T(8,128)(2,1)} %grid_hbm.3, s32[2,128]{1,0:T(2,128)} %window_hbm.3, s32[32,128]{1,0:T(8,128)} %bitcast.12, s32[32,128]{1,0:T(8,128)} %bitcast.13, s32[1,2]{1,0:T(1,128)} %bitcast.16, ...), custom_call_target="tpu_custom_call" | custom-call | tf_op jit(solution)/shard_map/pack/pallas_call | solution.py:48
  4.0 0.1 collective-permute-start
  4.1 4.5 %collective-permute-start.1 = (bf16[144,1024]{1,0:T(8,128)(2,1)}, bf16[144,1024]{1,0:T(8,128)(2,1)S(1)}, u32[]{:S(2)}, u32[]{:S(2)}) collective-permute-start(bf16[144,1024]{1,0:T(8,128)(2,1)} %get-tuple-element.33), channel_id=1, source_target_pairs={{1,2},{2,1},{3,4},{4,3},{5,6},{6,5},{7,8},{8,7},{9,10},{10,9},{11,... | collective-permute-start | bytes 884744 | tf_op jit(solution)/shard_map/ppermute | solution.py:80
  8.6 5.3 %all-to-all-start = ((bf16[16,8,640]{2,1,0:T(8,128)(2,1)}), bf16[16,8,640]{2,1,0:T(8,128)(2,1)S(1)}, u32[]{:S(2)}, u32[]{:S(2)}) async-start(bf16[16,8,640]{2,1,0:T(8,128)(2,1)} %bitcast.11), calls=%async_computation | async-start | bytes 327680 | tf_op jit(solution)/shard_map/all_to_all | solution.py:645
  13.9 4.3 %own.1 = (f32[128,1024]{1,0:T(8,128)S(1)}, bf16[128,1024]{1,0:T(8,128)(2,1)}) custom-call(bf16[512,1024]{1,0:T(8,128)(2,1)} %grid_hbm.3, bf16[128,1024]{1,0:T(8,128)(2,1)} %mesh_in_hbm.1, s32[8,128]{1,0:T(8,128)} %bitcast.14, s32[8,128]{1,0:T(8,128)} %bitcast.15, bf16[128,1024]{1,0:T(8,128)(2,1)} %cot_hbm.3, bf16[1024,1024]{1,0:T(8,128)(2,1)} %w_out_hbm.3, ...), custom_call_target="tpu_custom_call" | custom-call | tf_op jit(solution)/shard_map/own/pallas_call | solution.py:48
  18.3 0.0 collective-permute-done.chip.chip_first
  18.3 0.0 collective-permute-done.1.off.off_first
  18.3 1.4 %side.1.partial = f32[128,1024]{1,0:T(8,128)S(1)} custom-call(bf16[144,1024]{1,0:T(8,128)(2,1)S(1)} %collective-permute-done.chip.chip_first, bf16[144,1024]{1,0:T(8,128)(2,1)S(1)} %collective-permute-done.1.off.off_first, bf16[1024,1024]{1,0:T(8,128)(2,1)S(1)} %get-tuple-element.34.w_edge, f32[128,1024]{1,0:T(8,128)S(1)} %get-tuple-element.35.partial), custom_call_target="tpu_custom_call" | custom-call | flops 8000000000 | tf_op jit(solution)/shard_map/side/pallas_call | solution.py:48
  19.7 1.6 %all-to-all-done = bf16[16,8,640]{2,1,0:T(8,128)(2,1)S(1)} async-done(((bf16[16,8,640]{2,1,0:T(8,128)(2,1)}), bf16[16,8,640]{2,1,0:T(8,128)(2,1)S(1)}, u32[]{:S(2)}, u32[]{:S(2)}) %all-to-all-start) | async-done | bytes 163872 | tf_op jit(solution)/shard_map/all_to_all | solution.py:645
  21.3 0.5 %latent.1 = (bf16[128,1024]{1,0:T(8,128)(2,1)S(1)}, bf16[128,1024]{1,0:T(8,128)(2,1)S(1)}, f32[128,1024]{1,0:T(8,128)S(1)}, f32[128,128]{1,0:T(8,128)S(1)}) custom-call(bf16[128,640]{1,0:T(8,128)(2,1)S(1)} %bitcast.10, f32[128,1024]{1,0:T(8,128)S(1)} %side.1.partial), custom_call_target="tpu_custom_call" | custom-call | tf_op jit(solution)/shard_map/latent/pallas_call | solution.py:48
  21.8 1.2 %collective-permute-start.2 = (bf16[128,1024]{1,0:T(8,128)(2,1)S(1)}, bf16[128,1024]{1,0:T(8,128)(2,1)S(1)}, u32[]{:S(2)}, u32[]{:S(2)}) collective-permute-start(bf16[128,1024]{1,0:T(8,128)(2,1)S(1)} %get-tuple-element.36.normed), channel_id=1, source_target_pairs={{0,1},{1,0},{2,3},{3,2},{4,5},{5,4},{6,7},{7,6},{8,9},{9,8},{10,11... | collective-permute-start | bytes 786440 | tf_op jit(solution)/shard_map/ppermute | solution.py:83
  23.1 1.9 %collective-permute-start.3 = (bf16[128,1024]{1,0:T(8,128)(2,1)S(1)}, bf16[128,1024]{1,0:T(8,128)(2,1)S(1)}, u32[]{:S(2)}, u32[]{:S(2)}) collective-permute-start(bf16[128,1024]{1,0:T(8,128)(2,1)S(1)} %get-tuple-element.36.normed), channel_id=1, source_target_pairs={{1,2},{2,1},{3,4},{4,3},{5,6},{6,5},{7,8},{8,7},{9,10},{10,9},{11,... | collective-permute-start | bytes 786440 | tf_op jit(solution)/shard_map/ppermute | solution.py:80
  25.0 5.1 %project.1 = (bf16[128,3072]{1,0:T(8,128)(2,1)S(1)}, bf16[1024,3072]{1,0:T(8,128)(2,1)S(1)}, bf16[128,1024]{1,0:T(8,128)(2,1)S(1)}, f32[8,256,128]{2,1,0:T(8,128...) custom-call(bf16[128,1024]{1,0:T(8,128)(2,1)S(1)} %get-tuple-element.36.normed, ...), custom_call_target="tpu_custom_call" | custom-call | tf_op jit(solution)/shard_map/project/pallas_call | solution.py:48
  30.0 0.1 collective-permute-start.6
  30.1 3.6 %collective-permute-start.7 = (bf16[128,1024]{1,0:T(8,128)(2,1)S(1)}, bf16[128,1024]{1,0:T(8,128)(2,1)S(1)}, u32[]{:S(2)}, u32[]{:S(2)}) collective-permute-start(bf16[128,1024]{1,0:T(8,128)(2,1)S(1)} %get-tuple-element.40.own_grad), channel_id=1, source_target_pairs={{1,2},{2,1},{3,4},{4,3},{5,6},{6,5},{7,8},{8,7},{9,10},{10,9},{11,... | collective-permute-start | bytes 786440 | tf_op jit(solution)/shard_map/ppermute | solution.py:80
  33.8 0.0 collective-permute-done.2.chip_normed
  33.8 0.0 collective-permute-done.3.off_normed
  33.8 4.2 %attend.1 = (f32[24,256]{1,0:T(8,128)S(1)}, bf16[128,1024]{1,0:T(8,128)(2,1)S(1)}, bf16[128,1024]{1,0:T(8,128)(2,1)S(1)}, bf16[8,256,128]{2,1,0:T(8,128)(2,1)S(1...) custom-call(bf16[128,1024]{1,0:T(8,128)(2,1)S(1)} %collective-permut, ...), custom_call_target="tpu_custom_call" | custom-call | tf_op jit(solution)/shard_map/attend/pallas_call | solution.py:48
  38.0 0.1 collective-permute-start.4
  38.1 2.4 %collective-permute-start.5 = (f32[24,256]{1,0:T(8,128)S(1)}, f32[24,256]{1,0:T(8,128)S(1)}, u32[]{:S(2)}, u32[]{:S(2)}) collective-permute-start(f32[24,256]{1,0:T(8,128)S(1)} %get-tuple-element.51), channel_id=1, source_target_pairs={{1,2},{2,1},{3,4},{4,3},{5,6},{6,5},{7,8},{8,7},{9,10},{10,9},{11,... | collective-permute-start | bytes 73736 | tf_op jit(solution)/shard_map/ppermute | solution.py:80
  40.4 1.8 %product.1 = (bf16[128,1024]{1,0:T(8,128)(2,1)}, f32[128,1024]{1,0:T(8,128)S(1)}, f32[128,1024]{1,0:T(8,128)S(1)}, f32[128,1024]{1,0:T(8,128)S(1)}) custom-call(bf16[8,256,128]{2,1,0:T(8,128)(2,1)S(1)} %get-tuple-element.44.weights, bf16[8,256,128]{2,1,0:T(8,128)(2,1)S(1)} %get-tuple-element.45.grad_scores, ...), custom_call_target="tpu_custom_call" | custom-call | tf_op jit(solution)/shard_map/product/pallas_call | solution.py:48
  42.3 0.0 collective-permute-done.6.chip_grad
  42.3 0.0 collective-permute-done.7.off_grad
  42.3 0.0 collective-permute-done.4.chip_stats
  42.3 0.9 %collective-permute-done.5.off_stats = f32[24,256]{1,0:T(8,128)S(1)} collective-permute-done((f32[24,256]{1,0:T(8,128)S(1)}, f32[24,256]{1,0:T(8,128)S(1)}, u32[]{:S(2)}, u32[]{:S(2)}) %collective-permute-start.5) | collective-permute-done | bytes 24608 | tf_op jit(solution)/shard_map/ppermute | solution.py:80
  43.2 3.8 %finish.1 = bf16[128,1024]{1,0:T(8,128)(2,1)} custom-call(f32[24,256]{1,0:T(8,128)S(1)} %collective-permute-done.4.chip_stats, f32[24,256]{1,0:T(8,128)S(1)} %collective-permute-done.5.off_stats, f32[128,256]{1,0:T(8,128)S(1)} %get-tuple-element.52.bias, bf16[256,1024]{1,0:T(8,128)(2,1)S(1)} %get-tuple-element.53.near_q, ...), custom_call_target="tpu_custom_call" | custom-call | tf_op jit(solution)/shard_map/finish/pallas_call | solution.py:48
Async XLA Ops:
  4.0 14.3 %collective-permute-start = (bf16[144,1024]{1,0:T(8,128)(2,1)}, bf16[144,1024]{1,0:T(8,128)(2,1)S(1)}, u32[]{:S(2)}, u32[]{:S(2)}) collective-permute-start(bf16[144,1024]{1,0:T(8,128)(2,1)} %get-tuple-element.32), channel_id=1, source_target_pairs={{0,1},{1,0},{2,3},{3,2},{4,5},{5,4},{6,7},{7,6},{8,9},{9,8},{10,11... | collective-permute-start | bytes 884744 | tf_op jit(solution)/shard_map/ppermute | solution.py:83
  4.1 14.2 %collective-permute-start.1 = (bf16[144,1024]{1,0:T(8,128)(2,1)}, bf16[144,1024]{1,0:T(8,128)(2,1)S(1)}, u32[]{:S(2)}, u32[]{:S(2)}) collective-permute-start(bf16[144,1024]{1,0:T(8,128)(2,1)} %get-tuple-element.33), channel_id=1, source_target_pairs={{1,2},{2,1},{3,4},{4,3},{5,6},{6,5},{7,8},{8,7},{9,10},{10,9},{11,... | collective-permute-start | bytes 884744 | tf_op jit(solution)/shard_map/ppermute | solution.py:80
  8.6 12.7 %all-to-all-start = ((bf16[16,8,640]{2,1,0:T(8,128)(2,1)}), bf16[16,8,640]{2,1,0:T(8,128)(2,1)S(1)}, u32[]{:S(2)}, u32[]{:S(2)}) async-start(bf16[16,8,640]{2,1,0:T(8,128)(2,1)} %bitcast.11), calls=%async_computation | async-start | bytes 327680 | tf_op jit(solution)/shard_map/all_to_all | solution.py:645
  21.8 11.9 %collective-permute-start.2 = (bf16[128,1024]{1,0:T(8,128)(2,1)S(1)}, bf16[128,1024]{1,0:T(8,128)(2,1)S(1)}, u32[]{:S(2)}, u32[]{:S(2)}) collective-permute-start(bf16[128,1024]{1,0:T(8,128)(2,1)S(1)} %get-tuple-element.36.normed), channel_id=1, source_target_pairs={{0,1},{1,0},{2,3},{3,2},{4,5},{5,4},{6,7},{7,6},{8,9},{9,8},{10,11... | collective-permute-start | bytes 786440 | tf_op jit(solution)/shard_map/ppermute | solution.py:83
  23.1 10.7 %collective-permute-start.3 = (bf16[128,1024]{1,0:T(8,128)(2,1)S(1)}, bf16[128,1024]{1,0:T(8,128)(2,1)S(1)}, u32[]{:S(2)}, u32[]{:S(2)}) collective-permute-start(bf16[128,1024]{1,0:T(8,128)(2,1)S(1)} %get-tuple-element.36.normed), channel_id=1, source_target_pairs={{1,2},{2,1},{3,4},{4,3},{5,6},{6,5},{7,8},{8,7},{9,10},{10,9},{11,... | collective-permute-start | bytes 786440 | tf_op jit(solution)/shard_map/ppermute | solution.py:80
  30.0 12.2 %collective-permute-start.6 = (bf16[128,1024]{1,0:T(8,128)(2,1)S(1)}, bf16[128,1024]{1,0:T(8,128)(2,1)S(1)}, u32[]{:S(2)}, u32[]{:S(2)}) collective-permute-start(bf16[128,1024]{1,0:T(8,128)(2,1)S(1)} %get-tuple-element.40.own_grad), channel_id=1, source_target_pairs={{0,1},{1,0},{2,3},{3,2},{4,5},{5,4},{6,7},{7,6},{8,9},{9,8},{10,11... | collective-permute-start | bytes 786440 | tf_op jit(solution)/shard_map/ppermute | solution.py:83
  30.1 12.2 %collective-permute-start.7 = (bf16[128,1024]{1,0:T(8,128)(2,1)S(1)}, bf16[128,1024]{1,0:T(8,128)(2,1)S(1)}, u32[]{:S(2)}, u32[]{:S(2)}) collective-permute-start(bf16[128,1024]{1,0:T(8,128)(2,1)S(1)} %get-tuple-element.40.own_grad), channel_id=1, source_target_pairs={{1,2},{2,1},{3,4},{4,3},{5,6},{6,5},{7,8},{8,7},{9,10},{10,9},{11,... | collective-permute-start | bytes 786440 | tf_op jit(solution)/shard_map/ppermute | solution.py:80
  38.0 4.3 %collective-permute-start.4 = (f32[24,256]{1,0:T(8,128)S(1)}, f32[24,256]{1,0:T(8,128)S(1)}, u32[]{:S(2)}, u32[]{:S(2)}) collective-permute-start(f32[24,256]{1,0:T(8,128)S(1)} %get-tuple-element.51), channel_id=1, source_target_pairs={{0,1},{1,0},{2,3},{3,2},{4,5},{5,4},{6,7},{7,6},{8,9},{9,8},{10,11... | collective-permute-start | bytes 73736 | tf_op jit(solution)/shard_map/ppermute | solution.py:83
  38.1 5.1 %collective-permute-start.5 = (f32[24,256]{1,0:T(8,128)S(1)}, f32[24,256]{1,0:T(8,128)S(1)}, u32[]{:S(2)}, u32[]{:S(2)}) collective-permute-start(f32[24,256]{1,0:T(8,128)S(1)} %get-tuple-element.51), channel_id=1, source_target_pairs={{1,2},{2,1},{3,4},{4,3},{5,6},{6,5},{7,8},{8,7},{9,10},{10,9},{11,... | collective-permute-start | bytes 73736 | tf_op jit(solution)/shard_map/ppermute | solution.py:80

commit v17 on v16

--- a/solution.py
+++ b/solution.py
@@ -14,7 +14,7 @@
 BF16 = jnp.bfloat16
 I32 = jnp.int32
 VMEM_LIMIT = 28 * 2**20
-PIECES = 2
+PIECES = 4
 CHUNK = 64
 
 
@@ -346,11 +346,11 @@
     width = channels // PIECES
     starts = [part * channels + c * width for c in range(PIECES) for part in range(3)]
     copies = start_all(
-        [(grad_hbm, grad_out)]
-        + [(w_qkv_hbm.at[:, pl.ds(at, width)], w_qkv.at[:, pl.ds(at, width)]) for at in starts]
-        + [(window_hbm, window)],
+        [(window_hbm, window), (grad_hbm, grad_out)]
+        + [(w_qkv_hbm.at[:, pl.ds(at, width)], w_qkv.at[:, pl.ds(at, width)]) for at in starts],
         sems,
     )
+    copies[0].wait()
     def masks():
         chip_at, off_at = near_places(m)
         reach = [meta_of(side, count)[:8, 2 * LANES : 2 * LANES + m] for side in (chip_first, off_first)]
@@ -360,7 +360,6 @@
         query_at = jnp.where(lane < m, lane + chip_at, lane - m + off_at)
         keep = (key_at >= query_at - reach[0:1, :]) & (key_at <= query_at + reach[1:2, :])
         near_bias_out[...] = jnp.where(keep, 0.0, -jnp.inf).astype(F32)
-        copies[-1].wait()
         me = lax.axis_index("node")
         row = iota((3 * m, m), 0)
         key_at = jnp.where(row < m, row + chip_at, jnp.where(row < 2 * m, row - m + off_at, row - m))
@@ -371,23 +370,21 @@
         bias = jnp.where(keep & jnp.logical_not(missing), 0.0, -jnp.inf).astype(F32)
         bias_out[...] = jnp.transpose(bias)
 
+    masks()
+    copies[1].wait()
     for i, at in enumerate(starts):
-        copies[1 + i].wait()
+        copies[2 + i].wait()
         cols = slice(at, at + width)
         qkv_out[:, cols] = mm(normed[...], w_qkv[:, cols]).astype(BF16)
-        if i == 0:
-            masks()
-        if i % 3 < 2:
-            continue
-        if i == 2:
-            copies[0].wait()
         for p in range(i // 3 * width // pair, (i // 3 + 1) * width // pair):
             q, k, v = (
                 slice(part * channels + p * pair, part * channels + (p + 1) * pair)
                 for part in range(3)
             )
-            scores_out[p] = mm_nt(halves(qkv_out[:, q], scale), qkv_out[:, k])
-            products_out[p] = mm_nt(halves(grad_out[:, q]), qkv_out[:, v])
+            if i % 3 == 1:
+                scores_out[p] = mm_nt(halves(qkv_out[:, q], scale), qkv_out[:, k])
+            if i % 3 == 2:
+                products_out[p] = mm_nt(halves(grad_out[:, q]), qkv_out[:, v])
 
 
 def attend_kernel(

time: 47.4 us -> 48.8 us (1.030)
  Pallas kernels: 24.4 us -> 25.7 us
    pallas_call x8, Pallas kernels: 24.4 us -> 25.7 us  [call(): pl.pallas_call(kernel, out_shape=[(pltpu.HBM if i in hbm_outs else jax.Sh...]
  transfers between devices with their start and end apart: 9 -> 9, of which waited for: 2 -> 2; matrix products, arithmetic and copies ran while one was open for 0% -> 0% of each run, Pallas kernels for 36% -> 37%
where the time goes in v17:
time: 48.8 us; the launch traced here: 48.4 us
  Pallas kernels  25.7 us (53%)
  starting transfers between devices  19.2 us (39%)
  waiting for transfers between devices  2.69 us (6%)
  between operations  0.79 us (2%)
    pallas_call x8, Pallas kernels, call(): pl.pallas_call(kernel, out_shape=[(pltpu.HBM if i in hbm_outs else jax.Sh...  25.7 us
    ppermute x4, starting transfers between devices, exchange(): lax.ppermute(off_message, axis, [p for i in range(1, n - 1, 2) for p in (...  12.4 us
    all_to_all x1, starting transfers between devices, body(): lax.all_to_all(far_message.reshape(devices, 2 * far_depth, far_block[1]),...  5.33 us
    all_to_all x1, waiting for transfers between devices, body(): lax.all_to_all(far_message.reshape(devices, 2 * far_depth, far_block[1]),...  1.6 us
    ppermute x4, starting transfers between devices, exchange(): lax.ppermute(chip_message, axis, [p for i in range(0, n, 2) for p in ((i,...  1.49 us
    ppermute x4, waiting for transfers between devices, exchange(): lax.ppermute(off_message, axis, [p for i in range(1, n - 1, 2) for p in (...  1.08 us
  transfers between devices with their start and end apart: 9, of which 2 were waited for; matrix products, arithmetic and copies ran while one was open for 0% of the time, Pallas kernels for 37%

profile of v17, /device:TPU:1, one launch (start us, length us, event | category | flops | bytes accessed | tf_op | source)
XLA Modules:
  0.0 48.4 jit_solution(34437122341902854)
XLA Ops:
  0.6 3.4 %pack.1 = (bf16[128,640]{1,0:T(8,128)(2,1)}, bf16[144,1024]{1,0:T(8,128)(2,1)}, bf16[144,1024]{1,0:T(8,128)(2,1)}, bf16[1024,1024]{1,0:T(8,128)(2,1)S(1)}) custom-call(bf16[512,1024]{1,0:T(8,128)(2,1)} %grid_hbm.3, s32[2,128]{1,0:T(2,128)} %window_hbm.3, s32[32,128]{1,0:T(8,128)} %bitcast.12, s32[32,128]{1,0:T(8,128)} %bitcast.13, s32[1,2]{1,0:T(1,128)} %bitcast.16, ...), custom_call_target="tpu_custom_call" | custom-call | tf_op jit(solution)/shard_map/pack/pallas_call | solution.py:48
  4.0 0.1 collective-permute-start
  4.1 4.5 %collective-permute-start.1 = (bf16[144,1024]{1,0:T(8,128)(2,1)}, bf16[144,1024]{1,0:T(8,128)(2,1)S(1)}, u32[]{:S(2)}, u32[]{:S(2)}) collective-permute-start(bf16[144,1024]{1,0:T(8,128)(2,1)} %get-tuple-element.33), channel_id=1, source_target_pairs={{1,2},{2,1},{3,4},{4,3},{5,6},{6,5},{7,8},{8,7},{9,10},{10,9},{11,... | collective-permute-start | bytes 884744 | tf_op jit(solution)/shard_map/ppermute | solution.py:80
  8.6 5.3 %all-to-all-start = ((bf16[16,8,640]{2,1,0:T(8,128)(2,1)}), bf16[16,8,640]{2,1,0:T(8,128)(2,1)S(1)}, u32[]{:S(2)}, u32[]{:S(2)}) async-start(bf16[16,8,640]{2,1,0:T(8,128)(2,1)} %bitcast.11), calls=%async_computation | async-start | bytes 327680 | tf_op jit(solution)/shard_map/all_to_all | solution.py:642
  13.9 4.3 %own.1 = (f32[128,1024]{1,0:T(8,128)S(1)}, bf16[128,1024]{1,0:T(8,128)(2,1)}) custom-call(bf16[512,1024]{1,0:T(8,128)(2,1)} %grid_hbm.3, bf16[128,1024]{1,0:T(8,128)(2,1)} %mesh_in_hbm.1, s32[8,128]{1,0:T(8,128)} %bitcast.14, s32[8,128]{1,0:T(8,128)} %bitcast.15, bf16[128,1024]{1,0:T(8,128)(2,1)} %cot_hbm.3, bf16[1024,1024]{1,0:T(8,128)(2,1)} %w_out_hbm.3, ...), custom_call_target="tpu_custom_call" | custom-call | tf_op jit(solution)/shard_map/own/pallas_call | solution.py:48
  18.3 0.0 collective-permute-done.chip.chip_first
  18.3 0.0 collective-permute-done.1.off.off_first
  18.3 1.4 %side.1.partial = f32[128,1024]{1,0:T(8,128)S(1)} custom-call(bf16[144,1024]{1,0:T(8,128)(2,1)S(1)} %collective-permute-done.chip.chip_first, bf16[144,1024]{1,0:T(8,128)(2,1)S(1)} %collective-permute-done.1.off.off_first, bf16[1024,1024]{1,0:T(8,128)(2,1)S(1)} %get-tuple-element.34.w_edge, f32[128,1024]{1,0:T(8,128)S(1)} %get-tuple-element.35.partial), custom_call_target="tpu_custom_call" | custom-call | flops 8000000000 | tf_op jit(solution)/shard_map/side/pallas_call | solution.py:48
  19.7 1.6 %all-to-all-done = bf16[16,8,640]{2,1,0:T(8,128)(2,1)S(1)} async-done(((bf16[16,8,640]{2,1,0:T(8,128)(2,1)}), bf16[16,8,640]{2,1,0:T(8,128)(2,1)S(1)}, u32[]{:S(2)}, u32[]{:S(2)}) %all-to-all-start) | async-done | bytes 163872 | tf_op jit(solution)/shard_map/all_to_all | solution.py:642
  21.3 0.5 %latent.1 = (bf16[128,1024]{1,0:T(8,128)(2,1)S(1)}, bf16[128,1024]{1,0:T(8,128)(2,1)S(1)}, f32[128,1024]{1,0:T(8,128)S(1)}, f32[128,128]{1,0:T(8,128)S(1)}) custom-call(bf16[128,640]{1,0:T(8,128)(2,1)S(1)} %bitcast.10, f32[128,1024]{1,0:T(8,128)S(1)} %side.1.partial), custom_call_target="tpu_custom_call" | custom-call | tf_op jit(solution)/shard_map/latent/pallas_call | solution.py:48
  21.8 1.2 %collective-permute-start.2 = (bf16[128,1024]{1,0:T(8,128)(2,1)S(1)}, bf16[128,1024]{1,0:T(8,128)(2,1)S(1)}, u32[]{:S(2)}, u32[]{:S(2)}) collective-permute-start(bf16[128,1024]{1,0:T(8,128)(2,1)S(1)} %get-tuple-element.36.normed), channel_id=1, source_target_pairs={{0,1},{1,0},{2,3},{3,2},{4,5},{5,4},{6,7},{7,6},{8,9},{9,8},{10,11... | collective-permute-start | bytes 786440 | tf_op jit(solution)/shard_map/ppermute | solution.py:83
  23.1 1.9 %collective-permute-start.3 = (bf16[128,1024]{1,0:T(8,128)(2,1)S(1)}, bf16[128,1024]{1,0:T(8,128)(2,1)S(1)}, u32[]{:S(2)}, u32[]{:S(2)}) collective-permute-start(bf16[128,1024]{1,0:T(8,128)(2,1)S(1)} %get-tuple-element.36.normed), channel_id=1, source_target_pairs={{1,2},{2,1},{3,4},{4,3},{5,6},{6,5},{7,8},{8,7},{9,10},{10,9},{11,... | collective-permute-start | bytes 786440 | tf_op jit(solution)/shard_map/ppermute | solution.py:80
  25.0 6.3 %project.1 = (bf16[128,3072]{1,0:T(8,128)(2,1)S(1)}, bf16[1024,3072]{1,0:T(8,128)(2,1)S(1)}, bf16[128,1024]{1,0:T(8,128)(2,1)S(1)}, f32[8,256,128]{2,1,0:T(8,128...) custom-call(bf16[128,1024]{1,0:T(8,128)(2,1)S(1)} %get-tuple-element.36.normed, ...), custom_call_target="tpu_custom_call" | custom-call | tf_op jit(solution)/shard_map/project/pallas_call | solution.py:48
  31.3 0.1 collective-permute-start.6
  31.4 3.6 %collective-permute-start.7 = (bf16[128,1024]{1,0:T(8,128)(2,1)S(1)}, bf16[128,1024]{1,0:T(8,128)(2,1)S(1)}, u32[]{:S(2)}, u32[]{:S(2)}) collective-permute-start(bf16[128,1024]{1,0:T(8,128)(2,1)S(1)} %get-tuple-element.40.own_grad), channel_id=1, source_target_pairs={{1,2},{2,1},{3,4},{4,3},{5,6},{6,5},{7,8},{8,7},{9,10},{10,9},{11,... | collective-permute-start | bytes 786440 | tf_op jit(solution)/shard_map/ppermute | solution.py:80
  35.0 0.0 collective-permute-done.2.chip_normed
  35.0 0.0 collective-permute-done.3.off_normed
  35.0 4.4 %attend.1 = (f32[24,256]{1,0:T(8,128)S(1)}, bf16[128,1024]{1,0:T(8,128)(2,1)S(1)}, bf16[128,1024]{1,0:T(8,128)(2,1)S(1)}, bf16[8,256,128]{2,1,0:T(8,128)(2,1)S(1...) custom-call(bf16[128,1024]{1,0:T(8,128)(2,1)S(1)} %collective-permut, ...), custom_call_target="tpu_custom_call" | custom-call | tf_op jit(solution)/shard_map/attend/pallas_call | solution.py:48
  39.4 0.1 collective-permute-start.4
  39.5 2.4 %collective-permute-start.5 = (f32[24,256]{1,0:T(8,128)S(1)}, f32[24,256]{1,0:T(8,128)S(1)}, u32[]{:S(2)}, u32[]{:S(2)}) collective-permute-start(f32[24,256]{1,0:T(8,128)S(1)} %get-tuple-element.51), channel_id=1, source_target_pairs={{1,2},{2,1},{3,4},{4,3},{5,6},{6,5},{7,8},{8,7},{9,10},{10,9},{11,... | collective-permute-start | bytes 73736 | tf_op jit(solution)/shard_map/ppermute | solution.py:80
  41.9 1.6 %product.1 = (bf16[128,1024]{1,0:T(8,128)(2,1)}, f32[128,1024]{1,0:T(8,128)S(1)}, f32[128,1024]{1,0:T(8,128)S(1)}, f32[128,1024]{1,0:T(8,128)S(1)}) custom-call(bf16[8,256,128]{2,1,0:T(8,128)(2,1)S(1)} %get-tuple-element.44.weights, bf16[8,256,128]{2,1,0:T(8,128)(2,1)S(1)} %get-tuple-element.45.grad_scores, ...), custom_call_target="tpu_custom_call" | custom-call | tf_op jit(solution)/shard_map/product/pallas_call | solution.py:48
  43.5 0.0 collective-permute-done.6.chip_grad
  43.5 0.0 collective-permute-done.7.off_grad
  43.5 0.0 collective-permute-done.4.chip_stats
  43.5 1.1 %collective-permute-done.5.off_stats = f32[24,256]{1,0:T(8,128)S(1)} collective-permute-done((f32[24,256]{1,0:T(8,128)S(1)}, f32[24,256]{1,0:T(8,128)S(1)}, u32[]{:S(2)}, u32[]{:S(2)}) %collective-permute-start.5) | collective-permute-done | bytes 24608 | tf_op jit(solution)/shard_map/ppermute | solution.py:80
  44.6 3.8 %finish.1 = bf16[128,1024]{1,0:T(8,128)(2,1)} custom-call(f32[24,256]{1,0:T(8,128)S(1)} %collective-permute-done.4.chip_stats, f32[24,256]{1,0:T(8,128)S(1)} %collective-permute-done.5.off_stats, f32[128,256]{1,0:T(8,128)S(1)} %get-tuple-element.52.bias, bf16[256,1024]{1,0:T(8,128)(2,1)S(1)} %get-tuple-element.53.near_q, ...), custom_call_target="tpu_custom_call" | custom-call | tf_op jit(solution)/shard_map/finish/pallas_call | solution.py:48
Async XLA Ops:
  4.0 14.3 %collective-permute-start = (bf16[144,1024]{1,0:T(8,128)(2,1)}, bf16[144,1024]{1,0:T(8,128)(2,1)S(1)}, u32[]{:S(2)}, u32[]{:S(2)}) collective-permute-start(bf16[144,1024]{1,0:T(8,128)(2,1)} %get-tuple-element.32), channel_id=1, source_target_pairs={{0,1},{1,0},{2,3},{3,2},{4,5},{5,4},{6,7},{7,6},{8,9},{9,8},{10,11... | collective-permute-start | bytes 884744 | tf_op jit(solution)/shard_map/ppermute | solution.py:83
  4.1 14.2 %collective-permute-start.1 = (bf16[144,1024]{1,0:T(8,128)(2,1)}, bf16[144,1024]{1,0:T(8,128)(2,1)S(1)}, u32[]{:S(2)}, u32[]{:S(2)}) collective-permute-start(bf16[144,1024]{1,0:T(8,128)(2,1)} %get-tuple-element.33), channel_id=1, source_target_pairs={{1,2},{2,1},{3,4},{4,3},{5,6},{6,5},{7,8},{8,7},{9,10},{10,9},{11,... | collective-permute-start | bytes 884744 | tf_op jit(solution)/shard_map/ppermute | solution.py:80
  8.6 12.7 %all-to-all-start = ((bf16[16,8,640]{2,1,0:T(8,128)(2,1)}), bf16[16,8,640]{2,1,0:T(8,128)(2,1)S(1)}, u32[]{:S(2)}, u32[]{:S(2)}) async-start(bf16[16,8,640]{2,1,0:T(8,128)(2,1)} %bitcast.11), calls=%async_computation | async-start | bytes 327680 | tf_op jit(solution)/shard_map/all_to_all | solution.py:642
  21.8 13.2 %collective-permute-start.2 = (bf16[128,1024]{1,0:T(8,128)(2,1)S(1)}, bf16[128,1024]{1,0:T(8,128)(2,1)S(1)}, u32[]{:S(2)}, u32[]{:S(2)}) collective-permute-start(bf16[128,1024]{1,0:T(8,128)(2,1)S(1)} %get-tuple-element.36.normed), channel_id=1, source_target_pairs={{0,1},{1,0},{2,3},{3,2},{4,5},{5,4},{6,7},{7,6},{8,9},{9,8},{10,11... | collective-permute-start | bytes 786440 | tf_op jit(solution)/shard_map/ppermute | solution.py:83
  23.1 12.0 %collective-permute-start.3 = (bf16[128,1024]{1,0:T(8,128)(2,1)S(1)}, bf16[128,1024]{1,0:T(8,128)(2,1)S(1)}, u32[]{:S(2)}, u32[]{:S(2)}) collective-permute-start(bf16[128,1024]{1,0:T(8,128)(2,1)S(1)} %get-tuple-element.36.normed), channel_id=1, source_target_pairs={{1,2},{2,1},{3,4},{4,3},{5,6},{6,5},{7,8},{8,7},{9,10},{10,9},{11,... | collective-permute-start | bytes 786440 | tf_op jit(solution)/shard_map/ppermute | solution.py:80
  31.3 12.2 %collective-permute-start.6 = (bf16[128,1024]{1,0:T(8,128)(2,1)S(1)}, bf16[128,1024]{1,0:T(8,128)(2,1)S(1)}, u32[]{:S(2)}, u32[]{:S(2)}) collective-permute-start(bf16[128,1024]{1,0:T(8,128)(2,1)S(1)} %get-tuple-element.40.own_grad), channel_id=1, source_target_pairs={{0,1},{1,0},{2,3},{3,2},{4,5},{5,4},{6,7},{7,6},{8,9},{9,8},{10,11... | collective-permute-start | bytes 786440 | tf_op jit(solution)/shard_map/ppermute | solution.py:83
  31.4 12.2 %collective-permute-start.7 = (bf16[128,1024]{1,0:T(8,128)(2,1)S(1)}, bf16[128,1024]{1,0:T(8,128)(2,1)S(1)}, u32[]{:S(2)}, u32[]{:S(2)}) collective-permute-start(bf16[128,1024]{1,0:T(8,128)(2,1)S(1)} %get-tuple-element.40.own_grad), channel_id=1, source_target_pairs={{1,2},{2,1},{3,4},{4,3},{5,6},{6,5},{7,8},{8,7},{9,10},{10,9},{11,... | collective-permute-start | bytes 786440 | tf_op jit(solution)/shard_map/ppermute | solution.py:80
  39.4 4.1 %collective-permute-start.4 = (f32[24,256]{1,0:T(8,128)S(1)}, f32[24,256]{1,0:T(8,128)S(1)}, u32[]{:S(2)}, u32[]{:S(2)}) collective-permute-start(f32[24,256]{1,0:T(8,128)S(1)} %get-tuple-element.51), channel_id=1, source_target_pairs={{0,1},{1,0},{2,3},{3,2},{4,5},{5,4},{6,7},{7,6},{8,9},{9,8},{10,11... | collective-permute-start | bytes 73736 | tf_op jit(solution)/shard_map/ppermute | solution.py:83
  39.5 5.1 %collective-permute-start.5 = (f32[24,256]{1,0:T(8,128)S(1)}, f32[24,256]{1,0:T(8,128)S(1)}, u32[]{:S(2)}, u32[]{:S(2)}) collective-permute-start(f32[24,256]{1,0:T(8,128)S(1)} %get-tuple-element.51), channel_id=1, source_target_pairs={{1,2},{2,1},{3,4},{4,3},{5,6},{6,5},{7,8},{8,7},{9,10},{10,9},{11,... | collective-permute-start | bytes 73736 | tf_op jit(solution)/shard_map/ppermute | solution.py:80

commit v18 on v17

--- a/solution.py
+++ b/solution.py
@@ -14,7 +14,7 @@
 BF16 = jnp.bfloat16
 I32 = jnp.int32
 VMEM_LIMIT = 28 * 2**20
-PIECES = 4
+PIECES = 2
 CHUNK = 64
 
 

time: 48.8 us -> 46.6 us (0.955)
  Pallas kernels: 25.7 us -> 23.6 us
    pallas_call x8, Pallas kernels: 25.7 us -> 23.6 us  [call(): pl.pallas_call(kernel, out_shape=[(pltpu.HBM if i in hbm_outs else jax.Sh...]
  transfers between devices with their start and end apart: 9 -> 9, of which waited for: 2 -> 2; matrix products, arithmetic and copies ran while one was open for 0% -> 0% of each run, Pallas kernels for 37% -> 35%
where the time goes in v18:
time: 46.6 us; the launch traced here: 46.1 us
  Pallas kernels  23.6 us (51%)
  starting transfers between devices  19.4 us (42%)
  waiting for transfers between devices  2.37 us (5%)
  between operations  0.79 us (2%)
    pallas_call x8, Pallas kernels, call(): pl.pallas_call(kernel, out_shape=[(pltpu.HBM if i in hbm_outs else jax.Sh...  23.6 us
    ppermute x4, starting transfers between devices, exchange(): lax.ppermute(off_message, axis, [p for i in range(1, n - 1, 2) for p in (...  12.6 us
    all_to_all x1, starting transfers between devices, body(): lax.all_to_all(far_message.reshape(devices, 2 * far_depth, far_block[1]),...  5.33 us
    all_to_all x1, waiting for transfers between devices, body(): lax.all_to_all(far_message.reshape(devices, 2 * far_depth, far_block[1]),...  1.6 us
    ppermute x4, starting transfers between devices, exchange(): lax.ppermute(chip_message, axis, [p for i in range(0, n, 2) for p in ((i,...  1.49 us
  transfers between devices with their start and end apart: 9, of which 2 were waited for; matrix products, arithmetic and copies ran while one was open for 0% of the time, Pallas kernels for 35%

profile of v18, /device:TPU:1, one launch (start us, length us, event | category | flops | bytes accessed | tf_op | source)
XLA Modules:
  0.0 46.1 jit_solution(10968359764424539866)
XLA Ops:
  0.6 3.4 %pack.1 = (bf16[128,640]{1,0:T(8,128)(2,1)}, bf16[144,1024]{1,0:T(8,128)(2,1)}, bf16[144,1024]{1,0:T(8,128)(2,1)}, bf16[1024,1024]{1,0:T(8,128)(2,1)S(1)}) custom-call(bf16[512,1024]{1,0:T(8,128)(2,1)} %grid_hbm.3, s32[2,128]{1,0:T(2,128)} %window_hbm.3, s32[32,128]{1,0:T(8,128)} %bitcast.12, s32[32,128]{1,0:T(8,128)} %bitcast.13, s32[1,2]{1,0:T(1,128)} %bitcast.16, ...), custom_call_target="tpu_custom_call" | custom-call | tf_op jit(solution)/shard_map/pack/pallas_call | solution.py:48
  4.0 0.1 collective-permute-start
  4.1 4.5 %collective-permute-start.1 = (bf16[144,1024]{1,0:T(8,128)(2,1)}, bf16[144,1024]{1,0:T(8,128)(2,1)S(1)}, u32[]{:S(2)}, u32[]{:S(2)}) collective-permute-start(bf16[144,1024]{1,0:T(8,128)(2,1)} %get-tuple-element.33), channel_id=1, source_target_pairs={{1,2},{2,1},{3,4},{4,3},{5,6},{6,5},{7,8},{8,7},{9,10},{10,9},{11,... | collective-permute-start | bytes 884744 | tf_op jit(solution)/shard_map/ppermute | solution.py:80
  8.6 5.3 %all-to-all-start = ((bf16[16,8,640]{2,1,0:T(8,128)(2,1)}), bf16[16,8,640]{2,1,0:T(8,128)(2,1)S(1)}, u32[]{:S(2)}, u32[]{:S(2)}) async-start(bf16[16,8,640]{2,1,0:T(8,128)(2,1)} %bitcast.11), calls=%async_computation | async-start | bytes 327680 | tf_op jit(solution)/shard_map/all_to_all | solution.py:642
  13.9 4.3 %own.1 = (f32[128,1024]{1,0:T(8,128)S(1)}, bf16[128,1024]{1,0:T(8,128)(2,1)}) custom-call(bf16[512,1024]{1,0:T(8,128)(2,1)} %grid_hbm.3, bf16[128,1024]{1,0:T(8,128)(2,1)} %mesh_in_hbm.1, s32[8,128]{1,0:T(8,128)} %bitcast.14, s32[8,128]{1,0:T(8,128)} %bitcast.15, bf16[128,1024]{1,0:T(8,128)(2,1)} %cot_hbm.3, bf16[1024,1024]{1,0:T(8,128)(2,1)} %w_out_hbm.3, ...), custom_call_target="tpu_custom_call" | custom-call | tf_op jit(solution)/shard_map/own/pallas_call | solution.py:48
  18.3 0.0 collective-permute-done.chip.chip_first
  18.3 0.0 collective-permute-done.1.off.off_first
  18.3 1.4 %side.1.partial = f32[128,1024]{1,0:T(8,128)S(1)} custom-call(bf16[144,1024]{1,0:T(8,128)(2,1)S(1)} %collective-permute-done.chip.chip_first, bf16[144,1024]{1,0:T(8,128)(2,1)S(1)} %collective-permute-done.1.off.off_first, bf16[1024,1024]{1,0:T(8,128)(2,1)S(1)} %get-tuple-element.34.w_edge, f32[128,1024]{1,0:T(8,128)S(1)} %get-tuple-element.35.partial), custom_call_target="tpu_custom_call" | custom-call | flops 8000000000 | tf_op jit(solution)/shard_map/side/pallas_call | solution.py:48
  19.7 1.6 %all-to-all-done = bf16[16,8,640]{2,1,0:T(8,128)(2,1)S(1)} async-done(((bf16[16,8,640]{2,1,0:T(8,128)(2,1)}), bf16[16,8,640]{2,1,0:T(8,128)(2,1)S(1)}, u32[]{:S(2)}, u32[]{:S(2)}) %all-to-all-start) | async-done | bytes 163872 | tf_op jit(solution)/shard_map/all_to_all | solution.py:642
  21.3 0.5 %latent.1 = (bf16[128,1024]{1,0:T(8,128)(2,1)S(1)}, bf16[128,1024]{1,0:T(8,128)(2,1)S(1)}, f32[128,1024]{1,0:T(8,128)S(1)}, f32[128,128]{1,0:T(8,128)S(1)}) custom-call(bf16[128,640]{1,0:T(8,128)(2,1)S(1)} %bitcast.10, f32[128,1024]{1,0:T(8,128)S(1)} %side.1.partial), custom_call_target="tpu_custom_call" | custom-call | tf_op jit(solution)/shard_map/latent/pallas_call | solution.py:48
  21.8 1.2 %collective-permute-start.2 = (bf16[128,1024]{1,0:T(8,128)(2,1)S(1)}, bf16[128,1024]{1,0:T(8,128)(2,1)S(1)}, u32[]{:S(2)}, u32[]{:S(2)}) collective-permute-start(bf16[128,1024]{1,0:T(8,128)(2,1)S(1)} %get-tuple-element.36.normed), channel_id=1, source_target_pairs={{0,1},{1,0},{2,3},{3,2},{4,5},{5,4},{6,7},{7,6},{8,9},{9,8},{10,11... | collective-permute-start | bytes 786440 | tf_op jit(solution)/shard_map/ppermute | solution.py:83
  23.1 1.9 %collective-permute-start.3 = (bf16[128,1024]{1,0:T(8,128)(2,1)S(1)}, bf16[128,1024]{1,0:T(8,128)(2,1)S(1)}, u32[]{:S(2)}, u32[]{:S(2)}) collective-permute-start(bf16[128,1024]{1,0:T(8,128)(2,1)S(1)} %get-tuple-element.36.normed), channel_id=1, source_target_pairs={{1,2},{2,1},{3,4},{4,3},{5,6},{6,5},{7,8},{8,7},{9,10},{10,9},{11,... | collective-permute-start | bytes 786440 | tf_op jit(solution)/shard_map/ppermute | solution.py:80
  25.0 4.2 %project.1 = (bf16[128,3072]{1,0:T(8,128)(2,1)S(1)}, bf16[1024,3072]{1,0:T(8,128)(2,1)S(1)}, bf16[128,1024]{1,0:T(8,128)(2,1)S(1)}, f32[8,256,128]{2,1,0:T(8,128...) custom-call(bf16[128,1024]{1,0:T(8,128)(2,1)S(1)} %get-tuple-element.36.normed, ...), custom_call_target="tpu_custom_call" | custom-call | tf_op jit(solution)/shard_map/project/pallas_call | solution.py:48
  29.2 0.1 collective-permute-start.6
  29.3 3.6 %collective-permute-start.7 = (bf16[128,1024]{1,0:T(8,128)(2,1)S(1)}, bf16[128,1024]{1,0:T(8,128)(2,1)S(1)}, u32[]{:S(2)}, u32[]{:S(2)}) collective-permute-start(bf16[128,1024]{1,0:T(8,128)(2,1)S(1)} %get-tuple-element.40.own_grad), channel_id=1, source_target_pairs={{1,2},{2,1},{3,4},{4,3},{5,6},{6,5},{7,8},{8,7},{9,10},{10,9},{11,... | collective-permute-start | bytes 786440 | tf_op jit(solution)/shard_map/ppermute | solution.py:80
  32.9 0.0 collective-permute-done.2.chip_normed
  32.9 0.0 collective-permute-done.3.off_normed
  32.9 4.2 %attend.1 = (f32[24,256]{1,0:T(8,128)S(1)}, bf16[128,1024]{1,0:T(8,128)(2,1)S(1)}, bf16[128,1024]{1,0:T(8,128)(2,1)S(1)}, bf16[8,256,128]{2,1,0:T(8,128)(2,1)S(1...) custom-call(bf16[128,1024]{1,0:T(8,128)(2,1)S(1)} %collective-permut, ...), custom_call_target="tpu_custom_call" | custom-call | tf_op jit(solution)/shard_map/attend/pallas_call | solution.py:48
  37.1 0.1 collective-permute-start.4
  37.2 2.5 %collective-permute-start.5 = (f32[24,256]{1,0:T(8,128)S(1)}, f32[24,256]{1,0:T(8,128)S(1)}, u32[]{:S(2)}, u32[]{:S(2)}) collective-permute-start(f32[24,256]{1,0:T(8,128)S(1)} %get-tuple-element.51), channel_id=1, source_target_pairs={{1,2},{2,1},{3,4},{4,3},{5,6},{6,5},{7,8},{8,7},{9,10},{10,9},{11,... | collective-permute-start | bytes 73736 | tf_op jit(solution)/shard_map/ppermute | solution.py:80
  39.7 1.8 %product.1 = (bf16[128,1024]{1,0:T(8,128)(2,1)}, f32[128,1024]{1,0:T(8,128)S(1)}, f32[128,1024]{1,0:T(8,128)S(1)}, f32[128,1024]{1,0:T(8,128)S(1)}) custom-call(bf16[8,256,128]{2,1,0:T(8,128)(2,1)S(1)} %get-tuple-element.44.weights, bf16[8,256,128]{2,1,0:T(8,128)(2,1)S(1)} %get-tuple-element.45.grad_scores, ...), custom_call_target="tpu_custom_call" | custom-call | tf_op jit(solution)/shard_map/product/pallas_call | solution.py:48
  41.6 0.0 collective-permute-done.6.chip_grad
  41.6 0.0 collective-permute-done.7.off_grad
  41.6 0.0 collective-permute-done.4.chip_stats
  41.6 0.7 %collective-permute-done.5.off_stats = f32[24,256]{1,0:T(8,128)S(1)} collective-permute-done((f32[24,256]{1,0:T(8,128)S(1)}, f32[24,256]{1,0:T(8,128)S(1)}, u32[]{:S(2)}, u32[]{:S(2)}) %collective-permute-start.5) | collective-permute-done | bytes 24608 | tf_op jit(solution)/shard_map/ppermute | solution.py:80
  42.4 3.8 %finish.1 = bf16[128,1024]{1,0:T(8,128)(2,1)} custom-call(f32[24,256]{1,0:T(8,128)S(1)} %collective-permute-done.4.chip_stats, f32[24,256]{1,0:T(8,128)S(1)} %collective-permute-done.5.off_stats, f32[128,256]{1,0:T(8,128)S(1)} %get-tuple-element.52.bias, bf16[256,1024]{1,0:T(8,128)(2,1)S(1)} %get-tuple-element.53.near_q, ...), custom_call_target="tpu_custom_call" | custom-call | tf_op jit(solution)/shard_map/finish/pallas_call | solution.py:48
Async XLA Ops:
  4.0 14.3 %collective-permute-start = (bf16[144,1024]{1,0:T(8,128)(2,1)}, bf16[144,1024]{1,0:T(8,128)(2,1)S(1)}, u32[]{:S(2)}, u32[]{:S(2)}) collective-permute-start(bf16[144,1024]{1,0:T(8,128)(2,1)} %get-tuple-element.32), channel_id=1, source_target_pairs={{0,1},{1,0},{2,3},{3,2},{4,5},{5,4},{6,7},{7,6},{8,9},{9,8},{10,11... | collective-permute-start | bytes 884744 | tf_op jit(solution)/shard_map/ppermute | solution.py:83
  4.1 14.2 %collective-permute-start.1 = (bf16[144,1024]{1,0:T(8,128)(2,1)}, bf16[144,1024]{1,0:T(8,128)(2,1)S(1)}, u32[]{:S(2)}, u32[]{:S(2)}) collective-permute-start(bf16[144,1024]{1,0:T(8,128)(2,1)} %get-tuple-element.33), channel_id=1, source_target_pairs={{1,2},{2,1},{3,4},{4,3},{5,6},{6,5},{7,8},{8,7},{9,10},{10,9},{11,... | collective-permute-start | bytes 884744 | tf_op jit(solution)/shard_map/ppermute | solution.py:80
  8.6 12.7 %all-to-all-start = ((bf16[16,8,640]{2,1,0:T(8,128)(2,1)}), bf16[16,8,640]{2,1,0:T(8,128)(2,1)S(1)}, u32[]{:S(2)}, u32[]{:S(2)}) async-start(bf16[16,8,640]{2,1,0:T(8,128)(2,1)} %bitcast.11), calls=%async_computation | async-start | bytes 327680 | tf_op jit(solution)/shard_map/all_to_all | solution.py:642
  21.8 11.1 %collective-permute-start.2 = (bf16[128,1024]{1,0:T(8,128)(2,1)S(1)}, bf16[128,1024]{1,0:T(8,128)(2,1)S(1)}, u32[]{:S(2)}, u32[]{:S(2)}) collective-permute-start(bf16[128,1024]{1,0:T(8,128)(2,1)S(1)} %get-tuple-element.36.normed), channel_id=1, source_target_pairs={{0,1},{1,0},{2,3},{3,2},{4,5},{5,4},{6,7},{7,6},{8,9},{9,8},{10,11... | collective-permute-start | bytes 786440 | tf_op jit(solution)/shard_map/ppermute | solution.py:83
  23.1 9.9 %collective-permute-start.3 = (bf16[128,1024]{1,0:T(8,128)(2,1)S(1)}, bf16[128,1024]{1,0:T(8,128)(2,1)S(1)}, u32[]{:S(2)}, u32[]{:S(2)}) collective-permute-start(bf16[128,1024]{1,0:T(8,128)(2,1)S(1)} %get-tuple-element.36.normed), channel_id=1, source_target_pairs={{1,2},{2,1},{3,4},{4,3},{5,6},{6,5},{7,8},{8,7},{9,10},{10,9},{11,... | collective-permute-start | bytes 786440 | tf_op jit(solution)/shard_map/ppermute | solution.py:80
  29.2 12.4 %collective-permute-start.6 = (bf16[128,1024]{1,0:T(8,128)(2,1)S(1)}, bf16[128,1024]{1,0:T(8,128)(2,1)S(1)}, u32[]{:S(2)}, u32[]{:S(2)}) collective-permute-start(bf16[128,1024]{1,0:T(8,128)(2,1)S(1)} %get-tuple-element.40.own_grad), channel_id=1, source_target_pairs={{0,1},{1,0},{2,3},{3,2},{4,5},{5,4},{6,7},{7,6},{8,9},{9,8},{10,11... | collective-permute-start | bytes 786440 | tf_op jit(solution)/shard_map/ppermute | solution.py:83
  29.3 12.3 %collective-permute-start.7 = (bf16[128,1024]{1,0:T(8,128)(2,1)S(1)}, bf16[128,1024]{1,0:T(8,128)(2,1)S(1)}, u32[]{:S(2)}, u32[]{:S(2)}) collective-permute-start(bf16[128,1024]{1,0:T(8,128)(2,1)S(1)} %get-tuple-element.40.own_grad), channel_id=1, source_target_pairs={{1,2},{2,1},{3,4},{4,3},{5,6},{6,5},{7,8},{8,7},{9,10},{10,9},{11,... | collective-permute-start | bytes 786440 | tf_op jit(solution)/shard_map/ppermute | solution.py:80
  37.1 4.5 %collective-permute-start.4 = (f32[24,256]{1,0:T(8,128)S(1)}, f32[24,256]{1,0:T(8,128)S(1)}, u32[]{:S(2)}, u32[]{:S(2)}) collective-permute-start(f32[24,256]{1,0:T(8,128)S(1)} %get-tuple-element.51), channel_id=1, source_target_pairs={{0,1},{1,0},{2,3},{3,2},{4,5},{5,4},{6,7},{7,6},{8,9},{9,8},{10,11... | collective-permute-start | bytes 73736 | tf_op jit(solution)/shard_map/ppermute | solution.py:83
  37.2 5.1 %collective-permute-start.5 = (f32[24,256]{1,0:T(8,128)S(1)}, f32[24,256]{1,0:T(8,128)S(1)}, u32[]{:S(2)}, u32[]{:S(2)}) collective-permute-start(f32[24,256]{1,0:T(8,128)S(1)} %get-tuple-element.51), channel_id=1, source_target_pairs={{1,2},{2,1},{3,4},{4,3},{5,6},{6,5},{7,8},{8,7},{9,10},{10,9},{11,... | collective-permute-start | bytes 73736 | tf_op jit(solution)/shard_map/ppermute | solution.py:80

commit v19 on v18

--- a/solution.py
+++ b/solution.py
@@ -75,15 +75,20 @@
     return [pltpu.VMEM(a.shape, a.dtype) for a in arrays]
 
 
+def swap_off(rows, axis):
+    n = lax.axis_size(axis)
+    pairs = [p for i in range(1, n - 1, 2) for p in ((i, i + 1), (i + 1, i))]
+    return lax.ppermute(rows, axis, pairs)
+
+
+def swap_chip(rows, axis):
+    n = lax.axis_size(axis)
+    return lax.ppermute(rows, axis, [p for i in range(0, n, 2) for p in ((i, i + 1), (i + 1, i))])
+
+
 def exchange(chip_message, off_message, axis):
-    n = lax.axis_size(axis)
-    from_off = lax.ppermute(
-        off_message, axis, [p for i in range(1, n - 1, 2) for p in ((i, i + 1), (i + 1, i))]
-    )
-    from_chip = lax.ppermute(
-        chip_message, axis, [p for i in range(0, n, 2) for p in ((i, i + 1), (i + 1, i))]
-    )
-    return from_chip, from_off
+    from_off = swap_off(off_message, axis)
+    return swap_chip(chip_message, axis), from_off
 
 
 def is_odd():
@@ -339,9 +344,11 @@
     products_out,
     bias_out,
     near_bias_out,
+    normed_out,
     window,
     sems,
 ):
+    normed_out[...] = normed[...]
     m, channels = normed.shape
     width = channels // PIECES
     starts = [part * channels + c * width for c in range(PIECES) for part in range(3)]
@@ -401,8 +408,7 @@
     w_out_hbm,
     cot_hbm,
     stats_out,
-    attention,
-    grad_query,
+    kv,
     weights_out,
     scores_out,
     near_q,
@@ -424,10 +430,13 @@
             blocks = []
             for part in range(1, 3):
                 at = part * channels + group * 2 * pair
-                blocks.append(mm(near, w_qkv[:, at : at + 2 * pair]).astype(BF16))
+                block = mm(near, w_qkv[:, at : at + 2 * pair]).astype(BF16)
+                kv[: 2 * m, at - channels : at - channels + 2 * pair] = block
+                blocks.append(block)
             return blocks
 
         brought = {0: bring(0)}
+        kv[2 * m :] = own_qkv[:, channels:]
         lane = iota((CHUNK, LANES), 1)
         stats = [jnp.zeros((CHUNK, LANES), F32) for _ in range(2 * m // CHUNK)]
 
@@ -464,17 +473,8 @@
                 grad_scores.append((probs * (product - delta)).astype(BF16))
                 for k, column in enumerate((top, inv_sum, delta)):
                     stats[at // CHUNK] = jnp.where(lane == k * pairs + p, column, stats[at // CHUNK])
-            weights = jnp.concatenate(weights, 0)
-            grad_scores = jnp.concatenate(grad_scores, 0)
-            weights_out[p] = weights[:, 2 * m :]
-            scores_out[p] = grad_scores[:, 2 * m :]
-            keys, values = (
-                jnp.concatenate([block, own_qkv[:, at + p * pair : at + (p + 1) * pair]], 0)
-                for block, at in zip(near_of(p), (channels, 2 * channels))
-            )
-            cols = slice(p * pair, (p + 1) * pair)
-            attention[:, cols] = merge(mm(weights, values)).astype(BF16)
-            grad_query[:, cols] = (merge(mm(grad_scores, keys)) * scale).astype(BF16)
+            weights_out[p] = jnp.concatenate(weights, 0)
+            scores_out[p] = jnp.concatenate(grad_scores, 0)
         stats_out[...] = jnp.transpose(jnp.concatenate(stats, 0))[: 3 * pairs]
 
     for copy in fetch:
@@ -486,8 +486,7 @@
     pair,
     weights,
     grad_scores,
-    attention,
-    grad_query,
+    kv,
     own_qkv,
     own_grad,
     latent,
@@ -497,20 +496,30 @@
     grad_normed,
     grad_key,
     grad_value,
+    attention,
+    grad_query,
     mesh_out,
     sems,
 ):
     m, channels = latent.shape
+    pairs = channels // pair
+    for p in range(pairs):
+        cols = slice(p * pair, (p + 1) * pair)
+        value = kv[:, channels + p * pair : channels + (p + 1) * pair]
+        attention[:, cols] = merge(mm(weights[p], value)).astype(BF16)
     mesh_out[...] = (latent[...].astype(F32) + mm(attention[...], w_out[...])).astype(BF16)
     out = pltpu.make_async_copy(mesh_out, mesh_out_hbm, sems.at[0])
     out.start()
 
     @pl.when(everywhere())
     def _():
-        for p in range(channels // pair):
+        for p in range(pairs):
             cols = slice(p * pair, (p + 1) * pair)
-            grad_key[:, cols] = mm_tn(grad_scores[p], halves(own_qkv[:, cols], scale))
-            grad_value[:, cols] = mm_tn(weights[p], halves(own_grad[:, cols]))
+            grad_query[:, cols] = (merge(mm(grad_scores[p], kv[:, cols])) * scale).astype(BF16)
+        for p in range(pairs):
+            cols = slice(p * pair, (p + 1) * pair)
+            grad_key[:, cols] = mm_tn(grad_scores[p, :, 2 * m :], halves(own_qkv[:, cols], scale))
+            grad_value[:, cols] = mm_tn(weights[p, :, 2 * m :], halves(own_grad[:, cols]))
         grad_normed[...] = mm_nt(grad_query[...], w_qkv[:, :channels])
 
     out.wait()
@@ -670,25 +679,25 @@
         [got_far, partial],
         name="latent",
     )
-    chip_normed, off_normed = exchange(normed, normed, "node")
+    off_normed = swap_off(normed, "node")
     own_block = ((pairs, 2 * m, m), F32)
-    own_qkv, w_qkv, own_grad, own_scores, own_products, bias, near_bias = call(
+    own_qkv, w_qkv, own_grad, own_scores, own_products, bias, near_bias, normed = call(
         functools.partial(project_kernel, scale, pair, meta_rows),
         [((m, 3 * channels), BF16), (w_qkv.shape, BF16), rows, own_block, own_block]
-        + [((m, 3 * m), F32), ((m, 2 * m), F32)],
+        + [((m, 3 * m), F32), ((m, 2 * m), F32), rows],
         [normed, from_chip, from_off, window, own_grad, w_qkv],
         hbm=(3, 4, 5),
         scratch=like(window) + [dma(3 * PIECES + 2)],
         name="project",
     )
+    chip_normed = swap_chip(normed, "node")
     chip_grad, off_grad = exchange(own_grad, own_grad, "node")
-    probs = ((pairs, 2 * m, m), BF16)
-    stats, attention, grad_query, weights, grad_scores, near_q, w_out, cotangent = call(
+    probs = ((pairs, 2 * m, 3 * m), BF16)
+    stats, kv, weights, grad_scores, near_q, w_out, cotangent = call(
         functools.partial(attend_kernel, scale, pair),
         [
             ((3 * pairs, 2 * m), F32),
-            rows,
-            rows,
+            ((3 * m, 2 * channels), BF16),
             probs,
             probs,
             ((2 * m, channels), BF16),
@@ -713,8 +722,7 @@
         [
             weights,
             grad_scores,
-            attention,
-            grad_query,
+            kv,
             own_qkv,
             own_grad,
             latent,
@@ -722,7 +730,7 @@
             w_qkv,
         ],
         hbm_outs=(0,),
-        scratch=[pltpu.VMEM((m, channels), BF16), dma(1)],
+        scratch=[pltpu.VMEM((m, channels), BF16)] * 3 + [dma(1)],
         name="product",
     )
     (mesh_grad,) = call(

time: 46.6 us -> 52.8 us (1.13)
  waiting for transfers between devices: 2.37 us -> 6.79 us
  starting transfers between devices: 19.4 us -> 21.3 us
    ppermute x8, waiting for transfers between devices: 0.77 us -> 5.19 us  [the longest x4 5.18 us: swap_off(): return lax.ppermute(rows, axis, pairs)]
    ppermute x8, starting transfers between devices: 14.1 us -> 15.9 us  [the longest x4 14.4 us: swap_off(): return lax.ppermute(rows, axis, pairs)]
  transfers between devices with their start and end apart: 9 -> 9, of which waited for: 2 -> 2; matrix products, arithmetic and copies ran while one was open for 0% -> 0% of each run, Pallas kernels for 35% -> 22%
where the time goes in v19:
time: 52.8 us; the launch traced here: 52.4 us
  Pallas kernels  23.6 us (45%)
  starting transfers between devices  21.3 us (40%)
  waiting for transfers between devices  6.79 us (13%)
  between operations  0.79 us (1%)
    pallas_call x8, Pallas kernels, call(): pl.pallas_call(kernel, out_shape=[(pltpu.HBM if i in hbm_outs else jax.Sh...  23.6 us
    ppermute x4, starting transfers between devices, swap_off(): return lax.ppermute(rows, axis, pairs)  14.4 us
    all_to_all x1, starting transfers between devices, body(): lax.all_to_all(far_message.reshape(devices, 2 * far_depth, far_block[1]),...  5.33 us
    ppermute x4, waiting for transfers between devices, swap_off(): return lax.ppermute(rows, axis, pairs)  5.18 us
    all_to_all x1, waiting for transfers between devices, body(): lax.all_to_all(far_message.reshape(devices, 2 * far_depth, far_block[1]),...  1.6 us
    ppermute x4, starting transfers between devices, swap_chip(): lax.ppermute(rows, axis, [p for i in range(0, n, 2) for p in ((i, i + 1),...  1.49 us
  transfers between devices with their start and end apart: 9, of which 2 were waited for; matrix products, arithmetic and copies ran while one was open for 0% of the time, Pallas kernels for 22%

profile of v19, /device:TPU:1, one launch (start us, length us, event | category | flops | bytes accessed | tf_op | source)
XLA Modules:
  0.0 52.4 jit_solution(17941007272424842986)
XLA Ops:
  0.6 3.4 %pack.1 = (bf16[128,640]{1,0:T(8,128)(2,1)}, bf16[144,1024]{1,0:T(8,128)(2,1)}, bf16[144,1024]{1,0:T(8,128)(2,1)}, bf16[1024,1024]{1,0:T(8,128)(2,1)S(1)}) custom-call(bf16[512,1024]{1,0:T(8,128)(2,1)} %grid_hbm.3, s32[2,128]{1,0:T(2,128)} %window_hbm.3, s32[32,128]{1,0:T(8,128)} %bitcast.12, s32[32,128]{1,0:T(8,128)} %bitcast.13, s32[1,2]{1,0:T(1,128)} %bitcast.16, ...), custom_call_target="tpu_custom_call" | custom-call | tf_op jit(solution)/shard_map/pack/pallas_call | solution.py:48
  4.0 0.1 collective-permute-start
  4.1 4.5 %collective-permute-start.1 = (bf16[144,1024]{1,0:T(8,128)(2,1)}, bf16[144,1024]{1,0:T(8,128)(2,1)S(1)}, u32[]{:S(2)}, u32[]{:S(2)}) collective-permute-start(bf16[144,1024]{1,0:T(8,128)(2,1)} %get-tuple-element.33), channel_id=1, source_target_pairs={{1,2},{2,1},{3,4},{4,3},{5,6},{6,5},{7,8},{8,7},{9,10},{10,9},{11,... | collective-permute-start | bytes 884744 | tf_op jit(solution)/shard_map/ppermute | solution.py:81
  8.6 5.3 %all-to-all-start = ((bf16[16,8,640]{2,1,0:T(8,128)(2,1)}), bf16[16,8,640]{2,1,0:T(8,128)(2,1)S(1)}, u32[]{:S(2)}, u32[]{:S(2)}) async-start(bf16[16,8,640]{2,1,0:T(8,128)(2,1)} %bitcast.11), calls=%async_computation | async-start | bytes 327680 | tf_op jit(solution)/shard_map/all_to_all | solution.py:651
  13.9 4.3 %own.1 = (f32[128,1024]{1,0:T(8,128)S(1)}, bf16[128,1024]{1,0:T(8,128)(2,1)}) custom-call(bf16[512,1024]{1,0:T(8,128)(2,1)} %grid_hbm.3, bf16[128,1024]{1,0:T(8,128)(2,1)} %mesh_in_hbm.1, s32[8,128]{1,0:T(8,128)} %bitcast.14, s32[8,128]{1,0:T(8,128)} %bitcast.15, bf16[128,1024]{1,0:T(8,128)(2,1)} %cot_hbm.3, bf16[1024,1024]{1,0:T(8,128)(2,1)} %w_out_hbm.3, ...), custom_call_target="tpu_custom_call" | custom-call | tf_op jit(solution)/shard_map/own/pallas_call | solution.py:48
  18.3 0.0 collective-permute-done.chip.chip_first
  18.3 0.0 collective-permute-done.1.off.off_first
  18.3 1.4 %side.1.partial = f32[128,1024]{1,0:T(8,128)S(1)} custom-call(bf16[144,1024]{1,0:T(8,128)(2,1)S(1)} %collective-permute-done.chip.chip_first, bf16[144,1024]{1,0:T(8,128)(2,1)S(1)} %collective-permute-done.1.off.off_first, bf16[1024,1024]{1,0:T(8,128)(2,1)S(1)} %get-tuple-element.34.w_edge, f32[128,1024]{1,0:T(8,128)S(1)} %get-tuple-element.35.partial), custom_call_target="tpu_custom_call" | custom-call | flops 8000000000 | tf_op jit(solution)/shard_map/side/pallas_call | solution.py:48
  19.7 1.6 %all-to-all-done = bf16[16,8,640]{2,1,0:T(8,128)(2,1)S(1)} async-done(((bf16[16,8,640]{2,1,0:T(8,128)(2,1)}), bf16[16,8,640]{2,1,0:T(8,128)(2,1)S(1)}, u32[]{:S(2)}, u32[]{:S(2)}) %all-to-all-start) | async-done | bytes 163872 | tf_op jit(solution)/shard_map/all_to_all | solution.py:651
  21.3 0.5 latent.1
  21.8 4.2 %project.1 = (bf16[128,3072]{1,0:T(8,128)(2,1)S(1)}, bf16[1024,3072]{1,0:T(8,128)(2,1)S(1)}, bf16[128,1024]{1,0:T(8,128)(2,1)S(1)}, f32[8,256,128]{2,1,0:T(8,128...) custom-call(bf16[128,1024]{1,0:T(8,128)(2,1)S(1)} %get-tuple-element, ...), custom_call_target="tpu_custom_call" | custom-call | tf_op jit(solution)/shard_map/project/pallas_call | solution.py:48
  26.0 1.2 %collective-permute-start.2 = (bf16[128,1024]{1,0:T(8,128)(2,1)S(1)}, bf16[128,1024]{1,0:T(8,128)(2,1)S(1)}, u32[]{:S(2)}, u32[]{:S(2)}) collective-permute-start(bf16[128,1024]{1,0:T(8,128)(2,1)S(1)} %get-tuple-element.38), channel_id=1, source_target_pairs={{0,1},{1,0},{2,3},{3,2},{4,5},{5,4},{6,7},{7,6},{8,9},{9,8},{10,11... | collective-permute-start | bytes 786440 | tf_op jit(solution)/shard_map/ppermute | solution.py:86
  27.3 1.9 %collective-permute-start.3 = (bf16[128,1024]{1,0:T(8,128)(2,1)S(1)}, bf16[128,1024]{1,0:T(8,128)(2,1)S(1)}, u32[]{:S(2)}, u32[]{:S(2)}) collective-permute-start(bf16[128,1024]{1,0:T(8,128)(2,1)S(1)} %get-tuple-element.36.normed), channel_id=1, source_target_pairs={{1,2},{2,1},{3,4},{4,3},{5,6},{6,5},{7,8},{8,7},{9,10},{10,9},{11,... | collective-permute-start | bytes 786440 | tf_op jit(solution)/shard_map/ppermute | solution.py:81
  29.2 0.1 collective-permute-start.6
  29.3 3.6 %collective-permute-start.7 = (bf16[128,1024]{1,0:T(8,128)(2,1)S(1)}, bf16[128,1024]{1,0:T(8,128)(2,1)S(1)}, u32[]{:S(2)}, u32[]{:S(2)}) collective-permute-start(bf16[128,1024]{1,0:T(8,128)(2,1)S(1)} %get-tuple-element.41.own_grad), channel_id=1, source_target_pairs={{1,2},{2,1},{3,4},{4,3},{5,6},{6,5},{7,8},{8,7},{9,10},{10,9},{11,... | collective-permute-start | bytes 786440 | tf_op jit(solution)/shard_map/ppermute | solution.py:81
  32.9 0.0 collective-permute-done.2.chip_normed
  32.9 5.2 %collective-permute-done.3.off_normed = bf16[128,1024]{1,0:T(8,128)(2,1)S(1)} collective-permute-done((bf16[128,1024]{1,0:T(8,128)(2,1)S(1)}, bf16[128,1024]{1,0:T(8,128)(2,1)S(1)}, u32[]{:S(2)}, u32[]{:S(2)}) %collective-permute-start.3) | collective-permute-done | bytes 262176 | tf_op jit(solution)/shard_map/ppermute | solution.py:81
  38.1 3.4 %attend.1 = (f32[24,256]{1,0:T(8,128)S(1)}, bf16[384,2048]{1,0:T(8,128)(2,1)S(1)}, bf16[8,256,384]{2,1,0:T(8,128)(2,1)S(1)}, bf16[8,256,384]{2,1,0:T(8,128)(2,1)...) custom-call(bf16[128,1024]{1,0:T(8,128)(2,1)S(1)} %collective-permute-done.2.chip, ...), custom_call_target="tpu_custom_call" | custom-call | tf_op jit(solution)/shard_map/attend/pallas_call | solution.py:48
  41.5 0.1 collective-permute-start.4
  41.6 4.4 %collective-permute-start.5 = (f32[24,256]{1,0:T(8,128)S(1)}, f32[24,256]{1,0:T(8,128)S(1)}, u32[]{:S(2)}, u32[]{:S(2)}) collective-permute-start(f32[24,256]{1,0:T(8,128)S(1)} %get-tuple-element.51), channel_id=1, source_target_pairs={{1,2},{2,1},{3,4},{4,3},{5,6},{6,5},{7,8},{8,7},{9,10},{10,9},{11,... | collective-permute-start | bytes 73736 | tf_op jit(solution)/shard_map/ppermute | solution.py:81
  46.0 2.6 %product.1 = (bf16[128,1024]{1,0:T(8,128)(2,1)}, f32[128,1024]{1,0:T(8,128)S(1)}, f32[128,1024]{1,0:T(8,128)S(1)}, f32[128,1024]{1,0:T(8,128)S(1)}) custom-call(bf16[8,256,384]{2,1,0:T(8,128)(2,1)S(1)} %get-tuple-element.45.weights, bf16[8,256,384]{2,1,0:T(8,128)(2,1)S(1)} %get-tuple-element.46.grad_scores, bf16[384,2048]{1,0:T(8,128)(2,1)S(1)} %get-tuple-element.47.kv, ...), custom_call_target="tpu_custom_call" | custom-call | tf_op jit(solution)/shard_map/product/pallas_call | solution.py:48
  48.6 0.0 collective-permute-done.6.chip_grad
  48.6 0.0 collective-permute-done.7.off_grad
  48.6 0.0 collective-permute-done.4.chip_stats
  48.6 0.0 collective-permute-done.5.off_stats
  48.6 3.8 %finish.1 = bf16[128,1024]{1,0:T(8,128)(2,1)} custom-call(f32[24,256]{1,0:T(8,128)S(1)} %collective-permute-done.4.chip_stats, f32[24,256]{1,0:T(8,128)S(1)} %collective-permute-done.5.off_stats, f32[128,256]{1,0:T(8,128)S(1)} %get-tuple-element.52.bias, bf16[256,1024]{1,0:T(8,128)(2,1)S(1)} %get-tuple-element.53.near_q, ...), custom_call_target="tpu_custom_call" | custom-call | tf_op jit(solution)/shard_map/finish/pallas_call | solution.py:48
Async XLA Ops:
  4.0 14.3 %collective-permute-start = (bf16[144,1024]{1,0:T(8,128)(2,1)}, bf16[144,1024]{1,0:T(8,128)(2,1)S(1)}, u32[]{:S(2)}, u32[]{:S(2)}) collective-permute-start(bf16[144,1024]{1,0:T(8,128)(2,1)} %get-tuple-element.32), channel_id=1, source_target_pairs={{0,1},{1,0},{2,3},{3,2},{4,5},{5,4},{6,7},{7,6},{8,9},{9,8},{10,11... | collective-permute-start | bytes 884744 | tf_op jit(solution)/shard_map/ppermute | solution.py:86
  4.1 14.2 %collective-permute-start.1 = (bf16[144,1024]{1,0:T(8,128)(2,1)}, bf16[144,1024]{1,0:T(8,128)(2,1)S(1)}, u32[]{:S(2)}, u32[]{:S(2)}) collective-permute-start(bf16[144,1024]{1,0:T(8,128)(2,1)} %get-tuple-element.33), channel_id=1, source_target_pairs={{1,2},{2,1},{3,4},{4,3},{5,6},{6,5},{7,8},{8,7},{9,10},{10,9},{11,... | collective-permute-start | bytes 884744 | tf_op jit(solution)/shard_map/ppermute | solution.py:81
  8.6 12.7 %all-to-all-start = ((bf16[16,8,640]{2,1,0:T(8,128)(2,1)}), bf16[16,8,640]{2,1,0:T(8,128)(2,1)S(1)}, u32[]{:S(2)}, u32[]{:S(2)}) async-start(bf16[16,8,640]{2,1,0:T(8,128)(2,1)} %bitcast.11), calls=%async_computation | async-start | bytes 327680 | tf_op jit(solution)/shard_map/all_to_all | solution.py:651
  26.0 6.9 %collective-permute-start.2 = (bf16[128,1024]{1,0:T(8,128)(2,1)S(1)}, bf16[128,1024]{1,0:T(8,128)(2,1)S(1)}, u32[]{:S(2)}, u32[]{:S(2)}) collective-permute-start(bf16[128,1024]{1,0:T(8,128)(2,1)S(1)} %get-tuple-element.38), channel_id=1, source_target_pairs={{0,1},{1,0},{2,3},{3,2},{4,5},{5,4},{6,7},{7,6},{8,9},{9,8},{10,11... | collective-permute-start | bytes 786440 | tf_op jit(solution)/shard_map/ppermute | solution.py:86
  27.3 10.8 %collective-permute-start.3 = (bf16[128,1024]{1,0:T(8,128)(2,1)S(1)}, bf16[128,1024]{1,0:T(8,128)(2,1)S(1)}, u32[]{:S(2)}, u32[]{:S(2)}) collective-permute-start(bf16[128,1024]{1,0:T(8,128)(2,1)S(1)} %get-tuple-element.36.normed), channel_id=1, source_target_pairs={{1,2},{2,1},{3,4},{4,3},{5,6},{6,5},{7,8},{8,7},{9,10},{10,9},{11,... | collective-permute-start | bytes 786440 | tf_op jit(solution)/shard_map/ppermute | solution.py:81
  29.2 19.4 %collective-permute-start.6 = (bf16[128,1024]{1,0:T(8,128)(2,1)S(1)}, bf16[128,1024]{1,0:T(8,128)(2,1)S(1)}, u32[]{:S(2)}, u32[]{:S(2)}) collective-permute-start(bf16[128,1024]{1,0:T(8,128)(2,1)S(1)} %get-tuple-element.41.own_grad), channel_id=1, source_target_pairs={{0,1},{1,0},{2,3},{3,2},{4,5},{5,4},{6,7},{7,6},{8,9},{9,8},{10,11... | collective-permute-start | bytes 786440 | tf_op jit(solution)/shard_map/ppermute | solution.py:86
  29.3 19.3 %collective-permute-start.7 = (bf16[128,1024]{1,0:T(8,128)(2,1)S(1)}, bf16[128,1024]{1,0:T(8,128)(2,1)S(1)}, u32[]{:S(2)}, u32[]{:S(2)}) collective-permute-start(bf16[128,1024]{1,0:T(8,128)(2,1)S(1)} %get-tuple-element.41.own_grad), channel_id=1, source_target_pairs={{1,2},{2,1},{3,4},{4,3},{5,6},{6,5},{7,8},{8,7},{9,10},{10,9},{11,... | collective-permute-start | bytes 786440 | tf_op jit(solution)/shard_map/ppermute | solution.py:81
  41.5 7.1 %collective-permute-start.4 = (f32[24,256]{1,0:T(8,128)S(1)}, f32[24,256]{1,0:T(8,128)S(1)}, u32[]{:S(2)}, u32[]{:S(2)}) collective-permute-start(f32[24,256]{1,0:T(8,128)S(1)} %get-tuple-element.51), channel_id=1, source_target_pairs={{0,1},{1,0},{2,3},{3,2},{4,5},{5,4},{6,7},{7,6},{8,9},{9,8},{10,11... | collective-permute-start | bytes 73736 | tf_op jit(solution)/shard_map/ppermute | solution.py:86
  41.6 7.0 %collective-permute-start.5 = (f32[24,256]{1,0:T(8,128)S(1)}, f32[24,256]{1,0:T(8,128)S(1)}, u32[]{:S(2)}, u32[]{:S(2)}) collective-permute-start(f32[24,256]{1,0:T(8,128)S(1)} %get-tuple-element.51), channel_id=1, source_target_pairs={{1,2},{2,1},{3,4},{4,3},{5,6},{6,5},{7,8},{8,7},{9,10},{10,9},{11,... | collective-permute-start | bytes 73736 | tf_op jit(solution)/shard_map/ppermute | solution.py:81

commit v20 on v19

--- a/solution.py
+++ b/solution.py
@@ -87,8 +87,8 @@
 
 
 def exchange(chip_message, off_message, axis):
-    from_off = swap_off(off_message, axis)
-    return swap_chip(chip_message, axis), from_off
+    from_chip = swap_chip(chip_message, axis)
+    return from_chip, swap_off(off_message, axis)
 
 
 def is_odd():
@@ -344,11 +344,9 @@
     products_out,
     bias_out,
     near_bias_out,
-    normed_out,
     window,
     sems,
 ):
-    normed_out[...] = normed[...]
     m, channels = normed.shape
     width = channels // PIECES
     starts = [part * channels + c * width for c in range(PIECES) for part in range(3)]
@@ -679,18 +677,17 @@
         [got_far, partial],
         name="latent",
     )
-    off_normed = swap_off(normed, "node")
+    chip_normed, off_normed = exchange(normed, normed, "node")
     own_block = ((pairs, 2 * m, m), F32)
-    own_qkv, w_qkv, own_grad, own_scores, own_products, bias, near_bias, normed = call(
+    own_qkv, w_qkv, own_grad, own_scores, own_products, bias, near_bias = call(
         functools.partial(project_kernel, scale, pair, meta_rows),
         [((m, 3 * channels), BF16), (w_qkv.shape, BF16), rows, own_block, own_block]
-        + [((m, 3 * m), F32), ((m, 2 * m), F32), rows],
+        + [((m, 3 * m), F32), ((m, 2 * m), F32)],
         [normed, from_chip, from_off, window, own_grad, w_qkv],
         hbm=(3, 4, 5),
         scratch=like(window) + [dma(3 * PIECES + 2)],
         name="project",
     )
-    chip_normed = swap_chip(normed, "node")
     chip_grad, off_grad = exchange(own_grad, own_grad, "node")
     probs = ((pairs, 2 * m, 3 * m), BF16)
     stats, kv, weights, grad_scores, near_q, w_out, cotangent = call(

time: 52.8 us -> 46 us (0.87)
  waiting for transfers between devices: 6.79 us -> 1.62 us
  starting transfers between devices: 21.3 us -> 19.4 us
    ppermute x4, waiting for transfers between devices: 5.18 us -> 0.01 us  [swap_off(): return lax.ppermute(rows, axis, pairs)]
    ppermute x4, starting transfers between devices: 14.4 us -> 12.6 us  [swap_off(): return lax.ppermute(rows, axis, pairs)]
  transfers between devices with their start and end apart: 9 -> 9, of which waited for: 2 -> 1; matrix products, arithmetic and copies ran while one was open for 0% -> 0% of each run, Pallas kernels for 22% -> 35%
where the time goes in v20:
time: 46 us; the launch traced here: 45.5 us
  Pallas kernels  23.7 us (52%)
  starting transfers between devices  19.4 us (42%)
  waiting for transfers between devices  1.62 us (4%)
  between operations  0.8 us (2%)
    pallas_call x8, Pallas kernels, call(): pl.pallas_call(kernel, out_shape=[(pltpu.HBM if i in hbm_outs else jax.Sh...  23.7 us
    ppermute x4, starting transfers between devices, swap_off(): return lax.ppermute(rows, axis, pairs)  12.6 us
    all_to_all x1, starting transfers between devices, body(): lax.all_to_all(far_message.reshape(devices, 2 * far_depth, far_block[1]),...  5.33 us
    all_to_all x1, waiting for transfers between devices, body(): lax.all_to_all(far_message.reshape(devices, 2 * far_depth, far_block[1]),...  1.6 us
    ppermute x4, starting transfers between devices, swap_chip(): lax.ppermute(rows, axis, [p for i in range(0, n, 2) for p in ((i, i + 1),...  1.49 us
  transfers between devices with their start and end apart: 9, of which 1 were waited for; matrix products, arithmetic and copies ran while one was open for 0% of the time, Pallas kernels for 35%

profile of v20, /device:TPU:1, one launch (start us, length us, event | category | flops | bytes accessed | tf_op | source)
XLA Modules:
  0.0 45.5 jit_solution(2540877587653412378)
XLA Ops:
  0.6 3.4 %pack.1 = (bf16[128,640]{1,0:T(8,128)(2,1)}, bf16[144,1024]{1,0:T(8,128)(2,1)}, bf16[144,1024]{1,0:T(8,128)(2,1)}, bf16[1024,1024]{1,0:T(8,128)(2,1)S(1)}) custom-call(bf16[512,1024]{1,0:T(8,128)(2,1)} %grid_hbm.3, s32[2,128]{1,0:T(2,128)} %window_hbm.3, s32[32,128]{1,0:T(8,128)} %bitcast.12, s32[32,128]{1,0:T(8,128)} %bitcast.13, s32[1,2]{1,0:T(1,128)} %bitcast.16, ...), custom_call_target="tpu_custom_call" | custom-call | tf_op jit(solution)/shard_map/pack/pallas_call | solution.py:48
  4.0 0.1 collective-permute-start
  4.1 4.5 %collective-permute-start.1 = (bf16[144,1024]{1,0:T(8,128)(2,1)}, bf16[144,1024]{1,0:T(8,128)(2,1)S(1)}, u32[]{:S(2)}, u32[]{:S(2)}) collective-permute-start(bf16[144,1024]{1,0:T(8,128)(2,1)} %get-tuple-element.32), channel_id=1, source_target_pairs={{1,2},{2,1},{3,4},{4,3},{5,6},{6,5},{7,8},{8,7},{9,10},{10,9},{11,... | collective-permute-start | bytes 884744 | tf_op jit(solution)/shard_map/ppermute | solution.py:81
  8.6 5.3 %all-to-all-start = ((bf16[16,8,640]{2,1,0:T(8,128)(2,1)}), bf16[16,8,640]{2,1,0:T(8,128)(2,1)S(1)}, u32[]{:S(2)}, u32[]{:S(2)}) async-start(bf16[16,8,640]{2,1,0:T(8,128)(2,1)} %bitcast.11), calls=%async_computation | async-start | bytes 327680 | tf_op jit(solution)/shard_map/all_to_all | solution.py:649
  13.9 4.3 %own.1 = (f32[128,1024]{1,0:T(8,128)S(1)}, bf16[128,1024]{1,0:T(8,128)(2,1)}) custom-call(bf16[512,1024]{1,0:T(8,128)(2,1)} %grid_hbm.3, bf16[128,1024]{1,0:T(8,128)(2,1)} %mesh_in_hbm.1, s32[8,128]{1,0:T(8,128)} %bitcast.14, s32[8,128]{1,0:T(8,128)} %bitcast.15, bf16[128,1024]{1,0:T(8,128)(2,1)} %cot_hbm.3, bf16[1024,1024]{1,0:T(8,128)(2,1)} %w_out_hbm.3, ...), custom_call_target="tpu_custom_call" | custom-call | tf_op jit(solution)/shard_map/own/pallas_call | solution.py:48
  18.3 0.0 collective-permute-done.chip.chip_first
  18.3 0.0 collective-permute-done.1.off.off_first
  18.3 1.4 %side.1.partial = f32[128,1024]{1,0:T(8,128)S(1)} custom-call(bf16[144,1024]{1,0:T(8,128)(2,1)S(1)} %collective-permute-done.chip.chip_first, bf16[144,1024]{1,0:T(8,128)(2,1)S(1)} %collective-permute-done.1.off.off_first, bf16[1024,1024]{1,0:T(8,128)(2,1)S(1)} %get-tuple-element.33.w_edge, f32[128,1024]{1,0:T(8,128)S(1)} %get-tuple-element.34.partial), custom_call_target="tpu_custom_call" | custom-call | flops 8000000000 | tf_op jit(solution)/shard_map/side/pallas_call | solution.py:48
  19.7 1.6 %all-to-all-done = bf16[16,8,640]{2,1,0:T(8,128)(2,1)S(1)} async-done(((bf16[16,8,640]{2,1,0:T(8,128)(2,1)}), bf16[16,8,640]{2,1,0:T(8,128)(2,1)S(1)}, u32[]{:S(2)}, u32[]{:S(2)}) %all-to-all-start) | async-done | bytes 163872 | tf_op jit(solution)/shard_map/all_to_all | solution.py:649
  21.3 0.5 %latent.1 = (bf16[128,1024]{1,0:T(8,128)(2,1)S(1)}, bf16[128,1024]{1,0:T(8,128)(2,1)S(1)}, f32[128,1024]{1,0:T(8,128)S(1)}, f32[128,128]{1,0:T(8,128)S(1)}) custom-call(bf16[128,640]{1,0:T(8,128)(2,1)S(1)} %bitcast.10, f32[128,1024]{1,0:T(8,128)S(1)} %side.1.partial), custom_call_target="tpu_custom_call" | custom-call | tf_op jit(solution)/shard_map/latent/pallas_call | solution.py:48
  21.8 1.2 %collective-permute-start.2 = (bf16[128,1024]{1,0:T(8,128)(2,1)S(1)}, bf16[128,1024]{1,0:T(8,128)(2,1)S(1)}, u32[]{:S(2)}, u32[]{:S(2)}) collective-permute-start(bf16[128,1024]{1,0:T(8,128)(2,1)S(1)} %get-tuple-element.35.normed), channel_id=1, source_target_pairs={{0,1},{1,0},{2,3},{3,2},{4,5},{5,4},{6,7},{7,6},{8,9},{9,8},{10,11... | collective-permute-start | bytes 786440 | tf_op jit(solution)/shard_map/ppermute | solution.py:86
  23.1 1.9 %collective-permute-start.3 = (bf16[128,1024]{1,0:T(8,128)(2,1)S(1)}, bf16[128,1024]{1,0:T(8,128)(2,1)S(1)}, u32[]{:S(2)}, u32[]{:S(2)}) collective-permute-start(bf16[128,1024]{1,0:T(8,128)(2,1)S(1)} %get-tuple-element.35.normed), channel_id=1, source_target_pairs={{1,2},{2,1},{3,4},{4,3},{5,6},{6,5},{7,8},{8,7},{9,10},{10,9},{11,... | collective-permute-start | bytes 786440 | tf_op jit(solution)/shard_map/ppermute | solution.py:81
  25.0 4.2 %project.1 = (bf16[128,3072]{1,0:T(8,128)(2,1)S(1)}, bf16[1024,3072]{1,0:T(8,128)(2,1)S(1)}, bf16[128,1024]{1,0:T(8,128)(2,1)S(1)}, f32[8,256,128]{2,1,0:T(8,128...) custom-call(bf16[128,1024]{1,0:T(8,128)(2,1)S(1)} %get-tuple-element.35.normed, ...), custom_call_target="tpu_custom_call" | custom-call | tf_op jit(solution)/shard_map/project/pallas_call | solution.py:48
  29.2 0.1 collective-permute-start.6
  29.3 3.6 %collective-permute-start.7 = (bf16[128,1024]{1,0:T(8,128)(2,1)S(1)}, bf16[128,1024]{1,0:T(8,128)(2,1)S(1)}, u32[]{:S(2)}, u32[]{:S(2)}) collective-permute-start(bf16[128,1024]{1,0:T(8,128)(2,1)S(1)} %get-tuple-element.39.own_grad), channel_id=1, source_target_pairs={{1,2},{2,1},{3,4},{4,3},{5,6},{6,5},{7,8},{8,7},{9,10},{10,9},{11,... | collective-permute-start | bytes 786440 | tf_op jit(solution)/shard_map/ppermute | solution.py:81
  32.9 0.0 collective-permute-done.2.chip_normed
  32.9 0.0 collective-permute-done.3.off_normed
  32.9 3.5 %attend.1 = (f32[24,256]{1,0:T(8,128)S(1)}, bf16[384,2048]{1,0:T(8,128)(2,1)S(1)}, bf16[8,256,384]{2,1,0:T(8,128)(2,1)S(1)}, bf16[8,256,384]{2,1,0:T(8,128)(2,1)...) custom-call(bf16[128,1024]{1,0:T(8,128)(2,1)S(1)} %collective-permute-done.2.chip, ...), custom_call_target="tpu_custom_call" | custom-call | tf_op jit(solution)/shard_map/attend/pallas_call | solution.py:48
  36.5 0.1 collective-permute-start.4
  36.6 2.5 %collective-permute-start.5 = (f32[24,256]{1,0:T(8,128)S(1)}, f32[24,256]{1,0:T(8,128)S(1)}, u32[]{:S(2)}, u32[]{:S(2)}) collective-permute-start(f32[24,256]{1,0:T(8,128)S(1)} %get-tuple-element.49), channel_id=1, source_target_pairs={{1,2},{2,1},{3,4},{4,3},{5,6},{6,5},{7,8},{8,7},{9,10},{10,9},{11,... | collective-permute-start | bytes 73736 | tf_op jit(solution)/shard_map/ppermute | solution.py:81
  39.1 2.6 %product.1 = (bf16[128,1024]{1,0:T(8,128)(2,1)}, f32[128,1024]{1,0:T(8,128)S(1)}, f32[128,1024]{1,0:T(8,128)S(1)}, f32[128,1024]{1,0:T(8,128)S(1)}) custom-call(bf16[8,256,384]{2,1,0:T(8,128)(2,1)S(1)} %get-tuple-element.43.weights, bf16[8,256,384]{2,1,0:T(8,128)(2,1)S(1)} %get-tuple-element.44.grad_scores, bf16[384,2048]{1,0:T(8,128)(2,1)S(1)} %get-tuple-element.45.kv, ...), custom_call_target="tpu_custom_call" | custom-call | tf_op jit(solution)/shard_map/product/pallas_call | solution.py:48
  41.7 0.0 collective-permute-done.6.chip_grad
  41.7 0.0 collective-permute-done.7.off_grad
  41.7 0.0 collective-permute-done.4.chip_stats
  41.8 0.0 collective-permute-done.5.off_stats
  41.8 3.8 %finish.1 = bf16[128,1024]{1,0:T(8,128)(2,1)} custom-call(f32[24,256]{1,0:T(8,128)S(1)} %collective-permute-done.4.chip_stats, f32[24,256]{1,0:T(8,128)S(1)} %collective-permute-done.5.off_stats, f32[128,256]{1,0:T(8,128)S(1)} %get-tuple-element.50.bias, bf16[256,1024]{1,0:T(8,128)(2,1)S(1)} %get-tuple-element.51.near_q, ...), custom_call_target="tpu_custom_call" | custom-call | tf_op jit(solution)/shard_map/finish/pallas_call | solution.py:48
Async XLA Ops:
  4.0 14.3 %collective-permute-start = (bf16[144,1024]{1,0:T(8,128)(2,1)}, bf16[144,1024]{1,0:T(8,128)(2,1)S(1)}, u32[]{:S(2)}, u32[]{:S(2)}) collective-permute-start(bf16[144,1024]{1,0:T(8,128)(2,1)} %get-tuple-element.31), channel_id=1, source_target_pairs={{0,1},{1,0},{2,3},{3,2},{4,5},{5,4},{6,7},{7,6},{8,9},{9,8},{10,11... | collective-permute-start | bytes 884744 | tf_op jit(solution)/shard_map/ppermute | solution.py:86
  4.1 14.2 %collective-permute-start.1 = (bf16[144,1024]{1,0:T(8,128)(2,1)}, bf16[144,1024]{1,0:T(8,128)(2,1)S(1)}, u32[]{:S(2)}, u32[]{:S(2)}) collective-permute-start(bf16[144,1024]{1,0:T(8,128)(2,1)} %get-tuple-element.32), channel_id=1, source_target_pairs={{1,2},{2,1},{3,4},{4,3},{5,6},{6,5},{7,8},{8,7},{9,10},{10,9},{11,... | collective-permute-start | bytes 884744 | tf_op jit(solution)/shard_map/ppermute | solution.py:81
  8.6 12.7 %all-to-all-start = ((bf16[16,8,640]{2,1,0:T(8,128)(2,1)}), bf16[16,8,640]{2,1,0:T(8,128)(2,1)S(1)}, u32[]{:S(2)}, u32[]{:S(2)}) async-start(bf16[16,8,640]{2,1,0:T(8,128)(2,1)} %bitcast.11), calls=%async_computation | async-start | bytes 327680 | tf_op jit(solution)/shard_map/all_to_all | solution.py:649
  21.8 11.1 %collective-permute-start.2 = (bf16[128,1024]{1,0:T(8,128)(2,1)S(1)}, bf16[128,1024]{1,0:T(8,128)(2,1)S(1)}, u32[]{:S(2)}, u32[]{:S(2)}) collective-permute-start(bf16[128,1024]{1,0:T(8,128)(2,1)S(1)} %get-tuple-element.35.normed), channel_id=1, source_target_pairs={{0,1},{1,0},{2,3},{3,2},{4,5},{5,4},{6,7},{7,6},{8,9},{9,8},{10,11... | collective-permute-start | bytes 786440 | tf_op jit(solution)/shard_map/ppermute | solution.py:86
  23.1 9.9 %collective-permute-start.3 = (bf16[128,1024]{1,0:T(8,128)(2,1)S(1)}, bf16[128,1024]{1,0:T(8,128)(2,1)S(1)}, u32[]{:S(2)}, u32[]{:S(2)}) collective-permute-start(bf16[128,1024]{1,0:T(8,128)(2,1)S(1)} %get-tuple-element.35.normed), channel_id=1, source_target_pairs={{1,2},{2,1},{3,4},{4,3},{5,6},{6,5},{7,8},{8,7},{9,10},{10,9},{11,... | collective-permute-start | bytes 786440 | tf_op jit(solution)/shard_map/ppermute | solution.py:81
  29.2 12.5 %collective-permute-start.6 = (bf16[128,1024]{1,0:T(8,128)(2,1)S(1)}, bf16[128,1024]{1,0:T(8,128)(2,1)S(1)}, u32[]{:S(2)}, u32[]{:S(2)}) collective-permute-start(bf16[128,1024]{1,0:T(8,128)(2,1)S(1)} %get-tuple-element.39.own_grad), channel_id=1, source_target_pairs={{0,1},{1,0},{2,3},{3,2},{4,5},{5,4},{6,7},{7,6},{8,9},{9,8},{10,11... | collective-permute-start | bytes 786440 | tf_op jit(solution)/shard_map/ppermute | solution.py:86
  29.3 12.5 %collective-permute-start.7 = (bf16[128,1024]{1,0:T(8,128)(2,1)S(1)}, bf16[128,1024]{1,0:T(8,128)(2,1)S(1)}, u32[]{:S(2)}, u32[]{:S(2)}) collective-permute-start(bf16[128,1024]{1,0:T(8,128)(2,1)S(1)} %get-tuple-element.39.own_grad), channel_id=1, source_target_pairs={{1,2},{2,1},{3,4},{4,3},{5,6},{6,5},{7,8},{8,7},{9,10},{10,9},{11,... | collective-permute-start | bytes 786440 | tf_op jit(solution)/shard_map/ppermute | solution.py:81
  36.5 5.3 %collective-permute-start.4 = (f32[24,256]{1,0:T(8,128)S(1)}, f32[24,256]{1,0:T(8,128)S(1)}, u32[]{:S(2)}, u32[]{:S(2)}) collective-permute-start(f32[24,256]{1,0:T(8,128)S(1)} %get-tuple-element.49), channel_id=1, source_target_pairs={{0,1},{1,0},{2,3},{3,2},{4,5},{5,4},{6,7},{7,6},{8,9},{9,8},{10,11... | collective-permute-start | bytes 73736 | tf_op jit(solution)/shard_map/ppermute | solution.py:86
  36.6 5.2 %collective-permute-start.5 = (f32[24,256]{1,0:T(8,128)S(1)}, f32[24,256]{1,0:T(8,128)S(1)}, u32[]{:S(2)}, u32[]{:S(2)}) collective-permute-start(f32[24,256]{1,0:T(8,128)S(1)} %get-tuple-element.49), channel_id=1, source_target_pairs={{1,2},{2,1},{3,4},{4,3},{5,6},{6,5},{7,8},{8,7},{9,10},{10,9},{11,... | collective-permute-start | bytes 73736 | tf_op jit(solution)/shard_map/ppermute | solution.py:81

commit v21 on v19

--- a/solution.py
+++ b/solution.py
@@ -15,6 +15,7 @@
 I32 = jnp.int32
 VMEM_LIMIT = 28 * 2**20
 PIECES = 2
+PAD = 8
 CHUNK = 64
 
 
@@ -87,8 +88,8 @@
 
 
 def exchange(chip_message, off_message, axis):
-    from_off = swap_off(off_message, axis)
-    return swap_chip(chip_message, axis), from_off
+    from_chip = swap_chip(chip_message, axis)
+    return from_chip, swap_off(off_message, axis)
 
 
 def is_odd():
@@ -287,7 +288,9 @@
     partial_out[...] = partial[...] + mm(landing, jnp.concatenate([active, active], 0))
 
 
-def latent_kernel(depth, far, partial, latent_out, normed_out, normal_out, inv_std_out):
+def latent_kernel(
+    depth, far, partial, latent_out, normed_out, off_out, normal_out, inv_std_out
+):
     mesh_rows, channels = partial.shape
     slots = far.shape[0]
     half = channels // 2
@@ -303,7 +306,9 @@
     latent = total.astype(BF16)
     latent_out[...] = latent
     normal, inv_std = norm_stats(latent)
-    normed_out[...] = normal.astype(BF16)
+    normed = normal.astype(BF16)
+    normed_out[...] = normed
+    off_out[...] = jnp.concatenate([normed, jnp.zeros((PAD, channels), BF16)], 0)
     normal_out[...] = normal
     inv_std_out[...] = jnp.broadcast_to(inv_std, inv_std_out.shape)
 
@@ -348,8 +353,8 @@
     window,
     sems,
 ):
+    m, channels = normed.shape
     normed_out[...] = normed[...]
-    m, channels = normed.shape
     width = channels // PIECES
     starts = [part * channels + c * width for c in range(PIECES) for part in range(3)]
     copies = start_all(
@@ -422,7 +427,7 @@
 
     @pl.when(everywhere())
     def _():
-        near = jnp.concatenate([chip_normed[...], off_normed[...]], 0)
+        near = jnp.concatenate([chip_normed[...], off_normed[:m]], 0)
 
         def bring(group):
             cols = slice(group * 2 * pair, (group + 1) * 2 * pair)
@@ -673,13 +678,13 @@
         name="side",
         flops=8 * 10**9,
     )
-    latent, normed, normal, inv_std = call(
+    latent, normed, off_message, normal, inv_std = call(
         functools.partial(latent_kernel, far_depth),
-        [rows, rows, ((m, channels), F32), ((m, LANES), F32)],
+        [rows, rows, ((m + PAD, channels), BF16), ((m, channels), F32), ((m, LANES), F32)],
         [got_far, partial],
         name="latent",
     )
-    off_normed = swap_off(normed, "node")
+    off_normed = swap_off(off_message, "node")
     own_block = ((pairs, 2 * m, m), F32)
     own_qkv, w_qkv, own_grad, own_scores, own_products, bias, near_bias, normed = call(
         functools.partial(project_kernel, scale, pair, meta_rows),

time: 52.8 us -> 46 us (0.87)
  waiting for transfers between devices: 6.79 us -> 1.62 us
  starting transfers between devices: 21.3 us -> 19.6 us
    ppermute x4, waiting for transfers between devices: 5.18 us -> 0.01 us  [swap_off(): return lax.ppermute(rows, axis, pairs)]
    ppermute x4, starting transfers between devices: 14.4 us -> 13.5 us  [swap_off(): return lax.ppermute(rows, axis, pairs)]
    ppermute x4, starting transfers between devices: 1.49 us -> 0.76 us  [swap_chip(): lax.ppermute(rows, axis, [p for i in range(0, n, 2) for p in ((i, i + 1),...]
  transfers between devices with their start and end apart: 9 -> 9, of which waited for: 2 -> 1; matrix products, arithmetic and copies ran while one was open for 0% -> 0% of each run, Pallas kernels for 22% -> 35%
where the time goes in v21:
time: 46 us; the launch traced here: 45.6 us
  Pallas kernels  23.6 us (51%)
  starting transfers between devices  19.6 us (43%)
  waiting for transfers between devices  1.62 us (4%)
  between operations  0.8 us (2%)
    pallas_call x8, Pallas kernels, call(): pl.pallas_call(kernel, out_shape=[(pltpu.HBM if i in hbm_outs else jax.Sh...  23.6 us
    ppermute x4, starting transfers between devices, swap_off(): return lax.ppermute(rows, axis, pairs)  13.5 us
    all_to_all x1, starting transfers between devices, body(): lax.all_to_all(far_message.reshape(devices, 2 * far_depth, far_block[1]),...  5.33 us
    all_to_all x1, waiting for transfers between devices, body(): lax.all_to_all(far_message.reshape(devices, 2 * far_depth, far_block[1]),...  1.6 us
  transfers between devices with their start and end apart: 9, of which 1 were waited for; matrix products, arithmetic and copies ran while one was open for 0% of the time, Pallas kernels for 35%

profile of v21, /device:TPU:1, one launch (start us, length us, event | category | flops | bytes accessed | tf_op | source)
XLA Modules:
  0.0 45.6 jit_solution(837085284518963897)
XLA Ops:
  0.6 3.4 %pack.1 = (bf16[128,640]{1,0:T(8,128)(2,1)}, bf16[144,1024]{1,0:T(8,128)(2,1)}, bf16[144,1024]{1,0:T(8,128)(2,1)}, bf16[1024,1024]{1,0:T(8,128)(2,1)S(1)}) custom-call(bf16[512,1024]{1,0:T(8,128)(2,1)} %grid_hbm.3, s32[2,128]{1,0:T(2,128)} %window_hbm.3, s32[32,128]{1,0:T(8,128)} %bitcast.12, s32[32,128]{1,0:T(8,128)} %bitcast.13, s32[1,2]{1,0:T(1,128)} %bitcast.16, ...), custom_call_target="tpu_custom_call" | custom-call | tf_op jit(solution)/shard_map/pack/pallas_call | solution.py:49
  4.0 0.1 collective-permute-start
  4.1 4.5 %collective-permute-start.1 = (bf16[144,1024]{1,0:T(8,128)(2,1)}, bf16[144,1024]{1,0:T(8,128)(2,1)S(1)}, u32[]{:S(2)}, u32[]{:S(2)}) collective-permute-start(bf16[144,1024]{1,0:T(8,128)(2,1)} %get-tuple-element.34), channel_id=1, source_target_pairs={{1,2},{2,1},{3,4},{4,3},{5,6},{6,5},{7,8},{8,7},{9,10},{10,9},{11,... | collective-permute-start | bytes 884744 | tf_op jit(solution)/shard_map/ppermute | solution.py:82
  8.6 5.3 %all-to-all-start = ((bf16[16,8,640]{2,1,0:T(8,128)(2,1)}), bf16[16,8,640]{2,1,0:T(8,128)(2,1)S(1)}, u32[]{:S(2)}, u32[]{:S(2)}) async-start(bf16[16,8,640]{2,1,0:T(8,128)(2,1)} %bitcast.11), calls=%async_computation | async-start | bytes 327680 | tf_op jit(solution)/shard_map/all_to_all | solution.py:656
  13.9 4.3 %own.1 = (f32[128,1024]{1,0:T(8,128)S(1)}, bf16[128,1024]{1,0:T(8,128)(2,1)}) custom-call(bf16[512,1024]{1,0:T(8,128)(2,1)} %grid_hbm.3, bf16[128,1024]{1,0:T(8,128)(2,1)} %mesh_in_hbm.1, s32[8,128]{1,0:T(8,128)} %bitcast.14, s32[8,128]{1,0:T(8,128)} %bitcast.15, bf16[128,1024]{1,0:T(8,128)(2,1)} %cot_hbm.3, bf16[1024,1024]{1,0:T(8,128)(2,1)} %w_out_hbm.3, ...), custom_call_target="tpu_custom_call" | custom-call | tf_op jit(solution)/shard_map/own/pallas_call | solution.py:49
  18.3 0.0 collective-permute-done.chip.chip_first
  18.3 0.0 collective-permute-done.1.off.off_first
  18.3 1.4 %side.1.partial = f32[128,1024]{1,0:T(8,128)S(1)} custom-call(bf16[144,1024]{1,0:T(8,128)(2,1)S(1)} %collective-permute-done.chip.chip_first, bf16[144,1024]{1,0:T(8,128)(2,1)S(1)} %collective-permute-done.1.off.off_first, bf16[1024,1024]{1,0:T(8,128)(2,1)S(1)} %get-tuple-element.35.w_edge, f32[128,1024]{1,0:T(8,128)S(1)} %get-tuple-element.36.partial), custom_call_target="tpu_custom_call" | custom-call | flops 8000000000 | tf_op jit(solution)/shard_map/side/pallas_call | solution.py:49
  19.7 1.6 %all-to-all-done = bf16[16,8,640]{2,1,0:T(8,128)(2,1)S(1)} async-done(((bf16[16,8,640]{2,1,0:T(8,128)(2,1)}), bf16[16,8,640]{2,1,0:T(8,128)(2,1)S(1)}, u32[]{:S(2)}, u32[]{:S(2)}) %all-to-all-start) | async-done | bytes 163872 | tf_op jit(solution)/shard_map/all_to_all | solution.py:656
  21.3 0.5 %latent.1 = (bf16[128,1024]{1,0:T(8,128)(2,1)S(1)}, bf16[128,1024]{1,0:T(8,128)(2,1)S(1)}, bf16[136,1024]{1,0:T(8,128)(2,1)S(1)}, f32[128,1024]{1,0:T(8,128)S(1)}, f32[128,128]{1,0:T(8,128)S(1)}) custom-call(bf16[128,640]{1,0:T(8,128)(2,1)S(1)} %bitcast.10, f32[128,1024]{1,0:T(8,128)S(1)} %side.1.partial), custom_call_target="tpu_custom_call" | custom-call | tf_op jit(solution)/shard_map/latent/pallas_call | solution.py:49
  21.8 2.0 %collective-permute-start.3 = (bf16[136,1024]{1,0:T(8,128)(2,1)S(1)}, bf16[136,1024]{1,0:T(8,128)(2,1)S(1)}, u32[]{:S(2)}, u32[]{:S(2)}) collective-permute-start(bf16[136,1024]{1,0:T(8,128)(2,1)S(1)} %get-tuple-element.40), channel_id=1, source_target_pairs={{1,2},{2,1},{3,4},{4,3},{5,6},{6,5},{7,8},{8,7},{9,10},{10,9},{11,... | collective-permute-start | bytes 835592 | tf_op jit(solution)/shard_map/ppermute | solution.py:82
  23.8 4.2 %project.1 = (bf16[128,3072]{1,0:T(8,128)(2,1)S(1)}, bf16[1024,3072]{1,0:T(8,128)(2,1)S(1)}, bf16[128,1024]{1,0:T(8,128)(2,1)S(1)}, f32[8,256,128]{2,1,0:T(8,128...) custom-call(bf16[128,1024]{1,0:T(8,128)(2,1)S(1)} %get-tuple-element, ...), custom_call_target="tpu_custom_call" | custom-call | tf_op jit(solution)/shard_map/project/pallas_call | solution.py:49
  28.0 0.1 collective-permute-start.2
  28.1 0.5 %collective-permute-start.6 = (bf16[128,1024]{1,0:T(8,128)(2,1)S(1)}, bf16[128,1024]{1,0:T(8,128)(2,1)S(1)}, u32[]{:S(2)}, u32[]{:S(2)}) collective-permute-start(bf16[128,1024]{1,0:T(8,128)(2,1)S(1)} %get-tuple-element.43.own_grad), channel_id=1, source_target_pairs={{0,1},{1,0},{2,3},{3,2},{4,5},{5,4},{6,7},{7,6},{8,9},{9,8},{10,11... | collective-permute-start | bytes 786440 | tf_op jit(solution)/shard_map/ppermute | solution.py:87
  28.6 3.6 %collective-permute-start.7 = (bf16[128,1024]{1,0:T(8,128)(2,1)S(1)}, bf16[128,1024]{1,0:T(8,128)(2,1)S(1)}, u32[]{:S(2)}, u32[]{:S(2)}) collective-permute-start(bf16[128,1024]{1,0:T(8,128)(2,1)S(1)} %get-tuple-element.43.own_grad), channel_id=1, source_target_pairs={{1,2},{2,1},{3,4},{4,3},{5,6},{6,5},{7,8},{8,7},{9,10},{10,9},{11,... | collective-permute-start | bytes 786440 | tf_op jit(solution)/shard_map/ppermute | solution.py:82
  32.2 0.0 collective-permute-done.2.chip_normed
  32.2 0.0 collective-permute-done.3.off_normed
  32.2 3.4 %attend.1 = (f32[24,256]{1,0:T(8,128)S(1)}, bf16[384,2048]{1,0:T(8,128)(2,1)S(1)}, bf16[8,256,384]{2,1,0:T(8,128)(2,1)S(1)}, bf16[8,256,384]{2,1,0:T(8,128)(2,1)...) custom-call(bf16[128,1024]{1,0:T(8,128)(2,1)S(1)} %collective-permute-done.2.chip, ...), custom_call_target="tpu_custom_call" | custom-call | tf_op jit(solution)/shard_map/attend/pallas_call | solution.py:49
  35.6 0.1 collective-permute-start.4
  35.7 3.5 %collective-permute-start.5 = (f32[24,256]{1,0:T(8,128)S(1)}, f32[24,256]{1,0:T(8,128)S(1)}, u32[]{:S(2)}, u32[]{:S(2)}) collective-permute-start(f32[24,256]{1,0:T(8,128)S(1)} %get-tuple-element.53), channel_id=1, source_target_pairs={{1,2},{2,1},{3,4},{4,3},{5,6},{6,5},{7,8},{8,7},{9,10},{10,9},{11,... | collective-permute-start | bytes 73736 | tf_op jit(solution)/shard_map/ppermute | solution.py:82
  39.2 2.6 %product.1 = (bf16[128,1024]{1,0:T(8,128)(2,1)}, f32[128,1024]{1,0:T(8,128)S(1)}, f32[128,1024]{1,0:T(8,128)S(1)}, f32[128,1024]{1,0:T(8,128)S(1)}) custom-call(bf16[8,256,384]{2,1,0:T(8,128)(2,1)S(1)} %get-tuple-element.47.weights, bf16[8,256,384]{2,1,0:T(8,128)(2,1)S(1)} %get-tuple-element.48.grad_scores, bf16[384,2048]{1,0:T(8,128)(2,1)S(1)} %get-tuple-element.49.kv, ...), custom_call_target="tpu_custom_call" | custom-call | tf_op jit(solution)/shard_map/product/pallas_call | solution.py:49
  41.8 0.0 collective-permute-done.6.chip_grad
  41.8 0.0 collective-permute-done.7.off_grad
  41.8 0.0 collective-permute-done.4.chip_stats
  41.8 0.0 collective-permute-done.5.off_stats
  41.8 3.8 %finish.1 = bf16[128,1024]{1,0:T(8,128)(2,1)} custom-call(f32[24,256]{1,0:T(8,128)S(1)} %collective-permute-done.4.chip_stats, f32[24,256]{1,0:T(8,128)S(1)} %collective-permute-done.5.off_stats, f32[128,256]{1,0:T(8,128)S(1)} %get-tuple-element.54.bias, bf16[256,1024]{1,0:T(8,128)(2,1)S(1)} %get-tuple-element.55.near_q, ...), custom_call_target="tpu_custom_call" | custom-call | tf_op jit(solution)/shard_map/finish/pallas_call | solution.py:49
Async XLA Ops:
  4.0 14.3 %collective-permute-start = (bf16[144,1024]{1,0:T(8,128)(2,1)}, bf16[144,1024]{1,0:T(8,128)(2,1)S(1)}, u32[]{:S(2)}, u32[]{:S(2)}) collective-permute-start(bf16[144,1024]{1,0:T(8,128)(2,1)} %get-tuple-element.33), channel_id=1, source_target_pairs={{0,1},{1,0},{2,3},{3,2},{4,5},{5,4},{6,7},{7,6},{8,9},{9,8},{10,11... | collective-permute-start | bytes 884744 | tf_op jit(solution)/shard_map/ppermute | solution.py:87
  4.1 14.2 %collective-permute-start.1 = (bf16[144,1024]{1,0:T(8,128)(2,1)}, bf16[144,1024]{1,0:T(8,128)(2,1)S(1)}, u32[]{:S(2)}, u32[]{:S(2)}) collective-permute-start(bf16[144,1024]{1,0:T(8,128)(2,1)} %get-tuple-element.34), channel_id=1, source_target_pairs={{1,2},{2,1},{3,4},{4,3},{5,6},{6,5},{7,8},{8,7},{9,10},{10,9},{11,... | collective-permute-start | bytes 884744 | tf_op jit(solution)/shard_map/ppermute | solution.py:82
  8.6 12.7 %all-to-all-start = ((bf16[16,8,640]{2,1,0:T(8,128)(2,1)}), bf16[16,8,640]{2,1,0:T(8,128)(2,1)S(1)}, u32[]{:S(2)}, u32[]{:S(2)}) async-start(bf16[16,8,640]{2,1,0:T(8,128)(2,1)} %bitcast.11), calls=%async_computation | async-start | bytes 327680 | tf_op jit(solution)/shard_map/all_to_all | solution.py:656
  21.8 10.4 %collective-permute-start.3 = (bf16[136,1024]{1,0:T(8,128)(2,1)S(1)}, bf16[136,1024]{1,0:T(8,128)(2,1)S(1)}, u32[]{:S(2)}, u32[]{:S(2)}) collective-permute-start(bf16[136,1024]{1,0:T(8,128)(2,1)S(1)} %get-tuple-element.40), channel_id=1, source_target_pairs={{1,2},{2,1},{3,4},{4,3},{5,6},{6,5},{7,8},{8,7},{9,10},{10,9},{11,... | collective-permute-start | bytes 835592 | tf_op jit(solution)/shard_map/ppermute | solution.py:82
  28.0 4.2 %collective-permute-start.2 = (bf16[128,1024]{1,0:T(8,128)(2,1)S(1)}, bf16[128,1024]{1,0:T(8,128)(2,1)S(1)}, u32[]{:S(2)}, u32[]{:S(2)}) collective-permute-start(bf16[128,1024]{1,0:T(8,128)(2,1)S(1)} %get-tuple-element.39), channel_id=1, source_target_pairs={{0,1},{1,0},{2,3},{3,2},{4,5},{5,4},{6,7},{7,6},{8,9},{9,8},{10,11... | collective-permute-start | bytes 786440 | tf_op jit(solution)/shard_map/ppermute | solution.py:87
  28.1 13.7 %collective-permute-start.6 = (bf16[128,1024]{1,0:T(8,128)(2,1)S(1)}, bf16[128,1024]{1,0:T(8,128)(2,1)S(1)}, u32[]{:S(2)}, u32[]{:S(2)}) collective-permute-start(bf16[128,1024]{1,0:T(8,128)(2,1)S(1)} %get-tuple-element.43.own_grad), channel_id=1, source_target_pairs={{0,1},{1,0},{2,3},{3,2},{4,5},{5,4},{6,7},{7,6},{8,9},{9,8},{10,11... | collective-permute-start | bytes 786440 | tf_op jit(solution)/shard_map/ppermute | solution.py:87
  28.6 13.2 %collective-permute-start.7 = (bf16[128,1024]{1,0:T(8,128)(2,1)S(1)}, bf16[128,1024]{1,0:T(8,128)(2,1)S(1)}, u32[]{:S(2)}, u32[]{:S(2)}) collective-permute-start(bf16[128,1024]{1,0:T(8,128)(2,1)S(1)} %get-tuple-element.43.own_grad), channel_id=1, source_target_pairs={{1,2},{2,1},{3,4},{4,3},{5,6},{6,5},{7,8},{8,7},{9,10},{10,9},{11,... | collective-permute-start | bytes 786440 | tf_op jit(solution)/shard_map/ppermute | solution.py:82
  35.6 6.2 %collective-permute-start.4 = (f32[24,256]{1,0:T(8,128)S(1)}, f32[24,256]{1,0:T(8,128)S(1)}, u32[]{:S(2)}, u32[]{:S(2)}) collective-permute-start(f32[24,256]{1,0:T(8,128)S(1)} %get-tuple-element.53), channel_id=1, source_target_pairs={{0,1},{1,0},{2,3},{3,2},{4,5},{5,4},{6,7},{7,6},{8,9},{9,8},{10,11... | collective-permute-start | bytes 73736 | tf_op jit(solution)/shard_map/ppermute | solution.py:87
  35.7 6.1 %collective-permute-start.5 = (f32[24,256]{1,0:T(8,128)S(1)}, f32[24,256]{1,0:T(8,128)S(1)}, u32[]{:S(2)}, u32[]{:S(2)}) collective-permute-start(f32[24,256]{1,0:T(8,128)S(1)} %get-tuple-element.53), channel_id=1, source_target_pairs={{1,2},{2,1},{3,4},{4,3},{5,6},{6,5},{7,8},{8,7},{9,10},{10,9},{11,... | collective-permute-start | bytes 73736 | tf_op jit(solution)/shard_map/ppermute | solution.py:82

commit v22 on v21

--- a/solution.py
+++ b/solution.py
@@ -35,15 +35,20 @@
     return lax.broadcasted_iota(I32, shape, dim)
 
 
-def call(kernel, outs, args, hbm=(), hbm_outs=(), scratch=(), name=None, flops=None):
+def call(
+    kernel, outs, args, hbm=(), hbm_outs=(), anywhere=(), scratch=(), name=None, flops=None
+):
     args = [
         pltpu.with_memory_space_constraint(a, pltpu.HBM) if i in hbm else a
         for i, a in enumerate(args)
     ]
 
-    def specs(count, far):
+    def specs(count, far, free=()):
         return [
-            pl.BlockSpec(memory_space=pltpu.HBM if i in far else pltpu.VMEM) for i in range(count)
+            pl.BlockSpec(
+                memory_space=pltpu.HBM if i in far else pl.ANY if i in free else pltpu.VMEM
+            )
+            for i in range(count)
         ]
 
     return pl.pallas_call(
@@ -52,7 +57,7 @@
             (pltpu.HBM if i in hbm_outs else jax.ShapeDtypeStruct)(shape, dtype)
             for i, (shape, dtype) in enumerate(outs)
         ],
-        in_specs=specs(len(args), hbm),
+        in_specs=specs(len(args), hbm, anywhere),
         out_specs=specs(len(outs), hbm_outs),
         scratch_shapes=list(scratch),
         compiler_params=pltpu.CompilerParams(vmem_limit_bytes=VMEM_LIMIT),
@@ -226,6 +231,7 @@
     cot_hbm,
     w_out_hbm,
     w_edge,
+    chip_message,
     partial_out,
     grad_hbm,
     grid,
@@ -342,9 +348,12 @@
     window_hbm,
     grad_hbm,
     w_qkv_hbm,
+    chip_grad,
+    off_grad,
     qkv_out,
     w_qkv,
     grad_out,
+    near_grad,
     scores_out,
     products_out,
     bias_out,
@@ -359,7 +368,8 @@
     starts = [part * channels + c * width for c in range(PIECES) for part in range(3)]
     copies = start_all(
         [(window_hbm, window), (grad_hbm, grad_out)]
-        + [(w_qkv_hbm.at[:, pl.ds(at, width)], w_qkv.at[:, pl.ds(at, width)]) for at in starts],
+        + [(w_qkv_hbm.at[:, pl.ds(at, width)], w_qkv.at[:, pl.ds(at, width)]) for at in starts]
+        + [(chip_grad, near_grad.at[pl.ds(0, m)]), (off_grad, near_grad.at[pl.ds(m, m)])],
         sems,
     )
     copies[0].wait()
@@ -397,6 +407,8 @@
                 scores_out[p] = mm_nt(halves(qkv_out[:, q], scale), qkv_out[:, k])
             if i % 3 == 2:
                 products_out[p] = mm_nt(halves(grad_out[:, q]), qkv_out[:, v])
+    for copy in copies[-2:]:
+        copy.wait()
 
 
 def attend_kernel(
@@ -536,8 +548,7 @@
     off_stats,
     bias,
     near_q,
-    chip_grad,
-    off_grad,
+    near_grad,
     own_qkv,
     grad_key,
     grad_value,
@@ -561,7 +572,7 @@
         key2 = halves(own_qkv[:, channels + p * pair : channels + (p + 1) * pair])
         value2 = halves(own_qkv[:, 2 * channels + p * pair : 2 * channels + (p + 1) * pair])
         query = near_q[:, cols]
-        grad = jnp.concatenate([chip_grad[:, cols], off_grad[:, cols]], 0)
+        grad = near_grad[:, cols]
         return query, grad, mm_nt(key2, query), mm_nt(value2, grad)
 
     total = grad_normed[...]
@@ -665,12 +676,14 @@
     partial, own_grad = call(
         own_kernel,
         [((m, channels), F32), rows],
-        [grid_in, mesh_in, own_src, own_dst, cotangent, w_out, w_edge],
+        [grid_in, mesh_in, own_src, own_dst, cotangent, w_out, w_edge, from_chip],
         hbm=range(6),
+        anywhere=(7,),
         hbm_outs=(1,),
         scratch=like(grid_in, mesh_in, own_src, own_dst, cotangent, w_out, cotangent) + [dma(7)],
         name="own",
     )
+    chip_grad, off_grad = exchange(own_grad, own_grad, "node")
     (partial,) = call(
         functools.partial(side_kernel, meta_rows),
         [((m, channels), F32)],
@@ -686,17 +699,18 @@
     )
     off_normed = swap_off(off_message, "node")
     own_block = ((pairs, 2 * m, m), F32)
-    own_qkv, w_qkv, own_grad, own_scores, own_products, bias, near_bias, normed = call(
+    own_qkv, w_qkv, own_grad, near_grad, own_scores, own_products, bias, near_bias, normed = call(
         functools.partial(project_kernel, scale, pair, meta_rows),
-        [((m, 3 * channels), BF16), (w_qkv.shape, BF16), rows, own_block, own_block]
+        [((m, 3 * channels), BF16), (w_qkv.shape, BF16), rows, ((2 * m, channels), BF16)]
+        + [own_block, own_block]
         + [((m, 3 * m), F32), ((m, 2 * m), F32), rows],
-        [normed, from_chip, from_off, window, own_grad, w_qkv],
+        [normed, from_chip, from_off, window, own_grad, w_qkv, chip_grad, off_grad],
         hbm=(3, 4, 5),
-        scratch=like(window) + [dma(3 * PIECES + 2)],
+        anywhere=(6, 7),
+        scratch=like(window) + [dma(3 * PIECES + 4)],
         name="project",
     )
     chip_normed = swap_chip(normed, "node")
-    chip_grad, off_grad = exchange(own_grad, own_grad, "node")
     probs = ((pairs, 2 * m, 3 * m), BF16)
     stats, kv, weights, grad_scores, near_q, w_out, cotangent = call(
         functools.partial(attend_kernel, scale, pair),
@@ -746,8 +760,7 @@
             off_stats,
             near_bias,
             near_q,
-            chip_grad,
-            off_grad,
+            near_grad,
             own_qkv,
             grad_key,
             grad_value,

time: 46 us -> 49.3 us (1.072); the launches traced: 45.6 us -> 48.4 us
  starting transfers between devices: 19.6 us -> 21.6 us
  waiting for transfers between devices: 1.62 us -> 2.49 us
    ppermute x4, waiting for transfers between devices: 0.01 us -> 2.47 us  [swap_off(): return lax.ppermute(rows, axis, pairs)]
    ppermute x4, starting transfers between devices: 13.5 us -> 15.9 us  [swap_off(): return lax.ppermute(rows, axis, pairs)]
    all_to_all x1, waiting for transfers between devices: 1.6 us -> 0.01 us  [body(): lax.all_to_all(far_message.reshape(devices, 2 * far_depth, far_block[1]),...]
  transfers between devices with their start and end apart: 9 -> 9, of which waited for: 1 -> 2; matrix products, arithmetic and copies ran while one was open for 0% -> 0% of each run, Pallas kernels for 35% -> 27%
where the time goes in v22:
time: 49.3 us; the launch traced here: 48.4 us
  Pallas kernels  23.6 us (48%)
  starting transfers between devices  21.6 us (44%)
  waiting for transfers between devices  2.49 us (5%)
  between operations  0.78 us (2%)
    pallas_call x8, Pallas kernels, call(): pl.pallas_call(kernel, out_shape=[(pltpu.HBM if i in hbm_outs else jax.Sh...  23.6 us
    ppermute x4, starting transfers between devices, swap_off(): return lax.ppermute(rows, axis, pairs)  15.9 us
    all_to_all x1, starting transfers between devices, body(): lax.all_to_all(far_message.reshape(devices, 2 * far_depth, far_block[1]),...  5.33 us
    ppermute x4, waiting for transfers between devices, swap_off(): return lax.ppermute(rows, axis, pairs)  2.47 us
  transfers between devices with their start and end apart: 9, of which 2 were waited for; matrix products, arithmetic and copies ran while one was open for 0% of the time, Pallas kernels for 27%

profile of v22, /device:TPU:1, one launch (start us, length us, event | category | flops | bytes accessed | tf_op | source)
XLA Modules:
  0.0 48.4 jit_solution(8464062393363130601)
XLA Ops:
  0.6 3.4 %pack.1 = (bf16[128,640]{1,0:T(8,128)(2,1)}, bf16[144,1024]{1,0:T(8,128)(2,1)}, bf16[144,1024]{1,0:T(8,128)(2,1)}, bf16[1024,1024]{1,0:T(8,128)(2,1)S(1)}) custom-call(bf16[512,1024]{1,0:T(8,128)(2,1)} %grid_hbm.3, s32[2,128]{1,0:T(2,128)} %window_hbm.3, s32[32,128]{1,0:T(8,128)} %bitcast.12, s32[32,128]{1,0:T(8,128)} %bitcast.13, s32[1,2]{1,0:T(1,128)} %bitcast.16, ...), custom_call_target="tpu_custom_call" | custom-call | tf_op jit(solution)/shard_map/pack/pallas_call | solution.py:54
  4.0 0.1 collective-permute-start
  4.1 4.5 %collective-permute-start.1 = (bf16[144,1024]{1,0:T(8,128)(2,1)}, bf16[144,1024]{1,0:T(8,128)(2,1)S(1)}, u32[]{:S(2)}, u32[]{:S(2)}) collective-permute-start(bf16[144,1024]{1,0:T(8,128)(2,1)} %get-tuple-element.35), channel_id=1, source_target_pairs={{1,2},{2,1},{3,4},{4,3},{5,6},{6,5},{7,8},{8,7},{9,10},{10,9},{11,... | collective-permute-start | bytes 884744 | tf_op jit(solution)/shard_map/ppermute | solution.py:87
  8.6 5.3 %all-to-all-start = ((bf16[16,8,640]{2,1,0:T(8,128)(2,1)}), bf16[16,8,640]{2,1,0:T(8,128)(2,1)S(1)}, u32[]{:S(2)}, u32[]{:S(2)}) async-start(bf16[16,8,640]{2,1,0:T(8,128)(2,1)} %bitcast.11), calls=%async_computation | async-start | bytes 327680 | tf_op jit(solution)/shard_map/all_to_all | solution.py:667
  13.9 0.0 collective-permute-done.chip_message.chip.chip_first
  14.0 4.3 %own.1 = (f32[128,1024]{1,0:T(8,128)S(1)}, bf16[128,1024]{1,0:T(8,128)(2,1)}) custom-call(bf16[512,1024]{1,0:T(8,128)(2,1)} %grid_hbm.3, bf16[128,1024]{1,0:T(8,128)(2,1)} %mesh_in_hbm.1, s32[8,128]{1,0:T(8,128)} %bitcast.14, s32[8,128]{1,0:T(8,128)} %bitcast.15, bf16[128,1024]{1,0:T(8,128)(2,1)} %cot_hbm.3, bf16[1024,1024]{1,0:T(8,128)(2,1)} %w_out_hbm.3, ...), custom_call_target="tpu_custom_call" | custom-call | tf_op jit(solution)/shard_map/own/pallas_call | solution.py:54
  18.3 3.5 %collective-permute-start.3 = (bf16[128,1024]{1,0:T(8,128)(2,1)}, bf16[128,1024]{1,0:T(8,128)(2,1)}, u32[]{:S(2)}, u32[]{:S(2)}) collective-permute-start(bf16[128,1024]{1,0:T(8,128)(2,1)} %get-tuple-element.39.grad_hbm), channel_id=1, source_target_pairs={{1,2},{2,1},{3,4},{4,3},{5,6},{6,5},{7,8},{8,7},{9,10},{10,9},{11,... | collective-permute-start | bytes 786440 | tf_op jit(solution)/shard_map/ppermute | solution.py:87
  21.8 0.1 collective-permute-start.2
  21.9 0.0 collective-permute-done.1.off.off_first
  21.9 1.4 %side.1.partial = f32[128,1024]{1,0:T(8,128)S(1)} custom-call(bf16[144,1024]{1,0:T(8,128)(2,1)S(1)} %collective-permute-done.chip_message.chip.chip_first, bf16[144,1024]{1,0:T(8,128)(2,1)S(1)} %collective-permute-done.1.off.off_first, bf16[1024,1024]{1,0:T(8,128)(2,1)S(1)} %get-tuple-element.36.w_edge, f32[128,1024]{1,0:T(8,128)S(1)} %get-tuple-element.37.partial), custom_call_target="tpu_custom_call" | custom-call | flops 8000000000 | tf_op jit(solution)/shard_map/side/pallas_call | solution.py:54
  23.4 0.0 all-to-all-done
  23.4 0.5 %latent.1 = (bf16[128,1024]{1,0:T(8,128)(2,1)S(1)}, bf16[128,1024]{1,0:T(8,128)(2,1)S(1)}, bf16[136,1024]{1,0:T(8,128)(2,1)S(1)}, f32[128,1024]{1,0:T(8,128)S(1)}, f32[128,128]{1,0:T(8,128)S(1)}) custom-call(bf16[128,640]{1,0:T(8,128)(2,1)S(1)} %bitcast.10, f32[128,1024]{1,0:T(8,128)S(1)} %side.1.partial), custom_call_target="tpu_custom_call" | custom-call | tf_op jit(solution)/shard_map/latent/pallas_call | solution.py:54
  23.9 3.5 %collective-permute-start.5 = (bf16[136,1024]{1,0:T(8,128)(2,1)S(1)}, bf16[136,1024]{1,0:T(8,128)(2,1)S(1)}, u32[]{:S(2)}, u32[]{:S(2)}) collective-permute-start(bf16[136,1024]{1,0:T(8,128)(2,1)S(1)} %get-tuple-element.41), channel_id=1, source_target_pairs={{1,2},{2,1},{3,4},{4,3},{5,6},{6,5},{7,8},{8,7},{9,10},{10,9},{11,... | collective-permute-start | bytes 835592 | tf_op jit(solution)/shard_map/ppermute | solution.py:87
  27.4 0.9 %collective-permute-done.3.off_grad = bf16[128,1024]{1,0:T(8,128)(2,1)} collective-permute-done((bf16[128,1024]{1,0:T(8,128)(2,1)}, bf16[128,1024]{1,0:T(8,128)(2,1)}, u32[]{:S(2)}, u32[]{:S(2)}) %collective-permute-start.3) | collective-permute-done | bytes 262176 | tf_op jit(solution)/shard_map/ppermute | solution.py:87
  28.3 0.0 collective-permute-done.2.chip_grad
  28.3 4.2 %project.1 = (bf16[128,3072]{1,0:T(8,128)(2,1)S(1)}, bf16[1024,3072]{1,0:T(8,128)(2,1)S(1)}, bf16[128,1024]{1,0:T(8,128)(2,1)S(1)}, bf16[256,1024]{1,0:T(8,128)(...) custom-call(bf16[128,1024]{1,0:T(8,128)(2,1)S(1)} %get-tuple-element, ...), custom_call_target="tpu_custom_call" | custom-call | tf_op jit(solution)/shard_map/project/pallas_call | solution.py:54
  32.5 0.1 collective-permute-start.4
  32.6 1.6 %collective-permute-done.5.off_normed = bf16[136,1024]{1,0:T(8,128)(2,1)S(1)} collective-permute-done((bf16[136,1024]{1,0:T(8,128)(2,1)S(1)}, bf16[136,1024]{1,0:T(8,128)(2,1)S(1)}, u32[]{:S(2)}, u32[]{:S(2)}) %collective-permute-start.5) | collective-permute-done | bytes 278560 | tf_op jit(solution)/shard_map/ppermute | solution.py:87
  34.1 0.0 collective-permute-done.4.chip_normed
  34.1 3.4 %attend.1 = (f32[24,256]{1,0:T(8,128)S(1)}, bf16[384,2048]{1,0:T(8,128)(2,1)S(1)}, bf16[8,256,384]{2,1,0:T(8,128)(2,1)S(1)}, bf16[8,256,384]{2,1,0:T(8,128)(2,1)...) custom-call(bf16[128,1024]{1,0:T(8,128)(2,1)S(1)} %collective-permute-done.4.chip, ...), custom_call_target="tpu_custom_call" | custom-call | tf_op jit(solution)/shard_map/attend/pallas_call | solution.py:54
  37.5 4.4 %collective-permute-start.7 = (f32[24,256]{1,0:T(8,128)S(1)}, f32[24,256]{1,0:T(8,128)S(1)}, u32[]{:S(2)}, u32[]{:S(2)}) collective-permute-start(f32[24,256]{1,0:T(8,128)S(1)} %get-tuple-element.54), channel_id=1, source_target_pairs={{1,2},{2,1},{3,4},{4,3},{5,6},{6,5},{7,8},{8,7},{9,10},{10,9},{11,... | collective-permute-start | bytes 73736 | tf_op jit(solution)/shard_map/ppermute | solution.py:87
  41.9 0.1 collective-permute-start.6
  42.0 2.6 %product.1 = (bf16[128,1024]{1,0:T(8,128)(2,1)}, f32[128,1024]{1,0:T(8,128)S(1)}, f32[128,1024]{1,0:T(8,128)S(1)}, f32[128,1024]{1,0:T(8,128)S(1)}) custom-call(bf16[8,256,384]{2,1,0:T(8,128)(2,1)S(1)} %get-tuple-element.48.weights, bf16[8,256,384]{2,1,0:T(8,128)(2,1)S(1)} %get-tuple-element.49.grad_scores, bf16[384,2048]{1,0:T(8,128)(2,1)S(1)} %get-tuple-element.50.kv, ...), custom_call_target="tpu_custom_call" | custom-call | tf_op jit(solution)/shard_map/product/pallas_call | solution.py:54
  44.6 0.0 collective-permute-done.7.off_stats
  44.6 0.0 collective-permute-done.6.chip_stats
  44.6 3.8 %finish.1 = bf16[128,1024]{1,0:T(8,128)(2,1)} custom-call(f32[24,256]{1,0:T(8,128)S(1)} %collective-permute-done.6.chip_stats, f32[24,256]{1,0:T(8,128)S(1)} %collective-permute-done.7.off_stats, f32[128,256]{1,0:T(8,128)S(1)} %get-tuple-element.55.bias, bf16[256,1024]{1,0:T(8,128)(2,1)S(1)} %get-tuple-element.56.near_q, ...), custom_call_target="tpu_custom_call" | custom-call | tf_op jit(solution)/shard_map/finish/pallas_call | solution.py:54
Async XLA Ops:
  4.0 10.0 %collective-permute-start = (bf16[144,1024]{1,0:T(8,128)(2,1)}, bf16[144,1024]{1,0:T(8,128)(2,1)S(1)}, u32[]{:S(2)}, u32[]{:S(2)}) collective-permute-start(bf16[144,1024]{1,0:T(8,128)(2,1)} %get-tuple-element.34), channel_id=1, source_target_pairs={{0,1},{1,0},{2,3},{3,2},{4,5},{5,4},{6,7},{7,6},{8,9},{9,8},{10,11... | collective-permute-start | bytes 884744 | tf_op jit(solution)/shard_map/ppermute | solution.py:92
  4.1 17.8 %collective-permute-start.1 = (bf16[144,1024]{1,0:T(8,128)(2,1)}, bf16[144,1024]{1,0:T(8,128)(2,1)S(1)}, u32[]{:S(2)}, u32[]{:S(2)}) collective-permute-start(bf16[144,1024]{1,0:T(8,128)(2,1)} %get-tuple-element.35), channel_id=1, source_target_pairs={{1,2},{2,1},{3,4},{4,3},{5,6},{6,5},{7,8},{8,7},{9,10},{10,9},{11,... | collective-permute-start | bytes 884744 | tf_op jit(solution)/shard_map/ppermute | solution.py:87
  8.6 14.8 %all-to-all-start = ((bf16[16,8,640]{2,1,0:T(8,128)(2,1)}), bf16[16,8,640]{2,1,0:T(8,128)(2,1)S(1)}, u32[]{:S(2)}, u32[]{:S(2)}) async-start(bf16[16,8,640]{2,1,0:T(8,128)(2,1)} %bitcast.11), calls=%async_computation | async-start | bytes 327680 | tf_op jit(solution)/shard_map/all_to_all | solution.py:667
  18.3 10.0 %collective-permute-start.3 = (bf16[128,1024]{1,0:T(8,128)(2,1)}, bf16[128,1024]{1,0:T(8,128)(2,1)}, u32[]{:S(2)}, u32[]{:S(2)}) collective-permute-start(bf16[128,1024]{1,0:T(8,128)(2,1)} %get-tuple-element.39.grad_hbm), channel_id=1, source_target_pairs={{1,2},{2,1},{3,4},{4,3},{5,6},{6,5},{7,8},{8,7},{9,10},{10,9},{11,... | collective-permute-start | bytes 786440 | tf_op jit(solution)/shard_map/ppermute | solution.py:87
  21.8 6.4 %collective-permute-start.2 = (bf16[128,1024]{1,0:T(8,128)(2,1)}, bf16[128,1024]{1,0:T(8,128)(2,1)}, u32[]{:S(2)}, u32[]{:S(2)}) collective-permute-start(bf16[128,1024]{1,0:T(8,128)(2,1)} %get-tuple-element.39.grad_hbm), channel_id=1, source_target_pairs={{0,1},{1,0},{2,3},{3,2},{4,5},{5,4},{6,7},{7,6},{8,9},{9,8},{10,11... | collective-permute-start | bytes 786440 | tf_op jit(solution)/shard_map/ppermute | solution.py:92
  23.9 10.2 %collective-permute-start.5 = (bf16[136,1024]{1,0:T(8,128)(2,1)S(1)}, bf16[136,1024]{1,0:T(8,128)(2,1)S(1)}, u32[]{:S(2)}, u32[]{:S(2)}) collective-permute-start(bf16[136,1024]{1,0:T(8,128)(2,1)S(1)} %get-tuple-element.41), channel_id=1, source_target_pairs={{1,2},{2,1},{3,4},{4,3},{5,6},{6,5},{7,8},{8,7},{9,10},{10,9},{11,... | collective-permute-start | bytes 835592 | tf_op jit(solution)/shard_map/ppermute | solution.py:87
  32.5 1.6 %collective-permute-start.4 = (bf16[128,1024]{1,0:T(8,128)(2,1)S(1)}, bf16[128,1024]{1,0:T(8,128)(2,1)S(1)}, u32[]{:S(2)}, u32[]{:S(2)}) collective-permute-start(bf16[128,1024]{1,0:T(8,128)(2,1)S(1)} %get-tuple-element.40), channel_id=1, source_target_pairs={{0,1},{1,0},{2,3},{3,2},{4,5},{5,4},{6,7},{7,6},{8,9},{9,8},{10,11... | collective-permute-start | bytes 786440 | tf_op jit(solution)/shard_map/ppermute | solution.py:92
  37.5 7.1 %collective-permute-start.7 = (f32[24,256]{1,0:T(8,128)S(1)}, f32[24,256]{1,0:T(8,128)S(1)}, u32[]{:S(2)}, u32[]{:S(2)}) collective-permute-start(f32[24,256]{1,0:T(8,128)S(1)} %get-tuple-element.54), channel_id=1, source_target_pairs={{1,2},{2,1},{3,4},{4,3},{5,6},{6,5},{7,8},{8,7},{9,10},{10,9},{11,... | collective-permute-start | bytes 73736 | tf_op jit(solution)/shard_map/ppermute | solution.py:87
  41.9 2.7 %collective-permute-start.6 = (f32[24,256]{1,0:T(8,128)S(1)}, f32[24,256]{1,0:T(8,128)S(1)}, u32[]{:S(2)}, u32[]{:S(2)}) collective-permute-start(f32[24,256]{1,0:T(8,128)S(1)} %get-tuple-element.54), channel_id=1, source_target_pairs={{0,1},{1,0},{2,3},{3,2},{4,5},{5,4},{6,7},{7,6},{8,9},{9,8},{10,11... | collective-permute-start | bytes 73736 | tf_op jit(solution)/shard_map/ppermute | solution.py:92

commit v23 on v21

--- a/solution.py
+++ b/solution.py
@@ -132,11 +132,9 @@
     far_src_hbm,
     far_dst_hbm,
     far_count_hbm,
-    w_edge_hbm,
     far_out,
     chip_out,
     off_out,
-    w_edge,
     grid,
     window,
     side_src,
@@ -167,7 +165,6 @@
             (far_src_hbm, far_src),
             (far_dst_hbm, far_dst),
             (far_count_hbm, far_count),
-            (w_edge_hbm, w_edge),
         ],
         sems,
     )
@@ -206,8 +203,6 @@
     column = jnp.sum(jnp.where(mine, target, 0.0), 1, keepdims=True)
     pick = jnp.where(iota((2 * slots, grid_rows), 1).astype(F32) == source, 1.0, 0.0).astype(BF16)
     rows = mm(pick, grid[...]).astype(BF16)
-    copies[8].wait()
-    rows = gelu(mm(rows, w_edge[...]))
     half = channels // 2
     is_first = iota((2 * slots, half), 0) % (2 * depth) < depth
     far[:, :half] = jnp.where(is_first, rows[:, :half], rows[:, half:])
@@ -225,9 +220,10 @@
     own_dst_hbm,
     cot_hbm,
     w_out_hbm,
-    w_edge,
+    w_edge_hbm,
     partial_out,
     grad_hbm,
+    w_edge,
     grid,
     mesh_in,
     own_src,
@@ -246,6 +242,7 @@
             (cot_hbm, cot),
             (w_out_hbm, w_out),
             (grid_hbm, grid),
+            (w_edge_hbm, w_edge),
             (mesh_in_hbm, mesh_in),
         ],
         sems,
@@ -259,7 +256,7 @@
     for copy in copies[2:4]:
         copy.wait()
     grad[...] = mm_nt(cot[...], w_out[...]).astype(BF16)
-    out = pltpu.make_async_copy(grad, grad_hbm, sems.at[6])
+    out = pltpu.make_async_copy(grad, grad_hbm, sems.at[7])
     out.start()
     for copy in copies[4:]:
         copy.wait()
@@ -289,7 +286,7 @@
 
 
 def latent_kernel(
-    depth, far, partial, latent_out, normed_out, off_out, normal_out, inv_std_out
+    depth, far, w_edge, partial, latent_out, normed_out, off_out, normal_out, inv_std_out
 ):
     mesh_rows, channels = partial.shape
     slots = far.shape[0]
@@ -302,7 +299,8 @@
     is_row = iota((mesh_rows, slots), 1) % (2 * depth) < depth
     hit = (target == iota((mesh_rows, slots), 0).astype(F32)) & is_row
     landing = jnp.where(hit, 1.0, 0.0).astype(BF16)
-    total = partial[...] + mm(landing, jnp.concatenate([first, second], 1))
+    active = gelu(mm(jnp.concatenate([first, second], 1), w_edge[...]))
+    total = partial[...] + mm(landing, active)
     latent = total.astype(BF16)
     latent_out[...] = latent
     normal, inv_std = norm_stats(latent)
@@ -637,17 +635,17 @@
     side_count, far_count = side_count.reshape(1, -1), far_count.reshape(1, -1)
     message = ((BAND + meta_rows, channels), BF16)
     far_block = (2 * far_slots, channels // 2 + LANES)
-    far_message, chip_message, off_message, w_edge = call(
+    far_message, chip_message, off_message = call(
         pack_kernel,
-        [(far_block, BF16), message, message, (w_edge.shape, BF16)],
-        [grid_in, window, side_src, side_dst, side_count, far_src, far_dst, far_count, w_edge],
-        hbm=range(9),
+        [(far_block, BF16), message, message],
+        [grid_in, window, side_src, side_dst, side_count, far_src, far_dst, far_count],
+        hbm=range(8),
         hbm_outs=range(3),
         scratch=like(grid_in, window, side_src, side_dst, side_count, far_src, far_dst, far_count)
         + [
             pltpu.VMEM(far_block, BF16),
             pltpu.VMEM((2, meta_rows, channels), BF16),
-            dma(9),
+            dma(8),
             dma(5),
         ],
         name="pack",
@@ -662,13 +660,13 @@
     ).reshape(far_block)
 
     rows = ((m, channels), BF16)
-    partial, own_grad = call(
+    partial, own_grad, w_edge = call(
         own_kernel,
-        [((m, channels), F32), rows],
+        [((m, channels), F32), rows, (w_edge.shape, BF16)],
         [grid_in, mesh_in, own_src, own_dst, cotangent, w_out, w_edge],
-        hbm=range(6),
+        hbm=range(7),
         hbm_outs=(1,),
-        scratch=like(grid_in, mesh_in, own_src, own_dst, cotangent, w_out, cotangent) + [dma(7)],
+        scratch=like(grid_in, mesh_in, own_src, own_dst, cotangent, w_out, cotangent) + [dma(8)],
         name="own",
     )
     (partial,) = call(
@@ -681,7 +679,7 @@
     latent, normed, off_message, normal, inv_std = call(
         functools.partial(latent_kernel, far_depth),
         [rows, rows, ((m + PAD, channels), BF16), ((m, channels), F32), ((m, LANES), F32)],
-        [got_far, partial],
+        [got_far, w_edge, partial],
         name="latent",
     )
     off_normed = swap_off(off_message, "node")

time: 46 us -> 45.6 us (level)
  transfers between devices with their start and end apart: 9 -> 9, of which waited for: 1 -> 1; matrix products, arithmetic and copies ran while one was open for 0% -> 0% of each run, Pallas kernels for 35% -> 36%
where the time goes in v23:
time: 45.6 us; the launch traced here: 45.2 us
  Pallas kernels  23.3 us (51%)
  starting transfers between devices  19.6 us (43%)
  waiting for transfers between devices  1.48 us (3%)
  between operations  0.8 us (2%)
    pallas_call x8, Pallas kernels, call(): pl.pallas_call(kernel, out_shape=[(pltpu.HBM if i in hbm_outs else jax.Sh...  23.3 us
    ppermute x4, starting transfers between devices, swap_off(): return lax.ppermute(rows, axis, pairs)  13.5 us
    all_to_all x1, starting transfers between devices, body(): lax.all_to_all(far_message.reshape(devices, 2 * far_depth, far_block[1]),...  5.33 us
    all_to_all x1, waiting for transfers between devices, body(): lax.all_to_all(far_message.reshape(devices, 2 * far_depth, far_block[1]),...  1.46 us
  transfers between devices with their start and end apart: 9, of which 1 were waited for; matrix products, arithmetic and copies ran while one was open for 0% of the time, Pallas kernels for 36%

profile of v23, /device:TPU:1, one launch (start us, length us, event | category | flops | bytes accessed | tf_op | source)
XLA Modules:
  0.0 45.2 jit_solution(17755354225676666561)
XLA Ops:
  0.6 2.4 %pack.1 = (bf16[128,640]{1,0:T(8,128)(2,1)}, bf16[144,1024]{1,0:T(8,128)(2,1)}, bf16[144,1024]{1,0:T(8,128)(2,1)}) custom-call(bf16[512,1024]{1,0:T(8,128)(2,1)} %grid_hbm.3, s32[2,128]{1,0:T(2,128)} %window_hbm.3, s32[32,128]{1,0:T(8,128)} %bitcast.12, s32[32,128]{1,0:T(8,128)} %bitcast.13, s32[1,2]{1,0:T(1,128)} %bitcast.16, s32[1,64]{1,0:T(1,128)} %bitcast.17, ...), custom_call_target="tpu_custom_call" | custom-call | tf_op jit(solution)/shard_map/pack/pallas_call | solution.py:49
  3.1 0.1 collective-permute-start
  3.2 4.5 %collective-permute-start.1 = (bf16[144,1024]{1,0:T(8,128)(2,1)}, bf16[144,1024]{1,0:T(8,128)(2,1)S(1)}, u32[]{:S(2)}, u32[]{:S(2)}) collective-permute-start(bf16[144,1024]{1,0:T(8,128)(2,1)} %get-tuple-element.35), channel_id=1, source_target_pairs={{1,2},{2,1},{3,4},{4,3},{5,6},{6,5},{7,8},{8,7},{9,10},{10,9},{11,... | collective-permute-start | bytes 884744 | tf_op jit(solution)/shard_map/ppermute | solution.py:82
  7.7 5.3 %all-to-all-start = ((bf16[16,8,640]{2,1,0:T(8,128)(2,1)}), bf16[16,8,640]{2,1,0:T(8,128)(2,1)S(1)}, u32[]{:S(2)}, u32[]{:S(2)}) async-start(bf16[16,8,640]{2,1,0:T(8,128)(2,1)} %bitcast.11), calls=%async_computation | async-start | bytes 327680 | tf_op jit(solution)/shard_map/all_to_all | solution.py:654
  13.0 4.5 %own.1 = (f32[128,1024]{1,0:T(8,128)S(1)}, bf16[128,1024]{1,0:T(8,128)(2,1)}, bf16[1024,1024]{1,0:T(8,128)(2,1)S(1)}) custom-call(bf16[512,1024]{1,0:T(8,128)(2,1)} %grid_hbm.3, bf16[128,1024]{1,0:T(8,128)(2,1)} %mesh_in_hbm.1, s32[8,128]{1,0:T(8,128)} %bitcast.14, s32[8,128]{1,0:T(8,128)} %bitcast.15, bf16[128,1024]{1,0:T(8,128)(2,1)} %cot_hbm.3, ...), custom_call_target="tpu_custom_call" | custom-call | tf_op jit(solution)/shard_map/own/pallas_call | solution.py:49
  17.5 0.0 collective-permute-done.chip.chip_first
  17.5 0.0 collective-permute-done.1.off.off_first
  17.5 1.4 %side.1.partial = f32[128,1024]{1,0:T(8,128)S(1)} custom-call(bf16[144,1024]{1,0:T(8,128)(2,1)S(1)} %collective-permute-done.chip.chip_first, bf16[144,1024]{1,0:T(8,128)(2,1)S(1)} %collective-permute-done.1.off.off_first, bf16[1024,1024]{1,0:T(8,128)(2,1)S(1)} %get-tuple-element.33.w_edge, f32[128,1024]{1,0:T(8,128)S(1)} %get-tuple-element.36.partial), custom_call_target="tpu_custom_call" | custom-call | flops 8000000000 | tf_op jit(solution)/shard_map/side/pallas_call | solution.py:49
  19.0 1.5 %all-to-all-done = bf16[16,8,640]{2,1,0:T(8,128)(2,1)S(1)} async-done(((bf16[16,8,640]{2,1,0:T(8,128)(2,1)}), bf16[16,8,640]{2,1,0:T(8,128)(2,1)S(1)}, u32[]{:S(2)}, u32[]{:S(2)}) %all-to-all-start) | async-done | bytes 163872 | tf_op jit(solution)/shard_map/all_to_all | solution.py:654
  20.4 0.9 %latent.1 = (bf16[128,1024]{1,0:T(8,128)(2,1)S(1)}, bf16[128,1024]{1,0:T(8,128)(2,1)S(1)}, bf16[136,1024]{1,0:T(8,128)(2,1)S(1)}, f32[128,1024]{1,0:T(8,128)S(1)}, f32[128,128]{1,0:T(8,128)S(1)}) custom-call(bf16[128,640]{1,0:T(8,128)(2,1)S(1)} %bitcast.10, bf16[1024,1024]{1,0:T(8,128)(2,1)S(1)} %get-tuple-element.33.w_edge, f32[128,1024]{1,0:T(8,128)S(1)} %side.1.partial), custom_call_target="tpu_custom_call" | custom-call | tf_op jit(solution)/shard_map/latent/pallas_call | solution.py:49
  21.4 2.1 %collective-permute-start.3 = (bf16[136,1024]{1,0:T(8,128)(2,1)S(1)}, bf16[136,1024]{1,0:T(8,128)(2,1)S(1)}, u32[]{:S(2)}, u32[]{:S(2)}) collective-permute-start(bf16[136,1024]{1,0:T(8,128)(2,1)S(1)} %get-tuple-element.40), channel_id=1, source_target_pairs={{1,2},{2,1},{3,4},{4,3},{5,6},{6,5},{7,8},{8,7},{9,10},{10,9},{11,... | collective-permute-start | bytes 835592 | tf_op jit(solution)/shard_map/ppermute | solution.py:82
  23.5 4.2 %project.1 = (bf16[128,3072]{1,0:T(8,128)(2,1)S(1)}, bf16[1024,3072]{1,0:T(8,128)(2,1)S(1)}, bf16[128,1024]{1,0:T(8,128)(2,1)S(1)}, f32[8,256,128]{2,1,0:T(8,128...) custom-call(bf16[128,1024]{1,0:T(8,128)(2,1)S(1)} %get-tuple-element, ...), custom_call_target="tpu_custom_call" | custom-call | tf_op jit(solution)/shard_map/project/pallas_call | solution.py:49
  27.7 0.1 collective-permute-start.2
  27.8 0.5 %collective-permute-start.6 = (bf16[128,1024]{1,0:T(8,128)(2,1)S(1)}, bf16[128,1024]{1,0:T(8,128)(2,1)S(1)}, u32[]{:S(2)}, u32[]{:S(2)}) collective-permute-start(bf16[128,1024]{1,0:T(8,128)(2,1)S(1)} %get-tuple-element.43.own_grad), channel_id=1, source_target_pairs={{0,1},{1,0},{2,3},{3,2},{4,5},{5,4},{6,7},{7,6},{8,9},{9,8},{10,11... | collective-permute-start | bytes 786440 | tf_op jit(solution)/shard_map/ppermute | solution.py:87
  28.3 3.5 %collective-permute-start.7 = (bf16[128,1024]{1,0:T(8,128)(2,1)S(1)}, bf16[128,1024]{1,0:T(8,128)(2,1)S(1)}, u32[]{:S(2)}, u32[]{:S(2)}) collective-permute-start(bf16[128,1024]{1,0:T(8,128)(2,1)S(1)} %get-tuple-element.43.own_grad), channel_id=1, source_target_pairs={{1,2},{2,1},{3,4},{4,3},{5,6},{6,5},{7,8},{8,7},{9,10},{10,9},{11,... | collective-permute-start | bytes 786440 | tf_op jit(solution)/shard_map/ppermute | solution.py:82
  31.7 0.0 collective-permute-done.2.chip_normed
  31.7 0.0 collective-permute-done.3.off_normed
  31.8 3.4 %attend.1 = (f32[24,256]{1,0:T(8,128)S(1)}, bf16[384,2048]{1,0:T(8,128)(2,1)S(1)}, bf16[8,256,384]{2,1,0:T(8,128)(2,1)S(1)}, bf16[8,256,384]{2,1,0:T(8,128)(2,1)...) custom-call(bf16[128,1024]{1,0:T(8,128)(2,1)S(1)} %collective-permute-done.2.chip, ...), custom_call_target="tpu_custom_call" | custom-call | tf_op jit(solution)/shard_map/attend/pallas_call | solution.py:49
  35.2 0.1 collective-permute-start.4
  35.2 3.5 %collective-permute-start.5 = (f32[24,256]{1,0:T(8,128)S(1)}, f32[24,256]{1,0:T(8,128)S(1)}, u32[]{:S(2)}, u32[]{:S(2)}) collective-permute-start(f32[24,256]{1,0:T(8,128)S(1)} %get-tuple-element.53), channel_id=1, source_target_pairs={{1,2},{2,1},{3,4},{4,3},{5,6},{6,5},{7,8},{8,7},{9,10},{10,9},{11,... | collective-permute-start | bytes 73736 | tf_op jit(solution)/shard_map/ppermute | solution.py:82
  38.7 2.6 %product.1 = (bf16[128,1024]{1,0:T(8,128)(2,1)}, f32[128,1024]{1,0:T(8,128)S(1)}, f32[128,1024]{1,0:T(8,128)S(1)}, f32[128,1024]{1,0:T(8,128)S(1)}) custom-call(bf16[8,256,384]{2,1,0:T(8,128)(2,1)S(1)} %get-tuple-element.47.weights, bf16[8,256,384]{2,1,0:T(8,128)(2,1)S(1)} %get-tuple-element.48.grad_scores, bf16[384,2048]{1,0:T(8,128)(2,1)S(1)} %get-tuple-element.49.kv, ...), custom_call_target="tpu_custom_call" | custom-call | tf_op jit(solution)/shard_map/product/pallas_call | solution.py:49
  41.3 0.0 collective-permute-done.6.chip_grad
  41.4 0.0 collective-permute-done.7.off_grad
  41.4 0.0 collective-permute-done.4.chip_stats
  41.4 0.0 collective-permute-done.5.off_stats
  41.4 3.8 %finish.1 = bf16[128,1024]{1,0:T(8,128)(2,1)} custom-call(f32[24,256]{1,0:T(8,128)S(1)} %collective-permute-done.4.chip_stats, f32[24,256]{1,0:T(8,128)S(1)} %collective-permute-done.5.off_stats, f32[128,256]{1,0:T(8,128)S(1)} %get-tuple-element.54.bias, bf16[256,1024]{1,0:T(8,128)(2,1)S(1)} %get-tuple-element.55.near_q, ...), custom_call_target="tpu_custom_call" | custom-call | tf_op jit(solution)/shard_map/finish/pallas_call | solution.py:49
Async XLA Ops:
  3.1 14.4 %collective-permute-start = (bf16[144,1024]{1,0:T(8,128)(2,1)}, bf16[144,1024]{1,0:T(8,128)(2,1)S(1)}, u32[]{:S(2)}, u32[]{:S(2)}) collective-permute-start(bf16[144,1024]{1,0:T(8,128)(2,1)} %get-tuple-element.34), channel_id=1, source_target_pairs={{0,1},{1,0},{2,3},{3,2},{4,5},{5,4},{6,7},{7,6},{8,9},{9,8},{10,11... | collective-permute-start | bytes 884744 | tf_op jit(solution)/shard_map/ppermute | solution.py:87
  3.2 14.3 %collective-permute-start.1 = (bf16[144,1024]{1,0:T(8,128)(2,1)}, bf16[144,1024]{1,0:T(8,128)(2,1)S(1)}, u32[]{:S(2)}, u32[]{:S(2)}) collective-permute-start(bf16[144,1024]{1,0:T(8,128)(2,1)} %get-tuple-element.35), channel_id=1, source_target_pairs={{1,2},{2,1},{3,4},{4,3},{5,6},{6,5},{7,8},{8,7},{9,10},{10,9},{11,... | collective-permute-start | bytes 884744 | tf_op jit(solution)/shard_map/ppermute | solution.py:82
  7.7 12.7 %all-to-all-start = ((bf16[16,8,640]{2,1,0:T(8,128)(2,1)}), bf16[16,8,640]{2,1,0:T(8,128)(2,1)S(1)}, u32[]{:S(2)}, u32[]{:S(2)}) async-start(bf16[16,8,640]{2,1,0:T(8,128)(2,1)} %bitcast.11), calls=%async_computation | async-start | bytes 327680 | tf_op jit(solution)/shard_map/all_to_all | solution.py:654
  21.4 10.4 %collective-permute-start.3 = (bf16[136,1024]{1,0:T(8,128)(2,1)S(1)}, bf16[136,1024]{1,0:T(8,128)(2,1)S(1)}, u32[]{:S(2)}, u32[]{:S(2)}) collective-permute-start(bf16[136,1024]{1,0:T(8,128)(2,1)S(1)} %get-tuple-element.40), channel_id=1, source_target_pairs={{1,2},{2,1},{3,4},{4,3},{5,6},{6,5},{7,8},{8,7},{9,10},{10,9},{11,... | collective-permute-start | bytes 835592 | tf_op jit(solution)/shard_map/ppermute | solution.py:82
  27.7 4.0 %collective-permute-start.2 = (bf16[128,1024]{1,0:T(8,128)(2,1)S(1)}, bf16[128,1024]{1,0:T(8,128)(2,1)S(1)}, u32[]{:S(2)}, u32[]{:S(2)}) collective-permute-start(bf16[128,1024]{1,0:T(8,128)(2,1)S(1)} %get-tuple-element.39), channel_id=1, source_target_pairs={{0,1},{1,0},{2,3},{3,2},{4,5},{5,4},{6,7},{7,6},{8,9},{9,8},{10,11... | collective-permute-start | bytes 786440 | tf_op jit(solution)/shard_map/ppermute | solution.py:87
  27.8 13.6 %collective-permute-start.6 = (bf16[128,1024]{1,0:T(8,128)(2,1)S(1)}, bf16[128,1024]{1,0:T(8,128)(2,1)S(1)}, u32[]{:S(2)}, u32[]{:S(2)}) collective-permute-start(bf16[128,1024]{1,0:T(8,128)(2,1)S(1)} %get-tuple-element.43.own_grad), channel_id=1, source_target_pairs={{0,1},{1,0},{2,3},{3,2},{4,5},{5,4},{6,7},{7,6},{8,9},{9,8},{10,11... | collective-permute-start | bytes 786440 | tf_op jit(solution)/shard_map/ppermute | solution.py:87
  28.3 13.1 %collective-permute-start.7 = (bf16[128,1024]{1,0:T(8,128)(2,1)S(1)}, bf16[128,1024]{1,0:T(8,128)(2,1)S(1)}, u32[]{:S(2)}, u32[]{:S(2)}) collective-permute-start(bf16[128,1024]{1,0:T(8,128)(2,1)S(1)} %get-tuple-element.43.own_grad), channel_id=1, source_target_pairs={{1,2},{2,1},{3,4},{4,3},{5,6},{6,5},{7,8},{8,7},{9,10},{10,9},{11,... | collective-permute-start | bytes 786440 | tf_op jit(solution)/shard_map/ppermute | solution.py:82
  35.2 6.2 %collective-permute-start.4 = (f32[24,256]{1,0:T(8,128)S(1)}, f32[24,256]{1,0:T(8,128)S(1)}, u32[]{:S(2)}, u32[]{:S(2)}) collective-permute-start(f32[24,256]{1,0:T(8,128)S(1)} %get-tuple-element.53), channel_id=1, source_target_pairs={{0,1},{1,0},{2,3},{3,2},{4,5},{5,4},{6,7},{7,6},{8,9},{9,8},{10,11... | collective-permute-start | bytes 73736 | tf_op jit(solution)/shard_map/ppermute | solution.py:87
  35.2 6.1 %collective-permute-start.5 = (f32[24,256]{1,0:T(8,128)S(1)}, f32[24,256]{1,0:T(8,128)S(1)}, u32[]{:S(2)}, u32[]{:S(2)}) collective-permute-start(f32[24,256]{1,0:T(8,128)S(1)} %get-tuple-element.53), channel_id=1, source_target_pairs={{1,2},{2,1},{3,4},{4,3},{5,6},{6,5},{7,8},{8,7},{9,10},{10,9},{11,... | collective-permute-start | bytes 73736 | tf_op jit(solution)/shard_map/ppermute | solution.py:82

commit v24 on v23

--- a/solution.py
+++ b/solution.py
@@ -15,6 +15,7 @@
 I32 = jnp.int32
 VMEM_LIMIT = 28 * 2**20
 PIECES = 2
+EARLY = 32
 PAD = 8
 CHUNK = 64
 
@@ -125,6 +126,7 @@
 
 def pack_kernel(
     grid_hbm,
+    cot_hbm,
     window_hbm,
     side_src_hbm,
     side_dst_hbm,
@@ -136,6 +138,7 @@
     chip_out,
     off_out,
     grid,
+    cot,
     window,
     side_src,
     side_dst,
@@ -162,6 +165,7 @@
             (side_count_hbm, side_count),
             (window_hbm, window),
             (grid_hbm, grid),
+            (cot_hbm.at[pl.ds(0, EARLY)], cot),
             (far_src_hbm, far_src),
             (far_dst_hbm, far_dst),
             (far_count_hbm, far_count),
@@ -178,7 +182,8 @@
         reach = jnp.concatenate([window[...], jnp.zeros((count - 2, mesh_rows), I32)], 0)
         blank = jnp.zeros((count, channels - 2 * LANES - mesh_rows), I32)
         meta[k] = jnp.concatenate([src, dst, reach, blank], 1).astype(F32).astype(BF16)
-    copies[4].wait()
+    for copy in copies[4:6]:
+        copy.wait()
     odd = is_odd()
     outs = start_all(
         [
@@ -187,11 +192,12 @@
             for pair in (
                 (grid.at[pl.ds(pl.multiple_of(k * first, BAND), BAND)], out.at[pl.ds(0, BAND)]),
                 (meta.at[k], out.at[pl.ds(BAND, count)]),
+                (cot, out.at[pl.ds(BAND + count, EARLY)]),
             )
         ],
         out_sems,
     )
-    for copy in copies[5:8]:
+    for copy in copies[6:9]:
         copy.wait()
     slot = iota((1, slots), 1)
     receiver = jnp.where(iota((devices, slots), 0) == iota((devices, slots), 1) // depth, 1.0, 0.0)
@@ -207,7 +213,7 @@
     is_first = iota((2 * slots, half), 0) % (2 * depth) < depth
     far[:, :half] = jnp.where(is_first, rows[:, :half], rows[:, half:])
     far[:, half:] = jnp.broadcast_to(column, (2 * slots, LANES)).astype(BF16)
-    last = pltpu.make_async_copy(far, far_out, out_sems.at[4])
+    last = pltpu.make_async_copy(far, far_out, out_sems.at[6])
     last.start()
     for copy in outs + [last]:
         copy.wait()
@@ -343,6 +349,7 @@
     qkv_out,
     w_qkv,
     grad_out,
+    late_out,
     scores_out,
     products_out,
     bias_out,
@@ -382,6 +389,7 @@
 
     masks()
     copies[1].wait()
+    late_out[...] = grad_out[EARLY:]
     for i, at in enumerate(starts):
         copies[2 + i].wait()
         cols = slice(at, at + width)
@@ -495,10 +503,13 @@
     latent,
     w_out,
     w_qkv,
+    chip_first,
+    off_first,
     mesh_out_hbm,
     grad_normed,
     grad_key,
     grad_value,
+    early_grad,
     attention,
     grad_query,
     mesh_out,
@@ -524,6 +535,8 @@
             grad_key[:, cols] = mm_tn(grad_scores[p, :, 2 * m :], halves(own_qkv[:, cols], scale))
             grad_value[:, cols] = mm_tn(weights[p, :, 2 * m :], halves(own_grad[:, cols]))
         grad_normed[...] = mm_nt(grad_query[...], w_qkv[:, :channels])
+        cots = jnp.concatenate([chip_first[-EARLY:], off_first[-EARLY:]], 0)
+        early_grad[...] = mm_nt(cots, w_out[...]).astype(BF16)
 
     out.wait()
 
@@ -534,6 +547,7 @@
     off_stats,
     bias,
     near_q,
+    early_grad,
     chip_grad,
     off_grad,
     own_qkv,
@@ -559,7 +573,10 @@
         key2 = halves(own_qkv[:, channels + p * pair : channels + (p + 1) * pair])
         value2 = halves(own_qkv[:, 2 * channels + p * pair : 2 * channels + (p + 1) * pair])
         query = near_q[:, cols]
-        grad = jnp.concatenate([chip_grad[:, cols], off_grad[:, cols]], 0)
+        grad = jnp.concatenate(
+            [early_grad[:EARLY, cols], chip_grad[:, cols], early_grad[EARLY:, cols], off_grad[:, cols]],
+            0,
+        )
         return query, grad, mm_nt(key2, query), mm_nt(value2, grad)
 
     total = grad_normed[...]
@@ -633,20 +650,22 @@
     own_src, own_dst = own_src.reshape(-1, LANES), own_dst.reshape(-1, LANES)
     far_src, far_dst = far_src.reshape(1, -1), far_dst.reshape(1, -1)
     side_count, far_count = side_count.reshape(1, -1), far_count.reshape(1, -1)
-    message = ((BAND + meta_rows, channels), BF16)
+    message = ((BAND + meta_rows + EARLY, channels), BF16)
     far_block = (2 * far_slots, channels // 2 + LANES)
     far_message, chip_message, off_message = call(
         pack_kernel,
         [(far_block, BF16), message, message],
-        [grid_in, window, side_src, side_dst, side_count, far_src, far_dst, far_count],
-        hbm=range(8),
+        [grid_in, cotangent, window, side_src, side_dst, side_count, far_src, far_dst, far_count],
+        hbm=range(9),
         hbm_outs=range(3),
-        scratch=like(grid_in, window, side_src, side_dst, side_count, far_src, far_dst, far_count)
+        scratch=like(grid_in)
+        + [pltpu.VMEM((EARLY, channels), BF16)]
+        + like(window, side_src, side_dst, side_count, far_src, far_dst, far_count)
         + [
             pltpu.VMEM(far_block, BF16),
             pltpu.VMEM((2, meta_rows, channels), BF16),
-            dma(8),
-            dma(5),
+            dma(9),
+            dma(7),
         ],
         name="pack",
     )
@@ -684,9 +703,10 @@
     )
     off_normed = swap_off(off_message, "node")
     own_block = ((pairs, 2 * m, m), F32)
-    own_qkv, w_qkv, own_grad, own_scores, own_products, bias, near_bias, normed = call(
+    own_qkv, w_qkv, own_grad, late_grad, own_scores, own_products, bias, near_bias, normed = call(
         functools.partial(project_kernel, scale, pair, meta_rows),
-        [((m, 3 * channels), BF16), (w_qkv.shape, BF16), rows, own_block, own_block]
+        [((m, 3 * channels), BF16), (w_qkv.shape, BF16), rows]
+        + [((m - EARLY, channels), BF16), own_block, own_block]
         + [((m, 3 * m), F32), ((m, 2 * m), F32), rows],
         [normed, from_chip, from_off, window, own_grad, w_qkv],
         hbm=(3, 4, 5),
@@ -694,7 +714,7 @@
         name="project",
     )
     chip_normed = swap_chip(normed, "node")
-    chip_grad, off_grad = exchange(own_grad, own_grad, "node")
+    chip_grad, off_grad = exchange(late_grad, late_grad, "node")
     probs = ((pairs, 2 * m, 3 * m), BF16)
     stats, kv, weights, grad_scores, near_q, w_out, cotangent = call(
         functools.partial(attend_kernel, scale, pair),
@@ -714,13 +734,14 @@
         name="attend",
     )
     chip_stats, off_stats = exchange(stats, stats, "node")
-    mesh_out, grad_normed, grad_key, grad_value = call(
+    mesh_out, grad_normed, grad_key, grad_value, early_grad = call(
         functools.partial(product_kernel, scale, pair),
         [
             rows,
             ((m, channels), F32),
             ((m, channels), F32),
             ((m, channels), F32),
+            ((2 * EARLY, channels), BF16),
         ],
         [
             weights,
@@ -731,6 +752,8 @@
             latent,
             w_out,
             w_qkv,
+            from_chip,
+            from_off,
         ],
         hbm_outs=(0,),
         scratch=[pltpu.VMEM((m, channels), BF16)] * 3 + [dma(1)],
@@ -744,6 +767,7 @@
             off_stats,
             near_bias,
             near_q,
+            early_grad,
             chip_grad,
             off_grad,
             own_qkv,

time: 45.6 us -> 47 us (1.031)
  Pallas kernels: 23.3 us -> 24.2 us
  starting transfers between devices: 19.6 us -> 20.1 us
    pallas_call x8, Pallas kernels: 23.3 us -> 24.2 us  [call(): pl.pallas_call(kernel, out_shape=[(pltpu.HBM if i in hbm_outs else jax.Sh...]
  transfers between devices with their start and end apart: 9 -> 9, of which waited for: 1 -> 1; matrix products, arithmetic and copies ran while one was open for 0% -> 0% of each run, Pallas kernels for 36% -> 37%
where the time goes in v24:
time: 47 us; the launch traced here: 46.5 us
  Pallas kernels  24.2 us (51%)
  starting transfers between devices  20.1 us (43%)
  waiting for transfers between devices  1.48 us (3%)
  between operations  0.8 us (2%)
    pallas_call x8, Pallas kernels, call(): pl.pallas_call(kernel, out_shape=[(pltpu.HBM if i in hbm_outs else jax.Sh...  24.2 us
    ppermute x4, starting transfers between devices, swap_off(): return lax.ppermute(rows, axis, pairs)  14 us
    all_to_all x1, starting transfers between devices, body(): lax.all_to_all(far_message.reshape(devices, 2 * far_depth, far_block[1]),...  5.33 us
    all_to_all x1, waiting for transfers between devices, body(): lax.all_to_all(far_message.reshape(devices, 2 * far_depth, far_block[1]),...  1.46 us
  transfers between devices with their start and end apart: 9, of which 1 were waited for; matrix products, arithmetic and copies ran while one was open for 0% of the time, Pallas kernels for 37%

profile of v24, /device:TPU:1, one launch (start us, length us, event | category | flops | bytes accessed | tf_op | source)
XLA Modules:
  0.0 46.5 jit_solution(1704316057282798955)
XLA Ops:
  0.6 2.5 %pack.1 = (bf16[128,640]{1,0:T(8,128)(2,1)}, bf16[176,1024]{1,0:T(8,128)(2,1)}, bf16[176,1024]{1,0:T(8,128)(2,1)}) custom-call(bf16[512,1024]{1,0:T(8,128)(2,1)} %grid_hbm.3, bf16[128,1024]{1,0:T(8,128)(2,1)} %cot_hbm.5, s32[2,128]{1,0:T(2,128)} %window_hbm.3, s32[32,128]{1,0:T(8,128)} %bitcast.12, s32[32,128]{1,0:T(8,128)} %bitcast.13, s32[1,2]{1,0:T(1,128)} %bitcast.16, ...), custom_call_target="tpu_custom_call" | custom-call | tf_op jit(solution)/shard_map/pack/pallas_call | solution.py:50
  3.1 0.1 collective-permute-start
  3.2 4.5 %collective-permute-start.1 = (bf16[176,1024]{1,0:T(8,128)(2,1)}, bf16[176,1024]{1,0:T(8,128)(2,1)S(1)}, u32[]{:S(2)}, u32[]{:S(2)}) collective-permute-start(bf16[176,1024]{1,0:T(8,128)(2,1)} %get-tuple-element.37), channel_id=1, source_target_pairs={{1,2},{2,1},{3,4},{4,3},{5,6},{6,5},{7,8},{8,7},{9,10},{10,9},{11,... | collective-permute-start | bytes 1081352 | tf_op jit(solution)/shard_map/ppermute | solution.py:83
  7.7 5.3 %all-to-all-start = ((bf16[16,8,640]{2,1,0:T(8,128)(2,1)}), bf16[16,8,640]{2,1,0:T(8,128)(2,1)S(1)}, u32[]{:S(2)}, u32[]{:S(2)}) async-start(bf16[16,8,640]{2,1,0:T(8,128)(2,1)} %bitcast.11), calls=%async_computation | async-start | bytes 327680 | tf_op jit(solution)/shard_map/all_to_all | solution.py:673
  13.1 4.5 %own.1 = (f32[128,1024]{1,0:T(8,128)S(1)}, bf16[128,1024]{1,0:T(8,128)(2,1)}, bf16[1024,1024]{1,0:T(8,128)(2,1)S(1)}) custom-call(bf16[512,1024]{1,0:T(8,128)(2,1)} %grid_hbm.3, bf16[128,1024]{1,0:T(8,128)(2,1)} %mesh_in_hbm.1, s32[8,128]{1,0:T(8,128)} %bitcast.14, s32[8,128]{1,0:T(8,128)} %bitcast.15, bf16[128,1024]{1,0:T(8,128)(2,1)} %cot_hbm.5, ...), custom_call_target="tpu_custom_call" | custom-call | tf_op jit(solution)/shard_map/own/pallas_call | solution.py:50
  17.5 0.0 collective-permute-done.chip.chip_first
  17.6 0.0 collective-permute-done.1.off.off_first
  17.6 1.4 %side.1.partial = f32[128,1024]{1,0:T(8,128)S(1)} custom-call(bf16[176,1024]{1,0:T(8,128)(2,1)S(1)} %collective-permute-done.chip.chip_first, bf16[176,1024]{1,0:T(8,128)(2,1)S(1)} %collective-permute-done.1.off.off_first, bf16[1024,1024]{1,0:T(8,128)(2,1)S(1)} %get-tuple-element.35.w_edge, f32[128,1024]{1,0:T(8,128)S(1)} %get-tuple-element.38.partial), custom_call_target="tpu_custom_call" | custom-call | flops 8000000000 | tf_op jit(solution)/shard_map/side/pallas_call | solution.py:50
  19.0 1.5 %all-to-all-done = bf16[16,8,640]{2,1,0:T(8,128)(2,1)S(1)} async-done(((bf16[16,8,640]{2,1,0:T(8,128)(2,1)}), bf16[16,8,640]{2,1,0:T(8,128)(2,1)S(1)}, u32[]{:S(2)}, u32[]{:S(2)}) %all-to-all-start) | async-done | bytes 163872 | tf_op jit(solution)/shard_map/all_to_all | solution.py:673
  20.5 0.9 %latent.1 = (bf16[128,1024]{1,0:T(8,128)(2,1)S(1)}, bf16[128,1024]{1,0:T(8,128)(2,1)S(1)}, bf16[136,1024]{1,0:T(8,128)(2,1)S(1)}, f32[128,1024]{1,0:T(8,128)S(1)}, f32[128,128]{1,0:T(8,128)S(1)}) custom-call(bf16[128,640]{1,0:T(8,128)(2,1)S(1)} %bitcast.10, bf16[1024,1024]{1,0:T(8,128)(2,1)S(1)} %get-tuple-element.35.w_edge, f32[128,1024]{1,0:T(8,128)S(1)} %side.1.partial), custom_call_target="tpu_custom_call" | custom-call | tf_op jit(solution)/shard_map/latent/pallas_call | solution.py:50
  21.4 2.6 %collective-permute-start.3 = (bf16[136,1024]{1,0:T(8,128)(2,1)S(1)}, bf16[136,1024]{1,0:T(8,128)(2,1)S(1)}, u32[]{:S(2)}, u32[]{:S(2)}) collective-permute-start(bf16[136,1024]{1,0:T(8,128)(2,1)S(1)} %get-tuple-element.42), channel_id=1, source_target_pairs={{1,2},{2,1},{3,4},{4,3},{5,6},{6,5},{7,8},{8,7},{9,10},{10,9},{11,... | collective-permute-start | bytes 835592 | tf_op jit(solution)/shard_map/ppermute | solution.py:83
  24.0 4.2 %project.1 = (bf16[128,3072]{1,0:T(8,128)(2,1)S(1)}, bf16[1024,3072]{1,0:T(8,128)(2,1)S(1)}, bf16[128,1024]{1,0:T(8,128)(2,1)S(1)}, bf16[96,1024]{1,0:T(8,128)(2...) custom-call(bf16[128,1024]{1,0:T(8,128)(2,1)S(1)} %get-tuple-element, ...), custom_call_target="tpu_custom_call" | custom-call | tf_op jit(solution)/shard_map/project/pallas_call | solution.py:50
  28.3 0.1 collective-permute-start.2
  28.4 0.5 %collective-permute-start.6 = (bf16[96,1024]{1,0:T(8,128)(2,1)S(1)}, bf16[96,1024]{1,0:T(8,128)(2,1)S(1)}, u32[]{:S(2)}, u32[]{:S(2)}) collective-permute-start(bf16[96,1024]{1,0:T(8,128)(2,1)S(1)} %get-tuple-element.59), channel_id=1, source_target_pairs={{0,1},{1,0},{2,3},{3,2},{4,5},{5,4},{6,7},{7,6},{8,9},{9,8},{10,11... | collective-permute-start | bytes 589832 | tf_op jit(solution)/shard_map/ppermute | solution.py:88
  28.9 2.9 %collective-permute-start.7 = (bf16[96,1024]{1,0:T(8,128)(2,1)S(1)}, bf16[96,1024]{1,0:T(8,128)(2,1)S(1)}, u32[]{:S(2)}, u32[]{:S(2)}) collective-permute-start(bf16[96,1024]{1,0:T(8,128)(2,1)S(1)} %get-tuple-element.59), channel_id=1, source_target_pairs={{1,2},{2,1},{3,4},{4,3},{5,6},{6,5},{7,8},{8,7},{9,10},{10,9},{11,... | collective-permute-start | bytes 589832 | tf_op jit(solution)/shard_map/ppermute | solution.py:83
  31.8 0.0 collective-permute-done.2.chip_normed
  31.8 0.0 collective-permute-done.3.off_normed
  31.8 3.6 %attend.1 = (f32[24,256]{1,0:T(8,128)S(1)}, bf16[384,2048]{1,0:T(8,128)(2,1)S(1)}, bf16[8,256,384]{2,1,0:T(8,128)(2,1)S(1)}, bf16[8,256,384]{2,1,0:T(8,128)(2,1)...) custom-call(bf16[128,1024]{1,0:T(8,128)(2,1)S(1)} %collective-permute-done.2.chip, ...), custom_call_target="tpu_custom_call" | custom-call | tf_op jit(solution)/shard_map/attend/pallas_call | solution.py:50
  35.4 0.1 collective-permute-start.4
  35.5 3.9 %collective-permute-start.5 = (f32[24,256]{1,0:T(8,128)S(1)}, f32[24,256]{1,0:T(8,128)S(1)}, u32[]{:S(2)}, u32[]{:S(2)}) collective-permute-start(f32[24,256]{1,0:T(8,128)S(1)} %get-tuple-element.55), channel_id=1, source_target_pairs={{1,2},{2,1},{3,4},{4,3},{5,6},{6,5},{7,8},{8,7},{9,10},{10,9},{11,... | collective-permute-start | bytes 73736 | tf_op jit(solution)/shard_map/ppermute | solution.py:83
  39.4 3.3 %product.1 = (bf16[128,1024]{1,0:T(8,128)(2,1)}, f32[128,1024]{1,0:T(8,128)S(1)}, f32[128,1024]{1,0:T(8,128)S(1)}, f32[128,1024]{1,0:T(8,128)S(1)}, bf16[64,1024]{1,0:T(8,128)(2,1)S(1)}) custom-call(bf16[8,256,384]{2,1,0:T(8,128)(2,1)S(1)} %get-tuple-element.49.weights, bf16[8,256,384]{2,1,0:T(8,128)(2,1)S(1)} %get-tuple-element.50.grad_scores, ...), custom_call_target="tpu_custom_call" | custom-call | tf_op jit(solution)/shard_map/product/pallas_call | solution.py:50
  42.7 0.0 collective-permute-done.6.chip_grad
  42.7 0.0 collective-permute-done.7.off_grad
  42.7 0.0 collective-permute-done.4.chip_stats
  42.7 0.0 collective-permute-done.5.off_stats
  42.7 3.8 %finish.1 = bf16[128,1024]{1,0:T(8,128)(2,1)} custom-call(f32[24,256]{1,0:T(8,128)S(1)} %collective-permute-done.4.chip_stats, f32[24,256]{1,0:T(8,128)S(1)} %collective-permute-done.5.off_stats, f32[128,256]{1,0:T(8,128)S(1)} %get-tuple-element.56.bias, bf16[256,1024]{1,0:T(8,128)(2,1)S(1)} %get-tuple-element.57.near_q, ...), custom_call_target="tpu_custom_call" | custom-call | tf_op jit(solution)/shard_map/finish/pallas_call | solution.py:50
Async XLA Ops:
  3.1 14.4 %collective-permute-start = (bf16[176,1024]{1,0:T(8,128)(2,1)}, bf16[176,1024]{1,0:T(8,128)(2,1)S(1)}, u32[]{:S(2)}, u32[]{:S(2)}) collective-permute-start(bf16[176,1024]{1,0:T(8,128)(2,1)} %get-tuple-element.36), channel_id=1, source_target_pairs={{0,1},{1,0},{2,3},{3,2},{4,5},{5,4},{6,7},{7,6},{8,9},{9,8},{10,11... | collective-permute-start | bytes 1081352 | tf_op jit(solution)/shard_map/ppermute | solution.py:88
  3.2 14.3 %collective-permute-start.1 = (bf16[176,1024]{1,0:T(8,128)(2,1)}, bf16[176,1024]{1,0:T(8,128)(2,1)S(1)}, u32[]{:S(2)}, u32[]{:S(2)}) collective-permute-start(bf16[176,1024]{1,0:T(8,128)(2,1)} %get-tuple-element.37), channel_id=1, source_target_pairs={{1,2},{2,1},{3,4},{4,3},{5,6},{6,5},{7,8},{8,7},{9,10},{10,9},{11,... | collective-permute-start | bytes 1081352 | tf_op jit(solution)/shard_map/ppermute | solution.py:83
  7.7 12.7 %all-to-all-start = ((bf16[16,8,640]{2,1,0:T(8,128)(2,1)}), bf16[16,8,640]{2,1,0:T(8,128)(2,1)S(1)}, u32[]{:S(2)}, u32[]{:S(2)}) async-start(bf16[16,8,640]{2,1,0:T(8,128)(2,1)} %bitcast.11), calls=%async_computation | async-start | bytes 327680 | tf_op jit(solution)/shard_map/all_to_all | solution.py:673
  21.4 10.4 %collective-permute-start.3 = (bf16[136,1024]{1,0:T(8,128)(2,1)S(1)}, bf16[136,1024]{1,0:T(8,128)(2,1)S(1)}, u32[]{:S(2)}, u32[]{:S(2)}) collective-permute-start(bf16[136,1024]{1,0:T(8,128)(2,1)S(1)} %get-tuple-element.42), channel_id=1, source_target_pairs={{1,2},{2,1},{3,4},{4,3},{5,6},{6,5},{7,8},{8,7},{9,10},{10,9},{11,... | collective-permute-start | bytes 835592 | tf_op jit(solution)/shard_map/ppermute | solution.py:83
  28.3 3.5 %collective-permute-start.2 = (bf16[128,1024]{1,0:T(8,128)(2,1)S(1)}, bf16[128,1024]{1,0:T(8,128)(2,1)S(1)}, u32[]{:S(2)}, u32[]{:S(2)}) collective-permute-start(bf16[128,1024]{1,0:T(8,128)(2,1)S(1)} %get-tuple-element.41), channel_id=1, source_target_pairs={{0,1},{1,0},{2,3},{3,2},{4,5},{5,4},{6,7},{7,6},{8,9},{9,8},{10,11... | collective-permute-start | bytes 786440 | tf_op jit(solution)/shard_map/ppermute | solution.py:88
  28.4 14.3 %collective-permute-start.6 = (bf16[96,1024]{1,0:T(8,128)(2,1)S(1)}, bf16[96,1024]{1,0:T(8,128)(2,1)S(1)}, u32[]{:S(2)}, u32[]{:S(2)}) collective-permute-start(bf16[96,1024]{1,0:T(8,128)(2,1)S(1)} %get-tuple-element.59), channel_id=1, source_target_pairs={{0,1},{1,0},{2,3},{3,2},{4,5},{5,4},{6,7},{7,6},{8,9},{9,8},{10,11... | collective-permute-start | bytes 589832 | tf_op jit(solution)/shard_map/ppermute | solution.py:88
  28.9 13.8 %collective-permute-start.7 = (bf16[96,1024]{1,0:T(8,128)(2,1)S(1)}, bf16[96,1024]{1,0:T(8,128)(2,1)S(1)}, u32[]{:S(2)}, u32[]{:S(2)}) collective-permute-start(bf16[96,1024]{1,0:T(8,128)(2,1)S(1)} %get-tuple-element.59), channel_id=1, source_target_pairs={{1,2},{2,1},{3,4},{4,3},{5,6},{6,5},{7,8},{8,7},{9,10},{10,9},{11,... | collective-permute-start | bytes 589832 | tf_op jit(solution)/shard_map/ppermute | solution.py:83
  35.4 7.3 %collective-permute-start.4 = (f32[24,256]{1,0:T(8,128)S(1)}, f32[24,256]{1,0:T(8,128)S(1)}, u32[]{:S(2)}, u32[]{:S(2)}) collective-permute-start(f32[24,256]{1,0:T(8,128)S(1)} %get-tuple-element.55), channel_id=1, source_target_pairs={{0,1},{1,0},{2,3},{3,2},{4,5},{5,4},{6,7},{7,6},{8,9},{9,8},{10,11... | collective-permute-start | bytes 73736 | tf_op jit(solution)/shard_map/ppermute | solution.py:88
  35.5 7.2 %collective-permute-start.5 = (f32[24,256]{1,0:T(8,128)S(1)}, f32[24,256]{1,0:T(8,128)S(1)}, u32[]{:S(2)}, u32[]{:S(2)}) collective-permute-start(f32[24,256]{1,0:T(8,128)S(1)} %get-tuple-element.55), channel_id=1, source_target_pairs={{1,2},{2,1},{3,4},{4,3},{5,6},{6,5},{7,8},{8,7},{9,10},{10,9},{11,... | collective-permute-start | bytes 73736 | tf_op jit(solution)/shard_map/ppermute | solution.py:83

commit v25 on v23

--- a/solution.py
+++ b/solution.py
@@ -563,7 +563,7 @@
         return query, grad, mm_nt(key2, query), mm_nt(value2, grad)
 
     total = grad_normed[...]
-    group = 2
+    group = pairs // 2
     gks, gvs = [], []
     ahead = multiply(0)
     for p in range(pairs):

time: 45.6 us -> 45.3 us (level)
  no operation moved by 1% of the time
where the time goes in v25:
time: 45.3 us; the launch traced here: 44.9 us
  Pallas kernels  23 us (51%)
  starting transfers between devices  19.6 us (43%)
  waiting for transfers between devices  1.48 us (3%)
  between operations  0.8 us (2%)
    pallas_call x8, Pallas kernels, call(): pl.pallas_call(kernel, out_shape=[(pltpu.HBM if i in hbm_outs else jax.Sh...  23 us
    ppermute x4, starting transfers between devices, swap_off(): return lax.ppermute(rows, axis, pairs)  13.5 us
    all_to_all x1, starting transfers between devices, body(): lax.all_to_all(far_message.reshape(devices, 2 * far_depth, far_block[1]),...  5.33 us
    all_to_all x1, waiting for transfers between devices, body(): lax.all_to_all(far_message.reshape(devices, 2 * far_depth, far_block[1]),...  1.46 us
  transfers between devices with their start and end apart: 9, of which 1 were waited for; matrix products, arithmetic and copies ran while one was open for 0% of the time, Pallas kernels for 36%

profile of v25, /device:TPU:1, one launch (start us, length us, event | category | flops | bytes accessed | tf_op | source)
XLA Modules:
  0.0 44.9 jit_solution(3499012065144606594)
XLA Ops:
  0.6 2.4 %pack.1 = (bf16[128,640]{1,0:T(8,128)(2,1)}, bf16[144,1024]{1,0:T(8,128)(2,1)}, bf16[144,1024]{1,0:T(8,128)(2,1)}) custom-call(bf16[512,1024]{1,0:T(8,128)(2,1)} %grid_hbm.3, s32[2,128]{1,0:T(2,128)} %window_hbm.3, s32[32,128]{1,0:T(8,128)} %bitcast.12, s32[32,128]{1,0:T(8,128)} %bitcast.13, s32[1,2]{1,0:T(1,128)} %bitcast.16, s32[1,64]{1,0:T(1,128)} %bitcast.17, ...), custom_call_target="tpu_custom_call" | custom-call | tf_op jit(solution)/shard_map/pack/pallas_call | solution.py:49
  3.1 0.1 collective-permute-start
  3.2 4.5 %collective-permute-start.1 = (bf16[144,1024]{1,0:T(8,128)(2,1)}, bf16[144,1024]{1,0:T(8,128)(2,1)S(1)}, u32[]{:S(2)}, u32[]{:S(2)}) collective-permute-start(bf16[144,1024]{1,0:T(8,128)(2,1)} %get-tuple-element.35), channel_id=1, source_target_pairs={{1,2},{2,1},{3,4},{4,3},{5,6},{6,5},{7,8},{8,7},{9,10},{10,9},{11,... | collective-permute-start | bytes 884744 | tf_op jit(solution)/shard_map/ppermute | solution.py:82
  7.7 5.3 %all-to-all-start = ((bf16[16,8,640]{2,1,0:T(8,128)(2,1)}), bf16[16,8,640]{2,1,0:T(8,128)(2,1)S(1)}, u32[]{:S(2)}, u32[]{:S(2)}) async-start(bf16[16,8,640]{2,1,0:T(8,128)(2,1)} %bitcast.11), calls=%async_computation | async-start | bytes 327680 | tf_op jit(solution)/shard_map/all_to_all | solution.py:654
  13.0 4.5 %own.1 = (f32[128,1024]{1,0:T(8,128)S(1)}, bf16[128,1024]{1,0:T(8,128)(2,1)}, bf16[1024,1024]{1,0:T(8,128)(2,1)S(1)}) custom-call(bf16[512,1024]{1,0:T(8,128)(2,1)} %grid_hbm.3, bf16[128,1024]{1,0:T(8,128)(2,1)} %mesh_in_hbm.1, s32[8,128]{1,0:T(8,128)} %bitcast.14, s32[8,128]{1,0:T(8,128)} %bitcast.15, bf16[128,1024]{1,0:T(8,128)(2,1)} %cot_hbm.3, ...), custom_call_target="tpu_custom_call" | custom-call | tf_op jit(solution)/shard_map/own/pallas_call | solution.py:49
  17.5 0.0 collective-permute-done.chip.chip_first
  17.5 0.0 collective-permute-done.1.off.off_first
  17.5 1.4 %side.1.partial = f32[128,1024]{1,0:T(8,128)S(1)} custom-call(bf16[144,1024]{1,0:T(8,128)(2,1)S(1)} %collective-permute-done.chip.chip_first, bf16[144,1024]{1,0:T(8,128)(2,1)S(1)} %collective-permute-done.1.off.off_first, bf16[1024,1024]{1,0:T(8,128)(2,1)S(1)} %get-tuple-element.33.w_edge, f32[128,1024]{1,0:T(8,128)S(1)} %get-tuple-element.36.partial), custom_call_target="tpu_custom_call" | custom-call | flops 8000000000 | tf_op jit(solution)/shard_map/side/pallas_call | solution.py:49
  19.0 1.5 %all-to-all-done = bf16[16,8,640]{2,1,0:T(8,128)(2,1)S(1)} async-done(((bf16[16,8,640]{2,1,0:T(8,128)(2,1)}), bf16[16,8,640]{2,1,0:T(8,128)(2,1)S(1)}, u32[]{:S(2)}, u32[]{:S(2)}) %all-to-all-start) | async-done | bytes 163872 | tf_op jit(solution)/shard_map/all_to_all | solution.py:654
  20.4 0.9 %latent.1 = (bf16[128,1024]{1,0:T(8,128)(2,1)S(1)}, bf16[128,1024]{1,0:T(8,128)(2,1)S(1)}, bf16[136,1024]{1,0:T(8,128)(2,1)S(1)}, f32[128,1024]{1,0:T(8,128)S(1)}, f32[128,128]{1,0:T(8,128)S(1)}) custom-call(bf16[128,640]{1,0:T(8,128)(2,1)S(1)} %bitcast.10, bf16[1024,1024]{1,0:T(8,128)(2,1)S(1)} %get-tuple-element.33.w_edge, f32[128,1024]{1,0:T(8,128)S(1)} %side.1.partial), custom_call_target="tpu_custom_call" | custom-call | tf_op jit(solution)/shard_map/latent/pallas_call | solution.py:49
  21.4 2.1 %collective-permute-start.3 = (bf16[136,1024]{1,0:T(8,128)(2,1)S(1)}, bf16[136,1024]{1,0:T(8,128)(2,1)S(1)}, u32[]{:S(2)}, u32[]{:S(2)}) collective-permute-start(bf16[136,1024]{1,0:T(8,128)(2,1)S(1)} %get-tuple-element.40), channel_id=1, source_target_pairs={{1,2},{2,1},{3,4},{4,3},{5,6},{6,5},{7,8},{8,7},{9,10},{10,9},{11,... | collective-permute-start | bytes 835592 | tf_op jit(solution)/shard_map/ppermute | solution.py:82
  23.5 4.2 %project.1 = (bf16[128,3072]{1,0:T(8,128)(2,1)S(1)}, bf16[1024,3072]{1,0:T(8,128)(2,1)S(1)}, bf16[128,1024]{1,0:T(8,128)(2,1)S(1)}, f32[8,256,128]{2,1,0:T(8,128...) custom-call(bf16[128,1024]{1,0:T(8,128)(2,1)S(1)} %get-tuple-element, ...), custom_call_target="tpu_custom_call" | custom-call | tf_op jit(solution)/shard_map/project/pallas_call | solution.py:49
  27.7 0.1 collective-permute-start.2
  27.8 0.5 %collective-permute-start.6 = (bf16[128,1024]{1,0:T(8,128)(2,1)S(1)}, bf16[128,1024]{1,0:T(8,128)(2,1)S(1)}, u32[]{:S(2)}, u32[]{:S(2)}) collective-permute-start(bf16[128,1024]{1,0:T(8,128)(2,1)S(1)} %get-tuple-element.43.own_grad), channel_id=1, source_target_pairs={{0,1},{1,0},{2,3},{3,2},{4,5},{5,4},{6,7},{7,6},{8,9},{9,8},{10,11... | collective-permute-start | bytes 786440 | tf_op jit(solution)/shard_map/ppermute | solution.py:87
  28.3 3.5 %collective-permute-start.7 = (bf16[128,1024]{1,0:T(8,128)(2,1)S(1)}, bf16[128,1024]{1,0:T(8,128)(2,1)S(1)}, u32[]{:S(2)}, u32[]{:S(2)}) collective-permute-start(bf16[128,1024]{1,0:T(8,128)(2,1)S(1)} %get-tuple-element.43.own_grad), channel_id=1, source_target_pairs={{1,2},{2,1},{3,4},{4,3},{5,6},{6,5},{7,8},{8,7},{9,10},{10,9},{11,... | collective-permute-start | bytes 786440 | tf_op jit(solution)/shard_map/ppermute | solution.py:82
  31.7 0.0 collective-permute-done.2.chip_normed
  31.7 0.0 collective-permute-done.3.off_normed
  31.8 3.4 %attend.1 = (f32[24,256]{1,0:T(8,128)S(1)}, bf16[384,2048]{1,0:T(8,128)(2,1)S(1)}, bf16[8,256,384]{2,1,0:T(8,128)(2,1)S(1)}, bf16[8,256,384]{2,1,0:T(8,128)(2,1)...) custom-call(bf16[128,1024]{1,0:T(8,128)(2,1)S(1)} %collective-permute-done.2.chip, ...), custom_call_target="tpu_custom_call" | custom-call | tf_op jit(solution)/shard_map/attend/pallas_call | solution.py:49
  35.2 0.1 collective-permute-start.4
  35.2 3.5 %collective-permute-start.5 = (f32[24,256]{1,0:T(8,128)S(1)}, f32[24,256]{1,0:T(8,128)S(1)}, u32[]{:S(2)}, u32[]{:S(2)}) collective-permute-start(f32[24,256]{1,0:T(8,128)S(1)} %get-tuple-element.53), channel_id=1, source_target_pairs={{1,2},{2,1},{3,4},{4,3},{5,6},{6,5},{7,8},{8,7},{9,10},{10,9},{11,... | collective-permute-start | bytes 73736 | tf_op jit(solution)/shard_map/ppermute | solution.py:82
  38.7 2.6 %product.1 = (bf16[128,1024]{1,0:T(8,128)(2,1)}, f32[128,1024]{1,0:T(8,128)S(1)}, f32[128,1024]{1,0:T(8,128)S(1)}, f32[128,1024]{1,0:T(8,128)S(1)}) custom-call(bf16[8,256,384]{2,1,0:T(8,128)(2,1)S(1)} %get-tuple-element.47.weights, bf16[8,256,384]{2,1,0:T(8,128)(2,1)S(1)} %get-tuple-element.48.grad_scores, bf16[384,2048]{1,0:T(8,128)(2,1)S(1)} %get-tuple-element.49.kv, ...), custom_call_target="tpu_custom_call" | custom-call | tf_op jit(solution)/shard_map/product/pallas_call | solution.py:49
  41.3 0.0 collective-permute-done.6.chip_grad
  41.4 0.0 collective-permute-done.7.off_grad
  41.4 0.0 collective-permute-done.4.chip_stats
  41.4 0.0 collective-permute-done.5.off_stats
  41.4 3.5 %finish.1 = bf16[128,1024]{1,0:T(8,128)(2,1)} custom-call(f32[24,256]{1,0:T(8,128)S(1)} %collective-permute-done.4.chip_stats, f32[24,256]{1,0:T(8,128)S(1)} %collective-permute-done.5.off_stats, f32[128,256]{1,0:T(8,128)S(1)} %get-tuple-element.54.bias, bf16[256,1024]{1,0:T(8,128)(2,1)S(1)} %get-tuple-element.55.near_q, ...), custom_call_target="tpu_custom_call" | custom-call | tf_op jit(solution)/shard_map/finish/pallas_call | solution.py:49
Async XLA Ops:
  3.1 14.4 %collective-permute-start = (bf16[144,1024]{1,0:T(8,128)(2,1)}, bf16[144,1024]{1,0:T(8,128)(2,1)S(1)}, u32[]{:S(2)}, u32[]{:S(2)}) collective-permute-start(bf16[144,1024]{1,0:T(8,128)(2,1)} %get-tuple-element.34), channel_id=1, source_target_pairs={{0,1},{1,0},{2,3},{3,2},{4,5},{5,4},{6,7},{7,6},{8,9},{9,8},{10,11... | collective-permute-start | bytes 884744 | tf_op jit(solution)/shard_map/ppermute | solution.py:87
  3.2 14.3 %collective-permute-start.1 = (bf16[144,1024]{1,0:T(8,128)(2,1)}, bf16[144,1024]{1,0:T(8,128)(2,1)S(1)}, u32[]{:S(2)}, u32[]{:S(2)}) collective-permute-start(bf16[144,1024]{1,0:T(8,128)(2,1)} %get-tuple-element.35), channel_id=1, source_target_pairs={{1,2},{2,1},{3,4},{4,3},{5,6},{6,5},{7,8},{8,7},{9,10},{10,9},{11,... | collective-permute-start | bytes 884744 | tf_op jit(solution)/shard_map/ppermute | solution.py:82
  7.7 12.7 %all-to-all-start = ((bf16[16,8,640]{2,1,0:T(8,128)(2,1)}), bf16[16,8,640]{2,1,0:T(8,128)(2,1)S(1)}, u32[]{:S(2)}, u32[]{:S(2)}) async-start(bf16[16,8,640]{2,1,0:T(8,128)(2,1)} %bitcast.11), calls=%async_computation | async-start | bytes 327680 | tf_op jit(solution)/shard_map/all_to_all | solution.py:654
  21.4 10.4 %collective-permute-start.3 = (bf16[136,1024]{1,0:T(8,128)(2,1)S(1)}, bf16[136,1024]{1,0:T(8,128)(2,1)S(1)}, u32[]{:S(2)}, u32[]{:S(2)}) collective-permute-start(bf16[136,1024]{1,0:T(8,128)(2,1)S(1)} %get-tuple-element.40), channel_id=1, source_target_pairs={{1,2},{2,1},{3,4},{4,3},{5,6},{6,5},{7,8},{8,7},{9,10},{10,9},{11,... | collective-permute-start | bytes 835592 | tf_op jit(solution)/shard_map/ppermute | solution.py:82
  27.7 4.0 %collective-permute-start.2 = (bf16[128,1024]{1,0:T(8,128)(2,1)S(1)}, bf16[128,1024]{1,0:T(8,128)(2,1)S(1)}, u32[]{:S(2)}, u32[]{:S(2)}) collective-permute-start(bf16[128,1024]{1,0:T(8,128)(2,1)S(1)} %get-tuple-element.39), channel_id=1, source_target_pairs={{0,1},{1,0},{2,3},{3,2},{4,5},{5,4},{6,7},{7,6},{8,9},{9,8},{10,11... | collective-permute-start | bytes 786440 | tf_op jit(solution)/shard_map/ppermute | solution.py:87
  27.8 13.6 %collective-permute-start.6 = (bf16[128,1024]{1,0:T(8,128)(2,1)S(1)}, bf16[128,1024]{1,0:T(8,128)(2,1)S(1)}, u32[]{:S(2)}, u32[]{:S(2)}) collective-permute-start(bf16[128,1024]{1,0:T(8,128)(2,1)S(1)} %get-tuple-element.43.own_grad), channel_id=1, source_target_pairs={{0,1},{1,0},{2,3},{3,2},{4,5},{5,4},{6,7},{7,6},{8,9},{9,8},{10,11... | collective-permute-start | bytes 786440 | tf_op jit(solution)/shard_map/ppermute | solution.py:87
  28.3 13.1 %collective-permute-start.7 = (bf16[128,1024]{1,0:T(8,128)(2,1)S(1)}, bf16[128,1024]{1,0:T(8,128)(2,1)S(1)}, u32[]{:S(2)}, u32[]{:S(2)}) collective-permute-start(bf16[128,1024]{1,0:T(8,128)(2,1)S(1)} %get-tuple-element.43.own_grad), channel_id=1, source_target_pairs={{1,2},{2,1},{3,4},{4,3},{5,6},{6,5},{7,8},{8,7},{9,10},{10,9},{11,... | collective-permute-start | bytes 786440 | tf_op jit(solution)/shard_map/ppermute | solution.py:82
  35.2 6.2 %collective-permute-start.4 = (f32[24,256]{1,0:T(8,128)S(1)}, f32[24,256]{1,0:T(8,128)S(1)}, u32[]{:S(2)}, u32[]{:S(2)}) collective-permute-start(f32[24,256]{1,0:T(8,128)S(1)} %get-tuple-element.53), channel_id=1, source_target_pairs={{0,1},{1,0},{2,3},{3,2},{4,5},{5,4},{6,7},{7,6},{8,9},{9,8},{10,11... | collective-permute-start | bytes 73736 | tf_op jit(solution)/shard_map/ppermute | solution.py:87
  35.2 6.1 %collective-permute-start.5 = (f32[24,256]{1,0:T(8,128)S(1)}, f32[24,256]{1,0:T(8,128)S(1)}, u32[]{:S(2)}, u32[]{:S(2)}) collective-permute-start(f32[24,256]{1,0:T(8,128)S(1)} %get-tuple-element.53), channel_id=1, source_target_pairs={{1,2},{2,1},{3,4},{4,3},{5,6},{6,5},{7,8},{8,7},{9,10},{10,9},{11,... | collective-permute-start | bytes 73736 | tf_op jit(solution)/shard_map/ppermute | solution.py:82

commit v26 on v25

--- a/solution.py
+++ b/solution.py
@@ -563,7 +563,7 @@
         return query, grad, mm_nt(key2, query), mm_nt(value2, grad)
 
     total = grad_normed[...]
-    group = pairs // 2
+    group_ends = (pairs * 3 // 4, pairs)
     gks, gvs = [], []
     ahead = multiply(0)
     for p in range(pairs):
@@ -585,9 +585,9 @@
         gv = grad_value[:, cols] + merge(mm(jnp.concatenate(weights, 0), grad))
         gks.append(gk.astype(BF16))
         gvs.append(gv.astype(BF16))
-        if len(gks) == group:
-            at = channels + (p + 1 - group) * pair
-            width = group * pair
+        if p + 1 in group_ends:
+            at = channels + (p + 1 - len(gks)) * pair
+            width = len(gks) * pair
             for blocks, start in ((gks, at), (gvs, at + channels)):
                 total = total + mm_nt(
                     jnp.concatenate(blocks, 1), w_qkv[:, start : start + width]

time: 45.3 us -> 45.5 us (level)
  no operation moved by 1% of the time
where the time goes in v26:
time: 45.5 us; the launch traced here: 45.1 us
  Pallas kernels  23.2 us (51%)
  starting transfers between devices  19.6 us (43%)
  waiting for transfers between devices  1.48 us (3%)
  between operations  0.8 us (2%)
    pallas_call x8, Pallas kernels, call(): pl.pallas_call(kernel, out_shape=[(pltpu.HBM if i in hbm_outs else jax.Sh...  23.2 us
    ppermute x4, starting transfers between devices, swap_off(): return lax.ppermute(rows, axis, pairs)  13.5 us
    all_to_all x1, starting transfers between devices, body(): lax.all_to_all(far_message.reshape(devices, 2 * far_depth, far_block[1]),...  5.33 us
    all_to_all x1, waiting for transfers between devices, body(): lax.all_to_all(far_message.reshape(devices, 2 * far_depth, far_block[1]),...  1.46 us
  transfers between devices with their start and end apart: 9, of which 1 were waited for; matrix products, arithmetic and copies ran while one was open for 0% of the time, Pallas kernels for 36%

profile of v26, /device:TPU:1, one launch (start us, length us, event | category | flops | bytes accessed | tf_op | source)
XLA Modules:
  0.0 45.1 jit_solution(12007422525608357802)
XLA Ops:
  0.6 2.4 %pack.1 = (bf16[128,640]{1,0:T(8,128)(2,1)}, bf16[144,1024]{1,0:T(8,128)(2,1)}, bf16[144,1024]{1,0:T(8,128)(2,1)}) custom-call(bf16[512,1024]{1,0:T(8,128)(2,1)} %grid_hbm.3, s32[2,128]{1,0:T(2,128)} %window_hbm.3, s32[32,128]{1,0:T(8,128)} %bitcast.12, s32[32,128]{1,0:T(8,128)} %bitcast.13, s32[1,2]{1,0:T(1,128)} %bitcast.16, s32[1,64]{1,0:T(1,128)} %bitcast.17, ...), custom_call_target="tpu_custom_call" | custom-call | tf_op jit(solution)/shard_map/pack/pallas_call | solution.py:49
  3.1 0.1 collective-permute-start
  3.2 4.5 %collective-permute-start.1 = (bf16[144,1024]{1,0:T(8,128)(2,1)}, bf16[144,1024]{1,0:T(8,128)(2,1)S(1)}, u32[]{:S(2)}, u32[]{:S(2)}) collective-permute-start(bf16[144,1024]{1,0:T(8,128)(2,1)} %get-tuple-element.35), channel_id=1, source_target_pairs={{1,2},{2,1},{3,4},{4,3},{5,6},{6,5},{7,8},{8,7},{9,10},{10,9},{11,... | collective-permute-start | bytes 884744 | tf_op jit(solution)/shard_map/ppermute | solution.py:82
  7.7 5.3 %all-to-all-start = ((bf16[16,8,640]{2,1,0:T(8,128)(2,1)}), bf16[16,8,640]{2,1,0:T(8,128)(2,1)S(1)}, u32[]{:S(2)}, u32[]{:S(2)}) async-start(bf16[16,8,640]{2,1,0:T(8,128)(2,1)} %bitcast.11), calls=%async_computation | async-start | bytes 327680 | tf_op jit(solution)/shard_map/all_to_all | solution.py:654
  13.0 4.5 %own.1 = (f32[128,1024]{1,0:T(8,128)S(1)}, bf16[128,1024]{1,0:T(8,128)(2,1)}, bf16[1024,1024]{1,0:T(8,128)(2,1)S(1)}) custom-call(bf16[512,1024]{1,0:T(8,128)(2,1)} %grid_hbm.3, bf16[128,1024]{1,0:T(8,128)(2,1)} %mesh_in_hbm.1, s32[8,128]{1,0:T(8,128)} %bitcast.14, s32[8,128]{1,0:T(8,128)} %bitcast.15, bf16[128,1024]{1,0:T(8,128)(2,1)} %cot_hbm.3, ...), custom_call_target="tpu_custom_call" | custom-call | tf_op jit(solution)/shard_map/own/pallas_call | solution.py:49
  17.5 0.0 collective-permute-done.chip.chip_first
  17.5 0.0 collective-permute-done.1.off.off_first
  17.5 1.4 %side.1.partial = f32[128,1024]{1,0:T(8,128)S(1)} custom-call(bf16[144,1024]{1,0:T(8,128)(2,1)S(1)} %collective-permute-done.chip.chip_first, bf16[144,1024]{1,0:T(8,128)(2,1)S(1)} %collective-permute-done.1.off.off_first, bf16[1024,1024]{1,0:T(8,128)(2,1)S(1)} %get-tuple-element.33.w_edge, f32[128,1024]{1,0:T(8,128)S(1)} %get-tuple-element.36.partial), custom_call_target="tpu_custom_call" | custom-call | flops 8000000000 | tf_op jit(solution)/shard_map/side/pallas_call | solution.py:49
  19.0 1.5 %all-to-all-done = bf16[16,8,640]{2,1,0:T(8,128)(2,1)S(1)} async-done(((bf16[16,8,640]{2,1,0:T(8,128)(2,1)}), bf16[16,8,640]{2,1,0:T(8,128)(2,1)S(1)}, u32[]{:S(2)}, u32[]{:S(2)}) %all-to-all-start) | async-done | bytes 163872 | tf_op jit(solution)/shard_map/all_to_all | solution.py:654
  20.4 0.9 %latent.1 = (bf16[128,1024]{1,0:T(8,128)(2,1)S(1)}, bf16[128,1024]{1,0:T(8,128)(2,1)S(1)}, bf16[136,1024]{1,0:T(8,128)(2,1)S(1)}, f32[128,1024]{1,0:T(8,128)S(1)}, f32[128,128]{1,0:T(8,128)S(1)}) custom-call(bf16[128,640]{1,0:T(8,128)(2,1)S(1)} %bitcast.10, bf16[1024,1024]{1,0:T(8,128)(2,1)S(1)} %get-tuple-element.33.w_edge, f32[128,1024]{1,0:T(8,128)S(1)} %side.1.partial), custom_call_target="tpu_custom_call" | custom-call | tf_op jit(solution)/shard_map/latent/pallas_call | solution.py:49
  21.4 2.1 %collective-permute-start.3 = (bf16[136,1024]{1,0:T(8,128)(2,1)S(1)}, bf16[136,1024]{1,0:T(8,128)(2,1)S(1)}, u32[]{:S(2)}, u32[]{:S(2)}) collective-permute-start(bf16[136,1024]{1,0:T(8,128)(2,1)S(1)} %get-tuple-element.40), channel_id=1, source_target_pairs={{1,2},{2,1},{3,4},{4,3},{5,6},{6,5},{7,8},{8,7},{9,10},{10,9},{11,... | collective-permute-start | bytes 835592 | tf_op jit(solution)/shard_map/ppermute | solution.py:82
  23.5 4.2 %project.1 = (bf16[128,3072]{1,0:T(8,128)(2,1)S(1)}, bf16[1024,3072]{1,0:T(8,128)(2,1)S(1)}, bf16[128,1024]{1,0:T(8,128)(2,1)S(1)}, f32[8,256,128]{2,1,0:T(8,128...) custom-call(bf16[128,1024]{1,0:T(8,128)(2,1)S(1)} %get-tuple-element, ...), custom_call_target="tpu_custom_call" | custom-call | tf_op jit(solution)/shard_map/project/pallas_call | solution.py:49
  27.7 0.1 collective-permute-start.2
  27.8 0.5 %collective-permute-start.6 = (bf16[128,1024]{1,0:T(8,128)(2,1)S(1)}, bf16[128,1024]{1,0:T(8,128)(2,1)S(1)}, u32[]{:S(2)}, u32[]{:S(2)}) collective-permute-start(bf16[128,1024]{1,0:T(8,128)(2,1)S(1)} %get-tuple-element.43.own_grad), channel_id=1, source_target_pairs={{0,1},{1,0},{2,3},{3,2},{4,5},{5,4},{6,7},{7,6},{8,9},{9,8},{10,11... | collective-permute-start | bytes 786440 | tf_op jit(solution)/shard_map/ppermute | solution.py:87
  28.3 3.5 %collective-permute-start.7 = (bf16[128,1024]{1,0:T(8,128)(2,1)S(1)}, bf16[128,1024]{1,0:T(8,128)(2,1)S(1)}, u32[]{:S(2)}, u32[]{:S(2)}) collective-permute-start(bf16[128,1024]{1,0:T(8,128)(2,1)S(1)} %get-tuple-element.43.own_grad), channel_id=1, source_target_pairs={{1,2},{2,1},{3,4},{4,3},{5,6},{6,5},{7,8},{8,7},{9,10},{10,9},{11,... | collective-permute-start | bytes 786440 | tf_op jit(solution)/shard_map/ppermute | solution.py:82
  31.7 0.0 collective-permute-done.2.chip_normed
  31.7 0.0 collective-permute-done.3.off_normed
  31.8 3.4 %attend.1 = (f32[24,256]{1,0:T(8,128)S(1)}, bf16[384,2048]{1,0:T(8,128)(2,1)S(1)}, bf16[8,256,384]{2,1,0:T(8,128)(2,1)S(1)}, bf16[8,256,384]{2,1,0:T(8,128)(2,1)...) custom-call(bf16[128,1024]{1,0:T(8,128)(2,1)S(1)} %collective-permute-done.2.chip, ...), custom_call_target="tpu_custom_call" | custom-call | tf_op jit(solution)/shard_map/attend/pallas_call | solution.py:49
  35.2 0.1 collective-permute-start.4
  35.2 3.5 %collective-permute-start.5 = (f32[24,256]{1,0:T(8,128)S(1)}, f32[24,256]{1,0:T(8,128)S(1)}, u32[]{:S(2)}, u32[]{:S(2)}) collective-permute-start(f32[24,256]{1,0:T(8,128)S(1)} %get-tuple-element.53), channel_id=1, source_target_pairs={{1,2},{2,1},{3,4},{4,3},{5,6},{6,5},{7,8},{8,7},{9,10},{10,9},{11,... | collective-permute-start | bytes 73736 | tf_op jit(solution)/shard_map/ppermute | solution.py:82
  38.7 2.6 %product.1 = (bf16[128,1024]{1,0:T(8,128)(2,1)}, f32[128,1024]{1,0:T(8,128)S(1)}, f32[128,1024]{1,0:T(8,128)S(1)}, f32[128,1024]{1,0:T(8,128)S(1)}) custom-call(bf16[8,256,384]{2,1,0:T(8,128)(2,1)S(1)} %get-tuple-element.47.weights, bf16[8,256,384]{2,1,0:T(8,128)(2,1)S(1)} %get-tuple-element.48.grad_scores, bf16[384,2048]{1,0:T(8,128)(2,1)S(1)} %get-tuple-element.49.kv, ...), custom_call_target="tpu_custom_call" | custom-call | tf_op jit(solution)/shard_map/product/pallas_call | solution.py:49
  41.3 0.0 collective-permute-done.6.chip_grad
  41.4 0.0 collective-permute-done.7.off_grad
  41.4 0.0 collective-permute-done.4.chip_stats
  41.4 0.0 collective-permute-done.5.off_stats
  41.4 3.7 %finish.1 = bf16[128,1024]{1,0:T(8,128)(2,1)} custom-call(f32[24,256]{1,0:T(8,128)S(1)} %collective-permute-done.4.chip_stats, f32[24,256]{1,0:T(8,128)S(1)} %collective-permute-done.5.off_stats, f32[128,256]{1,0:T(8,128)S(1)} %get-tuple-element.54.bias, bf16[256,1024]{1,0:T(8,128)(2,1)S(1)} %get-tuple-element.55.near_q, ...), custom_call_target="tpu_custom_call" | custom-call | tf_op jit(solution)/shard_map/finish/pallas_call | solution.py:49
Async XLA Ops:
  3.1 14.4 %collective-permute-start = (bf16[144,1024]{1,0:T(8,128)(2,1)}, bf16[144,1024]{1,0:T(8,128)(2,1)S(1)}, u32[]{:S(2)}, u32[]{:S(2)}) collective-permute-start(bf16[144,1024]{1,0:T(8,128)(2,1)} %get-tuple-element.34), channel_id=1, source_target_pairs={{0,1},{1,0},{2,3},{3,2},{4,5},{5,4},{6,7},{7,6},{8,9},{9,8},{10,11... | collective-permute-start | bytes 884744 | tf_op jit(solution)/shard_map/ppermute | solution.py:87
  3.2 14.3 %collective-permute-start.1 = (bf16[144,1024]{1,0:T(8,128)(2,1)}, bf16[144,1024]{1,0:T(8,128)(2,1)S(1)}, u32[]{:S(2)}, u32[]{:S(2)}) collective-permute-start(bf16[144,1024]{1,0:T(8,128)(2,1)} %get-tuple-element.35), channel_id=1, source_target_pairs={{1,2},{2,1},{3,4},{4,3},{5,6},{6,5},{7,8},{8,7},{9,10},{10,9},{11,... | collective-permute-start | bytes 884744 | tf_op jit(solution)/shard_map/ppermute | solution.py:82
  7.7 12.7 %all-to-all-start = ((bf16[16,8,640]{2,1,0:T(8,128)(2,1)}), bf16[16,8,640]{2,1,0:T(8,128)(2,1)S(1)}, u32[]{:S(2)}, u32[]{:S(2)}) async-start(bf16[16,8,640]{2,1,0:T(8,128)(2,1)} %bitcast.11), calls=%async_computation | async-start | bytes 327680 | tf_op jit(solution)/shard_map/all_to_all | solution.py:654
  21.4 10.4 %collective-permute-start.3 = (bf16[136,1024]{1,0:T(8,128)(2,1)S(1)}, bf16[136,1024]{1,0:T(8,128)(2,1)S(1)}, u32[]{:S(2)}, u32[]{:S(2)}) collective-permute-start(bf16[136,1024]{1,0:T(8,128)(2,1)S(1)} %get-tuple-element.40), channel_id=1, source_target_pairs={{1,2},{2,1},{3,4},{4,3},{5,6},{6,5},{7,8},{8,7},{9,10},{10,9},{11,... | collective-permute-start | bytes 835592 | tf_op jit(solution)/shard_map/ppermute | solution.py:82
  27.7 4.0 %collective-permute-start.2 = (bf16[128,1024]{1,0:T(8,128)(2,1)S(1)}, bf16[128,1024]{1,0:T(8,128)(2,1)S(1)}, u32[]{:S(2)}, u32[]{:S(2)}) collective-permute-start(bf16[128,1024]{1,0:T(8,128)(2,1)S(1)} %get-tuple-element.39), channel_id=1, source_target_pairs={{0,1},{1,0},{2,3},{3,2},{4,5},{5,4},{6,7},{7,6},{8,9},{9,8},{10,11... | collective-permute-start | bytes 786440 | tf_op jit(solution)/shard_map/ppermute | solution.py:87
  27.8 13.6 %collective-permute-start.6 = (bf16[128,1024]{1,0:T(8,128)(2,1)S(1)}, bf16[128,1024]{1,0:T(8,128)(2,1)S(1)}, u32[]{:S(2)}, u32[]{:S(2)}) collective-permute-start(bf16[128,1024]{1,0:T(8,128)(2,1)S(1)} %get-tuple-element.43.own_grad), channel_id=1, source_target_pairs={{0,1},{1,0},{2,3},{3,2},{4,5},{5,4},{6,7},{7,6},{8,9},{9,8},{10,11... | collective-permute-start | bytes 786440 | tf_op jit(solution)/shard_map/ppermute | solution.py:87
  28.3 13.1 %collective-permute-start.7 = (bf16[128,1024]{1,0:T(8,128)(2,1)S(1)}, bf16[128,1024]{1,0:T(8,128)(2,1)S(1)}, u32[]{:S(2)}, u32[]{:S(2)}) collective-permute-start(bf16[128,1024]{1,0:T(8,128)(2,1)S(1)} %get-tuple-element.43.own_grad), channel_id=1, source_target_pairs={{1,2},{2,1},{3,4},{4,3},{5,6},{6,5},{7,8},{8,7},{9,10},{10,9},{11,... | collective-permute-start | bytes 786440 | tf_op jit(solution)/shard_map/ppermute | solution.py:82
  35.2 6.2 %collective-permute-start.4 = (f32[24,256]{1,0:T(8,128)S(1)}, f32[24,256]{1,0:T(8,128)S(1)}, u32[]{:S(2)}, u32[]{:S(2)}) collective-permute-start(f32[24,256]{1,0:T(8,128)S(1)} %get-tuple-element.53), channel_id=1, source_target_pairs={{0,1},{1,0},{2,3},{3,2},{4,5},{5,4},{6,7},{7,6},{8,9},{9,8},{10,11... | collective-permute-start | bytes 73736 | tf_op jit(solution)/shard_map/ppermute | solution.py:87
  35.2 6.1 %collective-permute-start.5 = (f32[24,256]{1,0:T(8,128)S(1)}, f32[24,256]{1,0:T(8,128)S(1)}, u32[]{:S(2)}, u32[]{:S(2)}) collective-permute-start(f32[24,256]{1,0:T(8,128)S(1)} %get-tuple-element.53), channel_id=1, source_target_pairs={{1,2},{2,1},{3,4},{4,3},{5,6},{6,5},{7,8},{8,7},{9,10},{10,9},{11,... | collective-permute-start | bytes 73736 | tf_op jit(solution)/shard_map/ppermute | solution.py:82
